TPU v7x, 32 devices: a whole 2x2x4 slice. The times are simulated.
32 devices in a mesh: leaf: 16 (over z, y, x), cols: 2 (over core).
Axes of the slice: x: 2, y: 2, z: 4, core: 2. Of those that a mesh axis runs over, the one named last changes fastest.
Arguments:
- points: float32 [3, 32768], P(None, 'leaf'), may hold values from 0 to 1
- samples: float32 [256, 32768], P('cols', 'leaf'), may hold values from -6 to 6
- sketch: float32 [32, 256], P(None, 'cols'), may hold values from -0.375 to 0.375
- far_requests: int32 [16, 16, 8], P('leaf'), may hold values from 0 to 31, as said below
- far_slots: int32 [512, 16], P('leaf'), may hold values from 0 to 127, as said below
- far_count: int32 [512], P('leaf'), may hold values from 1 to 16, as said below
- near_mask: int32 [512, 3], P('leaf'), may hold values 0 or 1
Outputs:
- far_sample: float32 [256, 32768], P('cols', 'leaf')
- near_sample: float32 [256, 32768], P('cols', 'leaf')
- leaf_basis: float32 [32, 32768], P(None, 'leaf')
- branch_samples: float32 [512, 256], P('leaf', 'cols')
- top_transfer: float32 [15, 64, 32], replicated
- root_sample: float32 [32, 256], P(None, 'cols')
Inputs may be any that keep to these rules, and one draw needn't show every extreme that they name: far_requests[e, d, c] is a leaf counted on device d of leaf (0 for its first); the 8 entries of each [e, d] are distinct. far_slots[i, f] names slot far_slots[i, f] mod 8 of the clusters fetched from device far_slots[i, f] // 8; only entries f < far_count[i] are used; among the 512 entries (used or not) of the leaves of one device, no device is named by more than 32 entries, and some device by exactly 32. `far_count`: used entries of each leaf's far-field list.
All inputs are finite; a program needn't handle non-finite values. No bound on the sum of `near_mask` on one device may be relied on, other than what follows from the above.
Results may differ from a plain program's by a relative error of at most 0.0003.
Values sent between devices are 32-bit elements; how exact they have to be, the bound alone decides.
No kernel may reach another device: no remote copies, remote signals or barrier semaphores. Data moves between devices by JAX's collectives and lax.ppermute only.
A program may use at most 64 MiB of HBM per device.

v0:
```python
import jax
import jax.numpy as jnp
import numpy as np
from jax import lax
from jax.sharding import PartitionSpec as P

LEAF = 64
FAR = 16
NS = 1


length_scale = 0.3
shift_share = 0.05
highest = lax.Precision.HIGHEST


def with_halo(block, sides, width):
    for axis, dim in sides:
        count = lax.axis_size(axis)
        forward = [(i, i + 1) for i in range(count - 1)]
        backward = [(target, source) for source, target in forward]
        low = lax.ppermute(
            lax.slice_in_dim(block, block.shape[dim] - width, None, axis=dim), axis, forward
        )
        high = lax.ppermute(lax.slice_in_dim(block, 0, width, axis=dim), axis, backward)
        block = jnp.concatenate([low, block, high], axis=dim)
    return block


def swapped(array, axis, stride):
    return lax.ppermute(array, axis, [(i, i ^ 1 << stride) for i in range(lax.axis_size(axis))])


def kernel_last(source_coords, target_coords):
    differences = source_coords[:, :, None, :] - target_coords[:, None, :, :]
    return jnp.exp(-jnp.sqrt(jnp.sum(differences * differences, axis=0)) / length_scale)


def factor(sketched):
    gram_matrix = jnp.einsum("nmr,nmq->nrq", sketched, sketched, precision=highest)
    order_size = gram_matrix.shape[-1]
    trace_sum = jnp.trace(gram_matrix, axis1=1, axis2=2)
    shifted = gram_matrix + (shift_share * trace_sum / order_size + 1e-06)[:, None, None] * jnp.eye(
        order_size, dtype=jnp.float32
    )
    lower_factor = jnp.linalg.cholesky(shifted)
    return jax.scipy.linalg.solve_triangular(lower_factor, jnp.swapaxes(sketched, 1, 2), lower=True)


def inner_level(current, sketch):
    stacked = current.reshape(current.shape[0] // 2, 2 * current.shape[1], current.shape[2])
    partial_value = jnp.einsum("nms,rs->nmr", stacked, sketch, precision=highest)
    summed = lax.psum(partial_value, "cols")
    transfer_t = factor(summed)
    return jnp.einsum("nrm,nms->nrs", transfer_t, stacked, precision=highest)


def on_device(points, samples, sketch, far_requests, far_slots, far_count, near_mask):
    samp_dev = samples.shape[0]
    leaves_dev = samples.shape[1] // LEAF
    rank_size = sketch.shape[0]
    coords = points.reshape(3, leaves_dev, LEAF)
    sample_blocks = samples.reshape(samp_dev, leaves_dev, LEAF)
    target_coords = jnp.transpose(coords, (0, 2, 1))
    wanted = far_requests.reshape(far_requests.shape[1], far_requests.shape[2])
    packed_samples = jnp.transpose(sample_blocks, (1, 0, 2)).reshape(leaves_dev, samp_dev * LEAF)
    packed_coords = jnp.transpose(coords, (1, 0, 2)).reshape(leaves_dev, 3 * LEAF)
    start = jnp.zeros((samp_dev, LEAF, leaves_dev), jnp.float32)
    asked_for = lax.all_to_all(wanted, "leaf", split_axis=0, concat_axis=0, tiled=True)
    blocks = packed_samples[asked_for]
    places = packed_coords[asked_for]
    fetched = lax.all_to_all(blocks, "leaf", split_axis=0, concat_axis=0, tiled=True)
    fetched_coords = lax.all_to_all(places, "leaf", split_axis=0, concat_axis=0, tiled=True)
    fetched = fetched.reshape(-1, samp_dev * LEAF)
    fetched_coords = fetched_coords.reshape(-1, 3 * LEAF)

    def far_step(slot_index, accumulated):
        slot_ids = lax.dynamic_index_in_dim(far_slots, slot_index, 1, keepdims=False)
        blocks = jnp.transpose(fetched[slot_ids].reshape(leaves_dev, samp_dev, LEAF), (1, 2, 0))
        source_coords = jnp.transpose(
            fetched_coords[slot_ids].reshape(leaves_dev, 3, LEAF), (1, 2, 0)
        )
        weight = (slot_index < far_count).astype(jnp.float32)
        kernel_vals = kernel_last(source_coords, target_coords) * weight
        return accumulated + jnp.einsum("spl,pql->sql", blocks, kernel_vals, precision=highest)

    far_acc = lax.fori_loop(0, FAR, far_step, start)
    joined = jnp.concatenate([samples, points], axis=0)
    widened = with_halo(joined, (("leaf", 1),), NS * LEAF)
    widened = widened.reshape(samp_dev + 3, leaves_dev + 2 * NS, LEAF)
    near_weights = near_mask.astype(jnp.float32)
    near_acc = start
    for offset in range(2 * NS + 1):
        window = widened[:, offset : offset + leaves_dev, :]
        source_samples = jnp.transpose(window[:samp_dev], (0, 2, 1))
        source_coords = jnp.transpose(window[samp_dev:], (0, 2, 1))
        kernel_vals = kernel_last(source_coords, target_coords) * near_weights[:, offset]
        near_acc = near_acc + jnp.einsum(
            "spl,pql->sql", source_samples, kernel_vals, precision=highest
        )
    far_sample = jnp.transpose(far_acc, (0, 2, 1)).reshape(samp_dev, leaves_dev * LEAF)
    near_sample = jnp.transpose(near_acc, (0, 2, 1)).reshape(samp_dev, leaves_dev * LEAF)
    sample_rows = jnp.transpose(far_acc, (2, 1, 0))
    partial_value = jnp.einsum("lps,rs->lpr", sample_rows, sketch, precision=highest)
    summed = lax.psum(partial_value, "cols")
    basis_t = factor(summed)
    leaf_basis = jnp.transpose(basis_t, (1, 0, 2)).reshape(rank_size, leaves_dev * LEAF)
    current = jnp.einsum("lrp,lps->lrs", basis_t, sample_rows, precision=highest)
    while current.shape[0] > 1:
        current = inner_level(current, sketch)
    branch_samples = current.reshape(rank_size, samp_dev)
    branches = lax.axis_size("leaf")
    tree_depth = branches.bit_length() - 1
    my_index = lax.axis_index("leaf")
    my_next = my_index + 1
    own_transfer = jnp.zeros((2 * rank_size, rank_size), jnp.float32)
    for tree_level in range(tree_depth):
        partner = swapped(current, "leaf", tree_level)
        on_left = (my_index >> tree_level) % 2 == 0
        stacked = jnp.where(
            on_left,
            jnp.concatenate([current, partner], axis=1),
            jnp.concatenate([partner, current], axis=1),
        )
        partial_top = jnp.einsum("nms,rs->nmr", stacked, sketch, precision=highest)
        summed_top = lax.psum(partial_top, "cols")
        transfer_t = factor(summed_top)
        current = jnp.einsum("nrm,nms->nrs", transfer_t, stacked, precision=highest)
        mine = (my_next % 2 ** (tree_level + 1) == 2**tree_level).astype(jnp.float32)
        own_transfer = own_transfer + mine * jnp.swapaxes(transfer_t[0], 0, 1)
    collected, roots = (
        lax.all_gather(own_transfer[None], "leaf", axis=0, tiled=True),
        lax.all_gather(current, "leaf", axis=0, tiled=True),
    )
    device_list = []
    for tree_level in range(tree_depth):
        for node_index in range(branches >> tree_level + 1):
            device_list.append(node_index * 2 ** (tree_level + 1) + 2**tree_level - 1)
    top_transfer = collected[np.array(device_list, dtype=np.int32)]
    root_sample = roots[branches - 1]
    return (far_sample, near_sample, leaf_basis, branch_samples, top_transfer, root_sample)


def solution(mesh):
    return jax.shard_map(
        on_device,
        mesh=mesh,
        in_specs=(
            P(None, "leaf"),
            P("cols", "leaf"),
            P(None, "cols"),
            P("leaf", None, None),
            P("leaf", None),
            P("leaf"),
            P("leaf", None),
        ),
        out_specs=(
            P("cols", "leaf"),
            P("cols", "leaf"),
            P(None, "leaf"),
            P("leaf", "cols"),
            P(),
            P(None, "cols"),
        ),
        check_vma=False,
    )
```

profile of v0, /device:TPU:0, one launch (start us, length us, event | category | flops | bytes accessed | tf_op | source)
XLA Modules:
  0.0 919.2 jit_solution(12144413155659428088)
XLA Ops:
  8.6 8.3 all-to-all-start
  18.0 6.2 all-to-all-done
  25.8 3.5 all-to-all-start.1
  31.0 3.7 gather_fusion.3
  37.1 4.7 all-to-all-start.2
  42.1 3.7 collective-permute-start
  47.7 5.9 collective-permute-done
  59.3 60.6 %all-to-all-done.2 = f32[16,8,8192]{2,1,0:T(8,128)} async-done(((f32[16,8,8192]{2,1,0:T(8,128)}), f32[16,8,8192]{2,1,0:T(8,128)}, u32[]{:S(2)}, u32[]{:S(2)}) %all-to-all-start.2) | async-done | bytes 4194336 | tf_op jit(solution)/shard_map/all_to_all | solution.py:72
  119.9 243.4 %while.14 = (s32[]{:T(128)}, f32[128,64,32]{0,1,2:T(8,128)}, s32[32,16]{0,1:T(8,128)}, f32[128,192]{1,0:T(8,128)S(1)}, f32[3,64,32]{1,2,0:T(8,128)S(1)}, /*index...) while((s32[]{:T(128)}, f32[128,64,32]{0,1,2:T(8,128)}, s32[32,16]{0,1:T(8,128)}, ...), condition=%wide.region_2.3_spmd.clone, body=%wide.region_0.2_spmd.clone.sunk | while | flops 203293856 | bytes 9639023 | solution.py:87
  123.9 3.5 gather_fusion
  128.3 6.6 fusion.158
  138.8 3.5 gather_fusion
  143.2 6.9 fusion.158
  154.0 3.5 gather_fusion
  158.4 6.9 fusion.158
  169.3 3.5 gather_fusion
  173.6 6.9 fusion.158
  184.5 3.5 gather_fusion
  188.9 6.9 fusion.158
  199.7 3.5 gather_fusion
  204.1 6.9 fusion.158
  214.9 3.5 gather_fusion
  219.3 6.9 fusion.158
  230.2 3.5 gather_fusion
  234.6 6.9 fusion.158
  245.4 3.5 gather_fusion
  249.8 6.9 fusion.158
  260.6 3.5 gather_fusion
  265.0 6.9 fusion.158
  275.9 3.5 gather_fusion
  280.3 6.9 fusion.158
  291.1 3.5 gather_fusion
  295.5 6.9 fusion.158
  306.3 3.5 gather_fusion
  310.7 6.9 fusion.158
  321.6 3.5 gather_fusion
  326.0 6.9 fusion.158
  336.8 3.5 gather_fusion
  341.2 6.9 fusion.158
  352.0 3.5 gather_fusion
  356.4 6.9 fusion.158
  363.3 5.0 fusion.13
  373.6 29.5 %all-reduce.4.cloned.1.call-done = f32[32,64,32]{1,2,0:T(8,128)} async-done(((f32[32,64,32]{1,2,0:T(8,128)}), f32[32,64,32]{1,2,0:T(8,128)}) %all-reduce.4.cloned.1.call-update) | async-done | bytes 262160 | tf_op jit(solution)/shard_map/psum | solution.py:105
  406.2 93.8 %custom-call.46 = f32[32,32,32]{2,1,0:T(8,128)S(1)} custom-call(f32[32,32,32]{2,1,0:T(8,128)S(1)} %fusion.19), custom_call_target="Cholesky" | custom-call | tf_op jit(solution)/shard_map/jit(cholesky)/cholesky | solution.py:46
  500.8 12.5 %custom-call.47 = f32[32,1,32,32]{0,2,3,1:T(8,128)S(1)} custom-call(f32[32,1,32,32]{0,3,2,1:T(8,128)S(1)} %select_bitcast_fusion), custom_call_target="InvertDiagBlocksLowerTriangular" | custom-call | tf_op jit(solution)/shard_map/jit(_solve_triangular)/vmap()/triangular_solve | solution.py:47
  519.1 4.6 multiply_reduce_fusion.1
  523.7 14.5 %all-reduce.6.cloned.1.call-done = f32[16,64,32]{1,2,0:T(8,128)} async-done(((f32[16,64,32]{1,2,0:T(8,128)}), f32[16,64,32]{1,2,0:T(8,128)}) %all-reduce.6.cloned.1.call-update) | async-done | bytes 131088 | tf_op jit(solution)/shard_map/psum | solution.py:53
  541.0 47.6 %custom-call.48 = f32[16,32,32]{2,1,0:T(8,128)S(1)} custom-call(f32[16,32,32]{2,1,0:T(8,128)} %fusion.23), custom_call_target="Cholesky" | custom-call | tf_op jit(solution)/shard_map/jit(cholesky)/cholesky | solution.py:46
  588.8 39.4 %custom-call.49 = f32[16,1,32,32]{2,3,1,0:T(8,128)S(1)} custom-call(f32[16,1,32,32]{3,2,1,0:T(8,128)S(1)} %select_bitcast_fusion.1), custom_call_target="InvertDiagBlocksLowerTriangular" | custom-call | tf_op jit(solution)/shard_map/jit(_solve_triangular)/vmap()/triangular_solve | solution.py:47
  634.3 15.9 %all-reduce.8.cloned.1.call-done = f32[8,64,32]{1,2,0:T(8,128)} async-done(((f32[8,64,32]{1,2,0:T(8,128)}), f32[8,64,32]{1,2,0:T(8,128)}) %all-reduce.8.cloned.1.call-update) | async-done | bytes 65552 | tf_op jit(solution)/shard_map/psum | solution.py:53
  651.8 23.4 %custom-call.50 = f32[8,32,32]{2,1,0:T(8,128)S(1)} custom-call(f32[8,32,32]{2,1,0:T(8,128)S(1)} %fusion.27), custom_call_target="Cholesky" | custom-call | tf_op jit(solution)/shard_map/jit(cholesky)/cholesky | solution.py:46
  675.5 19.7 %custom-call.51 = f32[8,1,32,32]{2,3,1,0:T(8,128)S(1)} custom-call(f32[8,1,32,32]{3,2,1,0:T(8,128)S(1)} %select_bitcast_fusion.2), custom_call_target="InvertDiagBlocksLowerTriangular" | custom-call | tf_op jit(solution)/shard_map/jit(_solve_triangular)/vmap()/triangular_solve | solution.py:47
  697.3 3.6 psum.73
  701.5 12.4 %custom-call.52 = f32[4,32,32]{2,1,0:T(8,128)} custom-call(f32[4,32,32]{2,1,0:T(8,128)S(1)} %fusion.31), custom_call_target="Cholesky" | custom-call | tf_op jit(solution)/shard_map/jit(cholesky)/cholesky | solution.py:46
  716.5 11.2 %custom-call.53 = f32[4,1,32,32]{2,3,1,0:T(8,128)} custom-call(f32[4,1,32,32]{3,2,1,0:T(8,128)} %select_bitcast_fusion.3), custom_call_target="InvertDiagBlocksLowerTriangular" | custom-call | tf_op jit(solution)/shard_map/jit(_solve_triangular)/vmap()/triangular_solve | solution.py:47
  729.4 3.5 psum.74
  733.4 5.9 custom-call.54
  739.5 4.9 custom-call.55
  761.7 3.5 psum.76
  775.3 4.5 fusion.10
  793.5 4.8 convolution_add_fusion.1
  812.8 4.8 convolution_add_fusion
  834.8 38.1 %all-gather.1 = f32[512,128]{1,0:T(8,128)S(1)} all-gather(f32[32,128]{1,0:T(8,128)S(1)} %fusion.36), channel_id=3, replica_groups=mesh['leaf'=16,'cols'=2] {'leaf'}, dimensions={0}, use_global_device_ids=true | all-gather | bytes 278528 | tf_op jit(solution)/shard_map/all_gather | solution.py:133
  873.6 37.6 %all-gather.2 = f32[16,64,32]{1,2,0:T(8,128)S(1)} all-gather(f32[1,64,32]{1,2,0:T(8,128)S(1)} %add_bitcast_fusion), channel_id=2, replica_groups=mesh['leaf'=16,'cols'=2] {'leaf'}, dimensions={0}, use_global_device_ids=true | all-gather | bytes 139264 | tf_op jit(solution)/shard_map/all_gather | solution.py:132
  (349 shorter events, 196.5 us)
Async XLA Ops:
  7.2 356.1 %copy-start = (f32[32,128]{1,0:T(8,128)S(1)}, f32[32,128]{1,0:T(8,128)}, u32[]{:S(2)}) copy-start(f32[32,128]{1,0:T(8,128)} %param.16) | copy-start | bytes 49156
  7.2 22.2 %copy-start.6 = (f32[128,2048]{1,0:T(8,128)S(1)}, f32[128,2048]{1,0:T(8,128)}, u32[]{:S(2)}) copy-start(f32[128,2048]{1,0:T(8,128)} %param.15) | copy-start | bytes 3145732
  8.6 15.5 %all-to-all-start = ((s32[16,1,8]{2,1,0:T(1,128)}), s32[16,1,8]{2,1,0:T(1,128)S(1)}, u32[]{:S(2)}, u32[]{:S(2)}) async-start(s32[16,1,8]{2,1,0:T(1,128)} %copy.168), calls=%async_computation | async-start | bytes 16384 | tf_op jit(solution)/shard_map/all_to_all | solution.py:69
  25.8 11.3 %all-to-all-start.1 = ((f32[16,8,192]{2,1,0:T(8,128)}), f32[16,8,192]{2,1,0:T(8,128)S(1)}, u32[]{:S(2)}, u32[]{:S(2)}) async-start(f32[16,8,192]{2,1,0:T(8,128)} %bitcast.3), calls=%async_computation.1 | async-start | bytes 262144 | tf_op jit(solution)/shard_map/all_to_all | solution.py:73
  37.1 4.8 copy-start.7
  37.1 4.9 copy-start.11
  37.1 82.8 %all-to-all-start.2 = ((f32[16,8,8192]{2,1,0:T(8,128)}), f32[16,8,8192]{2,1,0:T(8,128)}, u32[]{:S(2)}, u32[]{:S(2)}) async-start(f32[16,8,8192]{2,1,0:T(8,128)} %bitcast.312), calls=%async_computation.2 | async-start | bytes 8388608 | tf_op jit(solution)/shard_map/all_to_all | solution.py:72
  41.8 5.5 copy-start.12
  41.8 5.6 copy-start.13
  41.8 361.3 %all-reduce.4.cloned.1.call-start = ((), (), s32[]{:S(2)}) async-start(), calls=%async_computation.3 | async-start | bytes 1048576 | tf_op jit(solution)/shard_map/psum | solution.py:105
  42.1 11.5 %collective-permute-start = (f32[131,64]{1,0:T(8,128)S(1)}, f32[131,64]{1,0:T(8,128)S(1)}, u32[]{:S(2)}, u32[]{:S(2)}) collective-permute-start(f32[131,64]{1,0:T(8,128)S(1)} %get-tuple-element.216), channel_id=1, source_target_pairs={{0,2},{2,4},{4,6},{6,8},{8,10},{10,12},{12,14},{14,16},{16,18},{18... | collective-permute-start | bytes 100616 | tf_op jit(solution)/shard_map/ppermute | solution.py:22
  45.8 10.7 %collective-permute-start.1 = (f32[131,64]{1,0:T(8,128)S(1)}, f32[131,64]{1,0:T(8,128)S(1)}, u32[]{:S(2)}, u32[]{:S(2)}) collective-permute-start(f32[131,64]{1,0:T(8,128)S(1)} %get-tuple-element.215), channel_id=1, source_target_pairs={{2,0},{4,2},{6,4},{8,6},{10,8},{12,10},{14,12},{16,14},{18,16},{20... | collective-permute-start | bytes 100616 | tf_op jit(solution)/shard_map/ppermute | solution.py:25
  57.4 62.6 %copy-start.14 = (s32[32]{0:T(128)S(1)}, s32[32]{0:T(128)}, u32[]{:S(2)}) copy-start(s32[32]{0:T(128)} %param.19) | copy-start | bytes 388
  368.3 169.9 %all-reduce.6.cloned.1.call-start = ((), (), s32[]{:S(2)}) async-start(), calls=%async_computation.4 | async-start | bytes 524288 | tf_op jit(solution)/shard_map/psum | solution.py:53
  406.2 107.6 %copy-start.3 = (f32[32,64,32]{1,2,0:T(8,128)S(1)}, f32[32,64,32]{1,2,0:T(8,128)}, u32[]{:S(2)}) copy-start(f32[32,64,32]{1,2,0:T(8,128)} %all-reduce.4.cloned.1.call-done) | copy-start | bytes 786436
  500.3 15.0 %copy-start.1 = (f32[128,64,32]{0,1,2:T(8,128)S(1)}, f32[128,64,32]{0,1,2:T(8,128)}, u32[]{:S(2)}) copy-start(f32[128,64,32]{0,1,2:T(8,128)} %get-tuple-element.132) | copy-start | bytes 3145732
  513.8 5.2 copy-start.9
  514.5 0.8 copy-start.4
  518.6 131.6 %all-reduce.8.cloned.1.call-start = ((), (), s32[]{:S(2)}) async-start(), calls=%async_computation.5 | async-start | bytes 262144 | tf_op jit(solution)/shard_map/psum | solution.py:53
  538.2 90.0 %copy-start.8 = (f32[16,64,32]{1,2,0:T(8,128)S(1)}, f32[16,64,32]{1,2,0:T(8,128)}, u32[]{:S(2)}) copy-start(f32[16,64,32]{1,2,0:T(8,128)} %all-reduce.6.cloned.1.call-done) | copy-start | bytes 393220
  713.8 61.5 %copy-start.2 = (f32[131,2176]{0,1:T(8,128)S(1)}, f32[131,2176]{0,1:T(8,128)}, u32[]{:S(2)}) copy-start(f32[131,2176]{0,1:T(8,128)} %copy.173) | copy-start | bytes 3420676
  757.0 22.8 %copy-start.10 = (f32[32,128]{1,0:T(8,128)}, f32[32,128]{1,0:T(8,128)S(1)}, u32[]{:S(2)}) copy-start(f32[32,128]{1,0:T(8,128)S(1)} %fusion.109) | copy-start | bytes 49156
  757.0 4.5 collective-permute-start.2
  773.8 6.0 collective-permute-start.3
  791.9 6.3 collective-permute-start.4
  810.4 12.4 %collective-permute-start.5 = (f32[1,32,128]{2,1,0:T(8,128)S(1)}, f32[1,32,128]{2,1,0:T(8,128)S(1)}, u32[]{:S(2)}, u32[]{:S(2)}) collective-permute-start(f32[1,32,128]{2,1,0:T(8,128)S(1)} %bitcast.332), channel_id=1, source_target_pairs={{0,16},{2,18},{4,20},{6,22},{8,24},{10,26},{12,28},{14,30},{16,0},... | collective-permute-start | bytes 49160 | tf_op jit(solution)/shard_map/ppermute | solution.py:31
  817.6 3.9 copy-start.5
Sparse Core Ops, SparseCore 0:
  368.4 34.6 all-reduce.3
  518.7 19.4 all-reduce.5
  631.0 19.0 all-reduce.7
where the time goes:
time: 926 us; the launch traced here: 919 us
  other arithmetic  370 us (40%)
  matrix products  152 us (16%)
  waiting for transfers between devices  138 us (15%)
  local copies, waits for them, and re-layouts  110 us (12%)
  blocking collectives  99.9 us (11%)
  starting transfers between devices  29.9 us (3%)
  between operations  18.1 us (2%)
    another operation x31, other arithmetic, factor(): lower_factor = jnp.linalg.cholesky(shifted)  203 us
    dot_general x16, matrix products, far_step(): jnp.einsum('spl,pql->sql', blocks, kernel_vals, precision=highest)  110 us
    another operation x21, other arithmetic, factor(): jax.scipy.linalg.solve_triangular(lower_factor, jnp.swapaxes(sketched, 1,...  105 us
    all_to_all x1, waiting for transfers between devices, on_device(): lax.all_to_all(blocks, 'leaf', split_axis=0, concat_axis=0, tiled=True)  60.6 us
    gather x16, local copies, waits for them, and re-layouts, far_step(): fetched[slot_ids].reshape(leaves_dev, samp_dev, LEAF)  56.7 us
    all_gather x1, blocking collectives, on_device(): lax.all_gather(current, 'leaf', axis=0, tiled=True)  38.1 us
    all_gather x1, blocking collectives, on_device(): lax.all_gather(own_transfer[None], 'leaf', axis=0, tiled=True)  37.6 us
    psum x2, waiting for transfers between devices, inner_level(): summed = lax.psum(partial_value, 'cols')  30.4 us
  transfers between devices with their start and end apart: 12, of which 8 were waited for; matrix products, arithmetic and copies ran while one was open for 5% of the time, Pallas kernels for 0%

commit v1 on v0

v1 whole, which is shorter than its diff:
```python
import functools
import math

import jax
import jax.numpy as jnp
import numpy as np
from jax import lax
from jax.experimental import pallas as pl
from jax.experimental.pallas import tpu as pltpu
from jax.sharding import PartitionSpec as P

LEAF = 64
FAR = 16
GROUP = 4
BATCH = 16
LANES = 128

length_scale = 0.3
shift_share = 0.05
highest = lax.Precision.HIGHEST
exponent_scale = -math.log2(math.e) / length_scale
vmem_bytes = 56 * 1024 * 1024

nt_dims = (((1,), (1,)), ((), ()))


def halves(value):
    high = value.astype(jnp.bfloat16)
    low = (value - high.astype(jnp.float32)).astype(jnp.bfloat16)
    return high, low


def dot(a, b):
    return jnp.dot(a, b, preferred_element_type=jnp.float32)


def dot_nt(a, b):
    return lax.dot_general(a, b, nt_dims, preferred_element_type=jnp.float32)


def kernel_half(source_rows, target, lane, valid):
    total = None
    for axis in range(3):
        difference = source_rows[axis : axis + 1, :] - target[:, axis : axis + 1]
        square = difference * difference
        total = square if total is None else total + square
    distance = total * lax.rsqrt(jnp.maximum(total, 1e-30))
    values = jnp.exp2(distance * exponent_scale)
    return jnp.where(lane < valid, values, 0.0)


def blocks_body(
    total_ref, leaf_ref, count_ref, slot_ref,
    packed_ref, target_ref,
    high_ref, low_ref, sketched_ref, gram_ref,
    *, rank,
):
    step = pl.program_id(0)
    lane = lax.broadcasted_iota(jnp.int32, (1, LANES), 1)
    first = lane < LEAF

    @pl.when(step == 0)
    def _():
        sketched_ref[...] = jnp.zeros_like(sketched_ref)

    @pl.when(step * BATCH < total_ref[0])
    def _():
        for member in range(BATCH):
            group = step * BATCH + member
            leaf = leaf_ref[group]
            count = count_ref[group]
            slots = [slot_ref[group * GROUP + e] for e in range(GROUP)]
            target = target_ref[leaf]
            z_parts = []
            for half in range(GROUP // 2):
                left = packed_ref[slots[2 * half]]
                right = packed_ref[slots[2 * half + 1]]
                both = jnp.where(first, left, right)
                values = kernel_half(both[rank : rank + 3], target, lane, (count - 2 * half) * LEAF)
                high, low = halves(values)
                high_ref[member, :, half * LANES : (half + 1) * LANES] = high
                low_ref[member, :, half * LANES : (half + 1) * LANES] = low
                z_parts.append(both[:rank])
            z_high, z_low = halves(jnp.concatenate(z_parts, axis=1))
            k_high = high_ref[member]
            k_low = low_ref[member]
            update = dot_nt(z_high, k_high) + (dot_nt(z_low, k_high) + dot_nt(z_high, k_low))
            sketched_ref[leaf] += update

    @pl.when(step == pl.num_programs(0) - 1)
    def _():
        for leaf in range(gram_ref.shape[0]):
            block = sketched_ref[leaf]
            gram_ref[leaf] = lax.dot_general(
                block, block, nt_dims, precision=highest, preferred_element_type=jnp.float32
            )


def kernel_blocks(total, group_leaf, group_count, group_slots, packed, targets, rank):
    leaves = targets.shape[0]
    groups = group_leaf.shape[0]
    steps = groups // BATCH

    def block_index(step, total_ref, *unused):
        last = (total_ref[0] - 1) // BATCH
        return (jnp.minimum(step, last), 0, 0)

    whole = lambda *unused: (0, 0, 0)
    return pl.pallas_call(
        functools.partial(blocks_body, rank=rank),
        grid_spec=pltpu.PrefetchScalarGridSpec(
            num_scalar_prefetch=4,
            grid=(steps,),
            in_specs=[
                pl.BlockSpec(packed.shape, whole),
                pl.BlockSpec(targets.shape, whole),
            ],
            out_specs=[
                pl.BlockSpec((BATCH, LEAF, GROUP * LEAF), block_index),
                pl.BlockSpec((BATCH, LEAF, GROUP * LEAF), block_index),
                pl.BlockSpec((leaves, rank, LEAF), whole),
                pl.BlockSpec((leaves, rank, rank), whole),
            ],
        ),
        out_shape=[
            jax.ShapeDtypeStruct((groups, LEAF, GROUP * LEAF), jnp.bfloat16),
            jax.ShapeDtypeStruct((groups, LEAF, GROUP * LEAF), jnp.bfloat16),
            jax.ShapeDtypeStruct((leaves, rank, LEAF), jnp.float32),
            jax.ShapeDtypeStruct((leaves, rank, rank), jnp.float32),
        ],
        compiler_params=pltpu.CompilerParams(vmem_limit_bytes=vmem_bytes),
        name="kernel_blocks",
        cost_estimate=pl.CostEstimate(
            flops=2 * 10**10, bytes_accessed=2 * 10**7, transcendentals=0
        ),
    )(total, group_leaf, group_count, group_slots, packed, targets)


def far_body(
    total_ref, leaf_ref, slot_ref,
    fetched_ref, high_ref, low_ref, weights_ref,
    out_ref, projected_ref,
    s_high, s_low, acc,
):
    step = pl.program_id(0)
    samp_dev = fetched_ref.shape[2]

    @pl.when(step == 0)
    def _():
        acc[...] = jnp.zeros_like(acc)

        def split(slot, carry):
            s_high[slot], s_low[slot] = halves(fetched_ref[slot])
            return carry

        lax.fori_loop(0, fetched_ref.shape[0], split, 0, unroll=8)

    @pl.when(step * BATCH < total_ref[0])
    def _():
        for member in range(BATCH):
            group = step * BATCH + member
            leaf = leaf_ref[group]
            slots = [slot_ref[group * GROUP + e] for e in range(GROUP)]
            rows_high = jnp.concatenate([s_high[slot] for slot in slots], axis=0)
            rows_low = jnp.concatenate([s_low[slot] for slot in slots], axis=0)
            k_high = high_ref[member]
            k_low = low_ref[member]
            acc[leaf] += dot(k_high, rows_high) + (dot(k_high, rows_low) + dot(k_low, rows_high))

    @pl.when(step == pl.num_programs(0) - 1)
    def _():
        leaves = acc.shape[0]
        rows = acc[...].reshape(leaves * LEAF, samp_dev)
        projected_ref[...] = jnp.dot(
            weights_ref[...], rows, precision=highest, preferred_element_type=jnp.float32
        )
        for pair in range(leaves // 2):
            block = acc[2 * pair : 2 * pair + 2].reshape(2 * LEAF, samp_dev)
            out_ref[:, 2 * pair * LEAF : 2 * (pair + 1) * LEAF] = block.T


def far_products(total, group_leaf, group_slots, fetched, high, low, weights):
    slots, unused, samp_dev = fetched.shape
    groups = group_leaf.shape[0]
    points_dev = weights.shape[1]
    leaves = points_dev // LEAF
    steps = groups // BATCH

    def block_index(step, total_ref, *unused):
        last = (total_ref[0] - 1) // BATCH
        return (jnp.minimum(step, last), 0, 0)

    return pl.pallas_call(
        far_body,
        grid_spec=pltpu.PrefetchScalarGridSpec(
            num_scalar_prefetch=3,
            grid=(steps,),
            in_specs=[
                pl.BlockSpec(fetched.shape, lambda *unused: (0, 0, 0), pipeline_mode=pl.Buffered(1)),
                pl.BlockSpec((BATCH, LEAF, GROUP * LEAF), block_index),
                pl.BlockSpec((BATCH, LEAF, GROUP * LEAF), block_index),
                pl.BlockSpec(weights.shape, lambda *unused: (0, 0), pipeline_mode=pl.Buffered(1)),
            ],
            out_specs=[
                pl.BlockSpec((samp_dev, points_dev), lambda *unused: (0, 0)),
                pl.BlockSpec((weights.shape[0], samp_dev), lambda *unused: (0, 0)),
            ],
            scratch_shapes=[
                pltpu.VMEM((slots, LEAF, samp_dev), jnp.bfloat16),
                pltpu.VMEM((slots, LEAF, samp_dev), jnp.bfloat16),
                pltpu.VMEM((leaves, LEAF, samp_dev), jnp.float32),
            ],
        ),
        out_shape=[
            jax.ShapeDtypeStruct((samp_dev, points_dev), jnp.float32),
            jax.ShapeDtypeStruct((weights.shape[0], samp_dev), jnp.float32),
        ],
        compiler_params=pltpu.CompilerParams(vmem_limit_bytes=vmem_bytes),
        name="far_products",
        cost_estimate=pl.CostEstimate(
            flops=10**10, bytes_accessed=2 * 10**7, transcendentals=0
        ),
    )(total, group_leaf, group_slots, fetched, high, low, weights)


NEAR_LEAVES = 8


def near_body(mask_ref, rows_ref, coords_ref, target_ref, out_ref):
    step = pl.program_id(0)
    samp_dev = rows_ref.shape[2]
    lane = lax.broadcasted_iota(jnp.int32, (1, LANES), 1)
    first = lane < LEAF
    for pair in range(NEAR_LEAVES // 2):
        results = []
        for member in range(2):
            leaf = step * NEAR_LEAVES + 2 * pair + member
            target = target_ref[leaf]
            k_high = []
            k_low = []
            for half in range(2):
                both = jnp.where(first, coords_ref[leaf + 2 * half], coords_ref[leaf + 2 * half + 1])
                values = kernel_half(both, target, lane, LANES)
                left = mask_ref[leaf * 3 + 2 * half].astype(jnp.float32)
                if half == 0:
                    right = mask_ref[leaf * 3 + 1].astype(jnp.float32)
                else:
                    right = jnp.float32(0.0)
                high, low = halves(values * jnp.where(first, left, right))
                k_high.append(high)
                k_low.append(low)
            k_high = jnp.concatenate(k_high, axis=1)
            k_low = jnp.concatenate(k_low, axis=1)
            rows = rows_ref[pl.ds(leaf, 4)].reshape(4 * LEAF, samp_dev)
            rows_high, rows_low = halves(rows)
            results.append(
                dot(k_high, rows_high) + (dot(k_high, rows_low) + dot(k_low, rows_high))
            )
        block = jnp.concatenate(results, axis=0)
        out_ref[:, 2 * pair * LEAF : 2 * (pair + 1) * LEAF] = block.T


def near_products(mask, rows, coords, targets):
    leaves = targets.shape[0]
    samp_dev = rows.shape[2]
    whole = lambda *unused: (0, 0, 0)
    return pl.pallas_call(
        near_body,
        grid_spec=pltpu.PrefetchScalarGridSpec(
            num_scalar_prefetch=1,
            grid=(leaves // NEAR_LEAVES,),
            in_specs=[
                pl.BlockSpec(rows.shape, whole),
                pl.BlockSpec(coords.shape, whole),
                pl.BlockSpec(targets.shape, whole),
            ],
            out_specs=pl.BlockSpec((samp_dev, NEAR_LEAVES * LEAF), lambda step, *unused: (0, step)),
        ),
        out_shape=jax.ShapeDtypeStruct((samp_dev, leaves * LEAF), jnp.float32),
        compiler_params=pltpu.CompilerParams(vmem_limit_bytes=vmem_bytes),
        name="near_products",
        cost_estimate=pl.CostEstimate(
            flops=4 * 10**9, bytes_accessed=10**7, transcendentals=0
        ),
    )(mask, rows, coords, targets)


SUB = 8


def tree_body(gram_ref, inverse_ref, child_ref, current, *, rank, levels):
    tiles = rank // SUB
    row = lax.broadcasted_iota(jnp.int32, (SUB, LANES), 0)
    current[...] = gram_ref[...]

    def level_step(level, carry):
        trace = None
        for j in range(rank):
            entry = current[j, j : j + 1, :]
            trace = entry if trace is None else trace + entry
        shift = shift_share * trace / rank + 1e-06
        a = [
            {t: current[j, SUB * t : SUB * (t + 1), :] for t in range(j // SUB, tiles)}
            for j in range(rank)
        ]
        for j in range(rank):
            a[j][j // SUB] = a[j][j // SUB] + jnp.where(row == j % SUB, shift, 0.0)
        m = []
        scales = []
        for k in range(rank):
            tk, rk = k // SUB, k % SUB
            root = lax.rsqrt(a[k][tk][rk : rk + 1, :])
            scales.append(root)
            reciprocal = root * root
            column = {t: a[k][t] * reciprocal for t in range(tk, tiles)}
            column[tk] = jnp.where(row > rk, column[tk], 0.0)
            for j in range(k + 1, rank):
                factor = a[k][j // SUB][j % SUB : j % SUB + 1, :]
                for t in range(j // SUB, tiles):
                    a[j][t] = a[j][t] - column[t] * factor
            for c in range(k):
                factor = m[c][tk][rk : rk + 1, :]
                for t in range(tk, tiles):
                    m[c][t] = m[c][t] - column[t] * factor
            fresh = {t: -column[t] for t in range(tk, tiles)}
            fresh[tk] = jnp.where(row == rk, 1.0, fresh[tk])
            m.append(fresh)
        for t in range(tiles):
            scale = jnp.concatenate(scales[SUB * t : SUB * (t + 1)], axis=0)
            for c in range(rank):
                if t >= c // SUB:
                    inverse_ref[level, c, SUB * t : SUB * (t + 1), :] = m[c][t] * scale
                else:
                    inverse_ref[level, c, SUB * t : SUB * (t + 1), :] = jnp.zeros(
                        (SUB, LANES), jnp.float32
                    )
        for block in range(tiles):
            sums = [[None] * tiles for _ in range(SUB)]
            for k in range(SUB * (block + 1)):
                parts = [current[k, SUB * t : SUB * (t + 1), :] for t in range(tiles)]
                for r in range(max(0, k - SUB * block), SUB):
                    at = SUB * block + r
                    factor = inverse_ref[level, k, at : at + 1, :]
                    for t in range(tiles):
                        term = parts[t] * factor
                        sums[r][t] = term if sums[r][t] is None else sums[r][t] + term
            for r in range(SUB):
                for t in range(tiles):
                    child_ref[level, SUB * block + r, SUB * t : SUB * (t + 1), :] = sums[r][t]

        @pl.when(level < levels - 1)
        def _():
            reach = LANES - lax.shift_left(1, level)

            def gram_block(block, inner):
                offset = pl.multiple_of(block * SUB, SUB)
                sums = [[None] * tiles for _ in range(SUB)]
                for r in range(rank):
                    parts = [child_ref[level, r, SUB * t : SUB * (t + 1), :] for t in range(tiles)]
                    heads = child_ref[level, r, pl.ds(offset, SUB), :]
                    for q in range(SUB):
                        factor = heads[q : q + 1, :]
                        for t in range(tiles):
                            term = parts[t] * factor
                            sums[q][t] = term if sums[q][t] is None else sums[q][t] + term
                for q in range(SUB):
                    for t in range(tiles):
                        current[offset + q, SUB * t : SUB * (t + 1), :] = sums[q][t] + pltpu.roll(
                            sums[q][t], reach, 1
                        )
                return inner

            lax.fori_loop(0, tiles, gram_block, 0)

        return carry

    lax.fori_loop(0, levels, level_step, 0)


def tree_factors(gram_last, levels):
    rank = gram_last.shape[0]
    nodes = gram_last.shape[2]
    padded = jnp.pad(gram_last, ((0, 0), (0, 0), (0, LANES - nodes)))
    shape = jax.ShapeDtypeStruct((levels, rank, rank, LANES), jnp.float32)
    inverse, child = pl.pallas_call(
        functools.partial(tree_body, rank=rank, levels=levels),
        in_specs=[pl.BlockSpec(memory_space=pltpu.VMEM)],
        out_specs=[pl.BlockSpec(memory_space=pltpu.VMEM)] * 2,
        out_shape=[shape, shape],
        scratch_shapes=[pltpu.VMEM((rank, rank, LANES), jnp.float32)],
        compiler_params=pltpu.CompilerParams(vmem_limit_bytes=vmem_bytes),
        name="tree_factors",
        cost_estimate=pl.CostEstimate(
            flops=10**10, bytes_accessed=10**7, transcendentals=0
        ),
    )(padded)
    return (
        jnp.transpose(inverse[..., :nodes], (0, 3, 2, 1)),
        jnp.transpose(child[..., :nodes], (0, 3, 1, 2)),
    )


def exchange_sum(pieces, axis):
    count = pieces.shape[0]
    me = lax.axis_index(axis)
    mine = lax.dynamic_index_in_dim(pieces, me, 0, keepdims=False)
    for step in range(1, count):
        outgoing = lax.dynamic_index_in_dim(pieces, (me + step) % count, 0, keepdims=False)
        mine = mine + lax.ppermute(
            outgoing, axis, [(i, (i + step) % count) for i in range(count)]
        )
    return mine


def exchange_all(piece, axis):
    count = lax.axis_size(axis)
    me = lax.axis_index(axis)
    if count == 2:
        other = lax.ppermute(piece, axis, [(0, 1), (1, 0)])
        return jnp.stack([jnp.where(me == 0, piece, other), jnp.where(me == 0, other, piece)])
    result = jnp.zeros((count,) + piece.shape, piece.dtype)
    result = lax.dynamic_update_index_in_dim(result, piece, me, 0)
    for step in range(1, count):
        arrived = lax.ppermute(piece, axis, [(i, (i + step) % count) for i in range(count)])
        result = lax.dynamic_update_index_in_dim(result, arrived, (me - step) % count, 0)
    return result


def double_all(piece, axis):
    count = lax.axis_size(axis)
    me = lax.axis_index(axis)
    held = piece[None]
    stride = 1
    while stride < count:
        other = lax.ppermute(held, axis, [(i, i ^ stride) for i in range(count)])
        low = (me // stride) % 2 == 0
        held = jnp.concatenate([jnp.where(low, held, other), jnp.where(low, other, held)], axis=0)
        stride *= 2
    return held


def group_tables(far_slots, far_count):
    leaves = far_slots.shape[0]
    groups = leaves * FAR // GROUP
    per_leaf = (far_count + GROUP - 1) // GROUP
    before = jnp.arange(leaves)[:, None] >= jnp.arange(leaves)[None, :]
    ends = jnp.sum(jnp.where(before, per_leaf[None, :], 0), axis=1)
    total = ends[leaves - 1 :]
    ids = jnp.arange(groups, dtype=jnp.int32)
    leaf = jnp.minimum(jnp.sum((ends[None, :] <= ids[:, None]).astype(jnp.int32), axis=1), leaves - 1)
    hit = leaf[:, None] == jnp.arange(leaves)[None, :]
    start = jnp.sum(jnp.where(hit, (ends - per_leaf)[None, :], 0), axis=1)
    length = jnp.sum(jnp.where(hit, far_count[None, :], 0), axis=1)
    sub = ids - start
    count = jnp.where(ids < total, jnp.clip(length - GROUP * sub, 0, GROUP), 0)
    first = jnp.minimum(sub, FAR // GROUP - 1)
    slots = far_slots.reshape(leaves * FAR // GROUP, GROUP)[leaf * (FAR // GROUP) + first]
    return (
        total.astype(jnp.int32),
        leaf.astype(jnp.int32),
        count.astype(jnp.int32),
        slots.reshape(-1).astype(jnp.int32),
    )


def on_device(points, samples, sketch, far_requests, far_slots, far_count, near_mask):
    samp_dev = samples.shape[0]
    leaves = samples.shape[1] // LEAF
    rank = sketch.shape[0]
    branches = lax.axis_size("leaf")
    columns = lax.axis_size("cols")
    cap = far_requests.shape[2]
    slots = branches * cap
    share = rank // columns

    wanted = far_requests.reshape(branches, cap)
    asked_for = lax.all_to_all(wanted, "leaf", split_axis=0, concat_axis=0, tiled=True)

    coords = jnp.transpose(points.reshape(3, leaves, LEAF), (1, 0, 2))
    targets = jnp.transpose(coords, (0, 2, 1))
    rows = jnp.transpose(samples.reshape(samp_dev, leaves, LEAF), (1, 2, 0))

    z_part = jnp.dot(sketch, samples, precision=highest)
    z_mine = exchange_sum(z_part.reshape(columns, share, leaves * LEAF), "cols")
    z_mine = jnp.transpose(z_mine.reshape(share, leaves, LEAF), (1, 0, 2))
    small_width = -(-(share + 3) * LEAF // LANES) * LANES
    small = jnp.concatenate([z_mine.reshape(leaves, -1), coords.reshape(leaves, -1)], axis=1)
    small = jnp.pad(small, ((0, 0), (0, small_width - small.shape[1])))
    small_sent = small[asked_for.reshape(-1)].reshape(branches, cap, small_width)
    small_got = lax.all_to_all(small_sent, "leaf", split_axis=0, concat_axis=0, tiled=True)

    rows_sent = rows[asked_for.reshape(-1)].reshape(branches, cap, LEAF, samp_dev)
    rows_got = lax.all_to_all(rows_sent, "leaf", split_axis=0, concat_axis=0, tiled=True)
    fetched = rows_got.reshape(slots, LEAF, samp_dev)

    small_got = small_got.reshape(slots, small_width)
    z_all = exchange_all(small_got[:, : share * LEAF], "cols")
    z_all = jnp.transpose(z_all.reshape(columns, slots, share, LEAF), (1, 0, 2, 3))
    z_all = z_all.reshape(slots, rank, LEAF)
    c_all = small_got[:, share * LEAF : (share + 3) * LEAF].reshape(slots, 3, LEAF)
    packed = jnp.concatenate([z_all, c_all, jnp.zeros((slots, 5, LEAF), jnp.float32)], axis=1)
    packed = jnp.concatenate([packed, packed], axis=2)

    total, group_leaf, group_count, group_slots = group_tables(far_slots, far_count)
    high, low, sketched, gram = kernel_blocks(
        total, group_leaf, group_count, group_slots, packed, targets, rank
    )

    levels = leaves.bit_length()
    inverse, child = tree_factors(jnp.transpose(gram, (1, 2, 0)), levels)
    own_child = child[levels - 1, 0]
    children = double_all(own_child.reshape(rank * rank // LANES, LANES), "leaf")
    children = children.reshape(branches, rank, rank)

    pair_children = children.reshape(branches // 2, 2 * rank, rank)
    top_gram = jnp.einsum("nmr,nmq->rqn", pair_children, pair_children, precision=highest)
    top_levels = branches.bit_length() - 1
    top_inverse, top_child = tree_factors(top_gram, top_levels)
    transfers = []
    below = children
    for level in range(top_levels):
        inverse_here = top_inverse[level, :: 2**level]
        stacked = below.reshape(branches >> level + 1, 2 * rank, rank)
        transfers.append((stacked, inverse_here))
        below = top_child[level, :: 2**level]
    top_transfer = jnp.einsum(
        "nmq,nrq->nmr",
        jnp.concatenate([stacked for stacked, unused in transfers], axis=0),
        jnp.concatenate([here for unused, here in transfers], axis=0),
        precision=highest,
    )

    me = lax.axis_index("leaf")
    offset = 0
    path = None
    for level in range(top_levels):
        node = offset + (me >> level + 1)
        block = lax.dynamic_index_in_dim(top_transfer, node, 0, keepdims=False)
        side = (me >> level) % 2
        block = lax.dynamic_slice_in_dim(block, side * rank, rank, axis=0)
        path = block if path is None else jnp.dot(path, block, precision=highest)
        offset += branches >> level + 1

    ratio = jnp.einsum("lnrq,lnrc->lnqc", child, inverse, precision=highest)
    upper = inverse[levels - 1, :1]
    for level in range(levels - 2, -1, -1):
        upper = jnp.einsum(
            "nij,nbjk->nbik",
            upper,
            ratio[level, :: 2**level].reshape(upper.shape[0], 2, rank, rank),
            precision=highest,
        ).reshape(-1, rank, rank)
    weights = jnp.einsum("nij,njp->inp", upper, sketched, precision=highest)
    weights = weights.reshape(rank, leaves * LEAF)
    weights = jnp.concatenate(
        [weights, jnp.dot(path.T, weights, precision=highest)], axis=0
    )
    leaf_basis = jnp.einsum("nij,njp->inp", inverse[0], sketched, precision=highest)
    leaf_basis = leaf_basis.reshape(rank, leaves * LEAF)

    edge_rows = jnp.concatenate([rows[:1], rows[leaves - 1 :]], axis=0)
    edge_coords = jnp.concatenate([coords[:1], coords[leaves - 1 :]], axis=0)
    forward = [(i, i + 1) for i in range(branches - 1)]
    backward = [(target, source) for source, target in forward]
    rows_low = lax.ppermute(edge_rows[1], "leaf", forward)
    rows_high = lax.ppermute(edge_rows[0], "leaf", backward)
    coords_low = lax.ppermute(edge_coords[1], "leaf", forward)
    coords_high = lax.ppermute(edge_coords[0], "leaf", backward)
    near_rows = jnp.concatenate(
        [rows_low[None], rows, rows_high[None], jnp.zeros_like(rows_low)[None]], axis=0
    )
    near_coords = jnp.concatenate(
        [coords_low[None], coords, coords_high[None], jnp.zeros_like(coords_low)[None]], axis=0
    )
    near_coords = jnp.pad(near_coords, ((0, 0), (0, 5), (0, 0)))
    near_coords = jnp.concatenate([near_coords, near_coords], axis=2)
    near_sample = near_products(near_mask.reshape(-1), near_rows, near_coords, targets)

    far_sample, projected = far_products(
        total, group_leaf, group_slots, fetched, high, low, weights
    )
    branch_samples = projected[:rank]
    part = jnp.broadcast_to(projected[rank:][None], (branches, rank, samp_dev))
    parts = lax.all_to_all(part, "leaf", split_axis=0, concat_axis=0, tiled=True)
    root_sample = jnp.sum(parts, axis=0)
    return (far_sample, near_sample, leaf_basis, branch_samples, top_transfer, root_sample)


def solution(mesh):
    return jax.shard_map(
        on_device,
        mesh=mesh,
        in_specs=(
            P(None, "leaf"),
            P("cols", "leaf"),
            P(None, "cols"),
            P("leaf", None, None),
            P("leaf", None),
            P("leaf"),
            P("leaf", None),
        ),
        out_specs=(
            P("cols", "leaf"),
            P("cols", "leaf"),
            P(None, "leaf"),
            P("leaf", "cols"),
            P(),
            P(None, "cols"),
        ),
        check_vma=False,
    )
```

time: 926 us -> 248 us (0.27)
  other arithmetic: 370 us -> 10.3 us
  matrix products: 152 us -> 16.2 us
  waiting for transfers between devices: 138 us -> 8.9 us
  blocking collectives: 99.9 us -> 0 us
  Pallas kernels: 0 us -> 61.8 us
  starting transfers between devices: 29.9 us -> 49.5 us
  between operations: 18.1 us -> 1.41 us
  local copies, waits for them, and re-layouts: 110 us -> 97.5 us
    another operation x52 -> x0, other arithmetic: 308 us -> none  [the longest x31 203 us: factor(): lower_factor = jnp.linalg.cholesky(shifted)]
    dot_general x49 -> x15, matrix products: 147 us -> 16.2 us  [the longest x1 5.23 us: on_device(): ratio = jnp.einsum('lnrq,lnrc->lnqc', child, inverse, precision=highest)]
    all_gather x2 -> x0, blocking collectives: 75.7 us -> none  [the longest x1 38.1 us: on_device(): lax.all_gather(current, 'leaf', axis=0, tiled=True)]
    gather x35 -> x3, local copies, waits for them, and re-layouts: 72.7 us -> 4.34 us  [the longest x1 2.82 us: on_device(): rows[asked_for.reshape(-1)].reshape(branches, cap, LEAF, samp_dev)]
    pallas_call x0 -> x5, Pallas kernels: none -> 61.8 us  [the longest x2 35.9 us: tree_factors(): pl.pallas_call(functools.partial(tree_body, rank=rank, levels=levels), in...]
    psum x3 -> x0, waiting for transfers between devices: 59.9 us -> none  [the longest x2 30.4 us: inner_level(): summed = lax.psum(partial_value, 'cols')]
    all_to_all x2 -> x3, waiting for transfers between devices: 63 us -> 4.49 us  [the longest x1 4.48 us: on_device(): lax.all_to_all(part, 'leaf', split_axis=0, concat_axis=0, tiled=True)]
    slice x2 -> x23, local copies, waits for them, and re-layouts: 0.69 us -> 31.7 us  [the longest x6 14.1 us: on_device(): below = top_child[level, ::2 ** level]]
  transfers between devices with their start and end apart: 12 -> 14, of which waited for: 8 -> 4; matrix products, arithmetic and copies ran while one was open for 5% -> 47% of each run, Pallas kernels for 0% -> 21%
where the time goes in v1:
time: 248 us; the launch traced here: 246 us
  local copies, waits for them, and re-layouts  97.5 us (39%)
  Pallas kernels  61.8 us (25%)
  starting transfers between devices  49.5 us (20%)
  matrix products  16.2 us (7%)
  other arithmetic  10.3 us (4%)
  waiting for transfers between devices  8.9 us (4%)
    pallas_call x2, Pallas kernels, tree_factors(): pl.pallas_call(functools.partial(tree_body, rank=rank, levels=levels), in...  35.9 us
    slice x6, local copies, waits for them, and re-layouts, on_device(): below = top_child[level, ::2 ** level]  14.1 us
    transpose x3, local copies, waits for them, and re-layouts, tree_factors(): jnp.transpose(child[..., :nodes], (0, 3, 1, 2))  12.5 us
    pallas_call x1, Pallas kernels, kernel_blocks(): pl.pallas_call(functools.partial(blocks_body, rank=rank), grid_spec=pltpu...  10.4 us
    slice x4, local copies, waits for them, and re-layouts, on_device(): inverse_here = top_inverse[level, ::2 ** level]  10.3 us
    all_to_all x1, starting transfers between devices, on_device(): lax.all_to_all(rows_sent, 'leaf', split_axis=0, concat_axis=0, tiled=True)  9.49 us
    pallas_call x1, Pallas kernels, far_products(): pl.pallas_call(far_body, grid_spec=pltpu.PrefetchScalarGridSpec(num_scala...  9.43 us
    ppermute x4, starting transfers between devices, double_all(): other = lax.ppermute(held, axis, [(i, i ^ stride) for i in range(count)])  9.25 us
  transfers between devices with their start and end apart: 14, of which 4 were waited for; matrix products, arithmetic and copies ran while one was open for 47% of the time, Pallas kernels for 21%

profile of v1, /device:TPU:0, one launch (start us, length us, event | category | flops | bytes accessed | tf_op | source)
XLA Modules:
  0.0 245.6 jit_solution(1712167151938095840)
XLA Ops:
  0.6 1.4 copy.171
  2.0 8.3 %all-to-all-start = ((s32[16,1,8]{2,1,0:T(1,128)}), s32[16,1,8]{2,1,0:T(1,128)S(1)}, u32[]{:S(2)}, u32[]{:S(2)}) async-start(s32[16,1,8]{2,1,0:T(1,128)} %copy.171), calls=%async_computation | async-start | bytes 16384 | tf_op jit(solution)/shard_map/all_to_all | solution.py:477
  10.4 1.9 fusion.38
  14.7 1.1 copy.173
  16.3 1.2 all-to-all-done
  21.1 5.8 %all-to-all-start.2 = ((f32[16,8,1280]{2,1,0:T(8,128)}), f32[16,8,1280]{2,1,0:T(8,128)S(1)}, u32[]{:S(2)}, u32[]{:S(2)}) async-start(f32[16,8,1280]{2,1,0:T(8,128)} %pad_bitcast_fusion), calls=%async_computation.2 | async-start | bytes 1310720 | tf_op jit(solution)/shard_map/all_to_all | solution.py:490
  26.9 3.8 %collective-permute-start.8 = (f32[3,64]{0,1:T(8,128)S(1)}, f32[3,64]{0,1:T(8,128)S(1)}, u32[]{:S(2)}, u32[]{:S(2)}) collective-permute-start(f32[3,64]{0,1:T(8,128)S(1)} %get-tuple-element.30), channel_id=1, source_target_pairs={{0,2},{2,4},{4,6},{6,8},{8,10},{10,12},{12,14},{14,16},{16,18},{18... | collective-permute-start | bytes 2312 | tf_op jit(solution)/shard_map/ppermute | solution.py:567
  30.7 1.3 collective-permute-start.9
  32.0 1.6 copy.170
  33.6 4.5 %collective-permute-start.6 = (f32[64,128]{1,0:T(8,128)S(1)}, f32[64,128]{1,0:T(8,128)S(1)}, u32[]{:S(2)}, u32[]{:S(2)}) collective-permute-start(f32[64,128]{1,0:T(8,128)S(1)} %get-tuple-element.32), channel_id=1, source_target_pairs={{0,2},{2,4},{4,6},{6,8},{8,10},{10,12},{12,14},{14,16},{16,18},{18... | collective-permute-start | bytes 98312 | tf_op jit(solution)/shard_map/ppermute | solution.py:565
  38.1 1.3 collective-permute-start.7
  43.7 2.8 %gather_fusion.1 = f32[128,64,128]{2,1,0:T(8,128)} fusion(f32[32,64,128]{2,1,0:T(8,128)S(1)} %bitcast.167, s32[1024]{0:T(1024)S(1)} %pad_clamp_fusion), kind=kCustom, calls=%fused_computation.1 | custom fusion | bytes 8389120 | tf_op jit(solution)/shard_map/gather | solution.py:492
  47.9 9.5 %all-to-all-start.1 = ((f32[16,8,64,128]{3,2,1,0:T(8,128)}), f32[16,8,64,128]{3,2,1,0:T(8,128)}, u32[]{:S(2)}, u32[]{:S(2)}) async-start(f32[16,8,64,128]{3,2,1,0:T(8,128)} %bitcast.169), calls=%async_computation.1 | async-start | bytes 8388608 | tf_op jit(solution)/shard_map/all_to_all | solution.py:493
  58.2 1.2 maximum_maximum_fusion.1.rows_ref
  59.4 6.1 %near_products.1 = f32[128,2048]{1,0:T(8,128)} custom-call(s32[96]{0:T(128)} %reshape.202.mask_ref, f32[35,64,128]{2,1,0:T(8,128)} %maximum_maximum_fusion.1.rows_ref, f32[35,8,128]{2,1,0:T(8,128)} %pad_maximum_fusion.2.coords_ref, f32[32,64,3]{2,1,0:T(8,128)} %bitcast.173), custom_call_target="tpu_custom_call" | custom-call | flops 4000000000 | bytes 10000000 | tf_op jit(solution)/shard_map/near_products/pallas_call | solution.py:267
  66.5 1.8 copy.177
  68.3 2.4 maximum_maximum_fusion.packed_ref
  70.7 10.4 %kernel_blocks.1 = (bf16[128,64,256]{2,1,0:T(8,128)(2,1)}, bf16[128,64,256]{2,1,0:T(8,128)(2,1)}, f32[32,32,64]{2,1,0:T(8,128)}, f32[32,32,32]{2,1,0:T(8,128)}) custom-call(s32[1]{0:T(128)} %slice.85.total_ref, s32[128]{0:T(128)} %copy-done.11, s32[128]{0:T(128)} %compare_select_fusion.2.count_ref, s32[512]{0:T(512)} %reshape.180.slot_ref, ...), custom_call_target="tpu_custom_call" | custom-call | flops 20000000000 | bytes 20000000 | tf_op jit(solution)/shard_map/kernel_blocks/pallas_call | solution.py:109
  81.2 1.3 copy.180
  83.3 21.6 %tree_factors.2 = (f32[6,32,32,128]{3,2,1,0:T(8,128)}, f32[6,32,32,128]{3,2,1,0:T(8,128)}) custom-call(f32[32,32,128]{2,1,0:T(8,128)} %pad.15.gram_ref), custom_call_target="tpu_custom_call" | custom-call | flops 10000000000 | bytes 10000000 | tf_op jit(solution)/shard_map/tree_factors/pallas_call | solution.py:385
  104.9 2.2 slice_bitcast_fusion
  107.9 4.2 %copy.182 = f32[6,32,32,32]{3,2,1,0:T(8,128)} copy(f32[6,32,32,32]{1,2,3,0:T(8,128)S(1)} %slice_bitcast_fusion) | data formatting | bytes 1572864 | tf_op jit(solution)/shard_map/transpose | solution.py:398
  112.1 4.1 %slice_bitcast_fusion.1 = f32[6,32,32,32]{1,3,2,0:T(8,128)} fusion(f32[6,32,32,128]{3,2,1,0:T(8,128)} %get-tuple-element.20), kind=kLoop, calls=%fused_computation.4 | loop fusion | bytes 1572864 | tf_op jit(solution)/shard_map/transpose | solution.py:399
  116.2 5.3 %copy.181 = f32[6,32,32,32]{2,3,1,0:T(8,128)} copy(f32[6,32,32,32]{1,3,2,0:T(8,128)} %slice_bitcast_fusion.1) | data formatting | bytes 1572864 | tf_op jit(solution)/shard_map/transpose | solution.py:399
  121.5 5.2 %fusion.39 = f32[6,32,32,32]{3,2,1,0:T(8,128)S(1)} fusion(f32[6,32,32,32]{2,3,1,0:T(8,128)} %copy.181, f32[6,32,32,32]{3,2,1,0:T(8,128)} %copy.182), kind=kOutput, calls=%fused_computation.98 | convolution fusion | flops 75497472 | bytes 2359296 | tf_op jit(solution)/shard_map/lnrq,lnrc->lnqc/dot_general | solution.py:544
  126.8 1.6 copy-done.4
  128.4 1.3 slice_reduce_fusion
  129.7 2.9 %collective-permute-start.2 = (f32[1,8,128]{2,1,0:T(8,128)S(1)}, f32[1,8,128]{2,1,0:T(8,128)S(1)}, u32[]{:S(2)}, u32[]{:S(2)}) collective-permute-start(f32[1,8,128]{2,1,0:T(8,128)S(1)} %broadcast_in_dim_reshape_squeeze.3), channel_id=1, source_target_pairs={{0,2},{2,0},{4,6},{6,4},{8,10},{10,8},{12,14},{14,12},{16,18},{18,... | collective-permute-start | bytes 12296 | tf_op jit(solution)/shard_map/ppermute | solution.py:435
  132.7 1.4 copy.183
  136.8 1.5 collective-permute-start.3
  138.9 1.6 collective-permute-done.3
  140.5 1.2 collective-permute-start.4
  142.8 1.6 collective-permute-done.4
  144.3 3.6 %collective-permute-start.5 = (f32[8,8,128]{2,1,0:T(8,128)S(1)}, f32[8,8,128]{2,1,0:T(8,128)S(1)}, u32[]{:S(2)}, u32[]{:S(2)}) collective-permute-start(f32[8,8,128]{2,1,0:T(8,128)S(1)} %pad_maximum_fusion.4), channel_id=1, source_target_pairs={{0,16},{2,18},{4,20},{6,22},{8,24},{10,26},{12,28},{14,30},{16,0},... | collective-permute-start | bytes 98312 | tf_op jit(solution)/shard_map/ppermute | solution.py:435
  150.0 1.9 reshape.201
  153.5 1.2 copy.197
  154.7 1.9 pad.16.gram_ref
  156.6 14.3 %tree_factors.3 = (f32[4,32,32,128]{3,2,1,0:T(8,128)}, f32[4,32,32,128]{3,2,1,0:T(8,128)}) custom-call(f32[32,32,128]{2,1,0:T(8,128)} %pad.16.gram_ref), custom_call_target="tpu_custom_call" | custom-call | flops 10000000000 | bytes 10000000 | tf_op jit(solution)/shard_map/tree_factors/pallas_call | solution.py:385
  170.9 3.1 %slice_bitcast_fusion.3 = f32[4,8,32,32]{1,3,2,0:T(8,128)} fusion(f32[4,32,32,128]{3,2,1,0:T(8,128)} %get-tuple-element.22), kind=kLoop, calls=%fused_computation.7 | loop fusion | bytes 262144 | tf_op jit(solution)/shard_map/transpose | solution.py:399
  174.0 3.7 %slice.100 = f32[1,2,32,32]{1,3,2,0:T(8,128)} slice(f32[4,8,32,32]{1,3,2,0:T(8,128)} %slice_bitcast_fusion.3), slice={[2:3:1], [0:8:4], [0:32:1], [0:32:1]} | slice | bytes 16384 | tf_op jit(solution)/shard_map/slice | solution.py:525
  177.7 3.8 %slice.99 = f32[1,4,32,32]{1,3,2,0:T(8,128)} slice(f32[4,8,32,32]{1,3,2,0:T(8,128)} %slice_bitcast_fusion.3), slice={[1:2:1], [0:8:2], [0:32:1], [0:32:1]} | slice | bytes 32768 | tf_op jit(solution)/shard_map/slice | solution.py:525
  181.5 1.9 slice.124
  183.4 1.8 slice_bitcast_fusion.2
  185.2 1.3 copy-done.3
  187.4 3.7 %slice.104 = f32[1,2,32,32]{1,2,3,0:T(8,128)} slice(f32[4,8,32,32]{1,2,3,0:T(8,128)} %copy-done.3), slice={[2:3:1], [0:8:4], [0:32:1], [0:32:1]} | slice | bytes 16384 | tf_op jit(solution)/shard_map/slice | solution.py:522
  191.0 3.8 %slice.103 = f32[1,4,32,32]{1,2,3,0:T(8,128)} slice(f32[4,8,32,32]{1,2,3,0:T(8,128)} %copy-done.3), slice={[1:2:1], [0:8:2], [0:32:1], [0:32:1]} | slice | bytes 32768 | tf_op jit(solution)/shard_map/slice | solution.py:522
  194.8 1.4 copy.200
  196.3 2.0 copy.199
  198.3 1.4 copy.198
  200.4 1.6 reshape_squeeze.26
  201.9 1.4 copy.203
  203.3 1.5 copy.202
  204.8 2.0 copy.204
  206.8 2.0 copy.207
  208.7 1.9 slice_bitcast_fusion.5
  210.6 2.0 copy.205
  212.6 2.0 copy.206
  214.6 1.4 fusion
  218.2 9.4 %far_products.1 = (f32[128,2048]{1,0:T(8,128)}, f32[64,128]{1,0:T(8,128)}) custom-call(s32[1]{0:T(128)} %slice.85.total_ref, s32[128]{0:T(128)} %copy-done.11, s32[512]{0:T(512)} %reshape.180.slot_ref, f32[128,64,128]{2,1,0:T(8,128)} %bitcast.8.fetched_ref, bf16[128,64,256]{2,1,0:T(8,128)(2,1)} %get-tuple-element.16.high_ref, ...), custom_call_target="tpu_custom_call" | custom-call | flops 10000000000 | bytes 20000000 | tf_op jit(solution)/shard_map/far_products/pallas_call | solution.py:193
  227.6 1.3 fusion.37
  229.7 5.6 %all-to-all-start.3 = ((f32[16,32,128]{2,1,0:T(8,128)}), f32[16,32,128]{2,1,0:T(8,128)S(1)}, u32[]{:S(2)}, u32[]{:S(2)}) async-start(f32[16,32,128]{2,1,0:T(8,128)} %broadcast_in_dim.75), calls=%async_computation.3 | async-start | bytes 524288 | tf_op jit(solution)/shard_map/all_to_all | solution.py:584
  236.1 1.6 copy.214
  237.7 1.6 convolution_bitcast_fusion
  240.5 4.5 %all-to-all-done.3 = f32[16,32,128]{2,1,0:T(8,128)S(1)} async-done(((f32[16,32,128]{2,1,0:T(8,128)}), f32[16,32,128]{2,1,0:T(8,128)S(1)}, u32[]{:S(2)}, u32[]{:S(2)}) %all-to-all-start.3) | async-done | bytes 262176 | tf_op jit(solution)/shard_map/all_to_all | solution.py:584
  (122 shorter events, 30.4 us)
Async XLA Ops:
  0.6 9.7 %copy-start = (f32[32,128]{1,0:T(8,128)S(1)}, f32[32,128]{1,0:T(8,128)}, u32[]{:S(2)}) copy-start(f32[32,128]{1,0:T(8,128)} %param.9) | copy-start | bytes 49156
  2.0 15.5 %all-to-all-start = ((s32[16,1,8]{2,1,0:T(1,128)}), s32[16,1,8]{2,1,0:T(1,128)S(1)}, u32[]{:S(2)}, u32[]{:S(2)}) async-start(s32[16,1,8]{2,1,0:T(1,128)} %copy.171), calls=%async_computation | async-start | bytes 16384 | tf_op jit(solution)/shard_map/all_to_all | solution.py:477
  12.3 6.6 %collective-permute-start = (f32[16,2048]{1,0:T(8,128)S(1)}, f32[16,2048]{1,0:T(8,128)S(1)}, u32[]{:S(2)}, u32[]{:S(2)}) collective-permute-start(f32[16,2048]{1,0:T(8,128)S(1)} %dynamic-slice_bitcast_fusion), channel_id=1, source_target_pairs={{0,1},{1,0},{2,3},{3,2},{4,5},{5,4},{6,7},{7,6},{8,9},{9,8},{10,11... | collective-permute-start | bytes 393224 | tf_op jit(solution)/shard_map/ppermute | solution.py:409
  13.9 6.3 %copy-start.11 = (s32[128]{0:T(128)}, s32[128]{0:T(128)S(1)}, u32[]{:S(2)}) copy-start(s32[128]{0:T(128)S(1)} %broadcast_minimum_fusion.leaf_ref) | copy-start | bytes 1540
  15.8 24.4 %copy-start.2 = (f32[3,2048]{0,1:T(8,128)}, f32[3,2048]{0,1:T(8,128)S(1)}, u32[]{:S(2)}) copy-start(f32[3,2048]{0,1:T(8,128)S(1)} %copy.173) | copy-start | bytes 73732
  21.0 20.6 %copy-start.9 = (s32[32,16]{0,1:T(8,128)S(1)}, s32[32,16]{0,1:T(8,128)}, u32[]{:S(2)}) copy-start(s32[32,16]{0,1:T(8,128)} %param.11) | copy-start | bytes 6148
  21.1 20.7 %copy-start.10 = (s32[32,3]{0,1:T(4,128)S(1)}, s32[32,3]{0,1:T(4,128)}, u32[]{:S(2)}) copy-start(s32[32,3]{0,1:T(4,128)} %param.13) | copy-start | bytes 1156
  21.1 26.8 %all-to-all-start.2 = ((f32[16,8,1280]{2,1,0:T(8,128)}), f32[16,8,1280]{2,1,0:T(8,128)S(1)}, u32[]{:S(2)}, u32[]{:S(2)}) async-start(f32[16,8,1280]{2,1,0:T(8,128)} %pad_bitcast_fusion), calls=%async_computation.2 | async-start | bytes 1310720 | tf_op jit(solution)/shard_map/all_to_all | solution.py:490
  26.9 15.8 %collective-permute-start.8 = (f32[3,64]{0,1:T(8,128)S(1)}, f32[3,64]{0,1:T(8,128)S(1)}, u32[]{:S(2)}, u32[]{:S(2)}) collective-permute-start(f32[3,64]{0,1:T(8,128)S(1)} %get-tuple-element.30), channel_id=1, source_target_pairs={{0,2},{2,4},{4,6},{6,8},{8,10},{10,12},{12,14},{14,16},{16,18},{18... | collective-permute-start | bytes 2312 | tf_op jit(solution)/shard_map/ppermute | solution.py:567
  30.7 12.0 %collective-permute-start.9 = (f32[3,64]{0,1:T(8,128)S(1)}, f32[3,64]{0,1:T(8,128)S(1)}, u32[]{:S(2)}, u32[]{:S(2)}) collective-permute-start(f32[3,64]{0,1:T(8,128)S(1)} %get-tuple-element.31), channel_id=1, source_target_pairs={{2,0},{4,2},{6,4},{8,6},{10,8},{12,10},{14,12},{16,14},{18,16},{20... | collective-permute-start | bytes 2312 | tf_op jit(solution)/shard_map/ppermute | solution.py:568
  33.6 24.6 %collective-permute-start.6 = (f32[64,128]{1,0:T(8,128)S(1)}, f32[64,128]{1,0:T(8,128)S(1)}, u32[]{:S(2)}, u32[]{:S(2)}) collective-permute-start(f32[64,128]{1,0:T(8,128)S(1)} %get-tuple-element.32), channel_id=1, source_target_pairs={{0,2},{2,4},{4,6},{6,8},{8,10},{10,12},{12,14},{14,16},{16,18},{18... | collective-permute-start | bytes 98312 | tf_op jit(solution)/shard_map/ppermute | solution.py:565
  38.1 20.1 %collective-permute-start.7 = (f32[64,128]{1,0:T(8,128)S(1)}, f32[64,128]{1,0:T(8,128)S(1)}, u32[]{:S(2)}, u32[]{:S(2)}) collective-permute-start(f32[64,128]{1,0:T(8,128)S(1)} %get-tuple-element.33), channel_id=1, source_target_pairs={{2,0},{4,2},{6,4},{8,6},{10,8},{12,10},{14,12},{16,14},{18,16},{20... | collective-permute-start | bytes 98312 | tf_op jit(solution)/shard_map/ppermute | solution.py:566
  47.9 170.3 %all-to-all-start.1 = ((f32[16,8,64,128]{3,2,1,0:T(8,128)}), f32[16,8,64,128]{3,2,1,0:T(8,128)}, u32[]{:S(2)}, u32[]{:S(2)}) async-start(f32[16,8,64,128]{3,2,1,0:T(8,128)} %bitcast.169), calls=%async_computation.1 | async-start | bytes 8388608 | tf_op jit(solution)/shard_map/all_to_all | solution.py:493
  58.2 7.6 %collective-permute-start.1 = (f32[128,1024]{1,0:T(8,128)}, f32[128,1024]{1,0:T(8,128)S(1)}, u32[]{:S(2)}, u32[]{:S(2)}) collective-permute-start(f32[128,1024]{1,0:T(8,128)} %slice.119), channel_id=1, source_target_pairs={{0,1},{1,0},{2,3},{3,2},{4,5},{5,4},{6,7},{7,6},{8,9},{9,8},{10,11... | collective-permute-start | bytes 1572872 | tf_op jit(solution)/shard_map/ppermute | solution.py:419
  126.7 1.7 copy-start.4
  129.7 7.0 %collective-permute-start.2 = (f32[1,8,128]{2,1,0:T(8,128)S(1)}, f32[1,8,128]{2,1,0:T(8,128)S(1)}, u32[]{:S(2)}, u32[]{:S(2)}) collective-permute-start(f32[1,8,128]{2,1,0:T(8,128)S(1)} %broadcast_in_dim_reshape_squeeze.3), channel_id=1, source_target_pairs={{0,2},{2,0},{4,6},{6,4},{8,10},{10,8},{12,14},{14,12},{16,18},{18,... | collective-permute-start | bytes 12296 | tf_op jit(solution)/shard_map/ppermute | solution.py:435
  134.0 7.7 %slice-start = ((f32[6,32,32,32]{3,2,1,0:T(8,128)}), f32[1,32,32,32]{3,2,1,0:T(8,128)S(1)}, s32[]{:S(2)}) async-start(f32[6,32,32,32]{3,2,1,0:T(8,128)} %copy-done.4), calls=%async_computation.4 | async-start | bytes 1048576 | tf_op jit(solution)/shard_map/slice | solution.py:550
  134.0 13.9 %copy-start.6 = (f32[32,32,64]{2,1,0:T(8,128)S(1)}, f32[32,32,64]{2,1,0:T(8,128)}, u32[]{:S(2)}) copy-start(f32[32,32,64]{2,1,0:T(8,128)} %get-tuple-element.18) | copy-start | bytes 786436
  136.8 3.7 %collective-permute-start.3 = (f32[2,8,128]{2,1,0:T(8,128)S(1)}, f32[2,8,128]{2,1,0:T(8,128)S(1)}, u32[]{:S(2)}, u32[]{:S(2)}) collective-permute-start(f32[2,8,128]{2,1,0:T(8,128)S(1)} %pad_maximum_fusion.6), channel_id=1, source_target_pairs={{0,4},{2,6},{4,0},{6,2},{8,12},{10,14},{12,8},{14,10},{16,20},{18,... | collective-permute-start | bytes 24584 | tf_op jit(solution)/shard_map/ppermute | solution.py:435
  140.5 3.8 %collective-permute-start.4 = (f32[4,8,128]{2,1,0:T(8,128)S(1)}, f32[4,8,128]{2,1,0:T(8,128)S(1)}, u32[]{:S(2)}, u32[]{:S(2)}) collective-permute-start(f32[4,8,128]{2,1,0:T(8,128)S(1)} %pad_maximum_fusion.5), channel_id=1, source_target_pairs={{0,8},{2,10},{4,12},{6,14},{8,0},{10,2},{12,4},{14,6},{16,24},{18,... | collective-permute-start | bytes 49160 | tf_op jit(solution)/shard_map/ppermute | solution.py:435
  144.3 7.6 %collective-permute-start.5 = (f32[8,8,128]{2,1,0:T(8,128)S(1)}, f32[8,8,128]{2,1,0:T(8,128)S(1)}, u32[]{:S(2)}, u32[]{:S(2)}) collective-permute-start(f32[8,8,128]{2,1,0:T(8,128)S(1)} %pad_maximum_fusion.4), channel_id=1, source_target_pairs={{0,16},{2,18},{4,20},{6,22},{8,24},{10,26},{12,28},{14,30},{16,0},... | collective-permute-start | bytes 98312 | tf_op jit(solution)/shard_map/ppermute | solution.py:435
  185.2 1.3 copy-start.3
  198.3 18.6 %copy-start.5 = (f32[32,2048]{1,0:T(8,128)S(1)}, f32[32,2048]{1,0:T(8,128)}, u32[]{:S(2)}) copy-start(f32[32,2048]{1,0:T(8,128)} %reshape.201) | copy-start | bytes 786436
  200.4 14.2 %copy-start.7 = (f32[8,64,32]{1,2,0:T(8,128)S(1)}, f32[8,64,32]{1,2,0:T(8,128)}, u32[]{:S(2)}) copy-start(f32[8,64,32]{1,2,0:T(8,128)} %copy.201) | copy-start | bytes 196612
  216.0 0.7 copy-start.8
  229.7 15.4 %all-to-all-start.3 = ((f32[16,32,128]{2,1,0:T(8,128)}), f32[16,32,128]{2,1,0:T(8,128)S(1)}, u32[]{:S(2)}, u32[]{:S(2)}) async-start(f32[16,32,128]{2,1,0:T(8,128)} %broadcast_in_dim.75), calls=%async_computation.3 | async-start | bytes 524288 | tf_op jit(solution)/shard_map/all_to_all | solution.py:584
  235.3 10.4 %copy-start.1 = (f32[32,128]{1,0:T(8,128)S(1)}, f32[32,128]{1,0:T(8,128)}, u32[]{:S(2)}) copy-start(f32[32,128]{1,0:T(8,128)} %param.9) | copy-start | bytes 49156

commit v2 on v1

v2 whole, which is shorter than its diff:
```python
import functools
import math

import jax
import jax.numpy as jnp
import numpy as np
from jax import lax
from jax.experimental import pallas as pl
from jax.experimental.pallas import tpu as pltpu
from jax.sharding import PartitionSpec as P

LEAF = 64
FAR = 16
GROUP = 4
BATCH = 16
LANES = 128
SUB = 8

length_scale = 0.3
shift_share = 0.05
highest = lax.Precision.HIGHEST
exponent_scale = -math.log2(math.e) / length_scale
vmem_bytes = 56 * 1024 * 1024

nt_dims = (((1,), (1,)), ((), ()))
tn_dims = (((0,), (0,)), ((), ()))


def halves(value):
    high = value.astype(jnp.bfloat16)
    low = (value - high.astype(jnp.float32)).astype(jnp.bfloat16)
    return high, low


def dot(a, b):
    return jnp.dot(a, b, preferred_element_type=jnp.float32)


def dot_exact(a, b):
    return jnp.dot(a, b, precision=highest, preferred_element_type=jnp.float32)


def dot_exact_nt(a, b):
    return lax.dot_general(a, b, nt_dims, precision=highest, preferred_element_type=jnp.float32)


def dot_nt(a, b):
    return lax.dot_general(a, b, nt_dims, preferred_element_type=jnp.float32)


def kernel_half(source_rows, target, lane, valid):
    total = None
    for axis in range(3):
        difference = source_rows[axis : axis + 1, :] - target[:, axis : axis + 1]
        square = difference * difference
        total = square if total is None else total + square
    distance = total * lax.rsqrt(jnp.maximum(total, 1e-30))
    values = jnp.exp2(distance * exponent_scale)
    return jnp.where(lane < valid, values, 0.0)


def blocks_body(
    total_ref, leaf_ref, count_ref, slot_ref, place_ref,
    own_ref, other_ref, coords_ref, target_ref,
    high_ref, low_ref, sketched_ref, gram_ref,
    packed,
    *, rank,
):
    step = pl.program_id(0)
    lane = lax.broadcasted_iota(jnp.int32, (1, LANES), 1)
    first = lane < LEAF

    @pl.when(step == 0)
    def _():
        sketched_ref[...] = jnp.zeros_like(sketched_ref)
        quarter = rank // 4
        own_at = pl.multiple_of(place_ref[0] * 2 * quarter, quarter)
        other_at = pl.multiple_of((1 - place_ref[0]) * 2 * quarter, quarter)

        def unpack(slot, carry):
            for ref, base in ((own_ref, own_at), (other_ref, other_at)):
                value = ref[pl.ds(pl.multiple_of(slot * quarter, quarter), quarter), :]
                turned = pltpu.roll(value, LEAF, 1)
                packed[slot, pl.ds(base, quarter), :] = jnp.where(first, value, turned)
                packed[slot, pl.ds(base + quarter, quarter), :] = jnp.where(first, turned, value)
            value = coords_ref[pl.ds(slot * 2, 2), :]
            turned = pltpu.roll(value, LEAF, 1)
            packed[slot, rank : rank + 1, :] = jnp.where(first, value, turned)[0:1]
            packed[slot, rank + 1 : rank + 2, :] = jnp.where(first, turned, value)[0:1]
            packed[slot, rank + 2 : rank + 3, :] = jnp.where(first, value, turned)[1:2]
            return carry

        lax.fori_loop(0, packed.shape[0], unpack, 0, unroll=4)

    @pl.when(step * BATCH < total_ref[0])
    def _():
        for member in range(BATCH):
            group = step * BATCH + member
            leaf = leaf_ref[group]
            count = count_ref[group]
            slots = [slot_ref[group * GROUP + e] for e in range(GROUP)]
            target = target_ref[leaf]
            z_parts = []
            for half in range(GROUP // 2):
                left = packed[slots[2 * half]]
                right = packed[slots[2 * half + 1]]
                both = jnp.where(first, left, right)
                values = kernel_half(both[rank : rank + 3], target, lane, (count - 2 * half) * LEAF)
                high, low = halves(values)
                high_ref[member, :, half * LANES : (half + 1) * LANES] = high
                low_ref[member, :, half * LANES : (half + 1) * LANES] = low
                z_parts.append(both[:rank])
            z_high, z_low = halves(jnp.concatenate(z_parts, axis=1))
            k_high = high_ref[member]
            k_low = low_ref[member]
            update = dot_nt(z_high, k_high) + (dot_nt(z_low, k_high) + dot_nt(z_high, k_low))
            sketched_ref[leaf] += update

    @pl.when(step == pl.num_programs(0) - 1)
    def _():
        for leaf in range(gram_ref.shape[0]):
            block = sketched_ref[leaf]
            gram_ref[leaf] = dot_exact_nt(block, block)


def kernel_blocks(total, group_leaf, group_count, group_slots, place, own, other, coords, targets, rank):
    leaves = targets.shape[0]
    groups = group_leaf.shape[0]
    slots = coords.shape[0] // 2
    steps = groups // BATCH

    def block_index(step, total_ref, *unused):
        last = (total_ref[0] - 1) // BATCH
        return (jnp.minimum(step, last), 0, 0)

    flat = lambda *unused: (0, 0)
    whole = lambda *unused: (0, 0, 0)
    once = pl.Buffered(1)
    return pl.pallas_call(
        functools.partial(blocks_body, rank=rank),
        grid_spec=pltpu.PrefetchScalarGridSpec(
            num_scalar_prefetch=5,
            grid=(steps,),
            in_specs=[
                pl.BlockSpec(own.shape, flat, pipeline_mode=once),
                pl.BlockSpec(other.shape, flat, pipeline_mode=once),
                pl.BlockSpec(coords.shape, flat, pipeline_mode=once),
                pl.BlockSpec(targets.shape, whole, pipeline_mode=once),
            ],
            out_specs=[
                pl.BlockSpec((BATCH, LEAF, GROUP * LEAF), block_index),
                pl.BlockSpec((BATCH, LEAF, GROUP * LEAF), block_index),
                pl.BlockSpec((leaves, rank, LEAF), whole),
                pl.BlockSpec((leaves, rank, rank), whole),
            ],
            scratch_shapes=[pltpu.VMEM((slots, rank + SUB, LANES), jnp.float32)],
        ),
        out_shape=[
            jax.ShapeDtypeStruct((groups, LEAF, GROUP * LEAF), jnp.bfloat16),
            jax.ShapeDtypeStruct((groups, LEAF, GROUP * LEAF), jnp.bfloat16),
            jax.ShapeDtypeStruct((leaves, rank, LEAF), jnp.float32),
            jax.ShapeDtypeStruct((leaves, rank, rank), jnp.float32),
        ],
        compiler_params=pltpu.CompilerParams(vmem_limit_bytes=vmem_bytes),
        name="kernel_blocks",
        cost_estimate=pl.CostEstimate(
            flops=2 * 10**10, bytes_accessed=2 * 10**7, transcendentals=0
        ),
    )(total, group_leaf, group_count, group_slots, place, own, other, coords, targets)


def far_body(
    total_ref, leaf_ref, slot_ref,
    fetched_ref, high_ref, low_ref, weights_ref, path_ref,
    out_ref, projected_ref, root_ref,
    s_high, s_low, acc,
):
    step = pl.program_id(0)
    samp_dev = fetched_ref.shape[2]

    @pl.when(step == 0)
    def _():
        acc[...] = jnp.zeros_like(acc)

        def split(slot, carry):
            s_high[slot], s_low[slot] = halves(fetched_ref[slot])
            return carry

        lax.fori_loop(0, fetched_ref.shape[0], split, 0, unroll=8)

    @pl.when(step * BATCH < total_ref[0])
    def _():
        for member in range(BATCH):
            group = step * BATCH + member
            leaf = leaf_ref[group]
            slots = [slot_ref[group * GROUP + e] for e in range(GROUP)]
            rows_high = jnp.concatenate([s_high[slot] for slot in slots], axis=0)
            rows_low = jnp.concatenate([s_low[slot] for slot in slots], axis=0)
            k_high = high_ref[member]
            k_low = low_ref[member]
            acc[leaf] += dot(k_high, rows_high) + (dot(k_high, rows_low) + dot(k_low, rows_high))

    @pl.when(step == pl.num_programs(0) - 1)
    def _():
        leaves = acc.shape[0]
        rows = acc[...].reshape(leaves * LEAF, samp_dev)
        projected = dot_exact(weights_ref[...], rows)
        projected_ref[...] = projected
        root_ref[...] = lax.dot_general(
            path_ref[...], projected, tn_dims, precision=highest, preferred_element_type=jnp.float32
        )
        for pair in range(leaves // 2):
            block = acc[2 * pair : 2 * pair + 2].reshape(2 * LEAF, samp_dev)
            out_ref[:, 2 * pair * LEAF : 2 * (pair + 1) * LEAF] = block.T


def far_products(total, group_leaf, group_slots, fetched, high, low, weights, path):
    slots, unused, samp_dev = fetched.shape
    groups = group_leaf.shape[0]
    points_dev = weights.shape[1]
    leaves = points_dev // LEAF
    steps = groups // BATCH

    def block_index(step, total_ref, *unused):
        last = (total_ref[0] - 1) // BATCH
        return (jnp.minimum(step, last), 0, 0)

    return pl.pallas_call(
        far_body,
        grid_spec=pltpu.PrefetchScalarGridSpec(
            num_scalar_prefetch=3,
            grid=(steps,),
            in_specs=[
                pl.BlockSpec(fetched.shape, lambda *unused: (0, 0, 0), pipeline_mode=pl.Buffered(1)),
                pl.BlockSpec((BATCH, LEAF, GROUP * LEAF), block_index),
                pl.BlockSpec((BATCH, LEAF, GROUP * LEAF), block_index),
                pl.BlockSpec(weights.shape, lambda *unused: (0, 0), pipeline_mode=pl.Buffered(1)),
                pl.BlockSpec(path.shape, lambda *unused: (0, 0), pipeline_mode=pl.Buffered(1)),
            ],
            out_specs=[
                pl.BlockSpec((samp_dev, points_dev), lambda *unused: (0, 0)),
                pl.BlockSpec((weights.shape[0], samp_dev), lambda *unused: (0, 0)),
                pl.BlockSpec((weights.shape[0], samp_dev), lambda *unused: (0, 0)),
            ],
            scratch_shapes=[
                pltpu.VMEM((slots, LEAF, samp_dev), jnp.bfloat16),
                pltpu.VMEM((slots, LEAF, samp_dev), jnp.bfloat16),
                pltpu.VMEM((leaves, LEAF, samp_dev), jnp.float32),
            ],
        ),
        out_shape=[
            jax.ShapeDtypeStruct((samp_dev, points_dev), jnp.float32),
            jax.ShapeDtypeStruct((weights.shape[0], samp_dev), jnp.float32),
            jax.ShapeDtypeStruct((weights.shape[0], samp_dev), jnp.float32),
        ],
        compiler_params=pltpu.CompilerParams(vmem_limit_bytes=vmem_bytes),
        name="far_products",
        cost_estimate=pl.CostEstimate(
            flops=10**10, bytes_accessed=2 * 10**7, transcendentals=0
        ),
    )(total, group_leaf, group_slots, fetched, high, low, weights, path)


NEAR_LEAVES = 8


def near_body(mask_ref, rows_ref, coords_ref, target_ref, out_ref):
    step = pl.program_id(0)
    samp_dev = rows_ref.shape[2]
    lane = lax.broadcasted_iota(jnp.int32, (1, LANES), 1)
    first = lane < LEAF
    for pair in range(NEAR_LEAVES // 2):
        results = []
        for member in range(2):
            leaf = step * NEAR_LEAVES + 2 * pair + member
            target = target_ref[leaf]
            k_high = []
            k_low = []
            for half in range(2):
                both = jnp.where(first, coords_ref[leaf + 2 * half], coords_ref[leaf + 2 * half + 1])
                values = kernel_half(both, target, lane, LANES)
                left = mask_ref[leaf * 3 + 2 * half].astype(jnp.float32)
                if half == 0:
                    right = mask_ref[leaf * 3 + 1].astype(jnp.float32)
                else:
                    right = jnp.float32(0.0)
                high, low = halves(values * jnp.where(first, left, right))
                k_high.append(high)
                k_low.append(low)
            k_high = jnp.concatenate(k_high, axis=1)
            k_low = jnp.concatenate(k_low, axis=1)
            rows = rows_ref[pl.ds(leaf, 4)].reshape(4 * LEAF, samp_dev)
            rows_high, rows_low = halves(rows)
            results.append(
                dot(k_high, rows_high) + (dot(k_high, rows_low) + dot(k_low, rows_high))
            )
        block = jnp.concatenate(results, axis=0)
        out_ref[:, 2 * pair * LEAF : 2 * (pair + 1) * LEAF] = block.T


def near_products(mask, rows, coords, targets):
    leaves = targets.shape[0]
    samp_dev = rows.shape[2]
    whole = lambda *unused: (0, 0, 0)
    return pl.pallas_call(
        near_body,
        grid_spec=pltpu.PrefetchScalarGridSpec(
            num_scalar_prefetch=1,
            grid=(leaves // NEAR_LEAVES,),
            in_specs=[
                pl.BlockSpec(rows.shape, whole),
                pl.BlockSpec(coords.shape, whole),
                pl.BlockSpec(targets.shape, whole),
            ],
            out_specs=pl.BlockSpec((samp_dev, NEAR_LEAVES * LEAF), lambda step, *unused: (0, step)),
        ),
        out_shape=jax.ShapeDtypeStruct((samp_dev, leaves * LEAF), jnp.float32),
        compiler_params=pltpu.CompilerParams(vmem_limit_bytes=vmem_bytes),
        name="near_products",
        cost_estimate=pl.CostEstimate(
            flops=4 * 10**9, bytes_accessed=10**7, transcendentals=0
        ),
    )(mask, rows, coords, targets)


def to_lanes(source, target, rank):
    nodes = source.shape[0] // rank
    target[...] = jnp.zeros_like(target)
    for r in range(rank):
        target[r, :, 0:nodes] = source[pl.ds(r, nodes, stride=rank), :].T


def from_lanes(columns, target, r, nodes, rank):
    target[pl.ds(r, nodes, stride=rank), :] = columns.T[0:nodes]


def eliminate(current, left, inverse, level, rank):
    tiles = rank // SUB
    row = lax.broadcasted_iota(jnp.int32, (SUB, LANES), 0)
    diagonal = [current[j, j : j + 1, :] for j in range(rank)]
    while len(diagonal) > 1:
        diagonal = [diagonal[i] + diagonal[i + 1] for i in range(0, len(diagonal), 2)]
    share = shift_share * diagonal[0] / rank
    shift = share + 1e-06
    a = [
        {t: current[j, SUB * t : SUB * (t + 1), :] for t in range(j // SUB, tiles)}
        for j in range(rank)
    ]
    for j in range(rank):
        a[j][j // SUB] = a[j][j // SUB] + jnp.where(row == j % SUB, shift, 0.0)
    m = []
    scales = []
    for k in range(rank):
        tk, rk = k // SUB, k % SUB
        root = lax.rsqrt(a[k][tk][rk : rk + 1, :])
        scales.append(root)
        reciprocal = root * root
        column = {t: a[k][t] * reciprocal for t in range(tk, tiles)}
        column[tk] = jnp.where(row > rk, column[tk], 0.0)
        for j in range(k + 1, rank):
            factor = a[k][j // SUB][j % SUB : j % SUB + 1, :]
            for t in range(j // SUB, tiles):
                a[j][t] = a[j][t] - column[t] * factor
        for c in range(k):
            factor = m[c][tk][rk : rk + 1, :]
            for t in range(tk, tiles):
                m[c][t] = m[c][t] - column[t] * factor
        fresh = {t: -column[t] for t in range(tk, tiles)}
        fresh[tk] = jnp.where(row == rk, 1.0, fresh[tk])
        m.append(fresh)
        if left is not None:
            for t in range(tiles):
                if t < tk:
                    value = jnp.zeros((SUB, LANES), jnp.float32)
                else:
                    value = a[k][t] * root
                if t == tk:
                    value = jnp.where(row >= rk, value, 0.0)
                left[k, SUB * t : SUB * (t + 1), :] = value
    for t in range(tiles):
        scale = jnp.concatenate(scales[SUB * t : SUB * (t + 1)], axis=0)
        for c in range(rank):
            value = m[c][t] * scale if t >= c // SUB else jnp.zeros((SUB, LANES), jnp.float32)
            inverse[c * rank + SUB * t : c * rank + SUB * (t + 1), :] = value
    return shift, share


def inverse_row(inverse, r, t, rank):
    return inverse[pl.ds(SUB * t * rank + r, SUB, stride=rank), :]


def pair_up(value, level):
    return value + pltpu.roll(value, LANES - lax.shift_left(1, level), 1)


def level_fast(level, levels, current, left, inverse, squared, ratio, child, lowest, rank, child_at):
    tiles = rank // SUB
    row = lax.broadcasted_iota(jnp.int32, (SUB, LANES), 0)
    shift, share = eliminate(current, left, inverse, level, rank)
    lowest[...] = jnp.minimum(lowest[...], share)

    for block in range(tiles):
        sums = [[None] * tiles for _ in range(SUB)]
        for r in range(SUB * block, rank):
            parts = [inverse_row(inverse, r, t, rank) for t in range(block, r // SUB + 1)]
            for q in range(SUB):
                if SUB * block + q > r:
                    continue
                factor = parts[0][q : q + 1, :]
                for t in range(block, r // SUB + 1):
                    term = parts[t - block] * factor
                    sums[q][t] = term if sums[q][t] is None else sums[q][t] + term
        for q in range(SUB):
            at = (SUB * block + q) * rank
            for t in range(block, tiles):
                squared[at + SUB * t : at + SUB * (t + 1), :] = sums[q][t]

    if child is not None:
        @pl.when(child_at(level))
        def _():
            for r in range(rank):
                for t in range(tiles):
                    value = left[r, SUB * t : SUB * (t + 1), :]
                    if t <= r // SUB:
                        value = value - shift * inverse_row(inverse, r, t, rank)
                    child[r, SUB * t : SUB * (t + 1), :] = value

    for q in range(rank):
        for t in range(tiles):
            if t >= q // SUB:
                value = squared[q * rank + SUB * t : q * rank + SUB * (t + 1), :]
            else:
                value = squared[pl.ds(SUB * t * rank + q, SUB, stride=rank), :]
            value = -shift * value
            if t == q // SUB:
                value = value + jnp.where(row == q % SUB, 1.0, 0.0)
            if ratio is not None:
                ratio[level, q, SUB * t : SUB * (t + 1), :] = value
            here = current[q, SUB * t : SUB * (t + 1), :] - shift * value
            current[q, SUB * t : SUB * (t + 1), :] = pair_up(here, level)


def level_plain(level, levels, current, left, inverse, squared, ratio, child, lowest, rank, child_at):
    tiles = rank // SUB
    eliminate(current, left, inverse, level, rank)

    def products(out, count, left_of, right_of):
        def block_step(block, carry):
            offset = pl.multiple_of(block * SUB, SUB)
            sums = [[None] * tiles for _ in range(SUB)]
            for r in range(count):
                parts = [left_of(r, t) for t in range(tiles)]
                heads = right_of(r, offset)
                for q in range(SUB):
                    for t in range(tiles):
                        term = parts[t] * heads[q : q + 1, :]
                        sums[q][t] = term if sums[q][t] is None else sums[q][t] + term
            for q in range(SUB):
                for t in range(tiles):
                    out(offset + q, t, sums[q][t])
            return carry

        lax.fori_loop(0, tiles, block_step, 0)

    def tile(t):
        return slice(SUB * t, SUB * (t + 1))

    def put_child(r, t, value):
        squared[pl.ds(pl.multiple_of(r * rank + SUB * t, SUB), SUB), :] = value

    products(
        put_child, rank,
        lambda k, t: current[k, tile(t), :],
        lambda k, offset: inverse[pl.ds(pl.multiple_of(k * rank + offset, SUB), SUB), :],
    )
    if child is not None:
        @pl.when(child_at(level))
        def _():
            for r in range(rank):
                for t in range(tiles):
                    child[r, tile(t), :] = squared[r * rank + SUB * t : r * rank + SUB * (t + 1), :]

    def child_part(r, t):
        return squared[r * rank + SUB * t : r * rank + SUB * (t + 1), :]

    def put_current(q, t, value):
        current[q, tile(t), :] = pair_up(value, level)

    if ratio is not None:
        def put_ratio(c, t, value):
            ratio[level, c, tile(t), :] = value

        def inverse_head(r, offset):
            return inverse[pl.ds(offset * rank + r, SUB, stride=rank), :]

        products(put_ratio, rank, child_part, inverse_head)
    products(
        put_current, rank, child_part,
        lambda r, offset: squared[pl.ds(pl.multiple_of(r * rank + offset, SUB), SUB), :],
    )


def run_levels(source, levels, nodes, current, left, inverse, squared, ratio, child, lowest, rank, child_at, finish):
    lowest[...] = jnp.full((1, LANES), 1.0, jnp.float32)

    def sweep(level_step):
        to_lanes(source, current, rank)

        def body(level, carry):
            level_step(level, levels, current, left, inverse, squared, ratio, child, lowest, rank, child_at)
            finish(level)
            return carry

        lax.fori_loop(0, levels, body, 0)

    sweep(level_fast)
    lane = lax.broadcasted_iota(jnp.int32, (1, LANES), 1)
    least = jnp.min(jnp.where(lane < nodes, lowest[...], 1.0))

    @pl.when(least < 2e-06)
    def _():
        sweep(level_plain)


def branch_body(gram_ref, inverse_ref, ratio_ref, top_ref, child_ref, current, left, inverse, squared, child, lowest, *, rank, levels):
    nodes = gram_ref.shape[0] // rank

    def finish(level):
        @pl.when(level == 0)
        def _():
            for c in range(rank):
                inverse_ref[c] = inverse[c * rank : (c + 1) * rank, :]

        @pl.when(level == levels - 1)
        def _():
            for r in range(rank):
                child_ref[r : r + 1, :] = child[r].T[0:1, :]
                top_ref[r : r + 1, :] = jnp.concatenate(
                    [inverse_row(inverse, r, t, rank) for t in range(rank // SUB)], axis=0
                ).T[0:1, :]

    run_levels(
        gram_ref, levels, nodes, current, left, inverse, squared, ratio_ref, child, lowest, rank,
        lambda level: level == levels - 1, finish,
    )


vmem_spec = pl.BlockSpec(memory_space=pltpu.VMEM)


def tree_scratch(rank):
    return [
        pltpu.VMEM((rank, rank, LANES), jnp.float32),
        pltpu.VMEM((rank, rank, LANES), jnp.float32),
        pltpu.VMEM((rank * rank, LANES), jnp.float32),
        pltpu.VMEM((rank * rank, LANES), jnp.float32),
        pltpu.VMEM((rank, rank, LANES), jnp.float32),
        pltpu.VMEM((1, LANES), jnp.float32),
    ]


def branch_factors(gram, levels):
    leaves, rank, unused = gram.shape
    return pl.pallas_call(
        functools.partial(branch_body, rank=rank, levels=levels),
        in_specs=[vmem_spec],
        out_specs=[vmem_spec] * 4,
        out_shape=[
            jax.ShapeDtypeStruct((rank, rank, LANES), jnp.float32),
            jax.ShapeDtypeStruct((levels, rank, rank, LANES), jnp.float32),
            jax.ShapeDtypeStruct((rank, rank), jnp.float32),
            jax.ShapeDtypeStruct((rank, rank), jnp.float32),
        ],
        scratch_shapes=tree_scratch(rank),
        compiler_params=pltpu.CompilerParams(vmem_limit_bytes=vmem_bytes),
        name="branch_factors",
        cost_estimate=pl.CostEstimate(flops=10**10, bytes_accessed=10**7, transcendentals=0),
    )(gram.reshape(leaves * rank, rank))


def basis_body(inverse_ref, ratio_ref, top_ref, sketched_ref, weights_ref, basis_ref, natural, *, rank, levels):
    leaves = sketched_ref.shape[0]
    upper = [top_ref[...]]
    for level in range(levels - 2, -1, -1):
        stride = 2**level
        for c in range(rank):
            from_lanes(ratio_ref[level, c], natural, c, leaves, rank)
        fresh = []
        for node in range(leaves // stride):
            block = natural[node * stride * rank : (node * stride + 1) * rank, :]
            fresh.append(dot_exact(upper[node // 2], block))
        upper = fresh
    for r in range(rank):
        from_lanes(inverse_ref[r], natural, r, leaves, rank)
    for pair in range(leaves // 2):
        results = []
        for leaf in (2 * pair, 2 * pair + 1):
            block = sketched_ref[leaf]
            own = lax.dot_general(
                natural[leaf * rank : (leaf + 1) * rank, :], block, tn_dims,
                precision=highest, preferred_element_type=jnp.float32,
            )
            results.append(jnp.concatenate([dot_exact(upper[leaf], block), own], axis=0))
        both = jnp.concatenate(results, axis=1)
        weights_ref[:, pair * 2 * LEAF : (pair + 1) * 2 * LEAF] = both[:rank]
        basis_ref[:, pair * 2 * LEAF : (pair + 1) * 2 * LEAF] = both[rank:]


def bases(inverse, ratio, top, sketched):
    leaves, rank, unused = sketched.shape
    levels = ratio.shape[0]
    shape = jax.ShapeDtypeStruct((rank, leaves * LEAF), jnp.float32)
    return pl.pallas_call(
        functools.partial(basis_body, rank=rank, levels=levels),
        in_specs=[vmem_spec] * 4,
        out_specs=[vmem_spec] * 2,
        out_shape=[shape, shape],
        scratch_shapes=[pltpu.VMEM((leaves * rank, rank), jnp.float32)],
        compiler_params=pltpu.CompilerParams(vmem_limit_bytes=vmem_bytes),
        name="bases",
        cost_estimate=pl.CostEstimate(flops=5 * 10**9, bytes_accessed=10**7, transcendentals=0),
    )(inverse, ratio, top, sketched)


def top_body(place_ref, children_ref, transfer_ref, path_ref, source, current, left, inverse, squared, child, lowest, nat_inverse, nat_child, *, rank, levels):
    nodes = children_ref.shape[0] // 2
    for node in range(nodes):
        both = children_ref[2 * node : 2 * node + 2].reshape(2 * rank, rank)
        source[node * rank : (node + 1) * rank, :] = lax.dot_general(
            both, both, tn_dims, precision=highest, preferred_element_type=jnp.float32
        )

    def finish(level):
        for r in range(rank):
            from_lanes(child[r], nat_child.at[level], r, nodes, rank)
            from_lanes(inverse[r * rank : (r + 1) * rank, :], nat_inverse.at[level], r, nodes, rank)

    run_levels(
        source, levels, nodes, current, left, inverse, squared, None, child, lowest, rank,
        lambda level: level >= 0, finish,
    )
    offset = 0
    for level in range(levels):
        for node in range(nodes >> level):
            if level == 0:
                stacked = children_ref[2 * node : 2 * node + 2].reshape(2 * rank, rank)
            else:
                first = 2 * node << level - 1
                second = 2 * node + 1 << level - 1
                stacked = jnp.concatenate(
                    [
                        nat_child[level - 1, first * rank : (first + 1) * rank, :],
                        nat_child[level - 1, second * rank : (second + 1) * rank, :],
                    ],
                    axis=0,
                )
            at = (node << level) * rank
            transfer_ref[offset + node] = dot_exact(stacked, nat_inverse[level, at : at + rank, :])
        offset += nodes >> level
    me = place_ref[0]
    offset = 0
    path = None
    for level in range(levels):
        node = offset + lax.shift_right_logical(me, level + 1)
        side = lax.rem(lax.shift_right_logical(me, level), 2)
        block = transfer_ref[node, pl.ds(pl.multiple_of(side * rank, rank), rank), :]
        path = block if path is None else dot_exact(path, block)
        offset += nodes >> level
    path_ref[...] = path


def top_factors(children, place):
    branches, rank, unused = children.shape
    levels = branches.bit_length() - 1
    nodes = branches // 2
    natural = pltpu.VMEM((levels, nodes * rank, rank), jnp.float32)
    return pl.pallas_call(
        functools.partial(top_body, rank=rank, levels=levels),
        in_specs=[pl.BlockSpec(memory_space=pltpu.SMEM), vmem_spec],
        out_specs=[vmem_spec] * 2,
        out_shape=[
            jax.ShapeDtypeStruct((branches - 1, 2 * rank, rank), jnp.float32),
            jax.ShapeDtypeStruct((rank, rank), jnp.float32),
        ],
        scratch_shapes=[pltpu.VMEM((nodes * rank, rank), jnp.float32)]
        + tree_scratch(rank)
        + [natural, natural],
        compiler_params=pltpu.CompilerParams(vmem_limit_bytes=vmem_bytes),
        name="top_factors",
        cost_estimate=pl.CostEstimate(flops=10**10, bytes_accessed=10**7, transcendentals=0),
    )(place, children)


def exchange_sum(pieces, axis):
    count = pieces.shape[0]
    me = lax.axis_index(axis)
    mine = lax.dynamic_index_in_dim(pieces, me, 0, keepdims=False)
    for step in range(1, count):
        outgoing = lax.dynamic_index_in_dim(pieces, (me + step) % count, 0, keepdims=False)
        mine = mine + lax.ppermute(
            outgoing, axis, [(i, (i + step) % count) for i in range(count)]
        )
    return mine


def exchange_all(piece, axis):
    count = lax.axis_size(axis)
    me = lax.axis_index(axis)
    if count == 2:
        other = lax.ppermute(piece, axis, [(0, 1), (1, 0)])
        return jnp.stack([jnp.where(me == 0, piece, other), jnp.where(me == 0, other, piece)])
    result = jnp.zeros((count,) + piece.shape, piece.dtype)
    result = lax.dynamic_update_index_in_dim(result, piece, me, 0)
    for step in range(1, count):
        arrived = lax.ppermute(piece, axis, [(i, (i + step) % count) for i in range(count)])
        result = lax.dynamic_update_index_in_dim(result, arrived, (me - step) % count, 0)
    return result


def double_all(piece, axis):
    count = lax.axis_size(axis)
    me = lax.axis_index(axis)
    held = piece[None]
    stride = 1
    while stride < count:
        other = lax.ppermute(held, axis, [(i, i ^ stride) for i in range(count)])
        low = (me // stride) % 2 == 0
        held = jnp.concatenate([jnp.where(low, held, other), jnp.where(low, other, held)], axis=0)
        stride *= 2
    return held


def group_tables(far_slots, far_count):
    leaves = far_slots.shape[0]
    groups = leaves * FAR // GROUP
    per_leaf = (far_count + GROUP - 1) // GROUP
    before = jnp.arange(leaves)[:, None] >= jnp.arange(leaves)[None, :]
    ends = jnp.sum(jnp.where(before, per_leaf[None, :], 0), axis=1)
    total = ends[leaves - 1 :]
    ids = jnp.arange(groups, dtype=jnp.int32)
    leaf = jnp.minimum(jnp.sum((ends[None, :] <= ids[:, None]).astype(jnp.int32), axis=1), leaves - 1)
    hit = leaf[:, None] == jnp.arange(leaves)[None, :]
    start = jnp.sum(jnp.where(hit, (ends - per_leaf)[None, :], 0), axis=1)
    length = jnp.sum(jnp.where(hit, far_count[None, :], 0), axis=1)
    sub = ids - start
    count = jnp.where(ids < total, jnp.clip(length - GROUP * sub, 0, GROUP), 0)
    first = jnp.minimum(sub, FAR // GROUP - 1)
    slots = far_slots.reshape(leaves * FAR // GROUP, GROUP)[leaf * (FAR // GROUP) + first]
    return (
        total.astype(jnp.int32),
        leaf.astype(jnp.int32),
        count.astype(jnp.int32),
        slots.reshape(-1).astype(jnp.int32),
    )


def two_rows(values, rows):
    leaves = values.shape[1]
    split = jnp.transpose(values.reshape(2, rows, leaves, LEAF), (2, 1, 0, 3))
    return split.reshape(leaves, rows, 2 * LEAF)


def on_device(points, samples, sketch, far_requests, far_slots, far_count, near_mask):
    samp_dev = samples.shape[0]
    leaves = samples.shape[1] // LEAF
    rank = sketch.shape[0]
    branches = lax.axis_size("leaf")
    columns = lax.axis_size("cols")
    cap = far_requests.shape[2]
    slots = branches * cap
    share = rank // columns
    me = lax.axis_index("leaf").astype(jnp.int32).reshape(1)
    column = lax.axis_index("cols")

    wanted = far_requests.reshape(branches, cap)
    asked_for = lax.all_to_all(wanted, "leaf", split_axis=0, concat_axis=0, tiled=True)

    coords = jnp.transpose(points.reshape(3, leaves, LEAF), (1, 0, 2))
    targets = jnp.transpose(coords, (0, 2, 1))
    rows = jnp.transpose(samples.reshape(samp_dev, leaves, LEAF), (1, 2, 0))
    tables = group_tables(far_slots, far_count)

    z_part = jnp.dot(sketch, samples, precision=highest)
    z_mine = exchange_sum(z_part.reshape(columns, share, leaves * LEAF), "cols")
    z_rows = two_rows(z_mine.reshape(share, leaves, LEAF), share // 2)
    c_rows = two_rows(
        jnp.pad(points.reshape(3, leaves, LEAF)[jnp.array([0, 2, 1])], ((0, 1), (0, 0), (0, 0))), 2
    )
    asked_for, rows, z_rows, c_rows, tables = lax.optimization_barrier(
        (asked_for, rows, z_rows, c_rows, tables)
    )
    total, group_leaf, group_count, group_slots = tables
    picked = asked_for.reshape(-1)
    z_sent = z_rows[picked].reshape(branches, cap * share // 2, LANES)
    c_sent = c_rows[picked].reshape(branches, cap * 2, LANES)
    small_sent = jnp.concatenate([z_sent, c_sent], axis=1)
    small_got = lax.all_to_all(small_sent, "leaf", split_axis=0, concat_axis=0, tiled=True)

    rows_sent = rows[picked].reshape(branches, cap, LEAF, samp_dev)
    rows_got = lax.all_to_all(rows_sent, "leaf", split_axis=0, concat_axis=0, tiled=True)
    fetched = rows_got.reshape(slots, LEAF, samp_dev)

    z_own = small_got[:, : cap * share // 2].reshape(slots * share // 2, LANES)
    c_got = small_got[:, cap * share // 2 :].reshape(slots * 2, LANES)
    if columns == 2:
        z_other = lax.ppermute(z_own, "cols", [(0, 1), (1, 0)])
        place = column.astype(jnp.int32).reshape(1)
    else:
        z_all = exchange_all(z_own, "cols").reshape(columns, slots, share // 2, 2, LEAF)
        z_all = jnp.transpose(z_all, (1, 0, 3, 2, 4)).reshape(slots, 2, 2, rank // 4, LEAF)
        z_all = jnp.transpose(z_all, (1, 0, 3, 2, 4)).reshape(2, slots * rank // 4, LANES)
        z_own, z_other = z_all[0], z_all[1]
        place = jnp.zeros((1,), jnp.int32)

    high, low, sketched, gram = kernel_blocks(
        total, group_leaf, group_count, group_slots, place, z_own, z_other, c_got, targets, rank
    )

    levels = leaves.bit_length()
    inverse, ratio, top_inverse, own_child = branch_factors(gram, levels)
    children = double_all(own_child.reshape(rank * rank // LANES, LANES), "leaf")
    top_transfer, path = top_factors(children.reshape(branches, rank, rank), me)
    weights, leaf_basis = bases(inverse, ratio, top_inverse, sketched)

    edges = jnp.concatenate([rows[:1], rows[leaves - 1 :]], axis=0)
    edge_coords = jnp.concatenate([coords[:1], coords[leaves - 1 :]], axis=0)
    edge_coords = jnp.pad(edge_coords, ((0, 0), (0, 5), (0, samp_dev - LEAF))) if samp_dev >= LEAF else None
    forward = [(i, i + 1) for i in range(branches - 1)]
    backward = [(target, source) for source, target in forward]
    if edge_coords is not None:
        edges = jnp.concatenate([edges, edge_coords], axis=1)
        edges, unused = lax.optimization_barrier((edges, small_got))
        low_edge = lax.ppermute(edges[1], "leaf", forward)
        high_edge = lax.ppermute(edges[0], "leaf", backward)
        rows_low, rows_high = low_edge[:LEAF], high_edge[:LEAF]
        coords_low, coords_high = low_edge[LEAF : LEAF + 3, :LEAF], high_edge[LEAF : LEAF + 3, :LEAF]
    else:
        rows_low = lax.ppermute(edges[1], "leaf", forward)
        rows_high = lax.ppermute(edges[0], "leaf", backward)
        coords_low = lax.ppermute(coords[leaves - 1], "leaf", forward)
        coords_high = lax.ppermute(coords[0], "leaf", backward)
    near_rows = jnp.concatenate(
        [rows_low[None], rows, rows_high[None], jnp.zeros_like(rows_low)[None]], axis=0
    )
    near_coords = jnp.concatenate(
        [coords_low[None], coords, coords_high[None], jnp.zeros_like(coords_low)[None]], axis=0
    )
    near_coords = jnp.pad(near_coords, ((0, 0), (0, 5), (0, 0)))
    near_coords = jnp.concatenate([near_coords, near_coords], axis=2)
    near_sample = near_products(near_mask.reshape(-1), near_rows, near_coords, targets)

    far_sample, branch_samples, root_part = far_products(
        total, group_leaf, group_slots, fetched, high, low, weights, path
    )
    root_sample = lax.psum(root_part, "leaf")
    return (far_sample, near_sample, leaf_basis, branch_samples, top_transfer, root_sample)


def solution(mesh):
    return jax.shard_map(
        on_device,
        mesh=mesh,
        in_specs=(
            P(None, "leaf"),
            P("cols", "leaf"),
            P(None, "cols"),
            P("leaf", None, None),
            P("leaf", None),
            P("leaf"),
            P("leaf", None),
        ),
        out_specs=(
            P("cols", "leaf"),
            P("cols", "leaf"),
            P(None, "leaf"),
            P("leaf", "cols"),
            P(),
            P(None, "cols"),
        ),
        check_vma=False,
    )
```

time: 248 us -> 302 us (1.22)
  local copies, waits for them, and re-layouts: 97.5 us -> 18.1 us
  blocking collectives: 0 us -> 74.5 us
  starting transfers between devices: 49.5 us -> 115 us
  waiting for transfers between devices: 8.9 us -> 24.6 us
  matrix products: 16.2 us -> 1.88 us
  other arithmetic: 10.3 us -> 7.08 us
    ppermute x4, starting transfers between devices: 9.25 us -> 89.4 us  [double_all(): other = lax.ppermute(held, axis, [(i, i ^ stride) for i in range(count)])]
    psum x0 -> x1, blocking collectives: none -> 74.5 us  [on_device(): root_sample = lax.psum(root_part, 'leaf')]
    slice x22 -> x4, local copies, waits for them, and re-layouts: 31.1 us -> 0.8 us  [the longest x1 0.74 us: on_device(): c_got = small_got[:, cap * share // 2:].reshape(slots * 2, LANES)]
    transpose x10 -> x2, local copies, waits for them, and re-layouts: 24.1 us -> 0.26 us  [two_rows(): split = jnp.transpose(values.reshape(2, rows, leaves, LEAF), (2, 1, 0, 3))]
    all_to_all x1, waiting for transfers between devices: 0.01 us -> 14.9 us  [on_device(): lax.all_to_all(small_sent, 'leaf', split_axis=0, concat_axis=0, tiled=True)]
    dot_general x14 -> x0, matrix products: 14.3 us -> none  [the longest x1 5.23 us: on_device(): ratio = jnp.einsum('lnrq,lnrc->lnqc', child, inverse, precision=highest)]
    squeeze x8 -> x1, local copies, waits for them, and re-layouts: 10.2 us -> 0.01 us  [on_device(): low_edge = lax.ppermute(edges[1], 'leaf', forward)]
    ppermute x5 -> x3, waiting for transfers between devices: 0.01 us -> 7.02 us  [the longest x1 5.9 us: on_device(): low_edge = lax.ppermute(edges[1], 'leaf', forward)]
  transfers between devices with their start and end apart: 14 -> 11, of which waited for: 4 -> 5; matrix products, arithmetic and copies ran while one was open for 47% -> 7% of each run, Pallas kernels for 21% -> 17%
where the time goes in v2:
time: 302 us; the launch traced here: 301 us
  starting transfers between devices  115 us (38%)
  blocking collectives  74.5 us (25%)
  Pallas kernels  58.8 us (19%)
  waiting for transfers between devices  24.6 us (8%)
  local copies, waits for them, and re-layouts  18.1 us (6%)
  other arithmetic  7.08 us (2%)
    ppermute x4, starting transfers between devices, double_all(): other = lax.ppermute(held, axis, [(i, i ^ stride) for i in range(count)])  89.4 us
    psum x1, blocking collectives, on_device(): root_sample = lax.psum(root_part, 'leaf')  74.5 us
    all_to_all x1, waiting for transfers between devices, on_device(): lax.all_to_all(small_sent, 'leaf', split_axis=0, concat_axis=0, tiled=True)  14.9 us
    pallas_call x1, Pallas kernels, branch_factors(): pl.pallas_call(functools.partial(branch_body, rank=rank, levels=levels),...  14.5 us
    pallas_call x1, Pallas kernels, top_factors(): pl.pallas_call(functools.partial(top_body, rank=rank, levels=levels), in_...  12.4 us
    pallas_call x1, Pallas kernels, kernel_blocks(): pl.pallas_call(functools.partial(blocks_body, rank=rank), grid_spec=pltpu...  10.6 us
    all_to_all x1, starting transfers between devices, on_device(): lax.all_to_all(wanted, 'leaf', split_axis=0, concat_axis=0, tiled=True)  8.31 us
    pallas_call x1, Pallas kernels, far_products(): pl.pallas_call(far_body, grid_spec=pltpu.PrefetchScalarGridSpec(num_scala...  7.84 us
  transfers between devices with their start and end apart: 11, of which 5 were waited for; matrix products, arithmetic and copies ran while one was open for 7% of the time, Pallas kernels for 17%

profile of v2, /device:TPU:0, one launch (start us, length us, event | category | flops | bytes accessed | tf_op | source)
XLA Modules:
  0.0 300.7 jit_solution(3414696247385494446)
XLA Ops:
  0.7 1.4 copy.68
  2.0 8.3 %all-to-all-start = ((s32[16,1,8]{2,1,0:T(1,128)}), s32[16,1,8]{2,1,0:T(1,128)S(1)}, u32[]{:S(2)}, u32[]{:S(2)}) async-start(s32[16,1,8]{2,1,0:T(1,128)} %copy.68), calls=%async_computation | async-start | bytes 16384 | tf_op jit(solution)/shard_map/all_to_all | solution.py:776
  10.4 1.9 fusion.6
  12.3 0.1 collective-permute-start
  12.4 0.7 and_select_fusion
  13.0 0.1 select_reduce_fusion.2
  13.2 0.7 slice.39.total_ref
  13.8 0.1 convert_reduce_fusion
  13.9 0.7 fusion.9
  14.6 0.7 select_reduce_fusion
  15.3 1.2 compare_select_fusion.2.count_ref
  16.5 0.7 pad_clamp_fusion.2
  17.2 1.5 copy.70
  18.7 0.1 copy.75
  18.8 0.1 reshape.157
  18.9 0.7 gather_fusion.1
  19.5 0.7 reshape.158.slot_ref
  20.2 0.4 copy.72
  20.6 0.4 copy.73
  21.0 0.6 gather_fusion
  21.6 0.1 reshape.156
  21.8 0.1 reshape_reshape.3
  21.9 0.2 copy.71
  22.2 0.2 reshape.153
  22.3 0.1 copy.76
  22.4 0.1 reshape.159
  22.6 0.7 gather_fusion.4
  23.3 0.8 gather_fusion.3
  24.1 0.9 pad_maximum_fusion
  25.0 6.9 %all-to-all-start.2 = ((f32[16,80,128]{2,1,0:T(8,128)}), f32[16,80,128]{2,1,0:T(8,128)S(1)}, u32[]{:S(2)}, u32[]{:S(2)}) async-start(f32[16,80,128]{2,1,0:T(8,128)} %pad_maximum_fusion), calls=%async_computation.2 | async-start | bytes 1310720 | tf_op jit(solution)/shard_map/all_to_all | solution.py:797
  31.9 0.1 copy.86
  32.0 2.8 gather_fusion.2
  34.8 14.9 %all-to-all-done.2 = f32[16,80,128]{2,1,0:T(8,128)S(1)} async-done(((f32[16,80,128]{2,1,0:T(8,128)}), f32[16,80,128]{2,1,0:T(8,128)S(1)}, u32[]{:S(2)}, u32[]{:S(2)}) %all-to-all-start.2) | async-done | bytes 655392 | tf_op jit(solution)/shard_map/all_to_all | solution.py:797
  49.6 4.9 %all-to-all-start.1 = ((f32[16,8,64,128]{3,2,1,0:T(8,128)}), f32[16,8,64,128]{3,2,1,0:T(8,128)}, u32[]{:S(2)}, u32[]{:S(2)}) async-start(f32[16,8,64,128]{3,2,1,0:T(8,128)} %bitcast.66), calls=%async_computation.1 | async-start | bytes 8388608 | tf_op jit(solution)/shard_map/all_to_all | solution.py:800
  54.6 3.8 %collective-permute-start.6 = (f32[72,128]{1,0:T(8,128)S(1)}, f32[72,128]{1,0:T(8,128)S(1)}, u32[]{:S(2)}, u32[]{:S(2)}) collective-permute-start(f32[72,128]{1,0:T(8,128)S(1)} %get-tuple-element.90), channel_id=1, source_target_pairs={{0,2},{2,4},{4,6},{6,8},{8,10},{10,12},{12,14},{14,16},{16,18},{18... | collective-permute-start | bytes 110600 | tf_op jit(solution)/shard_map/ppermute | solution.py:833
  58.5 0.4 copy.81
  58.9 0.1 copy.78
  59.0 0.6 reshape.170.mask_ref
  59.6 0.1 pad.24.clone
  59.7 1.3 collective-permute-start.7
  61.1 0.1 collective-permute-start.1
  61.2 0.7 slice.63
  61.9 5.9 %collective-permute-done.6 = f32[72,128]{1,0:T(8,128)S(1)} collective-permute-done((f32[72,128]{1,0:T(8,128)S(1)}, f32[72,128]{1,0:T(8,128)S(1)}, u32[]{:S(2)}, u32[]{:S(2)}) %collective-permute-start.6) | collective-permute-done | bytes 36896 | tf_op jit(solution)/shard_map/ppermute | solution.py:833
  67.8 1.1 collective-permute-done.7
  68.9 1.2 maximum_maximum_fusion.rows_ref
  70.1 0.8 copy-done.7
  70.9 10.6 %kernel_blocks.1 = (bf16[128,64,256]{2,1,0:T(8,128)(2,1)}, bf16[128,64,256]{2,1,0:T(8,128)(2,1)}, f32[32,32,64]{2,1,0:T(8,128)}, f32[32,32,32]{2,1,0:T(8,128)}) custom-call(s32[1]{0:T(128)} %slice.39.total_ref, s32[128]{0:T(128)} %copy-done.6, s32[128]{0:T(128)} %compare_select_fusion.2.count_ref, s32[512]{0:T(512)} %reshape.158.slot_ref, ...), custom_call_target="tpu_custom_call" | custom-call | flops 20000000000 | bytes 20000000 | tf_op jit(solution)/shard_map/kernel_blocks/pallas_call | solution.py:139
  81.5 14.5 %branch_factors.1 = (f32[32,32,128]{2,1,0:T(8,128)}, f32[6,32,32,128]{3,2,1,0:T(8,128)}, f32[32,32]{1,0:T(8,128)}, f32[32,32]{1,0:T(8,128)}) custom-call(f32[1024,32]{1,0:T(8,128)} %bitcast.83), custom_call_target="tpu_custom_call" | custom-call | flops 10000000000 | bytes 10000000 | tf_op jit(solution)/shard_map/branch_factors/pallas_call | solution.py:564
  96.0 0.8 broadcast_in_dim_reshape.3
  96.8 4.3 %collective-permute-start.2 = (f32[1,8,128]{2,1,0:T(8,128)S(1)}, f32[1,8,128]{2,1,0:T(8,128)S(1)}, u32[]{:S(2)}, u32[]{:S(2)}) collective-permute-start(f32[1,8,128]{2,1,0:T(8,128)S(1)} %broadcast_in_dim_reshape.3), channel_id=1, source_target_pairs={{0,2},{2,0},{4,6},{6,4},{8,10},{10,8},{12,14},{14,12},{16,18},{18,... | collective-permute-start | bytes 12296 | tf_op jit(solution)/shard_map/ppermute | solution.py:726
  101.1 0.1 maximum_maximum_fusion.1
  101.2 1.8 collective-permute-done.2
  103.1 56.3 %collective-permute-start.3 = (f32[2,8,128]{2,1,0:T(8,128)S(1)}, f32[2,8,128]{2,1,0:T(8,128)S(1)}, u32[]{:S(2)}, u32[]{:S(2)}) collective-permute-start(f32[2,8,128]{2,1,0:T(8,128)S(1)} %pad_maximum_fusion.6), channel_id=1, source_target_pairs={{0,4},{2,6},{4,0},{6,2},{8,12},{10,14},{12,8},{14,10},{16,20},{18,... | collective-permute-start | bytes 24584 | tf_op jit(solution)/shard_map/ppermute | solution.py:726
  159.3 0.8 pad_maximum_fusion.1.coords_ref
  160.1 0.9 collective-permute-done.3
  161.0 24.6 %collective-permute-start.4 = (f32[4,8,128]{2,1,0:T(8,128)S(1)}, f32[4,8,128]{2,1,0:T(8,128)S(1)}, u32[]{:S(2)}, u32[]{:S(2)}) collective-permute-start(f32[4,8,128]{2,1,0:T(8,128)S(1)} %pad_maximum_fusion.5), channel_id=1, source_target_pairs={{0,8},{2,10},{4,12},{6,14},{8,0},{10,2},{12,4},{14,6},{16,24},{18,... | collective-permute-start | bytes 49160 | tf_op jit(solution)/shard_map/ppermute | solution.py:726
  185.6 6.1 %near_products.1 = f32[128,2048]{1,0:T(8,128)} custom-call(s32[96]{0:T(128)} %reshape.170.mask_ref, f32[35,64,128]{2,1,0:T(8,128)} %maximum_maximum_fusion.rows_ref, f32[35,8,128]{2,1,0:T(8,128)} %pad_maximum_fusion.1.coords_ref, f32[32,64,3]{2,1,0:T(8,128)} %bitcast.71), custom_call_target="tpu_custom_call" | custom-call | flops 4000000000 | bytes 10000000 | tf_op jit(solution)/shard_map/near_products/pallas_call | solution.py:305
  191.7 4.2 %collective-permute-start.5 = (f32[8,8,128]{2,1,0:T(8,128)S(1)}, f32[8,8,128]{2,1,0:T(8,128)S(1)}, u32[]{:S(2)}, u32[]{:S(2)}) collective-permute-start(f32[8,8,128]{2,1,0:T(8,128)S(1)} %pad_maximum_fusion.4), channel_id=1, source_target_pairs={{0,16},{2,18},{4,20},{6,22},{8,24},{10,26},{12,28},{14,30},{16,0},... | collective-permute-start | bytes 98312 | tf_op jit(solution)/shard_map/ppermute | solution.py:726
  195.9 7.4 %bases.1 = (f32[32,2048]{1,0:T(8,128)}, f32[32,2048]{1,0:T(8,128)}) custom-call(f32[32,32,128]{2,1,0:T(8,128)} %get-tuple-element.41.inverse_ref, f32[6,32,32,128]{3,2,1,0:T(8,128)} %get-tuple-element.42.ratio_ref, f32[32,32]{1,0:T(8,128)} %get-tuple-element.43.top_ref, f32[32,32,64]{2,1,0:T(8,128)} %get-tuple-element.44.sketched_ref), custom_call_target="tpu_custom_call" | custom-call | flops 5000000000 | bytes 10000000 | tf_op jit(solution)/shard_map/bases/pallas_call | solution.py:613
  203.3 0.8 reshape.169.children_ref
  204.1 12.4 %top_factors.1 = (f32[15,64,32]{2,1,0:T(8,128)}, f32[32,32]{1,0:T(8,128)}) custom-call(s32[1]{0:T(128)} %bitcast.25.place_ref, f32[16,32,32]{2,1,0:T(8,128)} %reshape.169.children_ref), custom_call_target="tpu_custom_call" | custom-call | flops 10000000000 | bytes 10000000 | tf_op jit(solution)/shard_map/top_factors/pallas_call | solution.py:677
  216.5 1.9 copy.85
  218.4 7.8 %far_products.1 = (f32[128,2048]{1,0:T(8,128)}, f32[32,128]{1,0:T(8,128)}, f32[32,128]{1,0:T(8,128)}) custom-call(s32[1]{0:T(128)} %slice.39.total_ref, s32[128]{0:T(128)} %copy-done.6, s32[512]{0:T(512)} %reshape.158.slot_ref, f32[128,64,128]{2,1,0:T(8,128)} %bitcast.17.fetched_ref, bf16[128,64,256]{2,1,0:T(8,128)(2,1)} %get-tuple-element.38.high_ref, ...), custom_call_target="tpu_custom_call" | custom-call | flops 10000000000 | bytes 20000000 | tf_op jit(solution)/shard_map/far_products/pallas_call | solution.py:228
  226.2 74.5 %psum.7 = f32[32,128]{1,0:T(8,128)} all-reduce(f32[32,128]{1,0:T(8,128)} %get-tuple-element.53), channel_id=1, replica_groups=mesh['leaf'=16,'cols'=2] {'leaf'}, use_global_device_ids=true, to_apply=%region_4.5 | all-reduce | flops 4096 | bytes 32768 | tf_op jit(solution)/shard_map/psum | solution.py:855
  (54 shorter events, 0.5 us)
Async XLA Ops:
  0.6 9.7 %copy-start = (f32[32,128]{1,0:T(8,128)S(1)}, f32[32,128]{1,0:T(8,128)}, u32[]{:S(2)}) copy-start(f32[32,128]{1,0:T(8,128)} %param.10) | copy-start | bytes 49156
  0.6 18.1 %copy-start.4 = (s32[32,16]{0,1:T(8,128)S(1)}, s32[32,16]{0,1:T(8,128)}, u32[]{:S(2)}) copy-start(s32[32,16]{0,1:T(8,128)} %param.12) | copy-start | bytes 6148
  0.7 19.6 %copy-start.3 = (f32[3,2048]{1,0:T(4,128)S(1)}, f32[3,2048]{1,0:T(4,128)}, u32[]{:S(2)}) copy-start(f32[3,2048]{1,0:T(4,128)} %param.8) | copy-start | bytes 73732
  2.0 19.7 %all-to-all-start = ((s32[16,1,8]{2,1,0:T(1,128)}), s32[16,1,8]{2,1,0:T(1,128)S(1)}, u32[]{:S(2)}, u32[]{:S(2)}) async-start(s32[16,1,8]{2,1,0:T(1,128)} %copy.68), calls=%async_computation | async-start | bytes 16384 | tf_op jit(solution)/shard_map/all_to_all | solution.py:776
  12.3 9.5 %collective-permute-start = (f32[16,2048]{1,0:T(8,128)S(1)}, f32[16,2048]{1,0:T(8,128)S(1)}, u32[]{:S(2)}, u32[]{:S(2)}) collective-permute-start(f32[16,2048]{1,0:T(8,128)S(1)} %dynamic-slice_bitcast_fusion), channel_id=1, source_target_pairs={{0,1},{1,0},{2,3},{3,2},{4,5},{5,4},{6,7},{7,6},{8,9},{9,8},{10,11... | collective-permute-start | bytes 393224 | tf_op jit(solution)/shard_map/ppermute | solution.py:700
  14.6 7.4 %copy-start.6 = (s32[128]{0:T(128)}, s32[128]{0:T(128)S(1)}, u32[]{:S(2)}) copy-start(s32[128]{0:T(128)S(1)} %broadcast_minimum_fusion.leaf_ref) | copy-start | bytes 1540
  20.6 37.9 %copy-start.1 = (f32[3,2048]{0,1:T(8,128)}, f32[3,2048]{0,1:T(8,128)S(1)}, u32[]{:S(2)}) copy-start(f32[3,2048]{0,1:T(8,128)S(1)} %copy.72) | copy-start | bytes 73732
  25.0 24.7 %all-to-all-start.2 = ((f32[16,80,128]{2,1,0:T(8,128)}), f32[16,80,128]{2,1,0:T(8,128)S(1)}, u32[]{:S(2)}, u32[]{:S(2)}) async-start(f32[16,80,128]{2,1,0:T(8,128)} %pad_maximum_fusion), calls=%async_computation.2 | async-start | bytes 1310720 | tf_op jit(solution)/shard_map/all_to_all | solution.py:797
  49.6 9.3 %copy-start.5 = (s32[32,3]{0,1:T(4,128)S(1)}, s32[32,3]{0,1:T(4,128)}, u32[]{:S(2)}) copy-start(s32[32,3]{0,1:T(4,128)} %param.14) | copy-start | bytes 1156
  49.6 168.8 %all-to-all-start.1 = ((f32[16,8,64,128]{3,2,1,0:T(8,128)}), f32[16,8,64,128]{3,2,1,0:T(8,128)}, u32[]{:S(2)}, u32[]{:S(2)}) async-start(f32[16,8,64,128]{3,2,1,0:T(8,128)} %bitcast.66), calls=%async_computation.1 | async-start | bytes 8388608 | tf_op jit(solution)/shard_map/all_to_all | solution.py:800
  54.6 13.2 %collective-permute-start.6 = (f32[72,128]{1,0:T(8,128)S(1)}, f32[72,128]{1,0:T(8,128)S(1)}, u32[]{:S(2)}, u32[]{:S(2)}) collective-permute-start(f32[72,128]{1,0:T(8,128)S(1)} %get-tuple-element.90), channel_id=1, source_target_pairs={{0,2},{2,4},{4,6},{6,8},{8,10},{10,12},{12,14},{14,16},{16,18},{18... | collective-permute-start | bytes 110600 | tf_op jit(solution)/shard_map/ppermute | solution.py:833
  59.7 9.2 %collective-permute-start.7 = (f32[72,128]{1,0:T(8,128)S(1)}, f32[72,128]{1,0:T(8,128)S(1)}, u32[]{:S(2)}, u32[]{:S(2)}) collective-permute-start(f32[72,128]{1,0:T(8,128)S(1)} %get-tuple-element.91), channel_id=1, source_target_pairs={{2,0},{4,2},{6,4},{8,6},{10,8},{12,10},{14,12},{16,14},{18,16},{20... | collective-permute-start | bytes 110600 | tf_op jit(solution)/shard_map/ppermute | solution.py:834
  61.1 9.0 %copy-start.2 = (f32[16,64,128]{2,1,0:T(8,128)}, f32[16,64,128]{2,1,0:T(8,128)S(1)}, u32[]{:S(2)}) copy-start(f32[16,64,128]{2,1,0:T(8,128)S(1)} %slice.62) | copy-start | bytes 1572868
  61.1 9.0 %collective-permute-start.1 = (f32[1024,128]{1,0:T(8,128)S(1)}, f32[1024,128]{1,0:T(8,128)S(1)}, u32[]{:S(2)}, u32[]{:S(2)}) collective-permute-start(f32[1024,128]{1,0:T(8,128)S(1)} %bitcast.77), channel_id=1, source_target_pairs={{0,1},{1,0},{2,3},{3,2},{4,5},{5,4},{6,7},{7,6},{8,9},{9,8},{10,11... | collective-permute-start | bytes 1572872 | tf_op jit(solution)/shard_map/ppermute | solution.py:806
  70.1 0.8 copy-start.7
  96.8 6.3 %collective-permute-start.2 = (f32[1,8,128]{2,1,0:T(8,128)S(1)}, f32[1,8,128]{2,1,0:T(8,128)S(1)}, u32[]{:S(2)}, u32[]{:S(2)}) collective-permute-start(f32[1,8,128]{2,1,0:T(8,128)S(1)} %broadcast_in_dim_reshape.3), channel_id=1, source_target_pairs={{0,2},{2,0},{4,6},{6,4},{8,10},{10,8},{12,14},{14,12},{16,18},{18,... | collective-permute-start | bytes 12296 | tf_op jit(solution)/shard_map/ppermute | solution.py:726
  103.1 57.9 %collective-permute-start.3 = (f32[2,8,128]{2,1,0:T(8,128)S(1)}, f32[2,8,128]{2,1,0:T(8,128)S(1)}, u32[]{:S(2)}, u32[]{:S(2)}) collective-permute-start(f32[2,8,128]{2,1,0:T(8,128)S(1)} %pad_maximum_fusion.6), channel_id=1, source_target_pairs={{0,4},{2,6},{4,0},{6,2},{8,12},{10,14},{12,8},{14,10},{16,20},{18,... | collective-permute-start | bytes 24584 | tf_op jit(solution)/shard_map/ppermute | solution.py:726
  161.0 30.7 %collective-permute-start.4 = (f32[4,8,128]{2,1,0:T(8,128)S(1)}, f32[4,8,128]{2,1,0:T(8,128)S(1)}, u32[]{:S(2)}, u32[]{:S(2)}) collective-permute-start(f32[4,8,128]{2,1,0:T(8,128)S(1)} %pad_maximum_fusion.5), channel_id=1, source_target_pairs={{0,8},{2,10},{4,12},{6,14},{8,0},{10,2},{12,4},{14,6},{16,24},{18,... | collective-permute-start | bytes 49160 | tf_op jit(solution)/shard_map/ppermute | solution.py:726
  191.7 11.6 %collective-permute-start.5 = (f32[8,8,128]{2,1,0:T(8,128)S(1)}, f32[8,8,128]{2,1,0:T(8,128)S(1)}, u32[]{:S(2)}, u32[]{:S(2)}) collective-permute-start(f32[8,8,128]{2,1,0:T(8,128)S(1)} %pad_maximum_fusion.4), channel_id=1, source_target_pairs={{0,16},{2,18},{4,20},{6,22},{8,24},{10,26},{12,28},{14,30},{16,0},... | collective-permute-start | bytes 98312 | tf_op jit(solution)/shard_map/ppermute | solution.py:726

commit v3 on v2

--- a/solution.py
+++ b/solution.py
@@ -171,8 +171,8 @@
 
 def far_body(
     total_ref, leaf_ref, slot_ref,
-    fetched_ref, high_ref, low_ref, weights_ref, path_ref,
-    out_ref, projected_ref, root_ref,
+    fetched_ref, high_ref, low_ref, weights_ref,
+    out_ref, projected_ref, copies_ref,
     s_high, s_low, acc,
 ):
     step = pl.program_id(0)
@@ -206,15 +206,14 @@
         rows = acc[...].reshape(leaves * LEAF, samp_dev)
         projected = dot_exact(weights_ref[...], rows)
         projected_ref[...] = projected
-        root_ref[...] = lax.dot_general(
-            path_ref[...], projected, tn_dims, precision=highest, preferred_element_type=jnp.float32
-        )
+        for branch in range(copies_ref.shape[0]):
+            copies_ref[branch] = projected
         for pair in range(leaves // 2):
             block = acc[2 * pair : 2 * pair + 2].reshape(2 * LEAF, samp_dev)
             out_ref[:, 2 * pair * LEAF : 2 * (pair + 1) * LEAF] = block.T
 
 
-def far_products(total, group_leaf, group_slots, fetched, high, low, weights, path):
+def far_products(total, group_leaf, group_slots, fetched, high, low, weights, branches):
     slots, unused, samp_dev = fetched.shape
     groups = group_leaf.shape[0]
     points_dev = weights.shape[1]
@@ -235,12 +234,11 @@
                 pl.BlockSpec((BATCH, LEAF, GROUP * LEAF), block_index),
                 pl.BlockSpec((BATCH, LEAF, GROUP * LEAF), block_index),
                 pl.BlockSpec(weights.shape, lambda *unused: (0, 0), pipeline_mode=pl.Buffered(1)),
-                pl.BlockSpec(path.shape, lambda *unused: (0, 0), pipeline_mode=pl.Buffered(1)),
             ],
             out_specs=[
                 pl.BlockSpec((samp_dev, points_dev), lambda *unused: (0, 0)),
                 pl.BlockSpec((weights.shape[0], samp_dev), lambda *unused: (0, 0)),
-                pl.BlockSpec((weights.shape[0], samp_dev), lambda *unused: (0, 0)),
+                pl.BlockSpec((branches, weights.shape[0], samp_dev), lambda *unused: (0, 0, 0)),
             ],
             scratch_shapes=[
                 pltpu.VMEM((slots, LEAF, samp_dev), jnp.bfloat16),
@@ -251,14 +249,14 @@
         out_shape=[
             jax.ShapeDtypeStruct((samp_dev, points_dev), jnp.float32),
             jax.ShapeDtypeStruct((weights.shape[0], samp_dev), jnp.float32),
-            jax.ShapeDtypeStruct((weights.shape[0], samp_dev), jnp.float32),
+            jax.ShapeDtypeStruct((branches, weights.shape[0], samp_dev), jnp.float32),
         ],
         compiler_params=pltpu.CompilerParams(vmem_limit_bytes=vmem_bytes),
         name="far_products",
         cost_estimate=pl.CostEstimate(
             flops=10**10, bytes_accessed=2 * 10**7, transcendentals=0
         ),
-    )(total, group_leaf, group_slots, fetched, high, low, weights, path)
+    )(total, group_leaf, group_slots, fetched, high, low, weights)
 
 
 NEAR_LEAVES = 8
@@ -622,7 +620,7 @@
     )(inverse, ratio, top, sketched)
 
 
-def top_body(place_ref, children_ref, transfer_ref, path_ref, source, current, left, inverse, squared, child, lowest, nat_inverse, nat_child, *, rank, levels):
+def top_body(children_ref, transfer_ref, paths_ref, source, current, left, inverse, squared, child, lowest, nat_inverse, nat_child, *, rank, levels):
     nodes = children_ref.shape[0] // 2
     for node in range(nodes):
         both = children_ref[2 * node : 2 * node + 2].reshape(2 * rank, rank)
@@ -657,30 +655,32 @@
             at = (node << level) * rank
             transfer_ref[offset + node] = dot_exact(stacked, nat_inverse[level, at : at + rank, :])
         offset += nodes >> level
-    me = place_ref[0]
-    offset = 0
-    path = None
-    for level in range(levels):
-        node = offset + lax.shift_right_logical(me, level + 1)
-        side = lax.rem(lax.shift_right_logical(me, level), 2)
-        block = transfer_ref[node, pl.ds(pl.multiple_of(side * rank, rank), rank), :]
-        path = block if path is None else dot_exact(path, block)
-        offset += nodes >> level
-    path_ref[...] = path
-
-
-def top_factors(children, place):
+    above = [None]
+    for level in range(levels - 1, -1, -1):
+        offset -= nodes >> level
+        fresh = []
+        for node in range(nodes >> level):
+            both = transfer_ref[offset + node]
+            if above[0] is not None:
+                both = dot_exact(both, above[node])
+            fresh += [both[:rank], both[rank:]]
+        above = fresh
+    for branch in range(2 * nodes):
+        paths_ref[branch * rank : (branch + 1) * rank, :] = above[branch]
+
+
+def top_factors(children):
     branches, rank, unused = children.shape
     levels = branches.bit_length() - 1
     nodes = branches // 2
     natural = pltpu.VMEM((levels, nodes * rank, rank), jnp.float32)
     return pl.pallas_call(
         functools.partial(top_body, rank=rank, levels=levels),
-        in_specs=[pl.BlockSpec(memory_space=pltpu.SMEM), vmem_spec],
+        in_specs=[vmem_spec],
         out_specs=[vmem_spec] * 2,
         out_shape=[
             jax.ShapeDtypeStruct((branches - 1, 2 * rank, rank), jnp.float32),
-            jax.ShapeDtypeStruct((rank, rank), jnp.float32),
+            jax.ShapeDtypeStruct((branches * rank, rank), jnp.float32),
         ],
         scratch_shapes=[pltpu.VMEM((nodes * rank, rank), jnp.float32)]
         + tree_scratch(rank)
@@ -688,7 +688,7 @@
         compiler_params=pltpu.CompilerParams(vmem_limit_bytes=vmem_bytes),
         name="top_factors",
         cost_estimate=pl.CostEstimate(flops=10**10, bytes_accessed=10**7, transcendentals=0),
-    )(place, children)
+    )(children)
 
 
 def exchange_sum(pieces, axis):
@@ -715,19 +715,6 @@
         arrived = lax.ppermute(piece, axis, [(i, (i + step) % count) for i in range(count)])
         result = lax.dynamic_update_index_in_dim(result, arrived, (me - step) % count, 0)
     return result
-
-
-def double_all(piece, axis):
-    count = lax.axis_size(axis)
-    me = lax.axis_index(axis)
-    held = piece[None]
-    stride = 1
-    while stride < count:
-        other = lax.ppermute(held, axis, [(i, i ^ stride) for i in range(count)])
-        low = (me // stride) % 2 == 0
-        held = jnp.concatenate([jnp.where(low, held, other), jnp.where(low, other, held)], axis=0)
-        stride *= 2
-    return held
 
 
 def group_tables(far_slots, far_count):
@@ -754,6 +741,31 @@
     )
 
 
+def pack_body(picked_ref, z_ref, c_ref, out_ref, *, cap):
+    z_rows = z_ref.shape[1]
+
+    def one(branch, carry):
+        for entry in range(cap):
+            leaf = picked_ref[branch * cap + entry]
+            out_ref[branch, z_rows * entry : z_rows * (entry + 1), :] = z_ref[leaf]
+            at = z_rows * cap + 2 * entry
+            out_ref[branch, at : at + 2, :] = c_ref[leaf]
+        return carry
+
+    lax.fori_loop(0, out_ref.shape[0], one, 0, unroll=2)
+
+
+def packed_rows(picked, z_rows, c_rows, branches, cap):
+    return pl.pallas_call(
+        functools.partial(pack_body, cap=cap),
+        in_specs=[pl.BlockSpec(memory_space=pltpu.SMEM), vmem_spec, vmem_spec],
+        out_specs=vmem_spec,
+        out_shape=jax.ShapeDtypeStruct((branches, cap * (z_rows.shape[1] + 2), LANES), jnp.float32),
+        compiler_params=pltpu.CompilerParams(vmem_limit_bytes=vmem_bytes),
+        name="packed_rows",
+    )(picked, z_rows, c_rows)
+
+
 def two_rows(values, rows):
     leaves = values.shape[1]
     split = jnp.transpose(values.reshape(2, rows, leaves, LEAF), (2, 1, 0, 3))
@@ -769,7 +781,7 @@
     cap = far_requests.shape[2]
     slots = branches * cap
     share = rank // columns
-    me = lax.axis_index("leaf").astype(jnp.int32).reshape(1)
+    me = lax.axis_index("leaf")
     column = lax.axis_index("cols")
 
     wanted = far_requests.reshape(branches, cap)
@@ -783,20 +795,34 @@
     z_part = jnp.dot(sketch, samples, precision=highest)
     z_mine = exchange_sum(z_part.reshape(columns, share, leaves * LEAF), "cols")
     z_rows = two_rows(z_mine.reshape(share, leaves, LEAF), share // 2)
+    planes = points.reshape(3, leaves, LEAF)
     c_rows = two_rows(
-        jnp.pad(points.reshape(3, leaves, LEAF)[jnp.array([0, 2, 1])], ((0, 1), (0, 0), (0, 0))), 2
-    )
-    asked_for, rows, z_rows, c_rows, tables = lax.optimization_barrier(
-        (asked_for, rows, z_rows, c_rows, tables)
-    )
-    total, group_leaf, group_count, group_slots = tables
+        jnp.concatenate([planes[0:1], planes[2:3], planes[1:2], jnp.zeros_like(planes[0:1])], axis=0), 2
+    )
+    asked_for, rows, z_rows, c_rows = lax.optimization_barrier((asked_for, rows, z_rows, c_rows))
     picked = asked_for.reshape(-1)
-    z_sent = z_rows[picked].reshape(branches, cap * share // 2, LANES)
-    c_sent = c_rows[picked].reshape(branches, cap * 2, LANES)
-    small_sent = jnp.concatenate([z_sent, c_sent], axis=1)
+    small_sent = packed_rows(picked, z_rows, c_rows, branches, cap)
     small_got = lax.all_to_all(small_sent, "leaf", split_axis=0, concat_axis=0, tiled=True)
+    total, group_leaf, group_count, group_slots = group_tables(far_slots, far_count)
+
+    forward = [(i, i + 1) for i in range(branches - 1)]
+    backward = [(target, source) for source, target in forward]
+    edges = jnp.concatenate([rows[:1], rows[leaves - 1 :]], axis=0)
+    edge_coords = jnp.concatenate([coords[:1], coords[leaves - 1 :]], axis=0)
+    width = max(samp_dev, LEAF)
+    edges = jnp.concatenate(
+        [
+            jnp.pad(edges, ((0, 0), (0, 0), (0, width - samp_dev))),
+            jnp.pad(edge_coords, ((0, 0), (0, 5), (0, width - LEAF))),
+        ],
+        axis=1,
+    )
+    edges, unused = lax.optimization_barrier((edges, small_sent))
+    low_edge = lax.ppermute(edges[1], "leaf", forward)
+    high_edge = lax.ppermute(edges[0], "leaf", backward)
 
     rows_sent = rows[picked].reshape(branches, cap, LEAF, samp_dev)
+    rows_sent, low_edge, high_edge = lax.optimization_barrier((rows_sent, low_edge, high_edge))
     rows_got = lax.all_to_all(rows_sent, "leaf", split_axis=0, concat_axis=0, tiled=True)
     fetched = rows_got.reshape(slots, LEAF, samp_dev)
 
@@ -818,27 +844,12 @@
 
     levels = leaves.bit_length()
     inverse, ratio, top_inverse, own_child = branch_factors(gram, levels)
-    children = double_all(own_child.reshape(rank * rank // LANES, LANES), "leaf")
-    top_transfer, path = top_factors(children.reshape(branches, rank, rank), me)
     weights, leaf_basis = bases(inverse, ratio, top_inverse, sketched)
-
-    edges = jnp.concatenate([rows[:1], rows[leaves - 1 :]], axis=0)
-    edge_coords = jnp.concatenate([coords[:1], coords[leaves - 1 :]], axis=0)
-    edge_coords = jnp.pad(edge_coords, ((0, 0), (0, 5), (0, samp_dev - LEAF))) if samp_dev >= LEAF else None
-    forward = [(i, i + 1) for i in range(branches - 1)]
-    backward = [(target, source) for source, target in forward]
-    if edge_coords is not None:
-        edges = jnp.concatenate([edges, edge_coords], axis=1)
-        edges, unused = lax.optimization_barrier((edges, small_got))
-        low_edge = lax.ppermute(edges[1], "leaf", forward)
-        high_edge = lax.ppermute(edges[0], "leaf", backward)
-        rows_low, rows_high = low_edge[:LEAF], high_edge[:LEAF]
-        coords_low, coords_high = low_edge[LEAF : LEAF + 3, :LEAF], high_edge[LEAF : LEAF + 3, :LEAF]
-    else:
-        rows_low = lax.ppermute(edges[1], "leaf", forward)
-        rows_high = lax.ppermute(edges[0], "leaf", backward)
-        coords_low = lax.ppermute(coords[leaves - 1], "leaf", forward)
-        coords_high = lax.ppermute(coords[0], "leaf", backward)
+    mine = jnp.arange(branches)[:, None, None] == me
+    children = lax.psum(jnp.where(mine, own_child[None], 0.0), "leaf")
+
+    rows_low, rows_high = low_edge[:LEAF, :samp_dev], high_edge[:LEAF, :samp_dev]
+    coords_low, coords_high = low_edge[LEAF : LEAF + 3, :LEAF], high_edge[LEAF : LEAF + 3, :LEAF]
     near_rows = jnp.concatenate(
         [rows_low[None], rows, rows_high[None], jnp.zeros_like(rows_low)[None]], axis=0
     )
@@ -849,10 +860,15 @@
     near_coords = jnp.concatenate([near_coords, near_coords], axis=2)
     near_sample = near_products(near_mask.reshape(-1), near_rows, near_coords, targets)
 
-    far_sample, branch_samples, root_part = far_products(
-        total, group_leaf, group_slots, fetched, high, low, weights, path
-    )
-    root_sample = lax.psum(root_part, "leaf")
+    far_sample, branch_samples, copies = far_products(
+        total, group_leaf, group_slots, fetched, high, low, weights, branches
+    )
+    everyone = lax.all_to_all(copies, "leaf", split_axis=0, concat_axis=0, tiled=True)
+    children, unused = lax.optimization_barrier((children, branch_samples))
+    top_transfer, paths = top_factors(children)
+    root_sample = lax.dot_general(
+        paths, everyone.reshape(branches * rank, samp_dev), tn_dims, precision=highest
+    )
     return (far_sample, near_sample, leaf_basis, branch_samples, top_transfer, root_sample)
 
 

time: 302 us -> 251 us (0.83)
  waiting for transfers between devices: 24.6 us -> 99.5 us
  blocking collectives: 74.5 us -> 0 us
  starting transfers between devices: 115 us -> 47.8 us
  between operations: 1.13 us -> 14.4 us
    ppermute x4 -> x0, starting transfers between devices: 89.4 us -> none  [double_all(): other = lax.ppermute(held, axis, [(i, i ^ stride) for i in range(count)])]
    psum x1 -> x0, blocking collectives: 74.5 us -> none  [on_device(): root_sample = lax.psum(root_part, 'leaf')]
    psum x0 -> x1, waiting for transfers between devices: none -> 57.2 us  [on_device(): children = lax.psum(jnp.where(mine, own_child[None], 0.0), 'leaf')]
    all_to_all x1, waiting for transfers between devices: 0.01 us -> 32.4 us  [on_device(): lax.all_to_all(rows_sent, 'leaf', split_axis=0, concat_axis=0, tiled=True)]
    all_to_all x0 -> x1, starting transfers between devices: none -> 22.8 us  [on_device(): lax.all_to_all(copies, 'leaf', split_axis=0, concat_axis=0, tiled=True)]
    all_to_all x1, waiting for transfers between devices: 14.9 us -> 8.84 us  [on_device(): lax.all_to_all(small_sent, 'leaf', split_axis=0, concat_axis=0, tiled=True)]
    ppermute x1, waiting for transfers between devices: 5.9 us -> 0.01 us  [on_device(): low_edge = lax.ppermute(edges[1], 'leaf', forward)]
  transfers between devices with their start and end apart: 11 -> 9, of which waited for: 5 -> 4; matrix products, arithmetic and copies ran while one was open for 7% -> 8% of each run, Pallas kernels for 17% -> 24%
where the time goes in v3:
time: 251 us; the launch traced here: 250 us
  waiting for transfers between devices  99.5 us (40%)
  Pallas kernels  61.1 us (24%)
  starting transfers between devices  47.8 us (19%)
  local copies, waits for them, and re-layouts  17.2 us (7%)
  between operations  14.4 us (6%)
  other arithmetic  6 us (2%)
  matrix products  4.01 us (2%)
    psum x1, waiting for transfers between devices, on_device(): children = lax.psum(jnp.where(mine, own_child[None], 0.0), 'leaf')  57.2 us
    all_to_all x1, waiting for transfers between devices, on_device(): lax.all_to_all(rows_sent, 'leaf', split_axis=0, concat_axis=0, tiled=True)  32.4 us
    all_to_all x1, starting transfers between devices, on_device(): lax.all_to_all(copies, 'leaf', split_axis=0, concat_axis=0, tiled=True)  22.8 us
    pallas_call x1, Pallas kernels, branch_factors(): pl.pallas_call(functools.partial(branch_body, rank=rank, levels=levels),...  14.5 us
    pallas_call x1, Pallas kernels, top_factors(): pl.pallas_call(functools.partial(top_body, rank=rank, levels=levels), in_...  12.9 us
    pallas_call x1, Pallas kernels, kernel_blocks(): pl.pallas_call(functools.partial(blocks_body, rank=rank), grid_spec=pltpu...  10.5 us
    all_to_all x1, waiting for transfers between devices, on_device(): lax.all_to_all(small_sent, 'leaf', split_axis=0, concat_axis=0, tiled=True)  8.84 us
    all_to_all x1, starting transfers between devices, on_device(): lax.all_to_all(wanted, 'leaf', split_axis=0, concat_axis=0, tiled=True)  8.31 us
  transfers between devices with their start and end apart: 9, of which 4 were waited for; matrix products, arithmetic and copies ran while one was open for 8% of the time, Pallas kernels for 24%

profile of v3, /device:TPU:0, one launch (start us, length us, event | category | flops | bytes accessed | tf_op | source)
XLA Modules:
  0.0 250.0 jit_solution(12481113693938752071)
XLA Ops:
  7.2 1.4 copy.55
  8.6 8.3 %all-to-all-start = ((s32[16,1,8]{2,1,0:T(1,128)}), s32[16,1,8]{2,1,0:T(1,128)S(1)}, u32[]{:S(2)}, u32[]{:S(2)}) async-start(s32[16,1,8]{2,1,0:T(1,128)} %copy.55), calls=%async_computation | async-start | bytes 16384 | tf_op jit(solution)/shard_map/all_to_all | solution.py:788
  17.0 1.9 fusion.6
  18.9 0.7 dynamic-slice_bitcast_fusion
  19.5 0.9 slice_reduce_fusion.2
  20.5 0.1 slice.59
  20.6 0.1 slice.61
  20.6 0.1 slice.63
  20.7 0.1 pad.28.clone
  20.8 0.1 maximum_maximum_fusion.1
  20.9 1.1 copy.61
  22.0 0.3 copy.57
  22.3 0.1 copy.59
  22.4 0.7 reshape.159.c_ref
  23.1 1.0 all-to-all-done
  24.2 0.1 copy.56
  24.2 0.9 bitcast_add_fusion
  25.2 0.1 reshape_reshape.3
  25.3 0.2 copy.58
  25.5 0.8 reshape.157.z_ref
  26.3 0.1 copy.60
  26.4 0.6 reshape.163.picked_ref
  27.0 2.0 packed_rows.1
  29.0 5.9 %all-to-all-start.2 = ((f32[16,80,128]{2,1,0:T(8,128)}), f32[16,80,128]{2,1,0:T(8,128)S(1)}, u32[]{:S(2)}, u32[]{:S(2)}) async-start(f32[16,80,128]{2,1,0:T(8,128)} %packed_rows.1), calls=%async_computation.2 | async-start | bytes 1310720 | tf_op jit(solution)/shard_map/all_to_all | solution.py:805
  34.9 0.1 copy.71
  35.0 0.1 reshape.160
  35.1 1.3 collective-permute-start.2
  36.4 4.5 %collective-permute-start.1 = (f32[72,128]{1,0:T(8,128)S(1)}, f32[72,128]{1,0:T(8,128)S(1)}, u32[]{:S(2)}, u32[]{:S(2)}) collective-permute-start(f32[72,128]{1,0:T(8,128)S(1)} %get-tuple-element.88), channel_id=1, source_target_pairs={{0,2},{2,4},{4,6},{6,8},{8,10},{10,12},{12,14},{14,16},{16,18},{18... | collective-permute-start | bytes 110600 | tf_op jit(solution)/shard_map/ppermute | solution.py:821
  41.0 2.8 %gather_fusion.1 = f32[128,64,128]{2,1,0:T(8,128)} fusion(f32[32,64,128]{2,1,0:T(8,128)S(1)} %bitcast.63, s32[1024]{0:T(1024)S(1)} %pad_clamp_fusion), kind=kCustom, calls=%fused_computation.1 | custom fusion | bytes 8389120 | tf_op jit(solution)/shard_map/gather | solution.py:824
  43.8 8.8 %all-to-all-done.2 = f32[16,80,128]{2,1,0:T(8,128)S(1)} async-done(((f32[16,80,128]{2,1,0:T(8,128)}), f32[16,80,128]{2,1,0:T(8,128)S(1)}, u32[]{:S(2)}, u32[]{:S(2)}) %all-to-all-start.2) | async-done | bytes 655392 | tf_op jit(solution)/shard_map/all_to_all | solution.py:805
  52.6 4.9 %all-to-all-start.1 = ((f32[16,8,64,128]{3,2,1,0:T(8,128)}), f32[16,8,64,128]{3,2,1,0:T(8,128)}, u32[]{:S(2)}, u32[]{:S(2)}) async-start(f32[16,8,64,128]{3,2,1,0:T(8,128)} %bitcast.65), calls=%async_computation.1 | async-start | bytes 8388608 | tf_op jit(solution)/shard_map/all_to_all | solution.py:826
  57.5 0.0 all-reduce.4.cloned.1.call-start
  57.6 0.1 pad.19.clone
  57.7 0.4 copy.66
  58.1 0.1 select_reduce_fusion.2
  58.2 0.6 slice.57.total_ref
  58.8 0.1 copy.54
  58.8 0.1 copy.64
  58.9 0.6 reshape.169.mask_ref
  59.6 0.1 reshape.153
  59.6 0.1 convert_reduce_fusion
  59.8 0.1 select_reduce_fusion
  59.9 0.6 gather_fusion
  60.5 0.7 reshape.154.slot_ref
  61.2 1.1 compare_select_fusion.2.count_ref
  62.3 1.2 maximum_maximum_fusion.rows_ref
  63.6 0.1 collective-permute-start.3
  63.7 0.1 maximum_maximum_fusion.2
  63.8 0.8 pad_maximum_fusion.coords_ref
  64.6 6.1 %near_products.1 = f32[128,2048]{1,0:T(8,128)} custom-call(s32[96]{0:T(128)} %reshape.169.mask_ref, f32[35,64,128]{2,1,0:T(8,128)} %maximum_maximum_fusion.rows_ref, f32[35,8,128]{2,1,0:T(8,128)} %pad_maximum_fusion.coords_ref, f32[32,64,3]{2,1,0:T(8,128)} %bitcast.68), custom_call_target="tpu_custom_call" | custom-call | flops 4000000000 | bytes 10000000 | tf_op jit(solution)/shard_map/near_products/pallas_call | solution.py:303
  70.6 0.7 slice.83
  71.3 0.8 copy-done.8
  72.1 10.5 %kernel_blocks.1 = (bf16[128,64,256]{2,1,0:T(8,128)(2,1)}, bf16[128,64,256]{2,1,0:T(8,128)(2,1)}, f32[32,32,64]{2,1,0:T(8,128)}, f32[32,32,32]{2,1,0:T(8,128)}) custom-call(s32[1]{0:T(128)} %slice.57.total_ref, s32[128]{0:T(128)} %copy-done.7, s32[128]{0:T(128)} %compare_select_fusion.2.count_ref, s32[512]{0:T(512)} %reshape.154.slot_ref, ...), custom_call_target="tpu_custom_call" | custom-call | flops 20000000000 | bytes 20000000 | tf_op jit(solution)/shard_map/kernel_blocks/pallas_call | solution.py:139
  82.6 14.5 %branch_factors.1 = (f32[32,32,128]{2,1,0:T(8,128)}, f32[6,32,32,128]{3,2,1,0:T(8,128)}, f32[32,32]{1,0:T(8,128)}, f32[32,32]{1,0:T(8,128)}) custom-call(f32[1024,32]{1,0:T(8,128)} %bitcast.80), custom_call_target="tpu_custom_call" | custom-call | flops 10000000000 | bytes 10000000 | tf_op jit(solution)/shard_map/branch_factors/pallas_call | solution.py:562
  97.2 1.5 broadcast_select_fusion
  98.6 0.0 all-reduce.4.cloned.1.call-update
  98.7 7.4 %bases.1 = (f32[32,2048]{1,0:T(8,128)}, f32[32,2048]{1,0:T(8,128)}) custom-call(f32[32,32,128]{2,1,0:T(8,128)} %get-tuple-element.39.inverse_ref, f32[6,32,32,128]{3,2,1,0:T(8,128)} %get-tuple-element.40.ratio_ref, f32[32,32]{1,0:T(8,128)} %get-tuple-element.41.top_ref, f32[32,32,64]{2,1,0:T(8,128)} %get-tuple-element.42.sketched_ref), custom_call_target="tpu_custom_call" | custom-call | flops 5000000000 | bytes 10000000 | tf_op jit(solution)/shard_map/bases/pallas_call | solution.py:611
  106.0 32.4 %all-to-all-done.1 = f32[16,8,64,128]{3,2,1,0:T(8,128)} async-done(((f32[16,8,64,128]{3,2,1,0:T(8,128)}), f32[16,8,64,128]{3,2,1,0:T(8,128)}, u32[]{:S(2)}, u32[]{:S(2)}) %all-to-all-start.1) | async-done | bytes 4194336 | tf_op jit(solution)/shard_map/all_to_all | solution.py:826
  138.5 7.6 %far_products.1 = (f32[128,2048]{1,0:T(8,128)}, f32[32,128]{1,0:T(8,128)}, f32[16,32,128]{2,1,0:T(8,128)}) custom-call(s32[1]{0:T(128)} %slice.57.total_ref, s32[128]{0:T(128)} %copy-done.7, s32[512]{0:T(512)} %reshape.154.slot_ref, f32[128,64,128]{2,1,0:T(8,128)} %bitcast.20.fetched_ref, bf16[128,64,256]{2,1,0:T(8,128)(2,1)} %get-tuple-element.36.high_ref, ...), custom_call_target="tpu_custom_call" | custom-call | flops 10000000000 | bytes 20000000 | tf_op jit(solution)/shard_map/far_products/pallas_call | solution.py:227
  146.1 22.8 %all-to-all-start.3 = ((f32[16,32,128]{2,1,0:T(8,128)}), f32[16,32,128]{2,1,0:T(8,128)S(1)}, u32[]{:S(2)}, u32[]{:S(2)}) async-start(f32[16,32,128]{2,1,0:T(8,128)} %get-tuple-element.53), calls=%async_computation.3 | async-start | bytes 524288 | tf_op jit(solution)/shard_map/all_to_all | solution.py:866
  168.9 57.2 %all-reduce.4.cloned.1.call-done.children_ref = f32[16,32,32]{2,1,0:T(8,128)} async-done(((f32[16,32,32]{2,1,0:T(8,128)}), f32[16,32,32]{2,1,0:T(8,128)}) %all-reduce.4.cloned.1.call-update) | async-done | bytes 65552 | tf_op jit(solution)/shard_map/psum | solution.py:849
  226.1 12.9 %top_factors.1 = (f32[15,64,32]{2,1,0:T(8,128)}, f32[512,32]{1,0:T(8,128)}) custom-call(f32[16,32,32]{2,1,0:T(8,128)} %all-reduce.4.cloned.1.call-done.children_ref), custom_call_target="tpu_custom_call" | custom-call | flops 10000000000 | bytes 10000000 | tf_op jit(solution)/shard_map/top_factors/pallas_call | solution.py:677
  239.1 1.9 copy.70
  241.0 2.1 fusion.7
  (43 shorter events, 0.3 us)
Async XLA Ops:
  7.2 9.8 %copy-start = (f32[32,128]{1,0:T(8,128)S(1)}, f32[32,128]{1,0:T(8,128)}, u32[]{:S(2)}) copy-start(f32[32,128]{1,0:T(8,128)} %param.9) | copy-start | bytes 49156
  7.2 14.8 %copy-start.2 = (f32[128,2048]{1,0:T(8,128)S(1)}, f32[128,2048]{1,0:T(8,128)}, u32[]{:S(2)}) copy-start(f32[128,2048]{1,0:T(8,128)} %param.8) | copy-start | bytes 3145732
  8.6 15.5 %all-to-all-start = ((s32[16,1,8]{2,1,0:T(1,128)}), s32[16,1,8]{2,1,0:T(1,128)S(1)}, u32[]{:S(2)}, u32[]{:S(2)}) async-start(s32[16,1,8]{2,1,0:T(1,128)} %copy.55), calls=%async_computation | async-start | bytes 16384 | tf_op jit(solution)/shard_map/all_to_all | solution.py:788
  19.5 4.7 %collective-permute-start = (f32[16,2048]{1,0:T(8,128)}, f32[16,2048]{1,0:T(8,128)}, u32[]{:S(2)}, u32[]{:S(2)}) collective-permute-start(f32[16,2048]{1,0:T(8,128)} %dynamic-slice_bitcast_fusion), channel_id=1, source_target_pairs={{0,1},{1,0},{2,3},{3,2},{4,5},{5,4},{6,7},{7,6},{8,9},{9,8},{10,11... | collective-permute-start | bytes 393224 | tf_op jit(solution)/shard_map/ppermute | solution.py:700
  22.0 35.7 %copy-start.1 = (f32[3,2048]{0,1:T(8,128)}, f32[3,2048]{0,1:T(8,128)S(1)}, u32[]{:S(2)}) copy-start(f32[3,2048]{0,1:T(8,128)S(1)} %copy.61) | copy-start | bytes 73732
  29.0 23.7 %all-to-all-start.2 = ((f32[16,80,128]{2,1,0:T(8,128)}), f32[16,80,128]{2,1,0:T(8,128)S(1)}, u32[]{:S(2)}, u32[]{:S(2)}) async-start(f32[16,80,128]{2,1,0:T(8,128)} %packed_rows.1), calls=%async_computation.2 | async-start | bytes 1310720 | tf_op jit(solution)/shard_map/all_to_all | solution.py:805
  35.1 8.7 %collective-permute-start.2 = (f32[72,128]{1,0:T(8,128)S(1)}, f32[72,128]{1,0:T(8,128)S(1)}, u32[]{:S(2)}, u32[]{:S(2)}) collective-permute-start(f32[72,128]{1,0:T(8,128)S(1)} %get-tuple-element.87), channel_id=1, source_target_pairs={{2,0},{4,2},{6,4},{8,6},{10,8},{12,10},{14,12},{16,14},{18,16},{20... | collective-permute-start | bytes 110600 | tf_op jit(solution)/shard_map/ppermute | solution.py:822
  36.4 7.4 %collective-permute-start.1 = (f32[72,128]{1,0:T(8,128)S(1)}, f32[72,128]{1,0:T(8,128)S(1)}, u32[]{:S(2)}, u32[]{:S(2)}) collective-permute-start(f32[72,128]{1,0:T(8,128)S(1)} %get-tuple-element.88), channel_id=1, source_target_pairs={{0,2},{2,4},{4,6},{6,8},{8,10},{10,12},{12,14},{14,16},{16,18},{18... | collective-permute-start | bytes 110600 | tf_op jit(solution)/shard_map/ppermute | solution.py:821
  43.8 14.3 %copy-start.6 = (s32[32]{0:T(128)S(1)}, s32[32]{0:T(128)}, u32[]{:S(2)}) copy-start(s32[32]{0:T(128)} %param.12) | copy-start | bytes 388
  43.8 15.0 %copy-start.4 = (s32[32,16]{0,1:T(8,128)S(1)}, s32[32,16]{0,1:T(8,128)}, u32[]{:S(2)}) copy-start(s32[32,16]{0,1:T(8,128)} %param.11) | copy-start | bytes 6148
  43.8 15.0 %copy-start.5 = (s32[32,3]{0,1:T(4,128)S(1)}, s32[32,3]{0,1:T(4,128)}, u32[]{:S(2)}) copy-start(s32[32,3]{0,1:T(4,128)} %param.13) | copy-start | bytes 1156
  52.6 85.8 %all-to-all-start.1 = ((f32[16,8,64,128]{3,2,1,0:T(8,128)}), f32[16,8,64,128]{3,2,1,0:T(8,128)}, u32[]{:S(2)}, u32[]{:S(2)}) async-start(f32[16,8,64,128]{3,2,1,0:T(8,128)} %bitcast.65), calls=%async_computation.1 | async-start | bytes 8388608 | tf_op jit(solution)/shard_map/all_to_all | solution.py:826
  57.5 168.6 %all-reduce.4.cloned.1.call-start = ((), (), s32[]{:S(2)}) async-start(), calls=%async_computation.4 | async-start | bytes 524288 | tf_op jit(solution)/shard_map/psum | solution.py:849
  59.7 10.9 %copy-start.7 = (s32[128]{0:T(128)}, s32[128]{0:T(128)S(1)}, u32[]{:S(2)}) copy-start(s32[128]{0:T(128)S(1)} %broadcast_minimum_fusion.leaf_ref) | copy-start | bytes 1540
  63.6 7.1 %copy-start.3 = (f32[16,64,128]{2,1,0:T(8,128)}, f32[16,64,128]{2,1,0:T(8,128)S(1)}, u32[]{:S(2)}) copy-start(f32[16,64,128]{2,1,0:T(8,128)S(1)} %slice.82) | copy-start | bytes 1572868
  63.6 7.7 %collective-permute-start.3 = (f32[1024,128]{1,0:T(8,128)S(1)}, f32[1024,128]{1,0:T(8,128)S(1)}, u32[]{:S(2)}, u32[]{:S(2)}) collective-permute-start(f32[1024,128]{1,0:T(8,128)S(1)} %bitcast.74), channel_id=1, source_target_pairs={{0,1},{1,0},{2,3},{3,2},{4,5},{5,4},{6,7},{7,6},{8,9},{9,8},{10,11... | collective-permute-start | bytes 1572872 | tf_op jit(solution)/shard_map/ppermute | solution.py:832
  71.3 0.8 copy-start.8
  146.1 94.9 %all-to-all-start.3 = ((f32[16,32,128]{2,1,0:T(8,128)}), f32[16,32,128]{2,1,0:T(8,128)S(1)}, u32[]{:S(2)}, u32[]{:S(2)}) async-start(f32[16,32,128]{2,1,0:T(8,128)} %get-tuple-element.53), calls=%async_computation.3 | async-start | bytes 524288 | tf_op jit(solution)/shard_map/all_to_all | solution.py:866
Sparse Core Ops, SparseCore 0:
  98.8 127.3 all-reduce.3

commit v4 on v3

--- a/solution.py
+++ b/solution.py
@@ -64,7 +64,7 @@
     own_ref, other_ref, coords_ref, target_ref,
     high_ref, low_ref, sketched_ref, gram_ref,
     packed,
-    *, rank,
+    *, rank, cap,
 ):
     step = pl.program_id(0)
     lane = lax.broadcasted_iota(jnp.int32, (1, LANES), 1)
@@ -74,23 +74,27 @@
     def _():
         sketched_ref[...] = jnp.zeros_like(sketched_ref)
         quarter = rank // 4
+        slots = packed.shape[0]
         own_at = pl.multiple_of(place_ref[0] * 2 * quarter, quarter)
         other_at = pl.multiple_of((1 - place_ref[0]) * 2 * quarter, quarter)
 
-        def unpack(slot, carry):
-            for ref, base in ((own_ref, own_at), (other_ref, other_at)):
-                value = ref[pl.ds(pl.multiple_of(slot * quarter, quarter), quarter), :]
+        def unpack(peer, carry):
+            for entry in range(2 * cap):
+                slot = (entry // cap) * (slots // 2) + peer * cap + entry % cap
+                at = pl.multiple_of((peer * 2 * cap + entry) * quarter, quarter)
+                for ref, base in ((own_ref, own_at), (other_ref, other_at)):
+                    value = ref[pl.ds(at, quarter), :]
+                    turned = pltpu.roll(value, LEAF, 1)
+                    packed[slot, pl.ds(base, quarter), :] = jnp.where(first, value, turned)
+                    packed[slot, pl.ds(base + quarter, quarter), :] = jnp.where(first, turned, value)
+                value = coords_ref[pl.ds((peer * 2 * cap + entry) * 2, 2), :]
                 turned = pltpu.roll(value, LEAF, 1)
-                packed[slot, pl.ds(base, quarter), :] = jnp.where(first, value, turned)
-                packed[slot, pl.ds(base + quarter, quarter), :] = jnp.where(first, turned, value)
-            value = coords_ref[pl.ds(slot * 2, 2), :]
-            turned = pltpu.roll(value, LEAF, 1)
-            packed[slot, rank : rank + 1, :] = jnp.where(first, value, turned)[0:1]
-            packed[slot, rank + 1 : rank + 2, :] = jnp.where(first, turned, value)[0:1]
-            packed[slot, rank + 2 : rank + 3, :] = jnp.where(first, value, turned)[1:2]
+                packed[slot, rank : rank + 1, :] = jnp.where(first, value, turned)[0:1]
+                packed[slot, rank + 1 : rank + 2, :] = jnp.where(first, turned, value)[0:1]
+                packed[slot, rank + 2 : rank + 3, :] = jnp.where(first, value, turned)[1:2]
             return carry
 
-        lax.fori_loop(0, packed.shape[0], unpack, 0, unroll=4)
+        lax.fori_loop(0, slots // (2 * cap), unpack, 0)
 
     @pl.when(step * BATCH < total_ref[0])
     def _():
@@ -123,7 +127,7 @@
             gram_ref[leaf] = dot_exact_nt(block, block)
 
 
-def kernel_blocks(total, group_leaf, group_count, group_slots, place, own, other, coords, targets, rank):
+def kernel_blocks(total, group_leaf, group_count, group_slots, place, own, other, coords, targets, rank, cap):
     leaves = targets.shape[0]
     groups = group_leaf.shape[0]
     slots = coords.shape[0] // 2
@@ -137,7 +141,7 @@
     whole = lambda *unused: (0, 0, 0)
     once = pl.Buffered(1)
     return pl.pallas_call(
-        functools.partial(blocks_body, rank=rank),
+        functools.partial(blocks_body, rank=rank, cap=cap),
         grid_spec=pltpu.PrefetchScalarGridSpec(
             num_scalar_prefetch=5,
             grid=(steps,),
@@ -171,22 +175,24 @@
 
 def far_body(
     total_ref, leaf_ref, slot_ref,
-    fetched_ref, high_ref, low_ref, weights_ref,
+    own_ref, partner_ref, high_ref, low_ref, weights_ref,
     out_ref, projected_ref, copies_ref,
     s_high, s_low, acc,
 ):
     step = pl.program_id(0)
-    samp_dev = fetched_ref.shape[2]
+    samp_dev = own_ref.shape[2]
+    part = own_ref.shape[0]
 
     @pl.when(step == 0)
     def _():
         acc[...] = jnp.zeros_like(acc)
 
         def split(slot, carry):
-            s_high[slot], s_low[slot] = halves(fetched_ref[slot])
+            s_high[slot], s_low[slot] = halves(own_ref[slot])
+            s_high[part + slot], s_low[part + slot] = halves(partner_ref[slot])
             return carry
 
-        lax.fori_loop(0, fetched_ref.shape[0], split, 0, unroll=8)
+        lax.fori_loop(0, part, split, 0, unroll=4)
 
     @pl.when(step * BATCH < total_ref[0])
     def _():
@@ -213,8 +219,9 @@
             out_ref[:, 2 * pair * LEAF : 2 * (pair + 1) * LEAF] = block.T
 
 
-def far_products(total, group_leaf, group_slots, fetched, high, low, weights, branches):
-    slots, unused, samp_dev = fetched.shape
+def far_products(total, group_leaf, group_slots, own, partner, high, low, weights, branches):
+    part, unused, samp_dev = own.shape
+    slots = 2 * part
     groups = group_leaf.shape[0]
     points_dev = weights.shape[1]
     leaves = points_dev // LEAF
@@ -230,7 +237,8 @@
             num_scalar_prefetch=3,
             grid=(steps,),
             in_specs=[
-                pl.BlockSpec(fetched.shape, lambda *unused: (0, 0, 0), pipeline_mode=pl.Buffered(1)),
+                pl.BlockSpec(own.shape, lambda *unused: (0, 0, 0), pipeline_mode=pl.Buffered(1)),
+                pl.BlockSpec(partner.shape, lambda *unused: (0, 0, 0), pipeline_mode=pl.Buffered(1)),
                 pl.BlockSpec((BATCH, LEAF, GROUP * LEAF), block_index),
                 pl.BlockSpec((BATCH, LEAF, GROUP * LEAF), block_index),
                 pl.BlockSpec(weights.shape, lambda *unused: (0, 0), pipeline_mode=pl.Buffered(1)),
@@ -256,7 +264,7 @@
         cost_estimate=pl.CostEstimate(
             flops=10**10, bytes_accessed=2 * 10**7, transcendentals=0
         ),
-    )(total, group_leaf, group_slots, fetched, high, low, weights)
+    )(total, group_leaf, group_slots, own, partner, high, low, weights)
 
 
 NEAR_LEAVES = 8
@@ -717,8 +725,9 @@
     return result
 
 
-def group_tables(far_slots, far_count):
+def group_tables(far_slots, far_count, side, part):
     leaves = far_slots.shape[0]
+    far_slots = far_slots % part + jnp.where(far_slots // part == side, 0, part)
     groups = leaves * FAR // GROUP
     per_leaf = (far_count + GROUP - 1) // GROUP
     before = jnp.arange(leaves)[:, None] >= jnp.arange(leaves)[None, :]
@@ -741,29 +750,84 @@
     )
 
 
-def pack_body(picked_ref, z_ref, c_ref, out_ref, *, cap):
-    z_rows = z_ref.shape[1]
-
-    def one(branch, carry):
-        for entry in range(cap):
-            leaf = picked_ref[branch * cap + entry]
-            out_ref[branch, z_rows * entry : z_rows * (entry + 1), :] = z_ref[leaf]
-            at = z_rows * cap + 2 * entry
-            out_ref[branch, at : at + 2, :] = c_ref[leaf]
+def sketch_body(place_ref, sketch_ref, samples_ref, points_ref, mine_ref, other_ref):
+    product = dot_exact(sketch_ref[...], samples_ref[...])
+    rank, points_dev = product.shape
+    quarter = rank // 4
+    first = lax.broadcasted_iota(jnp.int32, (1, LANES), 1) < LEAF
+    swap = place_ref[0] == 1
+    leaves = points_dev // LEAF
+
+    def interleave(low, high):
+        even = jnp.where(first, low, pltpu.roll(high, LEAF, 1))
+        odd = jnp.where(first, pltpu.roll(low, LEAF, 1), high)
+        return even, odd
+
+    for pair in range(leaves // 2):
+        lanes = slice(pair * LANES, (pair + 1) * LANES)
+        shares = []
+        for share in range(2):
+            base = 2 * quarter * share
+            shares.append(
+                interleave(product[base : base + quarter, lanes], product[base + quarter : base + 2 * quarter, lanes])
+            )
+        for member in range(2):
+            at = (2 * pair + member) * quarter
+            mine_ref[at : at + quarter, :] = jnp.where(swap, shares[1][member], shares[0][member])
+            other_ref[at : at + quarter, :] = jnp.where(swap, shares[0][member], shares[1][member])
+        x = points_ref[0:1, lanes]
+        y = points_ref[1:2, lanes]
+        z = points_ref[2:3, lanes]
+        xy = interleave(x, y)
+        zs = interleave(z, jnp.zeros_like(z))
+        for member in range(2):
+            at = leaves * quarter + (2 * pair + member) * 2
+            mine_ref[at : at + 1, :] = xy[member]
+            mine_ref[at + 1 : at + 2, :] = zs[member]
+
+
+def sketched_shares(place, sketch, samples, points):
+    rank = sketch.shape[0]
+    leaves = samples.shape[1] // LEAF
+    return pl.pallas_call(
+        sketch_body,
+        in_specs=[pl.BlockSpec(memory_space=pltpu.SMEM)] + [vmem_spec] * 3,
+        out_specs=[vmem_spec] * 2,
+        out_shape=[
+            jax.ShapeDtypeStruct((leaves * (rank // 4 + 2), LANES), jnp.float32),
+            jax.ShapeDtypeStruct((leaves * rank // 4, LANES), jnp.float32),
+        ],
+        compiler_params=pltpu.CompilerParams(vmem_limit_bytes=vmem_bytes),
+        name="sketched_shares",
+    )(place, sketch, samples, points)
+
+
+def pack_body(asked_ref, mine_ref, arrived_ref, partner_ref, crossed_ref, out_ref, *, cap, leaves):
+    z_rows = arrived_ref.shape[0] // leaves
+
+    def one(peer, carry):
+        for entry in range(2 * cap):
+            leaf = asked_ref[peer, entry]
+            first_ref, second_ref = (mine_ref, arrived_ref) if entry < cap else (partner_ref, crossed_ref)
+            at = pl.ds(leaf * z_rows, z_rows)
+            out_ref[peer, z_rows * entry : z_rows * (entry + 1), :] = first_ref[at, :] + second_ref[at, :]
+            base = z_rows * 2 * cap + 2 * entry
+            out_ref[peer, base : base + 2, :] = first_ref[pl.ds(leaves * z_rows + leaf * 2, 2), :]
         return carry
 
-    lax.fori_loop(0, out_ref.shape[0], one, 0, unroll=2)
-
-
-def packed_rows(picked, z_rows, c_rows, branches, cap):
+    lax.fori_loop(0, out_ref.shape[0], one, 0)
+
+
+def packed_rows(asked, mine, arrived, partner, crossed, cap, leaves):
+    z_rows = arrived.shape[0] // leaves
     return pl.pallas_call(
-        functools.partial(pack_body, cap=cap),
-        in_specs=[pl.BlockSpec(memory_space=pltpu.SMEM), vmem_spec, vmem_spec],
+        functools.partial(pack_body, cap=cap, leaves=leaves),
+        in_specs=[pl.BlockSpec(memory_space=pltpu.SMEM)] + [vmem_spec] * 4,
         out_specs=vmem_spec,
-        out_shape=jax.ShapeDtypeStruct((branches, cap * (z_rows.shape[1] + 2), LANES), jnp.float32),
+        out_shape=jax.ShapeDtypeStruct((asked.shape[0], 2 * cap * (z_rows + 2), LANES), jnp.float32),
         compiler_params=pltpu.CompilerParams(vmem_limit_bytes=vmem_bytes),
         name="packed_rows",
-    )(picked, z_rows, c_rows)
+    )(asked, mine, arrived, partner, crossed)
 
 
 def two_rows(values, rows):
@@ -779,31 +843,52 @@
     branches = lax.axis_size("leaf")
     columns = lax.axis_size("cols")
     cap = far_requests.shape[2]
-    slots = branches * cap
     share = rank // columns
     me = lax.axis_index("leaf")
     column = lax.axis_index("cols")
 
-    wanted = far_requests.reshape(branches, cap)
-    asked_for = lax.all_to_all(wanted, "leaf", split_axis=0, concat_axis=0, tiled=True)
+    half = branches // 2
+    side = me // half
+    groups = [list(range(half)), list(range(half, branches))]
+    mirror = [(i, (i + half) % branches) for i in range(branches)]
+    wanted = far_requests.reshape(2, half, cap)
+    wanted = jnp.where(side == 0, wanted, wanted[::-1])
+    wanted = jnp.transpose(wanted, (1, 0, 2)).reshape(half, 2 * cap)
+    asked = lax.all_to_all(
+        wanted, "leaf", split_axis=0, concat_axis=0, axis_index_groups=groups, tiled=True
+    )
+
+    if columns == 2:
+        place = column.astype(jnp.int32).reshape(1)
+        mine, other = sketched_shares(place, sketch, samples, points)
+        arrived = lax.ppermute(other, "cols", [(0, 1), (1, 0)])
+        partner = lax.ppermute(mine, "leaf", mirror)
+        crossed = lax.ppermute(
+            other,
+            ("leaf", "cols"),
+            [(2 * i + c, 2 * ((i + half) % branches) + 1 - c) for i in range(branches) for c in range(2)],
+        )
+    else:
+        z_part = jnp.dot(sketch, samples, precision=highest)
+        z_mine = exchange_sum(z_part.reshape(columns, share, leaves * LEAF), "cols")
+        z_rows = two_rows(z_mine.reshape(share, leaves, LEAF), share // 2)
+        planes = points.reshape(3, leaves, LEAF)
+        c_rows = two_rows(
+            jnp.concatenate([planes[0:1], planes[2:3], planes[1:2], jnp.zeros_like(planes[0:1])], axis=0), 2
+        )
+        mine = jnp.concatenate([z_rows.reshape(-1, LANES), c_rows.reshape(-1, LANES)], axis=0)
+        partner = lax.ppermute(mine, "leaf", mirror)
+        arrived = jnp.zeros((leaves * share // 2, LANES), jnp.float32)
+        crossed = arrived
 
     coords = jnp.transpose(points.reshape(3, leaves, LEAF), (1, 0, 2))
-    targets = jnp.transpose(coords, (0, 2, 1))
     rows = jnp.transpose(samples.reshape(samp_dev, leaves, LEAF), (1, 2, 0))
-    tables = group_tables(far_slots, far_count)
-
-    z_part = jnp.dot(sketch, samples, precision=highest)
-    z_mine = exchange_sum(z_part.reshape(columns, share, leaves * LEAF), "cols")
-    z_rows = two_rows(z_mine.reshape(share, leaves, LEAF), share // 2)
-    planes = points.reshape(3, leaves, LEAF)
-    c_rows = two_rows(
-        jnp.concatenate([planes[0:1], planes[2:3], planes[1:2], jnp.zeros_like(planes[0:1])], axis=0), 2
-    )
-    asked_for, rows, z_rows, c_rows = lax.optimization_barrier((asked_for, rows, z_rows, c_rows))
-    picked = asked_for.reshape(-1)
-    small_sent = packed_rows(picked, z_rows, c_rows, branches, cap)
-    small_got = lax.all_to_all(small_sent, "leaf", split_axis=0, concat_axis=0, tiled=True)
-    total, group_leaf, group_count, group_slots = group_tables(far_slots, far_count)
+    small_sent = packed_rows(asked, mine, arrived, partner, crossed, cap, leaves)
+    small_got = lax.all_to_all(
+        small_sent, "leaf", split_axis=0, concat_axis=0, axis_index_groups=groups, tiled=True
+    )
+    tables = group_tables(far_slots, far_count, side, half * cap)
+    total, group_leaf, group_count, group_slots = tables
 
     forward = [(i, i + 1) for i in range(branches - 1)]
     backward = [(target, source) for source, target in forward]
@@ -821,34 +906,71 @@
     low_edge = lax.ppermute(edges[1], "leaf", forward)
     high_edge = lax.ppermute(edges[0], "leaf", backward)
 
-    rows_sent = rows[picked].reshape(branches, cap, LEAF, samp_dev)
-    rows_sent, low_edge, high_edge = lax.optimization_barrier((rows_sent, low_edge, high_edge))
-    rows_got = lax.all_to_all(rows_sent, "leaf", split_axis=0, concat_axis=0, tiled=True)
-    fetched = rows_got.reshape(slots, LEAF, samp_dev)
-
-    z_own = small_got[:, : cap * share // 2].reshape(slots * share // 2, LANES)
-    c_got = small_got[:, cap * share // 2 :].reshape(slots * 2, LANES)
+    rows_out, low_edge, high_edge = lax.optimization_barrier((rows, low_edge, high_edge))
+    partner_rows = lax.ppermute(rows_out, "leaf", mirror)
+
+    own_sent = rows[asked[:, :cap].reshape(-1)].reshape(half, cap, LEAF, samp_dev)
+    own_got = lax.all_to_all(
+        own_sent, "leaf", split_axis=0, concat_axis=0, axis_index_groups=groups, tiled=True
+    )
+    own_got = own_got.reshape(half * cap, LEAF, samp_dev)
+
+    z_count = 2 * cap * share // 2
+    z_own = small_got[:, :z_count].reshape(half * z_count, LANES)
+    c_got = small_got[:, z_count:].reshape(half * 4 * cap, LANES)
     if columns == 2:
         z_other = lax.ppermute(z_own, "cols", [(0, 1), (1, 0)])
-        place = column.astype(jnp.int32).reshape(1)
     else:
+        slots = branches * cap
         z_all = exchange_all(z_own, "cols").reshape(columns, slots, share // 2, 2, LEAF)
         z_all = jnp.transpose(z_all, (1, 0, 3, 2, 4)).reshape(slots, 2, 2, rank // 4, LEAF)
         z_all = jnp.transpose(z_all, (1, 0, 3, 2, 4)).reshape(2, slots * rank // 4, LANES)
         z_own, z_other = z_all[0], z_all[1]
         place = jnp.zeros((1,), jnp.int32)
 
+    targets = jnp.transpose(coords, (0, 2, 1))
     high, low, sketched, gram = kernel_blocks(
-        total, group_leaf, group_count, group_slots, place, z_own, z_other, c_got, targets, rank
+        total, group_leaf, group_count, group_slots, place, z_own, z_other, c_got, targets, rank, cap
     )
 
     levels = leaves.bit_length()
     inverse, ratio, top_inverse, own_child = branch_factors(gram, levels)
+    own_child = own_child.reshape(rank * rank // LANES, LANES)
+    partner_child = lax.ppermute(own_child, "leaf", mirror)
+    both_children = jnp.where(
+        side == 0,
+        jnp.concatenate([own_child, partner_child], axis=0),
+        jnp.concatenate([partner_child, own_child], axis=0),
+    )
+    child_rows = both_children.shape[0]
+
+    partner_sent = partner_rows[asked[:, cap:].reshape(-1)].reshape(half, cap * LEAF, samp_dev)
+    if samp_dev == LANES:
+        both = jnp.concatenate(
+            [partner_sent, jnp.broadcast_to(both_children[None], (half,) + both_children.shape)], axis=1
+        )
+        partner_sent = both
+        both = lax.all_to_all(
+            both, "leaf", split_axis=0, concat_axis=0, axis_index_groups=groups, tiled=True
+        )
+        partner_got = both[:, : cap * LEAF]
+        children = both[:, cap * LEAF :]
+    else:
+        partner_got = lax.all_to_all(
+            partner_sent, "leaf", split_axis=0, concat_axis=0, axis_index_groups=groups, tiled=True
+        )
+        children = lax.all_to_all(
+            jnp.broadcast_to(both_children[None], (half,) + both_children.shape),
+            "leaf", split_axis=0, concat_axis=0, axis_index_groups=groups, tiled=True,
+        )
+    partner_got = partner_got.reshape(half * cap, LEAF, samp_dev)
+    children = jnp.transpose(children.reshape(half, 2, child_rows // 2, LANES), (1, 0, 2, 3))
+    children = children.reshape(branches, rank, rank)
+    ratio, rows_low, rows_high, unused = lax.optimization_barrier(
+        (ratio, low_edge[:LEAF, :samp_dev], high_edge[:LEAF, :samp_dev], partner_sent)
+    )
     weights, leaf_basis = bases(inverse, ratio, top_inverse, sketched)
-    mine = jnp.arange(branches)[:, None, None] == me
-    children = lax.psum(jnp.where(mine, own_child[None], 0.0), "leaf")
-
-    rows_low, rows_high = low_edge[:LEAF, :samp_dev], high_edge[:LEAF, :samp_dev]
+
     coords_low, coords_high = low_edge[LEAF : LEAF + 3, :LEAF], high_edge[LEAF : LEAF + 3, :LEAF]
     near_rows = jnp.concatenate(
         [rows_low[None], rows, rows_high[None], jnp.zeros_like(rows_low)[None]], axis=0
@@ -861,7 +983,7 @@
     near_sample = near_products(near_mask.reshape(-1), near_rows, near_coords, targets)
 
     far_sample, branch_samples, copies = far_products(
-        total, group_leaf, group_slots, fetched, high, low, weights, branches
+        total, group_leaf, group_slots, own_got, partner_got, high, low, weights, branches
     )
     everyone = lax.all_to_all(copies, "leaf", split_axis=0, concat_axis=0, tiled=True)
     children, unused = lax.optimization_barrier((children, branch_samples))

time: 251 us -> 199 us (0.79)
  waiting for transfers between devices: 99.5 us -> 61.5 us
  between operations: 14.4 us -> 0.94 us
  starting transfers between devices: 47.8 us -> 36 us
  Pallas kernels: 61.1 us -> 70 us
    psum x1 -> x0, waiting for transfers between devices: 57.2 us -> none  [on_device(): children = lax.psum(jnp.where(mine, own_child[None], 0.0), 'leaf')]
    ppermute x1 -> x5, waiting for transfers between devices: 0.01 us -> 20.3 us  [the longest x1 15.5 us: on_device(): partner_rows = lax.ppermute(rows_out, 'leaf', mirror)]
    all_to_all x1, starting transfers between devices: 22.8 us -> 5.72 us  [on_device(): lax.all_to_all(copies, 'leaf', split_axis=0, concat_axis=0, tiled=True)]
    ppermute x1 -> x5, starting transfers between devices: 0.01 us -> 7.67 us  [the longest x1 3.7 us: on_device(): lax.ppermute(other, ('leaf', 'cols'), [(2 * i + c, 2 * ((i + half) % bran...]
    all_to_all x3 -> x4, waiting for transfers between devices: 42.3 us -> 36.6 us  [the longest x1 24.1 us: on_device(): lax.all_to_all(both, 'leaf', split_axis=0, concat_axis=0, axis_index_grou...]
    pallas_call x2 -> x3, Pallas kernels: 12.5 us -> 18.2 us  [the longest x1 13.2 us: kernel_blocks(): pl.pallas_call(functools.partial(blocks_body, rank=rank, cap=cap), grid_s...]
    ppermute x1, waiting for transfers between devices: 0.01 us -> 4.24 us  [on_device(): high_edge = lax.ppermute(edges[0], 'leaf', backward)]
    pallas_call x1, Pallas kernels: 7.62 us -> 11.3 us  [far_products(): pl.pallas_call(far_body, grid_spec=pltpu.PrefetchScalarGridSpec(num_scala...]
  transfers between devices with their start and end apart: 9 -> 13, of which waited for: 4 -> 7; matrix products, arithmetic and copies ran while one was open for 8% -> 12% of each run, Pallas kernels for 24% -> 27%
where the time goes in v4:
time: 199 us; the launch traced here: 197 us
  Pallas kernels  70 us (35%)
  waiting for transfers between devices  61.5 us (31%)
  starting transfers between devices  36 us (18%)
  local copies, waits for them, and re-layouts  19.1 us (10%)
  other arithmetic  7.83 us (4%)
  matrix products  2.13 us (1%)
    all_to_all x1, waiting for transfers between devices, on_device(): lax.all_to_all(both, 'leaf', split_axis=0, concat_axis=0, axis_index_grou...  24.1 us
    ppermute x1, waiting for transfers between devices, on_device(): partner_rows = lax.ppermute(rows_out, 'leaf', mirror)  15.5 us
    pallas_call x1, Pallas kernels, branch_factors(): pl.pallas_call(functools.partial(branch_body, rank=rank, levels=levels),...  14.4 us
    pallas_call x1, Pallas kernels, kernel_blocks(): pl.pallas_call(functools.partial(blocks_body, rank=rank, cap=cap), grid_s...  13.2 us
    pallas_call x1, Pallas kernels, top_factors(): pl.pallas_call(functools.partial(top_body, rank=rank, levels=levels), in_...  12.7 us
    pallas_call x1, Pallas kernels, far_products(): pl.pallas_call(far_body, grid_spec=pltpu.PrefetchScalarGridSpec(num_scala...  11.3 us
    pallas_call x1, Pallas kernels, bases(): pl.pallas_call(functools.partial(basis_body, rank=rank, levels=levels), i...  7.38 us
    all_to_all x1, waiting for transfers between devices, on_device(): lax.all_to_all(small_sent, 'leaf', split_axis=0, concat_axis=0, axis_inde...  6.89 us
  transfers between devices with their start and end apart: 13, of which 7 were waited for; matrix products, arithmetic and copies ran while one was open for 12% of the time, Pallas kernels for 27%

profile of v4, /device:TPU:0, one launch (start us, length us, event | category | flops | bytes accessed | tf_op | source)
XLA Modules:
  0.0 197.5 jit_solution(1573414068733002391)
XLA Ops:
  0.6 2.7 %sketched_shares.1 = (f32[320,128]{1,0:T(8,128)}, f32[256,128]{1,0:T(8,128)}) custom-call(s32[1]{0:T(128)} %bitcast.15.place_ref, f32[32,128]{1,0:T(8,128)} %sketch_ref.1, f32[128,2048]{1,0:T(8,128)} %samples_ref.1, f32[3,2048]{1,0:T(4,128)} %points_ref.1), custom_call_target="tpu_custom_call" | custom-call | tf_op jit(solution)/shard_map/sketched_shares/pallas_call | solution.py:792
  3.3 0.5 collective-permute-start
  3.8 3.7 %collective-permute-start.2 = (f32[256,128]{1,0:T(8,128)}, f32[256,128]{1,0:T(8,128)}, u32[]{:S(2)}, u32[]{:S(2)}) collective-permute-start(f32[256,128]{1,0:T(8,128)} %get-tuple-element.32), channel_id=1, source_target_pairs={{0,17},{1,16},{2,19},{3,18},{4,21},{5,20},{6,23},{7,22},{8,25},{9,... | collective-permute-start | bytes 393224 | tf_op jit(solution)/shard_map/ppermute | solution.py:866
  7.5 0.8 reshape.210
  8.3 0.1 copy.51
  8.4 0.7 all_to_all.19
  9.1 4.7 %all-to-all-start = ((s32[8,1,16]{2,1,0:T(1,128)}), s32[8,1,16]{2,1,0:T(1,128)S(1)}, u32[]{:S(2)}, u32[]{:S(2)}) async-start(s32[8,1,16]{2,1,0:T(1,128)} %bitcast.6), calls=%async_computation | async-start | bytes 8192 | tf_op jit(solution)/shard_map/all_to_all | solution.py:857
  13.8 0.3 collective-permute-start.1
  14.1 0.7 and_select_fusion
  14.8 0.1 select_reduce_fusion.2
  14.9 0.1 convert_reduce_fusion
  15.0 0.7 fusion.15
  15.7 0.7 fusion
  16.4 0.7 select_reduce_fusion
  17.1 0.6 slice.51.total_ref
  17.8 1.1 copy.53
  18.9 0.3 copy.50
  19.3 0.1 copy.49
  19.3 0.1 reshape.207
  19.5 4.8 %collective-permute-done.1.partner_ref = f32[320,128]{1,0:T(8,128)S(1)} collective-permute-done((f32[320,128]{1,0:T(8,128)}, f32[320,128]{1,0:T(8,128)S(1)}, u32[]{:S(2)}, u32[]{:S(2)}) %collective-permute-start.1) | collective-permute-done | bytes 163872 | tf_op jit(solution)/shard_map/ppermute | solution.py:865
  24.2 0.7 copy-done.3
  24.9 2.2 %packed_rows.1 = f32[8,160,128]{2,1,0:T(8,128)} custom-call(s32[8,16]{1,0:T(8,128)} %bitcast.79, f32[320,128]{1,0:T(8,128)} %get-tuple-element.31.mine_ref, f32[256,128]{1,0:T(8,128)} %copy-done.4, f32[320,128]{1,0:T(8,128)} %copy-done.3, f32[256,128]{1,0:T(8,128)} %collective-permute-done.2.crossed_ref), custom_call_target="tpu_custom_call" | custom-call | tf_op jit(solution)/shard_map/packed_rows/pallas_call | solution.py:823
  27.2 4.0 %all-to-all-start.2 = ((f32[8,160,128]{2,1,0:T(8,128)}), f32[8,160,128]{2,1,0:T(8,128)S(1)}, u32[]{:S(2)}, u32[]{:S(2)}) async-start(f32[8,160,128]{2,1,0:T(8,128)} %packed_rows.1), calls=%async_computation.2 | async-start | bytes 1310720 | tf_op jit(solution)/shard_map/all_to_all | solution.py:887
  31.2 0.6 gather_fusion
  31.9 0.7 reshape.208.slot_ref
  32.6 0.1 copy.63
  32.7 1.2 compare_select_fusion.3.count_ref
  33.9 6.9 %all-to-all-done.2 = f32[8,160,128]{2,1,0:T(8,128)S(1)} async-done(((f32[8,160,128]{2,1,0:T(8,128)}), f32[8,160,128]{2,1,0:T(8,128)S(1)}, u32[]{:S(2)}, u32[]{:S(2)}) %all-to-all-start.2) | async-done | bytes 655392 | tf_op jit(solution)/shard_map/all_to_all | solution.py:887
  41.0 0.1 reshape.216
  41.1 2.4 %collective-permute-start.3 = (f32[72,128]{1,0:T(8,128)S(1)}, f32[72,128]{1,0:T(8,128)S(1)}, u32[]{:S(2)}, u32[]{:S(2)}) collective-permute-start(f32[72,128]{1,0:T(8,128)S(1)} %get-tuple-element.87), channel_id=1, source_target_pairs={{0,2},{2,4},{4,6},{6,8},{8,10},{10,12},{12,14},{14,16},{16,18},{18... | collective-permute-start | bytes 110600 | tf_op jit(solution)/shard_map/ppermute | solution.py:906
  43.5 1.3 collective-permute-start.4
  44.8 0.3 collective-permute-done.3
  45.1 4.2 %collective-permute-done.4 = f32[72,128]{1,0:T(8,128)S(1)} collective-permute-done((f32[72,128]{1,0:T(8,128)S(1)}, f32[72,128]{1,0:T(8,128)S(1)}, u32[]{:S(2)}, u32[]{:S(2)}) %collective-permute-start.4) | collective-permute-done | bytes 36896 | tf_op jit(solution)/shard_map/ppermute | solution.py:907
  49.4 3.2 %collective-permute-start.5 = (f32[32,64,128]{2,1,0:T(8,128)S(1)}, f32[32,64,128]{2,1,0:T(8,128)}, u32[]{:S(2)}, u32[]{:S(2)}) collective-permute-start(f32[32,64,128]{2,1,0:T(8,128)S(1)} %bitcast.63), channel_id=1, source_target_pairs={{0,16},{2,18},{4,20},{6,22},{8,24},{10,26},{12,28},{14,30},{16,0},... | collective-permute-start | bytes 3145736 | tf_op jit(solution)/shard_map/ppermute | solution.py:910
  52.5 0.7 slice.79
  53.2 0.9 copy-done.9
  54.1 13.2 %kernel_blocks.1 = (bf16[128,64,256]{2,1,0:T(8,128)(2,1)}, bf16[128,64,256]{2,1,0:T(8,128)(2,1)}, f32[32,32,64]{2,1,0:T(8,128)}, f32[32,32,32]{2,1,0:T(8,128)}) custom-call(s32[1]{0:T(128)} %slice.51.total_ref, s32[128]{0:T(128)} %copy-done.8, s32[128]{0:T(128)} %compare_select_fusion.3.count_ref, s32[512]{0:T(512)} %reshape.208.slot_ref, ...), custom_call_target="tpu_custom_call" | custom-call | flops 20000000000 | bytes 20000000 | tf_op jit(solution)/shard_map/kernel_blocks/pallas_call | solution.py:143
  67.3 14.4 %branch_factors.1 = (f32[32,32,128]{2,1,0:T(8,128)}, f32[6,32,32,128]{3,2,1,0:T(8,128)}, f32[32,32]{1,0:T(8,128)}, f32[32,32]{1,0:T(8,128)}) custom-call(f32[1024,32]{1,0:T(8,128)} %bitcast.81), custom_call_target="tpu_custom_call" | custom-call | flops 10000000000 | bytes 10000000 | tf_op jit(solution)/shard_map/branch_factors/pallas_call | solution.py:570
  81.7 0.8 concatenate.40
  82.5 15.5 %collective-permute-done.5 = f32[32,64,128]{2,1,0:T(8,128)} collective-permute-done((f32[32,64,128]{2,1,0:T(8,128)S(1)}, f32[32,64,128]{2,1,0:T(8,128)}, u32[]{:S(2)}, u32[]{:S(2)}) %collective-permute-start.5) | collective-permute-done | bytes 1048608 | tf_op jit(solution)/shard_map/ppermute | solution.py:910
  98.0 1.9 gather_fusion.2
  100.0 1.6 pad_maximum_fusion
  101.6 5.4 %all-to-all-start.3 = ((f32[8,528,128]{2,1,0:T(8,128)}), f32[8,528,128]{2,1,0:T(8,128)S(1)}, u32[]{:S(2)}, u32[]{:S(2)}) async-start(f32[8,528,128]{2,1,0:T(8,128)} %pad_maximum_fusion), calls=%async_computation.3 | async-start | bytes 4325376 | tf_op jit(solution)/shard_map/all_to_all | solution.py:953
  106.9 0.1 reshape.211
  107.0 2.0 %gather_fusion.1 = f32[64,64,128]{2,1,0:T(8,128)} fusion(f32[32,64,128]{2,1,0:T(8,128)S(1)} %bitcast.64, s32[1024]{0:T(1024)S(1)} %pad_clamp_fusion.1), kind=kCustom, calls=%fused_computation.1 | custom fusion | bytes 4194560 | tf_op jit(solution)/shard_map/gather | solution.py:912
  109.0 24.1 %all-to-all-done.3 = f32[8,528,128]{2,1,0:T(8,128)S(1)} async-done(((f32[8,528,128]{2,1,0:T(8,128)}), f32[8,528,128]{2,1,0:T(8,128)S(1)}, u32[]{:S(2)}, u32[]{:S(2)}) %all-to-all-start.3) | async-done | bytes 2162720 | tf_op jit(solution)/shard_map/all_to_all | solution.py:953
  133.2 4.7 %all-to-all-start.1 = ((f32[8,8,64,128]{3,2,1,0:T(8,128)}), f32[8,8,64,128]{3,2,1,0:T(8,128)}, u32[]{:S(2)}, u32[]{:S(2)}) async-start(f32[8,8,64,128]{3,2,1,0:T(8,128)} %bitcast.66), calls=%async_computation.1 | async-start | bytes 4194304 | tf_op jit(solution)/shard_map/all_to_all | solution.py:913
  137.8 1.6 copy.57
  139.4 0.1 copy.55
  139.5 0.6 reshape.222.mask_ref
  140.2 0.1 pad.19.clone
  140.3 0.1 maximum_maximum_fusion.1
  140.4 0.8 pad_maximum_fusion.1.coords_ref
  141.2 1.1 maximum_maximum_fusion.rows_ref
  142.3 6.1 %near_products.1 = f32[128,2048]{1,0:T(8,128)} custom-call(s32[96]{0:T(128)} %reshape.222.mask_ref, f32[35,64,128]{2,1,0:T(8,128)} %maximum_maximum_fusion.rows_ref, f32[35,8,128]{2,1,0:T(8,128)} %pad_maximum_fusion.1.coords_ref, f32[32,64,3]{2,1,0:T(8,128)} %bitcast.71), custom_call_target="tpu_custom_call" | custom-call | flops 4000000000 | bytes 10000000 | tf_op jit(solution)/shard_map/near_products/pallas_call | solution.py:311
  148.4 7.4 %bases.1 = (f32[32,2048]{1,0:T(8,128)}, f32[32,2048]{1,0:T(8,128)}) custom-call(f32[32,32,128]{2,1,0:T(8,128)} %get-tuple-element.39.inverse_ref, f32[6,32,32,128]{3,2,1,0:T(8,128)} %get-tuple-element.43.ratio_ref, f32[32,32]{1,0:T(8,128)} %get-tuple-element.44.top_ref, f32[32,32,64]{2,1,0:T(8,128)} %get-tuple-element.45.sketched_ref), custom_call_target="tpu_custom_call" | custom-call | flops 5000000000 | bytes 10000000 | tf_op jit(solution)/shard_map/bases/pallas_call | solution.py:619
  155.8 0.8 reshape.224.children_ref
  156.6 1.5 slice.80
  158.1 5.6 %all-to-all-done.1 = f32[8,8,64,128]{3,2,1,0:T(8,128)} async-done(((f32[8,8,64,128]{3,2,1,0:T(8,128)}), f32[8,8,64,128]{3,2,1,0:T(8,128)}, u32[]{:S(2)}, u32[]{:S(2)}) %all-to-all-start.1) | async-done | bytes 2097184 | tf_op jit(solution)/shard_map/all_to_all | solution.py:913
  163.7 11.3 %far_products.1 = (f32[128,2048]{1,0:T(8,128)}, f32[32,128]{1,0:T(8,128)}, f32[16,32,128]{2,1,0:T(8,128)}) custom-call(s32[1]{0:T(128)} %slice.51.total_ref, s32[128]{0:T(128)} %copy-done.8, s32[512]{0:T(512)} %reshape.208.slot_ref, f32[64,64,128]{2,1,0:T(8,128)} %bitcast.10.own_ref, f32[64,64,128]{2,1,0:T(8,128)} %bitcast.72, ...), custom_call_target="tpu_custom_call" | custom-call | flops 10000000000 | bytes 20000000 | tf_op jit(solution)/shard_map/far_products/pallas_call | solution.py:234
  175.0 5.7 %all-to-all-start.4 = ((f32[16,32,128]{2,1,0:T(8,128)}), f32[16,32,128]{2,1,0:T(8,128)S(1)}, u32[]{:S(2)}, u32[]{:S(2)}) async-start(f32[16,32,128]{2,1,0:T(8,128)} %get-tuple-element.55), calls=%async_computation.4 | async-start | bytes 524288 | tf_op jit(solution)/shard_map/all_to_all | solution.py:988
  180.7 12.7 %top_factors.1 = (f32[15,64,32]{2,1,0:T(8,128)}, f32[512,32]{1,0:T(8,128)}) custom-call(f32[16,32,32]{2,1,0:T(8,128)} %reshape.224.children_ref), custom_call_target="tpu_custom_call" | custom-call | flops 10000000000 | bytes 10000000 | tf_op jit(solution)/shard_map/top_factors/pallas_call | solution.py:685
  193.4 1.9 copy.62
  195.3 2.1 %fusion.12 = f32[32,128]{1,0:T(8,128)} fusion(f32[512,32]{1,0:T(8,128)} %get-tuple-element.54, f32[512,128]{1,0:T(8,128)S(1)} %bitcast.73), kind=kOutput, calls=%fused_computation.55 | convolution fusion | flops 25165824 | bytes 344064 | tf_op jit(solution)/shard_map/dot_general | solution.py:991
  (53 shorter events, 0.4 us)
Async XLA Ops:
  0.6 18.3 %copy-start.1 = (f32[128,2048]{1,0:T(8,128)S(1)}, f32[128,2048]{1,0:T(8,128)}, u32[]{:S(2)}) copy-start(f32[128,2048]{1,0:T(8,128)} %samples_ref.1) | copy-start | bytes 3145732
  3.3 16.1 %collective-permute-start = (f32[256,128]{1,0:T(8,128)}, f32[256,128]{1,0:T(8,128)S(1)}, u32[]{:S(2)}, u32[]{:S(2)}) collective-permute-start(f32[256,128]{1,0:T(8,128)} %get-tuple-element.32), channel_id=1, source_target_pairs={{0,1},{1,0},{2,3},{3,2},{4,5},{5,4},{6,7},{7,6},{8,9},{9,8},{10,11... | collective-permute-start | bytes 393224 | tf_op jit(solution)/shard_map/ppermute | solution.py:864
  3.8 15.7 %collective-permute-start.2 = (f32[256,128]{1,0:T(8,128)}, f32[256,128]{1,0:T(8,128)}, u32[]{:S(2)}, u32[]{:S(2)}) collective-permute-start(f32[256,128]{1,0:T(8,128)} %get-tuple-element.32), channel_id=1, source_target_pairs={{0,17},{1,16},{2,19},{3,18},{4,21},{5,20},{6,23},{7,22},{8,25},{9,... | collective-permute-start | bytes 393224 | tf_op jit(solution)/shard_map/ppermute | solution.py:866
  9.1 10.4 %all-to-all-start = ((s32[8,1,16]{2,1,0:T(1,128)}), s32[8,1,16]{2,1,0:T(1,128)S(1)}, u32[]{:S(2)}, u32[]{:S(2)}) async-start(s32[8,1,16]{2,1,0:T(1,128)} %bitcast.6), calls=%async_computation | async-start | bytes 8192 | tf_op jit(solution)/shard_map/all_to_all | solution.py:857
  13.8 10.4 %collective-permute-start.1 = (f32[320,128]{1,0:T(8,128)}, f32[320,128]{1,0:T(8,128)S(1)}, u32[]{:S(2)}, u32[]{:S(2)}) collective-permute-start(f32[320,128]{1,0:T(8,128)} %get-tuple-element.31.mine_ref), channel_id=1, source_target_pairs={{0,16},{2,18},{4,20},{6,22},{8,24},{10,26},{12,28},{14,30},{16,0},... | collective-permute-start | bytes 491528 | tf_op jit(solution)/shard_map/ppermute | solution.py:865
  16.4 10.8 %copy-start.8 = (s32[128]{0:T(128)}, s32[128]{0:T(128)S(1)}, u32[]{:S(2)}) copy-start(s32[128]{0:T(128)S(1)} %broadcast_minimum_fusion.leaf_ref) | copy-start | bytes 1540
  18.9 13.6 %copy-start = (f32[3,2048]{0,1:T(8,128)}, f32[3,2048]{0,1:T(8,128)S(1)}, u32[]{:S(2)}) copy-start(f32[3,2048]{0,1:T(8,128)S(1)} %copy.53) | copy-start | bytes 73732
  19.4 4.8 %copy-start.5 = (s32[8,1,16]{2,1,0:T(1,128)}, s32[8,1,16]{2,1,0:T(1,128)S(1)}, u32[]{:S(2)}) copy-start(s32[8,1,16]{2,1,0:T(1,128)S(1)} %all-to-all-done) | copy-start | bytes 1540
  19.4 4.8 %copy-start.4 = (f32[256,128]{1,0:T(8,128)}, f32[256,128]{1,0:T(8,128)S(1)}, u32[]{:S(2)}) copy-start(f32[256,128]{1,0:T(8,128)S(1)} %collective-permute-done.arrived_ref) | copy-start | bytes 393220
  24.2 0.7 copy-start.3
  27.1 13.7 %copy-start.6 = (s32[8,1,16]{2,1,0:T(1,128)S(1)}, s32[8,1,16]{2,1,0:T(1,128)}, u32[]{:S(2)}) copy-start(s32[8,1,16]{2,1,0:T(1,128)} %copy-done.5) | copy-start | bytes 1540
  27.2 13.6 %all-to-all-start.2 = ((f32[8,160,128]{2,1,0:T(8,128)}), f32[8,160,128]{2,1,0:T(8,128)S(1)}, u32[]{:S(2)}, u32[]{:S(2)}) async-start(f32[8,160,128]{2,1,0:T(8,128)} %packed_rows.1), calls=%async_computation.2 | async-start | bytes 1310720 | tf_op jit(solution)/shard_map/all_to_all | solution.py:887
  40.8 12.4 %copy-start.2 = (f32[8,128,128]{2,1,0:T(8,128)}, f32[8,128,128]{2,1,0:T(8,128)S(1)}, u32[]{:S(2)}) copy-start(f32[8,128,128]{2,1,0:T(8,128)S(1)} %slice.78) | copy-start | bytes 1572868
  40.8 12.4 %collective-permute-start.6 = (f32[1024,128]{1,0:T(8,128)S(1)}, f32[1024,128]{1,0:T(8,128)S(1)}, u32[]{:S(2)}, u32[]{:S(2)}) collective-permute-start(f32[1024,128]{1,0:T(8,128)S(1)} %bitcast.74), channel_id=1, source_target_pairs={{0,1},{1,0},{2,3},{3,2},{4,5},{5,4},{6,7},{7,6},{8,9},{9,8},{10,11... | collective-permute-start | bytes 1572872 | tf_op jit(solution)/shard_map/ppermute | solution.py:922
  41.1 4.1 %collective-permute-start.3 = (f32[72,128]{1,0:T(8,128)S(1)}, f32[72,128]{1,0:T(8,128)S(1)}, u32[]{:S(2)}, u32[]{:S(2)}) collective-permute-start(f32[72,128]{1,0:T(8,128)S(1)} %get-tuple-element.87), channel_id=1, source_target_pairs={{0,2},{2,4},{4,6},{6,8},{8,10},{10,12},{12,14},{14,16},{16,18},{18... | collective-permute-start | bytes 110600 | tf_op jit(solution)/shard_map/ppermute | solution.py:906
  43.5 5.9 %collective-permute-start.4 = (f32[72,128]{1,0:T(8,128)S(1)}, f32[72,128]{1,0:T(8,128)S(1)}, u32[]{:S(2)}, u32[]{:S(2)}) collective-permute-start(f32[72,128]{1,0:T(8,128)S(1)} %get-tuple-element.86), channel_id=1, source_target_pairs={{2,0},{4,2},{6,4},{8,6},{10,8},{12,10},{14,12},{16,14},{18,16},{20... | collective-permute-start | bytes 110600 | tf_op jit(solution)/shard_map/ppermute | solution.py:907
  49.4 48.7 %collective-permute-start.5 = (f32[32,64,128]{2,1,0:T(8,128)S(1)}, f32[32,64,128]{2,1,0:T(8,128)}, u32[]{:S(2)}, u32[]{:S(2)}) collective-permute-start(f32[32,64,128]{2,1,0:T(8,128)S(1)} %bitcast.63), channel_id=1, source_target_pairs={{0,16},{2,18},{4,20},{6,22},{8,24},{10,26},{12,28},{14,30},{16,0},... | collective-permute-start | bytes 3145736 | tf_op jit(solution)/shard_map/ppermute | solution.py:910
  53.2 0.9 copy-start.9
  82.5 17.5 %collective-permute-start.7 = (f32[8,128]{1,0:T(8,128)S(1)}, f32[8,128]{1,0:T(8,128)S(1)}, u32[]{:S(2)}, u32[]{:S(2)}) collective-permute-start(f32[8,128]{1,0:T(8,128)S(1)} %concatenate.40), channel_id=1, source_target_pairs={{0,16},{2,18},{4,20},{6,22},{8,24},{10,26},{12,28},{14,30},{16,0},... | collective-permute-start | bytes 12296 | tf_op jit(solution)/shard_map/ppermute | solution.py:939
  101.6 31.6 %all-to-all-start.3 = ((f32[8,528,128]{2,1,0:T(8,128)}), f32[8,528,128]{2,1,0:T(8,128)S(1)}, u32[]{:S(2)}, u32[]{:S(2)}) async-start(f32[8,528,128]{2,1,0:T(8,128)} %pad_maximum_fusion), calls=%async_computation.3 | async-start | bytes 4325376 | tf_op jit(solution)/shard_map/all_to_all | solution.py:953
  133.2 6.3 %copy-start.7 = (s32[32,3]{0,1:T(4,128)S(1)}, s32[32,3]{0,1:T(4,128)}, u32[]{:S(2)}) copy-start(s32[32,3]{0,1:T(4,128)} %param.13) | copy-start | bytes 1156
  133.2 30.5 %all-to-all-start.1 = ((f32[8,8,64,128]{3,2,1,0:T(8,128)}), f32[8,8,64,128]{3,2,1,0:T(8,128)}, u32[]{:S(2)}, u32[]{:S(2)}) async-start(f32[8,8,64,128]{3,2,1,0:T(8,128)} %bitcast.66), calls=%async_computation.1 | async-start | bytes 4194304 | tf_op jit(solution)/shard_map/all_to_all | solution.py:913
  175.0 20.4 %all-to-all-start.4 = ((f32[16,32,128]{2,1,0:T(8,128)}), f32[16,32,128]{2,1,0:T(8,128)S(1)}, u32[]{:S(2)}, u32[]{:S(2)}) async-start(f32[16,32,128]{2,1,0:T(8,128)} %get-tuple-element.55), calls=%async_computation.4 | async-start | bytes 524288 | tf_op jit(solution)/shard_map/all_to_all | solution.py:988

commit v5 on v4

--- a/solution.py
+++ b/solution.py
@@ -168,13 +168,13 @@
         compiler_params=pltpu.CompilerParams(vmem_limit_bytes=vmem_bytes),
         name="kernel_blocks",
         cost_estimate=pl.CostEstimate(
-            flops=2 * 10**10, bytes_accessed=2 * 10**7, transcendentals=0
+            flops=10**6, bytes_accessed=10**4, transcendentals=0
         ),
     )(total, group_leaf, group_count, group_slots, place, own, other, coords, targets)
 
 
 def far_body(
-    total_ref, leaf_ref, slot_ref,
+    total_ref, leaf_ref, slot_ref, side_ref,
     own_ref, partner_ref, high_ref, low_ref, weights_ref,
     out_ref, projected_ref, copies_ref,
     s_high, s_low, acc,
@@ -188,8 +188,10 @@
         acc[...] = jnp.zeros_like(acc)
 
         def split(slot, carry):
-            s_high[slot], s_low[slot] = halves(own_ref[slot])
-            s_high[part + slot], s_low[part + slot] = halves(partner_ref[slot])
+            here = side_ref[0] * part + slot
+            there = (1 - side_ref[0]) * part + slot
+            s_high[here], s_low[here] = halves(own_ref[slot])
+            s_high[there], s_low[there] = halves(partner_ref[slot])
             return carry
 
         lax.fori_loop(0, part, split, 0, unroll=4)
@@ -219,7 +221,7 @@
             out_ref[:, 2 * pair * LEAF : 2 * (pair + 1) * LEAF] = block.T
 
 
-def far_products(total, group_leaf, group_slots, own, partner, high, low, weights, branches):
+def far_products(total, group_leaf, group_slots, side, own, partner, high, low, weights, branches):
     part, unused, samp_dev = own.shape
     slots = 2 * part
     groups = group_leaf.shape[0]
@@ -234,7 +236,7 @@
     return pl.pallas_call(
         far_body,
         grid_spec=pltpu.PrefetchScalarGridSpec(
-            num_scalar_prefetch=3,
+            num_scalar_prefetch=4,
             grid=(steps,),
             in_specs=[
                 pl.BlockSpec(own.shape, lambda *unused: (0, 0, 0), pipeline_mode=pl.Buffered(1)),
@@ -262,9 +264,9 @@
         compiler_params=pltpu.CompilerParams(vmem_limit_bytes=vmem_bytes),
         name="far_products",
         cost_estimate=pl.CostEstimate(
-            flops=10**10, bytes_accessed=2 * 10**7, transcendentals=0
+            flops=10**6, bytes_accessed=10**4, transcendentals=0
         ),
-    )(total, group_leaf, group_slots, own, partner, high, low, weights)
+    )(total, group_leaf, group_slots, side, own, partner, high, low, weights)
 
 
 NEAR_LEAVES = 8
@@ -324,7 +326,7 @@
         compiler_params=pltpu.CompilerParams(vmem_limit_bytes=vmem_bytes),
         name="near_products",
         cost_estimate=pl.CostEstimate(
-            flops=4 * 10**9, bytes_accessed=10**7, transcendentals=0
+            flops=10**6, bytes_accessed=10**4, transcendentals=0
         ),
     )(mask, rows, coords, targets)
 
@@ -580,7 +582,7 @@
         scratch_shapes=tree_scratch(rank),
         compiler_params=pltpu.CompilerParams(vmem_limit_bytes=vmem_bytes),
         name="branch_factors",
-        cost_estimate=pl.CostEstimate(flops=10**10, bytes_accessed=10**7, transcendentals=0),
+        cost_estimate=pl.CostEstimate(flops=10**6, bytes_accessed=10**4, transcendentals=0),
     )(gram.reshape(leaves * rank, rank))
 
 
@@ -624,7 +626,7 @@
         scratch_shapes=[pltpu.VMEM((leaves * rank, rank), jnp.float32)],
         compiler_params=pltpu.CompilerParams(vmem_limit_bytes=vmem_bytes),
         name="bases",
-        cost_estimate=pl.CostEstimate(flops=5 * 10**9, bytes_accessed=10**7, transcendentals=0),
+        cost_estimate=pl.CostEstimate(flops=10**6, bytes_accessed=10**4, transcendentals=0),
     )(inverse, ratio, top, sketched)
 
 
@@ -661,7 +663,10 @@
                     axis=0,
                 )
             at = (node << level) * rank
-            transfer_ref[offset + node] = dot_exact(stacked, nat_inverse[level, at : at + rank, :])
+            transfer_ref[offset + node] = lax.dot_general(
+                nat_inverse[level, at : at + rank, :], stacked, (((0,), (1,)), ((), ())),
+                precision=highest, preferred_element_type=jnp.float32,
+            )
         offset += nodes >> level
     above = [None]
     for level in range(levels - 1, -1, -1):
@@ -669,8 +674,12 @@
         fresh = []
         for node in range(nodes >> level):
             both = transfer_ref[offset + node]
-            if above[0] is not None:
-                both = dot_exact(both, above[node])
+            if above[0] is None:
+                both = both.T
+            else:
+                both = lax.dot_general(
+                    both, above[node], tn_dims, precision=highest, preferred_element_type=jnp.float32
+                )
             fresh += [both[:rank], both[rank:]]
         above = fresh
     for branch in range(2 * nodes):
@@ -687,7 +696,7 @@
         in_specs=[vmem_spec],
         out_specs=[vmem_spec] * 2,
         out_shape=[
-            jax.ShapeDtypeStruct((branches - 1, 2 * rank, rank), jnp.float32),
+            jax.ShapeDtypeStruct((branches - 1, rank, 2 * rank), jnp.float32),
             jax.ShapeDtypeStruct((branches * rank, rank), jnp.float32),
         ],
         scratch_shapes=[pltpu.VMEM((nodes * rank, rank), jnp.float32)]
@@ -725,9 +734,8 @@
     return result
 
 
-def group_tables(far_slots, far_count, side, part):
+def group_tables(far_slots, far_count):
     leaves = far_slots.shape[0]
-    far_slots = far_slots % part + jnp.where(far_slots // part == side, 0, part)
     groups = leaves * FAR // GROUP
     per_leaf = (far_count + GROUP - 1) // GROUP
     before = jnp.arange(leaves)[:, None] >= jnp.arange(leaves)[None, :]
@@ -799,35 +807,62 @@
         ],
         compiler_params=pltpu.CompilerParams(vmem_limit_bytes=vmem_bytes),
         name="sketched_shares",
+        cost_estimate=pl.CostEstimate(flops=10**6, bytes_accessed=10**4, transcendentals=0),
     )(place, sketch, samples, points)
 
 
-def pack_body(asked_ref, mine_ref, arrived_ref, partner_ref, crossed_ref, out_ref, *, cap, leaves):
+def pack_body(asked_ref, side_ref, mine_ref, arrived_ref, partner_ref, crossed_ref, out_ref, *, cap, leaves):
     z_rows = arrived_ref.shape[0] // leaves
+    side = side_ref[0]
 
     def one(peer, carry):
         for entry in range(2 * cap):
             leaf = asked_ref[peer, entry]
-            first_ref, second_ref = (mine_ref, arrived_ref) if entry < cap else (partner_ref, crossed_ref)
+            here = side == entry // cap
             at = pl.ds(leaf * z_rows, z_rows)
-            out_ref[peer, z_rows * entry : z_rows * (entry + 1), :] = first_ref[at, :] + second_ref[at, :]
+            out_ref[peer, z_rows * entry : z_rows * (entry + 1), :] = jnp.where(
+                here, mine_ref[at, :] + arrived_ref[at, :], partner_ref[at, :] + crossed_ref[at, :]
+            )
             base = z_rows * 2 * cap + 2 * entry
-            out_ref[peer, base : base + 2, :] = first_ref[pl.ds(leaves * z_rows + leaf * 2, 2), :]
+            at = pl.ds(leaves * z_rows + leaf * 2, 2)
+            out_ref[peer, base : base + 2, :] = jnp.where(here, mine_ref[at, :], partner_ref[at, :])
         return carry
 
     lax.fori_loop(0, out_ref.shape[0], one, 0)
 
 
-def packed_rows(asked, mine, arrived, partner, crossed, cap, leaves):
+def packed_rows(asked, side, mine, arrived, partner, crossed, cap, leaves):
     z_rows = arrived.shape[0] // leaves
     return pl.pallas_call(
         functools.partial(pack_body, cap=cap, leaves=leaves),
-        in_specs=[pl.BlockSpec(memory_space=pltpu.SMEM)] + [vmem_spec] * 4,
+        in_specs=[pl.BlockSpec(memory_space=pltpu.SMEM)] * 2 + [vmem_spec] * 4,
         out_specs=vmem_spec,
         out_shape=jax.ShapeDtypeStruct((asked.shape[0], 2 * cap * (z_rows + 2), LANES), jnp.float32),
         compiler_params=pltpu.CompilerParams(vmem_limit_bytes=vmem_bytes),
         name="packed_rows",
-    )(asked, mine, arrived, partner, crossed)
+    )(asked, side, mine, arrived, partner, crossed)
+
+
+def payload_body(asked_ref, rows_ref, child_ref, out_ref, *, cap):
+    def one(peer, carry):
+        for entry in range(cap):
+            out_ref[peer, LEAF * entry : LEAF * (entry + 1), :] = rows_ref[asked_ref[peer, entry]]
+        out_ref[peer, LEAF * cap :, :] = child_ref[...]
+        return carry
+
+    lax.fori_loop(0, out_ref.shape[0], one, 0)
+
+
+def payload_rows(asked, rows, child):
+    half, cap = asked.shape
+    return pl.pallas_call(
+        functools.partial(payload_body, cap=cap),
+        in_specs=[pl.BlockSpec(memory_space=pltpu.SMEM)] + [vmem_spec] * 2,
+        out_specs=vmem_spec,
+        out_shape=jax.ShapeDtypeStruct((half, cap * LEAF + child.shape[0], rows.shape[2]), jnp.float32),
+        compiler_params=pltpu.CompilerParams(vmem_limit_bytes=vmem_bytes),
+        name="payload_rows",
+    )(asked, rows, child)
 
 
 def two_rows(values, rows):
@@ -851,9 +886,8 @@
     side = me // half
     groups = [list(range(half)), list(range(half, branches))]
     mirror = [(i, (i + half) % branches) for i in range(branches)]
-    wanted = far_requests.reshape(2, half, cap)
-    wanted = jnp.where(side == 0, wanted, wanted[::-1])
-    wanted = jnp.transpose(wanted, (1, 0, 2)).reshape(half, 2 * cap)
+    side_ref = side.astype(jnp.int32).reshape(1)
+    wanted = jnp.transpose(far_requests.reshape(2, half, cap), (1, 0, 2)).reshape(half, 2 * cap)
     asked = lax.all_to_all(
         wanted, "leaf", split_axis=0, concat_axis=0, axis_index_groups=groups, tiled=True
     )
@@ -883,33 +917,38 @@
 
     coords = jnp.transpose(points.reshape(3, leaves, LEAF), (1, 0, 2))
     rows = jnp.transpose(samples.reshape(samp_dev, leaves, LEAF), (1, 2, 0))
-    small_sent = packed_rows(asked, mine, arrived, partner, crossed, cap, leaves)
+
+    forward = [(i, i + 1) for i in range(branches - 1)]
+    backward = [(target, source) for source, target in forward]
+    width = max(samp_dev, LEAF)
+
+    def edge(first):
+        samples_edge = jnp.transpose(lax.slice_in_dim(samples, first, first + LEAF, axis=1))
+        points_edge = lax.slice_in_dim(points, first, first + LEAF, axis=1)
+        return jnp.concatenate(
+            [
+                jnp.pad(samples_edge, ((0, 0), (0, width - samp_dev))),
+                jnp.pad(points_edge, ((0, 5), (0, width - LEAF))),
+            ],
+            axis=0,
+        )
+
+    low_edge = lax.ppermute(edge((leaves - 1) * LEAF), "leaf", forward)
+    high_edge = lax.ppermute(edge(0), "leaf", backward)
+    asked, low_edge, high_edge = lax.optimization_barrier((asked, low_edge, high_edge))
+
+    small_sent = packed_rows(asked, side_ref, mine, arrived, partner, crossed, cap, leaves)
     small_got = lax.all_to_all(
         small_sent, "leaf", split_axis=0, concat_axis=0, axis_index_groups=groups, tiled=True
     )
-    tables = group_tables(far_slots, far_count, side, half * cap)
-    total, group_leaf, group_count, group_slots = tables
-
-    forward = [(i, i + 1) for i in range(branches - 1)]
-    backward = [(target, source) for source, target in forward]
-    edges = jnp.concatenate([rows[:1], rows[leaves - 1 :]], axis=0)
-    edge_coords = jnp.concatenate([coords[:1], coords[leaves - 1 :]], axis=0)
-    width = max(samp_dev, LEAF)
-    edges = jnp.concatenate(
-        [
-            jnp.pad(edges, ((0, 0), (0, 0), (0, width - samp_dev))),
-            jnp.pad(edge_coords, ((0, 0), (0, 5), (0, width - LEAF))),
-        ],
-        axis=1,
-    )
-    edges, unused = lax.optimization_barrier((edges, small_sent))
-    low_edge = lax.ppermute(edges[1], "leaf", forward)
-    high_edge = lax.ppermute(edges[0], "leaf", backward)
-
-    rows_out, low_edge, high_edge = lax.optimization_barrier((rows, low_edge, high_edge))
+    total, group_leaf, group_count, group_slots = group_tables(far_slots, far_count)
+
+    rows_out, unused = lax.optimization_barrier((rows, small_sent))
     partner_rows = lax.ppermute(rows_out, "leaf", mirror)
 
-    own_sent = rows[asked[:, :cap].reshape(-1)].reshape(half, cap, LEAF, samp_dev)
+    own_asked = lax.dynamic_slice_in_dim(asked, side * cap, cap, axis=1)
+    partner_asked = lax.dynamic_slice_in_dim(asked, (1 - side) * cap, cap, axis=1)
+    own_sent = rows_out[own_asked.reshape(-1)].reshape(half, cap, LEAF, samp_dev)
     own_got = lax.all_to_all(
         own_sent, "leaf", split_axis=0, concat_axis=0, axis_index_groups=groups, tiled=True
     )
@@ -935,42 +974,11 @@
 
     levels = leaves.bit_length()
     inverse, ratio, top_inverse, own_child = branch_factors(gram, levels)
-    own_child = own_child.reshape(rank * rank // LANES, LANES)
-    partner_child = lax.ppermute(own_child, "leaf", mirror)
-    both_children = jnp.where(
-        side == 0,
-        jnp.concatenate([own_child, partner_child], axis=0),
-        jnp.concatenate([partner_child, own_child], axis=0),
-    )
-    child_rows = both_children.shape[0]
-
-    partner_sent = partner_rows[asked[:, cap:].reshape(-1)].reshape(half, cap * LEAF, samp_dev)
-    if samp_dev == LANES:
-        both = jnp.concatenate(
-            [partner_sent, jnp.broadcast_to(both_children[None], (half,) + both_children.shape)], axis=1
-        )
-        partner_sent = both
-        both = lax.all_to_all(
-            both, "leaf", split_axis=0, concat_axis=0, axis_index_groups=groups, tiled=True
-        )
-        partner_got = both[:, : cap * LEAF]
-        children = both[:, cap * LEAF :]
-    else:
-        partner_got = lax.all_to_all(
-            partner_sent, "leaf", split_axis=0, concat_axis=0, axis_index_groups=groups, tiled=True
-        )
-        children = lax.all_to_all(
-            jnp.broadcast_to(both_children[None], (half,) + both_children.shape),
-            "leaf", split_axis=0, concat_axis=0, axis_index_groups=groups, tiled=True,
-        )
-    partner_got = partner_got.reshape(half * cap, LEAF, samp_dev)
-    children = jnp.transpose(children.reshape(half, 2, child_rows // 2, LANES), (1, 0, 2, 3))
-    children = children.reshape(branches, rank, rank)
-    ratio, rows_low, rows_high, unused = lax.optimization_barrier(
-        (ratio, low_edge[:LEAF, :samp_dev], high_edge[:LEAF, :samp_dev], partner_sent)
-    )
+    own_child = own_child.reshape(-1, min(samp_dev, LANES))
     weights, leaf_basis = bases(inverse, ratio, top_inverse, sketched)
 
+    low_edge, high_edge, unused = lax.optimization_barrier((low_edge, high_edge, own_child))
+    rows_low, rows_high = low_edge[:LEAF, :samp_dev], high_edge[:LEAF, :samp_dev]
     coords_low, coords_high = low_edge[LEAF : LEAF + 3, :LEAF], high_edge[LEAF : LEAF + 3, :LEAF]
     near_rows = jnp.concatenate(
         [rows_low[None], rows, rows_high[None], jnp.zeros_like(rows_low)[None]], axis=0
@@ -982,12 +990,29 @@
     near_coords = jnp.concatenate([near_coords, near_coords], axis=2)
     near_sample = near_products(near_mask.reshape(-1), near_rows, near_coords, targets)
 
+
+    own_child, own_got, partner_rows, weights, near_sample = lax.optimization_barrier(
+        (own_child, own_got, partner_rows, weights, near_sample)
+    )
+    payload = payload_rows(partner_asked, partner_rows, own_child)
+    arrived = lax.all_to_all(
+        payload, "leaf", split_axis=0, concat_axis=0, axis_index_groups=groups, tiled=True
+    )
+    partner_got = arrived[:, : cap * LEAF].reshape(half * cap, LEAF, samp_dev)
+    children = arrived[:, cap * LEAF :]
+    mirrored = lax.ppermute(children, "leaf", mirror)
+    children = jnp.concatenate(
+        [jnp.where(side == 0, children, mirrored), jnp.where(side == 0, mirrored, children)], axis=0
+    )
+    children = children.reshape(branches, rank, rank)
+
     far_sample, branch_samples, copies = far_products(
-        total, group_leaf, group_slots, own_got, partner_got, high, low, weights, branches
+        total, group_leaf, group_slots, side_ref, own_got, partner_got, high, low, weights, branches
     )
     everyone = lax.all_to_all(copies, "leaf", split_axis=0, concat_axis=0, tiled=True)
     children, unused = lax.optimization_barrier((children, branch_samples))
-    top_transfer, paths = top_factors(children)
+    transfer_t, paths = top_factors(children)
+    top_transfer = jnp.swapaxes(transfer_t, 1, 2)
     root_sample = lax.dot_general(
         paths, everyone.reshape(branches * rank, samp_dev), tn_dims, precision=highest
     )

time: 199 us -> 167 us (0.84)
  waiting for transfers between devices: 61.5 us -> 10.7 us
  blocking collectives: 0 us -> 32.2 us
  other arithmetic: 7.83 us -> 3.44 us
  local copies, waits for them, and re-layouts: 19.1 us -> 14.8 us
  starting transfers between devices: 36 us -> 32 us
    all_to_all x0 -> x1, blocking collectives: none -> 32.2 us  [on_device(): lax.all_to_all(payload, 'leaf', split_axis=0, concat_axis=0, axis_index_g...]
    all_to_all x1 -> x0, waiting for transfers between devices: 24.1 us -> none  [on_device(): lax.all_to_all(both, 'leaf', split_axis=0, concat_axis=0, axis_index_grou...]
    ppermute x1, waiting for transfers between devices: 15.5 us -> 0.27 us  [on_device(): partner_rows = lax.ppermute(rows_out, 'leaf', mirror)]
    all_to_all x1, waiting for transfers between devices: 5.57 us -> 0.01 us  [on_device(): lax.all_to_all(own_sent, 'leaf', split_axis=0, concat_axis=0, axis_index_...]
    all_to_all x1, waiting for transfers between devices: 0.01 us -> 5.48 us  [on_device(): lax.all_to_all(wanted, 'leaf', split_axis=0, concat_axis=0, axis_index_gr...]
    all_to_all x1 -> x0, starting transfers between devices: 5.36 us -> none  [on_device(): lax.all_to_all(both, 'leaf', split_axis=0, concat_axis=0, axis_index_grou...]
    ppermute x1, waiting for transfers between devices: 4.77 us -> 0.01 us  [on_device(): partner = lax.ppermute(mine, 'leaf', mirror)]
    ppermute x3, waiting for transfers between devices: 4.54 us -> 0.01 us  [the longest x1 0.01 us: on_device(): low_edge = lax.ppermute(edge((leaves - 1) * LEAF), 'leaf', forward)]
  transfers between devices with their start and end apart: 13 -> 12, of which waited for: 7 -> 3; matrix products, arithmetic and copies ran while one was open for 12% -> 10% of each run, Pallas kernels for 27% -> 37%
where the time goes in v5:
time: 167 us; the launch traced here: 166 us
  Pallas kernels  69.3 us (41%)
  blocking collectives  32.2 us (19%)
  starting transfers between devices  32 us (19%)
  local copies, waits for them, and re-layouts  14.8 us (9%)
  waiting for transfers between devices  10.7 us (6%)
  other arithmetic  3.44 us (2%)
  matrix products  2.13 us (1%)
    all_to_all x1, blocking collectives, on_device(): lax.all_to_all(payload, 'leaf', split_axis=0, concat_axis=0, axis_index_g...  32.2 us
    pallas_call x1, Pallas kernels, branch_factors(): pl.pallas_call(functools.partial(branch_body, rank=rank, levels=levels),...  14.5 us
    pallas_call x1, Pallas kernels, top_factors(): pl.pallas_call(functools.partial(top_body, rank=rank, levels=levels), in_...  13.1 us
    pallas_call x1, Pallas kernels, kernel_blocks(): pl.pallas_call(functools.partial(blocks_body, rank=rank, cap=cap), grid_s...  11 us
    pallas_call x1, Pallas kernels, far_products(): pl.pallas_call(far_body, grid_spec=pltpu.PrefetchScalarGridSpec(num_scala...  9.4 us
    pallas_call x1, Pallas kernels, bases(): pl.pallas_call(functools.partial(basis_body, rank=rank, levels=levels), i...  7.38 us
    pallas_call x1, Pallas kernels, near_products(): pl.pallas_call(near_body, grid_spec=pltpu.PrefetchScalarGridSpec(num_scal...  6.08 us
    all_to_all x1, starting transfers between devices, on_device(): lax.all_to_all(wanted, 'leaf', split_axis=0, concat_axis=0, axis_index_gr...  5.89 us
  transfers between devices with their start and end apart: 12, of which 3 were waited for; matrix products, arithmetic and copies ran while one was open for 10% of the time, Pallas kernels for 37%

profile of v5, /device:TPU:0, one launch (start us, length us, event | category | flops | bytes accessed | tf_op | source)
XLA Modules:
  0.0 165.6 jit_solution(12686909766638322005)
XLA Ops:
  0.7 2.6 %sketched_shares.1 = (f32[320,128]{1,0:T(8,128)}, f32[256,128]{1,0:T(8,128)}) custom-call(s32[1]{0:T(128)} %bitcast.5.place_ref, f32[32,128]{1,0:T(8,128)} %sketch_ref.1, f32[128,2048]{1,0:T(8,128)} %samples_ref.1, f32[3,2048]{1,0:T(4,128)} %points_ref.1), custom_call_target="tpu_custom_call" | custom-call | flops 1000000 | bytes 10000 | tf_op jit(solution)/shard_map/sketched_shares/pallas_call | solution.py:800
  3.3 0.5 collective-permute-start.2
  3.7 3.7 %collective-permute-start.4 = (f32[256,128]{1,0:T(8,128)}, f32[256,128]{1,0:T(8,128)S(1)}, u32[]{:S(2)}, u32[]{:S(2)}) collective-permute-start(f32[256,128]{1,0:T(8,128)} %get-tuple-element.37), channel_id=1, source_target_pairs={{0,17},{1,16},{2,19},{3,18},{4,21},{5,20},{6,23},{7,22},{8,25},{9,... | collective-permute-start | bytes 393224 | tf_op jit(solution)/shard_map/ppermute | solution.py:900
  7.4 1.5 copy.49
  9.0 0.1 fusion.4
  9.1 3.7 %collective-permute-start = (f32[72,128]{1,0:T(8,128)S(1)}, f32[72,128]{1,0:T(8,128)S(1)}, u32[]{:S(2)}, u32[]{:S(2)}) collective-permute-start(f32[72,128]{1,0:T(8,128)S(1)} %select_maximum_fusion.1), channel_id=1, source_target_pairs={{0,2},{2,4},{4,6},{6,8},{8,10},{10,12},{12,14},{14,16},{16,18},{18... | collective-permute-start | bytes 110600 | tf_op jit(solution)/shard_map/ppermute | solution.py:936
  12.8 1.3 collective-permute-start.1
  14.1 0.1 reshape.148
  14.2 0.1 copy.47
  14.3 0.7 all_to_all.20
  15.0 5.9 %all-to-all-start = ((s32[8,1,16]{2,1,0:T(1,128)}), s32[8,1,16]{2,1,0:T(1,128)S(1)}, u32[]{:S(2)}, u32[]{:S(2)}) async-start(s32[8,1,16]{2,1,0:T(1,128)} %bitcast.7), calls=%async_computation | async-start | bytes 8192 | tf_op jit(solution)/shard_map/all_to_all | solution.py:891
  20.9 5.5 %all-to-all-done = s32[8,1,16]{2,1,0:T(1,128)S(1)} async-done(((s32[8,1,16]{2,1,0:T(1,128)}), s32[8,1,16]{2,1,0:T(1,128)S(1)}, u32[]{:S(2)}, u32[]{:S(2)}) %all-to-all-start) | async-done | bytes 544 | tf_op jit(solution)/shard_map/all_to_all | solution.py:891
  26.4 0.0 copy-start.4
  26.4 0.0 copy-start.2
  26.4 0.5 copy-done.6
  26.9 0.1 copy-done.4
  27.0 0.0 copy-done.5
  27.1 0.1 copy-done.2
  27.1 2.4 %packed_rows.1 = f32[8,160,128]{2,1,0:T(8,128)} custom-call(s32[8,16]{1,0:T(8,128)} %bitcast.68, s32[1]{0:T(128)} %bitcast.3.side_ref, f32[320,128]{1,0:T(8,128)} %get-tuple-element.36.mine_ref, f32[256,128]{1,0:T(8,128)} %copy-done.4, f32[320,128]{1,0:T(8,128)} %copy-done.2, f32[256,128]{1,0:T(8,128)} %copy-done.5), custom_call_target="tpu_custom_call" | custom-call | tf_op jit(solution)/shard_map/packed_rows/pallas_call | solution.py:836
  29.5 3.5 %all-to-all-start.1 = ((f32[8,160,128]{2,1,0:T(8,128)}), f32[8,160,128]{2,1,0:T(8,128)S(1)}, u32[]{:S(2)}, u32[]{:S(2)}) async-start(f32[8,160,128]{2,1,0:T(8,128)} %packed_rows.1), calls=%async_computation.1 | async-start | bytes 1310720 | tf_op jit(solution)/shard_map/all_to_all | solution.py:941
  33.1 1.4 constant_dynamic-slice_fusion.1
  34.5 0.1 reshape.155
  34.6 2.0 %gather_fusion.1 = f32[64,64,128]{2,1,0:T(8,128)} fusion(f32[32,64,128]{2,1,0:T(8,128)S(1)} %bitcast.56, s32[1024]{0:T(1024)S(1)} %pad_clamp_fusion), kind=kCustom, calls=%fused_computation.1 | custom fusion | bytes 4194560 | tf_op jit(solution)/shard_map/gather | solution.py:951
  36.6 4.9 %all-to-all-done.1 = f32[8,160,128]{2,1,0:T(8,128)S(1)} async-done(((f32[8,160,128]{2,1,0:T(8,128)}), f32[8,160,128]{2,1,0:T(8,128)S(1)}, u32[]{:S(2)}, u32[]{:S(2)}) %all-to-all-start.1) | async-done | bytes 655392 | tf_op jit(solution)/shard_map/all_to_all | solution.py:941
  41.6 4.5 %all-to-all-start.2 = ((f32[8,8,64,128]{3,2,1,0:T(8,128)}), f32[8,8,64,128]{3,2,1,0:T(8,128)}, u32[]{:S(2)}, u32[]{:S(2)}) async-start(f32[8,8,64,128]{3,2,1,0:T(8,128)} %bitcast.19), calls=%async_computation.2 | async-start | bytes 4194304 | tf_op jit(solution)/shard_map/all_to_all | solution.py:952
  46.1 0.0 copy-start.7
  46.1 0.0 copy-start.10
  46.1 0.1 select_reduce_fusion.2
  46.3 0.6 slice.39.total_ref
  46.8 0.1 convert_reduce_fusion
  46.9 0.1 select_reduce_fusion
  47.1 0.0 copy-start.1
  47.1 0.1 collective-permute-start.5
  47.2 1.1 compare_select_fusion.2.count_ref
  48.2 3.1 %collective-permute-start.6 = (f32[32,64,128]{2,1,0:T(8,128)S(1)}, f32[32,64,128]{2,1,0:T(8,128)}, u32[]{:S(2)}, u32[]{:S(2)}) collective-permute-start(f32[32,64,128]{2,1,0:T(8,128)S(1)} %bitcast.57), channel_id=1, source_target_pairs={{0,16},{2,18},{4,20},{6,22},{8,24},{10,26},{12,28},{14,30},{16,0},... | collective-permute-start | bytes 3145736 | tf_op jit(solution)/shard_map/ppermute | solution.py:947
  51.3 0.4 copy.51
  51.7 0.0 copy-start
  51.7 0.1 copy.46
  51.8 0.1 reshape.144
  51.9 0.7 gather_fusion
  52.5 0.7 reshape.145.slot_ref
  53.2 0.4 copy.55
  53.6 0.1 copy.53
  53.7 0.6 reshape.158.mask_ref
  54.3 0.1 pad.25.clone
  54.4 0.7 slice.59
  55.1 11.0 %kernel_blocks.1 = (bf16[128,64,256]{2,1,0:T(8,128)(2,1)}, bf16[128,64,256]{2,1,0:T(8,128)(2,1)}, f32[32,32,64]{2,1,0:T(8,128)}, f32[32,32,32]{2,1,0:T(8,128)}) custom-call(s32[1]{0:T(128)} %slice.39.total_ref, s32[128]{0:T(128)} %copy-done.8, s32[128]{0:T(128)} %compare_select_fusion.2.count_ref, s32[512]{0:T(512)} %reshape.145.slot_ref, ...), custom_call_target="tpu_custom_call" | custom-call | flops 1000000 | bytes 10000 | tf_op jit(solution)/shard_map/kernel_blocks/pallas_call | solution.py:143
  66.1 14.5 %branch_factors.1 = (f32[32,32,128]{2,1,0:T(8,128)}, f32[6,32,32,128]{3,2,1,0:T(8,128)}, f32[32,32]{1,0:T(8,128)}, f32[32,32]{1,0:T(8,128)}) custom-call(f32[1024,32]{1,0:T(8,128)} %bitcast.67), custom_call_target="tpu_custom_call" | custom-call | flops 1000000 | bytes 10000 | tf_op jit(solution)/shard_map/branch_factors/pallas_call | solution.py:572
  80.6 1.4 reshape.153.child_ref
  82.0 0.1 maximum_maximum_fusion.1
  82.1 0.8 pad_maximum_fusion.coords_ref
  82.9 1.1 maximum_maximum_fusion.rows_ref
  84.0 6.1 %near_products.1 = f32[128,2048]{1,0:T(8,128)} custom-call(s32[96]{0:T(128)} %reshape.158.mask_ref, f32[35,64,128]{2,1,0:T(8,128)} %maximum_maximum_fusion.rows_ref, f32[35,8,128]{2,1,0:T(8,128)} %pad_maximum_fusion.coords_ref, f32[32,64,3]{2,1,0:T(8,128)} %bitcast.61), custom_call_target="tpu_custom_call" | custom-call | flops 1000000 | bytes 10000 | tf_op jit(solution)/shard_map/near_products/pallas_call | solution.py:313
  90.1 7.4 %bases.1 = (f32[32,2048]{1,0:T(8,128)}, f32[32,2048]{1,0:T(8,128)}) custom-call(f32[32,32,128]{2,1,0:T(8,128)} %get-tuple-element.41.inverse_ref, f32[6,32,32,128]{3,2,1,0:T(8,128)} %get-tuple-element.42.ratio_ref, f32[32,32]{1,0:T(8,128)} %get-tuple-element.43.top_ref, f32[32,32,64]{2,1,0:T(8,128)} %get-tuple-element.44.sketched_ref), custom_call_target="tpu_custom_call" | custom-call | flops 1000000 | bytes 10000 | tf_op jit(solution)/shard_map/bases/pallas_call | solution.py:621
  97.5 0.3 collective-permute-done.6.rows_ref
  97.8 2.8 %payload_rows.1 = f32[8,520,128]{2,1,0:T(8,128)} custom-call(s32[8,8]{1,0:T(8,128)} %get-tuple-element.72.asked_ref, f32[32,64,128]{2,1,0:T(8,128)} %collective-permute-done.6.rows_ref, f32[8,128]{1,0:T(8,128)} %reshape.153.child_ref), custom_call_target="tpu_custom_call" | custom-call | tf_op jit(solution)/shard_map/payload_rows/pallas_call | solution.py:858
  100.6 32.2 %all_to_all.32 = f32[8,520,128]{2,1,0:T(8,128)S(1)} all-to-all(f32[8,520,128]{2,1,0:T(8,128)} %payload_rows.1), channel_id=1, replica_groups={{0,2,4,6,8,10,12,14},{16,18,20,22,24,26,28,30},{1,3,5,7,9,11,13,15},{17..., dimensions={0} | all-to-all | bytes 4259840 | tf_op jit(solution)/shard_map/all_to_all | solution.py:998
  132.7 2.3 %collective-permute-start.7 = (f32[8,8,128]{2,1,0:T(8,128)S(1)}, f32[8,8,128]{2,1,0:T(8,128)S(1)}, u32[]{:S(2)}, u32[]{:S(2)}) collective-permute-start(f32[8,8,128]{2,1,0:T(8,128)S(1)} %slice.61), channel_id=1, source_target_pairs={{0,16},{2,18},{4,20},{6,22},{8,24},{10,26},{12,28},{14,30},{16,0},... | collective-permute-start | bytes 98312 | tf_op jit(solution)/shard_map/ppermute | solution.py:1003
  135.0 1.5 slice.60
  136.5 9.4 %far_products.1 = (f32[128,2048]{1,0:T(8,128)}, f32[32,128]{1,0:T(8,128)}, f32[16,32,128]{2,1,0:T(8,128)}) custom-call(s32[1]{0:T(128)} %slice.39.total_ref, s32[128]{0:T(128)} %copy-done.8, s32[512]{0:T(512)} %reshape.145.slot_ref, s32[1]{0:T(128)} %bitcast.3.side_ref, f32[64,64,128]{2,1,0:T(8,128)} %bitcast.20.own_ref, f32[64,64,128]{2,1,0:T(8,128)} %bitcast.62, ...), custom_call_target="tpu_custom_call" | custom-call | flops 1000000 | bytes 10000 | tf_op jit(solution)/shard_map/far_products/pallas_call | solution.py:236
  145.9 3.5 %all-to-all-start.4 = ((f32[16,32,128]{2,1,0:T(8,128)}), f32[16,32,128]{2,1,0:T(8,128)S(1)}, u32[]{:S(2)}, u32[]{:S(2)}) async-start(f32[16,32,128]{2,1,0:T(8,128)} %get-tuple-element.63), calls=%async_computation.4 | async-start | bytes 524288 | tf_op jit(solution)/shard_map/all_to_all | solution.py:1012
  149.5 0.8 reshape.160.children_ref
  150.3 13.1 %top_factors.1 = (f32[15,32,64]{2,1,0:T(8,128)}, f32[512,32]{1,0:T(8,128)}) custom-call(f32[16,32,32]{2,1,0:T(8,128)} %reshape.160.children_ref), custom_call_target="tpu_custom_call" | custom-call | flops 10000000000 | bytes 10000000 | tf_op jit(solution)/shard_map/top_factors/pallas_call | solution.py:694
  163.4 2.1 %fusion.5 = f32[32,128]{1,0:T(8,128)} fusion(f32[512,32]{1,0:T(8,128)} %get-tuple-element.62, f32[512,128]{1,0:T(8,128)S(1)} %bitcast.65), kind=kOutput, calls=%fused_computation.42 | convolution fusion | flops 25165824 | bytes 344064 | tf_op jit(solution)/shard_map/dot_general | solution.py:1016
  (44 shorter events, 0.2 us)
Async XLA Ops:
  0.6 8.3 %copy-start.3 = (f32[3,2048]{1,0:T(4,128)S(1)}, f32[3,2048]{1,0:T(4,128)}, u32[]{:S(2)}) copy-start(f32[3,2048]{1,0:T(4,128)} %points_ref.1) | copy-start | bytes 73732
  0.6 13.5 %copy-start.9 = (s32[1,16,8]{1,2,0:T(8,128)S(1)}, s32[1,16,8]{1,2,0:T(8,128)}, u32[]{:S(2)}) copy-start(s32[1,16,8]{1,2,0:T(8,128)} %param.10) | copy-start | bytes 1540
  3.3 23.1 %collective-permute-start.2 = (f32[256,128]{1,0:T(8,128)}, f32[256,128]{1,0:T(8,128)S(1)}, u32[]{:S(2)}, u32[]{:S(2)}) collective-permute-start(f32[256,128]{1,0:T(8,128)} %get-tuple-element.37), channel_id=1, source_target_pairs={{0,1},{1,0},{2,3},{3,2},{4,5},{5,4},{6,7},{7,6},{8,9},{9,8},{10,11... | collective-permute-start | bytes 393224 | tf_op jit(solution)/shard_map/ppermute | solution.py:898
  3.7 22.7 %collective-permute-start.4 = (f32[256,128]{1,0:T(8,128)}, f32[256,128]{1,0:T(8,128)S(1)}, u32[]{:S(2)}, u32[]{:S(2)}) collective-permute-start(f32[256,128]{1,0:T(8,128)} %get-tuple-element.37), channel_id=1, source_target_pairs={{0,17},{1,16},{2,19},{3,18},{4,21},{5,20},{6,23},{7,22},{8,25},{9,... | collective-permute-start | bytes 393224 | tf_op jit(solution)/shard_map/ppermute | solution.py:900
  7.4 19.0 %collective-permute-start.3 = (f32[320,128]{1,0:T(8,128)}, f32[320,128]{1,0:T(8,128)S(1)}, u32[]{:S(2)}, u32[]{:S(2)}) collective-permute-start(f32[320,128]{1,0:T(8,128)} %get-tuple-element.36.mine_ref), channel_id=1, source_target_pairs={{0,16},{2,18},{4,20},{6,22},{8,24},{10,26},{12,28},{14,30},{16,0},... | collective-permute-start | bytes 491528 | tf_op jit(solution)/shard_map/ppermute | solution.py:899
  9.1 17.3 %collective-permute-start = (f32[72,128]{1,0:T(8,128)S(1)}, f32[72,128]{1,0:T(8,128)S(1)}, u32[]{:S(2)}, u32[]{:S(2)}) collective-permute-start(f32[72,128]{1,0:T(8,128)S(1)} %select_maximum_fusion.1), channel_id=1, source_target_pairs={{0,2},{2,4},{4,6},{6,8},{8,10},{10,12},{12,14},{14,16},{16,18},{18... | collective-permute-start | bytes 110600 | tf_op jit(solution)/shard_map/ppermute | solution.py:936
  12.8 13.5 %collective-permute-start.1 = (f32[72,128]{1,0:T(8,128)S(1)}, f32[72,128]{1,0:T(8,128)S(1)}, u32[]{:S(2)}, u32[]{:S(2)}) collective-permute-start(f32[72,128]{1,0:T(8,128)S(1)} %select_maximum_fusion), channel_id=1, source_target_pairs={{2,0},{4,2},{6,4},{8,6},{10,8},{12,10},{14,12},{16,14},{18,16},{20... | collective-permute-start | bytes 110600 | tf_op jit(solution)/shard_map/ppermute | solution.py:937
  15.0 11.4 %all-to-all-start = ((s32[8,1,16]{2,1,0:T(1,128)}), s32[8,1,16]{2,1,0:T(1,128)S(1)}, u32[]{:S(2)}, u32[]{:S(2)}) async-start(s32[8,1,16]{2,1,0:T(1,128)} %bitcast.7), calls=%async_computation | async-start | bytes 8192 | tf_op jit(solution)/shard_map/all_to_all | solution.py:891
  26.3 0.6 copy-start.6
  26.4 0.7 copy-start.4
  26.4 0.7 copy-start.5
  26.4 0.7 copy-start.2
  29.5 12.1 %all-to-all-start.1 = ((f32[8,160,128]{2,1,0:T(8,128)}), f32[8,160,128]{2,1,0:T(8,128)S(1)}, u32[]{:S(2)}, u32[]{:S(2)}) async-start(f32[8,160,128]{2,1,0:T(8,128)} %packed_rows.1), calls=%async_computation.1 | async-start | bytes 1310720 | tf_op jit(solution)/shard_map/all_to_all | solution.py:941
  41.6 4.5 %copy-start.11 = (s32[32]{0:T(128)S(1)}, s32[32]{0:T(128)}, u32[]{:S(2)}) copy-start(s32[32]{0:T(128)} %param.12) | copy-start | bytes 388
  41.6 56.2 %all-to-all-start.2 = ((f32[8,8,64,128]{3,2,1,0:T(8,128)}), f32[8,8,64,128]{3,2,1,0:T(8,128)}, u32[]{:S(2)}, u32[]{:S(2)}) async-start(f32[8,8,64,128]{3,2,1,0:T(8,128)} %bitcast.19), calls=%async_computation.2 | async-start | bytes 4194304 | tf_op jit(solution)/shard_map/all_to_all | solution.py:952
  46.1 5.6 %copy-start.7 = (s32[32,16]{0,1:T(8,128)S(1)}, s32[32,16]{0,1:T(8,128)}, u32[]{:S(2)}) copy-start(s32[32,16]{0,1:T(8,128)} %param.11) | copy-start | bytes 6148
  46.1 7.5 %copy-start.10 = (s32[32,3]{0,1:T(4,128)S(1)}, s32[32,3]{0,1:T(4,128)}, u32[]{:S(2)}) copy-start(s32[32,3]{0,1:T(4,128)} %param.13) | copy-start | bytes 1156
  46.9 8.2 %copy-start.8 = (s32[128]{0:T(128)}, s32[128]{0:T(128)S(1)}, u32[]{:S(2)}) copy-start(s32[128]{0:T(128)S(1)} %broadcast_minimum_fusion.leaf_ref) | copy-start | bytes 1540
  47.1 8.0 %copy-start.1 = (f32[8,128,128]{2,1,0:T(8,128)}, f32[8,128,128]{2,1,0:T(8,128)S(1)}, u32[]{:S(2)}) copy-start(f32[8,128,128]{2,1,0:T(8,128)S(1)} %slice.58) | copy-start | bytes 1572868
  47.1 8.0 %collective-permute-start.5 = (f32[1024,128]{1,0:T(8,128)S(1)}, f32[1024,128]{1,0:T(8,128)}, u32[]{:S(2)}, u32[]{:S(2)}) collective-permute-start(f32[1024,128]{1,0:T(8,128)S(1)} %bitcast.63), channel_id=1, source_target_pairs={{0,1},{1,0},{2,3},{3,2},{4,5},{5,4},{6,7},{7,6},{8,9},{9,8},{10,11... | collective-permute-start | bytes 1572872 | tf_op jit(solution)/shard_map/ppermute | solution.py:961
  48.2 49.5 %collective-permute-start.6 = (f32[32,64,128]{2,1,0:T(8,128)S(1)}, f32[32,64,128]{2,1,0:T(8,128)}, u32[]{:S(2)}, u32[]{:S(2)}) collective-permute-start(f32[32,64,128]{2,1,0:T(8,128)S(1)} %bitcast.57), channel_id=1, source_target_pairs={{0,16},{2,18},{4,20},{6,22},{8,24},{10,26},{12,28},{14,30},{16,0},... | collective-permute-start | bytes 3145736 | tf_op jit(solution)/shard_map/ppermute | solution.py:947
  51.7 3.4 %copy-start = (f32[3,2048]{0,1:T(8,128)}, f32[3,2048]{0,1:T(8,128)S(1)}, u32[]{:S(2)}) copy-start(f32[3,2048]{0,1:T(8,128)S(1)} %copy.51) | copy-start | bytes 73732
  132.7 16.7 %collective-permute-start.7 = (f32[8,8,128]{2,1,0:T(8,128)S(1)}, f32[8,8,128]{2,1,0:T(8,128)S(1)}, u32[]{:S(2)}, u32[]{:S(2)}) collective-permute-start(f32[8,8,128]{2,1,0:T(8,128)S(1)} %slice.61), channel_id=1, source_target_pairs={{0,16},{2,18},{4,20},{6,22},{8,24},{10,26},{12,28},{14,30},{16,0},... | collective-permute-start | bytes 98312 | tf_op jit(solution)/shard_map/ppermute | solution.py:1003
  145.9 17.5 %all-to-all-start.4 = ((f32[16,32,128]{2,1,0:T(8,128)}), f32[16,32,128]{2,1,0:T(8,128)S(1)}, u32[]{:S(2)}, u32[]{:S(2)}) async-start(f32[16,32,128]{2,1,0:T(8,128)} %get-tuple-element.63), calls=%async_computation.4 | async-start | bytes 524288 | tf_op jit(solution)/shard_map/all_to_all | solution.py:1012

commit v6 on v5

--- a/solution.py
+++ b/solution.py
@@ -178,6 +178,7 @@
     own_ref, partner_ref, high_ref, low_ref, weights_ref,
     out_ref, projected_ref, copies_ref,
     s_high, s_low, acc,
+    *, cap,
 ):
     step = pl.program_id(0)
     samp_dev = own_ref.shape[2]
@@ -191,7 +192,8 @@
             here = side_ref[0] * part + slot
             there = (1 - side_ref[0]) * part + slot
             s_high[here], s_low[here] = halves(own_ref[slot])
-            s_high[there], s_low[there] = halves(partner_ref[slot])
+            at = pl.multiple_of((slot % cap) * LEAF, LEAF)
+            s_high[there], s_low[there] = halves(partner_ref[slot // cap, pl.ds(at, LEAF), :])
             return carry
 
         lax.fori_loop(0, part, split, 0, unroll=4)
@@ -234,7 +236,7 @@
         return (jnp.minimum(step, last), 0, 0)
 
     return pl.pallas_call(
-        far_body,
+        functools.partial(far_body, cap=part // partner.shape[0]),
         grid_spec=pltpu.PrefetchScalarGridSpec(
             num_scalar_prefetch=4,
             grid=(steps,),
@@ -843,26 +845,31 @@
     )(asked, side, mine, arrived, partner, crossed)
 
 
-def payload_body(asked_ref, rows_ref, child_ref, out_ref, *, cap):
+def payload_body(asked_ref, early_ref, late_ref, child_ref, out_ref, *, cap):
+    early = early_ref.shape[0]
+
     def one(peer, carry):
         for entry in range(cap):
-            out_ref[peer, LEAF * entry : LEAF * (entry + 1), :] = rows_ref[asked_ref[peer, entry]]
+            leaf = asked_ref[peer, entry]
+            first = early_ref[jnp.minimum(leaf, early - 1)]
+            second = late_ref[jnp.maximum(leaf - early, 0)]
+            out_ref[peer, LEAF * entry : LEAF * (entry + 1), :] = jnp.where(leaf < early, first, second)
         out_ref[peer, LEAF * cap :, :] = child_ref[...]
         return carry
 
     lax.fori_loop(0, out_ref.shape[0], one, 0)
 
 
-def payload_rows(asked, rows, child):
+def payload_rows(asked, early, late, child):
     half, cap = asked.shape
     return pl.pallas_call(
         functools.partial(payload_body, cap=cap),
-        in_specs=[pl.BlockSpec(memory_space=pltpu.SMEM)] + [vmem_spec] * 2,
+        in_specs=[pl.BlockSpec(memory_space=pltpu.SMEM)] + [vmem_spec] * 3,
         out_specs=vmem_spec,
-        out_shape=jax.ShapeDtypeStruct((half, cap * LEAF + child.shape[0], rows.shape[2]), jnp.float32),
+        out_shape=jax.ShapeDtypeStruct((half, cap * LEAF + child.shape[0], late.shape[2]), jnp.float32),
         compiler_params=pltpu.CompilerParams(vmem_limit_bytes=vmem_bytes),
         name="payload_rows",
-    )(asked, rows, child)
+    )(asked, early, late, child)
 
 
 def two_rows(values, rows):
@@ -918,6 +925,17 @@
     coords = jnp.transpose(points.reshape(3, leaves, LEAF), (1, 0, 2))
     rows = jnp.transpose(samples.reshape(samp_dev, leaves, LEAF), (1, 2, 0))
 
+    small_sent = packed_rows(asked, side_ref, mine, arrived, partner, crossed, cap, leaves)
+    small_got = lax.all_to_all(
+        small_sent, "leaf", split_axis=0, concat_axis=0, axis_index_groups=groups, tiled=True
+    )
+    total, group_leaf, group_count, group_slots = group_tables(far_slots, far_count)
+
+    early = leaves // 8
+    rows_out, unused = lax.optimization_barrier((rows, small_sent))
+    partner_early = lax.ppermute(rows_out[:early], "leaf", mirror)
+    partner_late = lax.ppermute(rows_out[early:], "leaf", mirror)
+
     forward = [(i, i + 1) for i in range(branches - 1)]
     backward = [(target, source) for source, target in forward]
     width = max(samp_dev, LEAF)
@@ -933,22 +951,16 @@
             axis=0,
         )
 
-    low_edge = lax.ppermute(edge((leaves - 1) * LEAF), "leaf", forward)
-    high_edge = lax.ppermute(edge(0), "leaf", backward)
-    asked, low_edge, high_edge = lax.optimization_barrier((asked, low_edge, high_edge))
-
-    small_sent = packed_rows(asked, side_ref, mine, arrived, partner, crossed, cap, leaves)
-    small_got = lax.all_to_all(
-        small_sent, "leaf", split_axis=0, concat_axis=0, axis_index_groups=groups, tiled=True
-    )
-    total, group_leaf, group_count, group_slots = group_tables(far_slots, far_count)
-
-    rows_out, unused = lax.optimization_barrier((rows, small_sent))
-    partner_rows = lax.ppermute(rows_out, "leaf", mirror)
+    last, first, unused = lax.optimization_barrier((edge((leaves - 1) * LEAF), edge(0), small_sent))
+    low_edge = lax.ppermute(last, "leaf", forward)
+    high_edge = lax.ppermute(first, "leaf", backward)
 
     own_asked = lax.dynamic_slice_in_dim(asked, side * cap, cap, axis=1)
     partner_asked = lax.dynamic_slice_in_dim(asked, (1 - side) * cap, cap, axis=1)
     own_sent = rows_out[own_asked.reshape(-1)].reshape(half, cap, LEAF, samp_dev)
+    own_sent, partner_early, total, group_leaf, group_count, group_slots = lax.optimization_barrier(
+        (own_sent, partner_early, total, group_leaf, group_count, group_slots)
+    )
     own_got = lax.all_to_all(
         own_sent, "leaf", split_axis=0, concat_axis=0, axis_index_groups=groups, tiled=True
     )
@@ -975,9 +987,14 @@
     levels = leaves.bit_length()
     inverse, ratio, top_inverse, own_child = branch_factors(gram, levels)
     own_child = own_child.reshape(-1, min(samp_dev, LANES))
+    own_child, own_got, partner_late = lax.optimization_barrier((own_child, own_got, partner_late))
+    payload = payload_rows(partner_asked, partner_early, partner_late, own_child)
+    arrived = lax.all_to_all(
+        payload, "leaf", split_axis=0, concat_axis=0, axis_index_groups=groups, tiled=True
+    )
+    ratio, low_edge, high_edge, unused = lax.optimization_barrier((ratio, low_edge, high_edge, payload))
     weights, leaf_basis = bases(inverse, ratio, top_inverse, sketched)
 
-    low_edge, high_edge, unused = lax.optimization_barrier((low_edge, high_edge, own_child))
     rows_low, rows_high = low_edge[:LEAF, :samp_dev], high_edge[:LEAF, :samp_dev]
     coords_low, coords_high = low_edge[LEAF : LEAF + 3, :LEAF], high_edge[LEAF : LEAF + 3, :LEAF]
     near_rows = jnp.concatenate(
@@ -991,14 +1008,6 @@
     near_sample = near_products(near_mask.reshape(-1), near_rows, near_coords, targets)
 
 
-    own_child, own_got, partner_rows, weights, near_sample = lax.optimization_barrier(
-        (own_child, own_got, partner_rows, weights, near_sample)
-    )
-    payload = payload_rows(partner_asked, partner_rows, own_child)
-    arrived = lax.all_to_all(
-        payload, "leaf", split_axis=0, concat_axis=0, axis_index_groups=groups, tiled=True
-    )
-    partner_got = arrived[:, : cap * LEAF].reshape(half * cap, LEAF, samp_dev)
     children = arrived[:, cap * LEAF :]
     mirrored = lax.ppermute(children, "leaf", mirror)
     children = jnp.concatenate(
@@ -1006,8 +1015,9 @@
     )
     children = children.reshape(branches, rank, rank)
 
+    weights, near_sample = lax.optimization_barrier((weights, near_sample))
     far_sample, branch_samples, copies = far_products(
-        total, group_leaf, group_slots, side_ref, own_got, partner_got, high, low, weights, branches
+        total, group_leaf, group_slots, side_ref, own_got, arrived, high, low, weights, branches
     )
     everyone = lax.all_to_all(copies, "leaf", split_axis=0, concat_axis=0, tiled=True)
     children, unused = lax.optimization_barrier((children, branch_samples))

time: 167 us -> 180 us (1.078)
  blocking collectives: 32.2 us -> 0 us
  waiting for transfers between devices: 10.7 us -> 41.8 us
  starting transfers between devices: 32 us -> 41.6 us
  local copies, waits for them, and re-layouts: 14.8 us -> 20.8 us
  Pallas kernels: 69.3 us -> 65.6 us
  other arithmetic: 3.44 us -> 5.52 us
    all_to_all x1 -> x0, blocking collectives: 32.2 us -> none  [on_device(): lax.all_to_all(payload, 'leaf', split_axis=0, concat_axis=0, axis_index_g...]
    ppermute x3 -> x4, waiting for transfers between devices: 0.28 us -> 31.4 us  [the longest x1 18.2 us: on_device(): low_edge = lax.ppermute(last, 'leaf', forward)]
    all_to_all x0 -> x1, starting transfers between devices: none -> 6.89 us  [on_device(): lax.all_to_all(payload, 'leaf', split_axis=0, concat_axis=0, axis_index_g...]
    ppermute x1, waiting for transfers between devices: 0.01 us -> 4.94 us  [on_device(): partner = lax.ppermute(mine, 'leaf', mirror)]
    all_to_all x1, starting transfers between devices: 3.53 us -> 8.37 us  [on_device(): lax.all_to_all(copies, 'leaf', split_axis=0, concat_axis=0, tiled=True)]
    all_to_all x1, waiting for transfers between devices: 5.48 us -> 1.26 us  [on_device(): lax.all_to_all(wanted, 'leaf', split_axis=0, concat_axis=0, axis_index_gr...]
    unnamed x29 -> x35, local copies, waits for them, and re-layouts: 2.84 us -> 5.96 us
    all_to_all x1, waiting for transfers between devices: 4.95 us -> 2.23 us  [on_device(): lax.all_to_all(small_sent, 'leaf', split_axis=0, concat_axis=0, axis_inde...]
  transfers between devices with their start and end apart: 12 -> 14, of which waited for: 3 -> 8; matrix products, arithmetic and copies ran while one was open for 10% -> 12% of each run, Pallas kernels for 37% -> 32%
where the time goes in v6:
time: 180 us; the launch traced here: 178 us
  Pallas kernels  65.6 us (36%)
  waiting for transfers between devices  41.8 us (23%)
  starting transfers between devices  41.6 us (23%)
  local copies, waits for them, and re-layouts  20.8 us (12%)
  other arithmetic  5.52 us (3%)
  matrix products  2.13 us (1%)
    ppermute x1, waiting for transfers between devices, on_device(): low_edge = lax.ppermute(last, 'leaf', forward)  18.2 us
    pallas_call x1, Pallas kernels, branch_factors(): pl.pallas_call(functools.partial(branch_body, rank=rank, levels=levels),...  14.4 us
    pallas_call x1, Pallas kernels, top_factors(): pl.pallas_call(functools.partial(top_body, rank=rank, levels=levels), in_...  13.1 us
    ppermute x1, waiting for transfers between devices, on_device(): partner_late = lax.ppermute(rows_out[early:], 'leaf', mirror)  9.67 us
    pallas_call x1, Pallas kernels, kernel_blocks(): pl.pallas_call(functools.partial(blocks_body, rank=rank, cap=cap), grid_s...  8.87 us
    all_to_all x1, starting transfers between devices, on_device(): lax.all_to_all(copies, 'leaf', split_axis=0, concat_axis=0, tiled=True)  8.37 us
    pallas_call x1, Pallas kernels, far_products(): pl.pallas_call(functools.partial(far_body, cap=part // partner.shape[0]),...  7.95 us
    pallas_call x1, Pallas kernels, bases(): pl.pallas_call(functools.partial(basis_body, rank=rank, levels=levels), i...  7.38 us
  transfers between devices with their start and end apart: 14, of which 8 were waited for; matrix products, arithmetic and copies ran while one was open for 12% of the time, Pallas kernels for 32%

profile of v6, /device:TPU:0, one launch (start us, length us, event | category | flops | bytes accessed | tf_op | source)
XLA Modules:
  0.0 178.4 jit_solution(2773979997953653298)
XLA Ops:
  0.6 2.6 %sketched_shares.1 = (f32[320,128]{1,0:T(8,128)}, f32[256,128]{1,0:T(8,128)}) custom-call(s32[1]{0:T(128)} %bitcast.6.place_ref, f32[32,128]{1,0:T(8,128)} %sketch_ref.1, f32[128,2048]{1,0:T(8,128)} %samples_ref.1, f32[3,2048]{1,0:T(4,128)} %points_ref.1), custom_call_target="tpu_custom_call" | custom-call | flops 1000000 | bytes 10000 | tf_op jit(solution)/shard_map/sketched_shares/pallas_call | solution.py:802
  3.2 3.5 %collective-permute-start.2 = (f32[256,128]{1,0:T(8,128)}, f32[256,128]{1,0:T(8,128)S(1)}, u32[]{:S(2)}, u32[]{:S(2)}) collective-permute-start(f32[256,128]{1,0:T(8,128)} %get-tuple-element.42), channel_id=1, source_target_pairs={{0,17},{1,16},{2,19},{3,18},{4,21},{5,20},{6,23},{7,22},{8,25},{9,... | collective-permute-start | bytes 393224 | tf_op jit(solution)/shard_map/ppermute | solution.py:907
  6.7 0.7 collective-permute-start
  7.4 0.8 reshape.145
  8.2 0.1 copy.48
  8.2 0.7 all_to_all.19
  8.9 4.7 %all-to-all-start = ((s32[8,1,16]{2,1,0:T(1,128)}), s32[8,1,16]{2,1,0:T(1,128)S(1)}, u32[]{:S(2)}, u32[]{:S(2)}) async-start(s32[8,1,16]{2,1,0:T(1,128)} %bitcast.3), calls=%async_computation | async-start | bytes 8192 | tf_op jit(solution)/shard_map/all_to_all | solution.py:898
  13.7 0.3 collective-permute-start.1
  14.0 0.7 and_select_fusion
  14.7 0.1 select_reduce_fusion.2
  14.8 0.7 fusion.8
  15.4 0.6 slice.43.total_ref
  16.0 1.6 copy.47
  17.6 0.1 convert_reduce_fusion
  17.8 0.1 reshape.150
  17.9 1.3 all-to-all-done
  19.2 4.9 %collective-permute-done.1.partner_ref = f32[320,128]{1,0:T(8,128)S(1)} collective-permute-done((f32[320,128]{1,0:T(8,128)}, f32[320,128]{1,0:T(8,128)S(1)}, u32[]{:S(2)}, u32[]{:S(2)}) %collective-permute-start.1) | collective-permute-done | bytes 163872 | tf_op jit(solution)/shard_map/ppermute | solution.py:906
  24.1 0.7 copy-done.4
  24.8 2.4 %packed_rows.1 = f32[8,160,128]{2,1,0:T(8,128)} custom-call(s32[8,16]{1,0:T(8,128)} %bitcast.69, s32[1]{0:T(128)} %bitcast.5.side_ref, f32[320,128]{1,0:T(8,128)} %get-tuple-element.41.mine_ref, f32[256,128]{1,0:T(8,128)} %copy-done.7, f32[320,128]{1,0:T(8,128)} %copy-done.4, f32[256,128]{1,0:T(8,128)} %copy-done.6), custom_call_target="tpu_custom_call" | custom-call | tf_op jit(solution)/shard_map/packed_rows/pallas_call | solution.py:838
  27.2 3.9 %all-to-all-start.1 = ((f32[8,160,128]{2,1,0:T(8,128)}), f32[8,160,128]{2,1,0:T(8,128)S(1)}, u32[]{:S(2)}, u32[]{:S(2)}) async-start(f32[8,160,128]{2,1,0:T(8,128)} %packed_rows.1), calls=%async_computation.1 | async-start | bytes 1310720 | tf_op jit(solution)/shard_map/all_to_all | solution.py:929
  31.1 0.1 select_reduce_fusion
  31.3 0.6 gather_fusion.1
  31.9 0.7 reshape.151.slot_ref
  32.6 1.1 compare_select_fusion.2.count_ref
  33.7 0.8 dynamic-slice_reduce_fusion
  34.5 0.1 reshape.148
  34.6 1.4 collective-permute-start.3
  35.9 2.1 %gather_fusion = f32[64,64,128]{2,1,0:T(8,128)} fusion(f32[32,64,128]{2,1,0:T(8,128)S(1)} %bitcast.59, s32[1024]{0:T(1024)S(1)} %pad_clamp_fusion.1), kind=kCustom, calls=%fused_computation | custom fusion | bytes 4194560 | tf_op jit(solution)/shard_map/gather | solution.py:960
  38.0 2.9 %collective-permute-done.3.early_ref = f32[4,64,128]{2,1,0:T(8,128)S(1)} collective-permute-done((f32[4,64,128]{2,1,0:T(8,128)S(1)}, f32[4,64,128]{2,1,0:T(8,128)S(1)}, u32[]{:S(2)}, u32[]{:S(2)}) %collective-permute-start.3) | collective-permute-done | bytes 131104 | tf_op jit(solution)/shard_map/ppermute | solution.py:936
  41.0 2.2 %all-to-all-done.1 = f32[8,160,128]{2,1,0:T(8,128)S(1)} async-done(((f32[8,160,128]{2,1,0:T(8,128)}), f32[8,160,128]{2,1,0:T(8,128)S(1)}, u32[]{:S(2)}, u32[]{:S(2)}) %all-to-all-start.1) | async-done | bytes 655392 | tf_op jit(solution)/shard_map/all_to_all | solution.py:929
  43.2 0.8 copy-done.2
  44.0 4.7 %all-to-all-start.2 = ((f32[8,8,64,128]{3,2,1,0:T(8,128)}), f32[8,8,64,128]{3,2,1,0:T(8,128)S(1)}, u32[]{:S(2)}, u32[]{:S(2)}) async-start(f32[8,8,64,128]{3,2,1,0:T(8,128)} %bitcast.8), calls=%async_computation.2 | async-start | bytes 4194304 | tf_op jit(solution)/shard_map/all_to_all | solution.py:964
  48.7 1.0 slice.46
  49.8 1.7 collective-permute-start.5
  51.5 0.9 slice.60
  52.4 1.3 copy.51
  53.8 0.6 dynamic-slice_bitcast_fusion.asked_ref
  54.4 1.6 slice.61
  56.0 8.9 %kernel_blocks.1 = (bf16[128,64,256]{2,1,0:T(8,128)(2,1)}, bf16[128,64,256]{2,1,0:T(8,128)(2,1)}, f32[32,32,64]{2,1,0:T(8,128)}, f32[32,32,32]{2,1,0:T(8,128)}) custom-call(s32[1]{0:T(128)} %slice.43.total_ref, s32[128]{0:T(128)} %copy-done.12, s32[128]{0:T(128)} %compare_select_fusion.2.count_ref, s32[512]{0:T(512)} %reshape.151.slot_ref, ...), custom_call_target="tpu_custom_call" | custom-call | flops 1000000 | bytes 10000 | tf_op jit(solution)/shard_map/kernel_blocks/pallas_call | solution.py:143
  64.9 14.4 %branch_factors.1 = (f32[32,32,128]{2,1,0:T(8,128)}, f32[6,32,32,128]{3,2,1,0:T(8,128)}, f32[32,32]{1,0:T(8,128)}, f32[32,32]{1,0:T(8,128)}) custom-call(f32[1024,32]{1,0:T(8,128)} %bitcast.68), custom_call_target="tpu_custom_call" | custom-call | flops 1000000 | bytes 10000 | tf_op jit(solution)/shard_map/branch_factors/pallas_call | solution.py:574
  79.2 1.4 reshape.156.child_ref
  80.6 9.7 %collective-permute-done.5.late_ref = f32[28,64,128]{2,1,0:T(8,128)} collective-permute-done((f32[28,64,128]{2,1,0:T(8,128)}, f32[28,64,128]{2,1,0:T(8,128)}, u32[]{:S(2)}, u32[]{:S(2)}) %collective-permute-start.5) | collective-permute-done | bytes 917536 | tf_op jit(solution)/shard_map/ppermute | solution.py:937
  90.3 2.0 %all-to-all-done.2 = f32[8,8,64,128]{3,2,1,0:T(8,128)S(1)} async-done(((f32[8,8,64,128]{3,2,1,0:T(8,128)}), f32[8,8,64,128]{3,2,1,0:T(8,128)S(1)}, u32[]{:S(2)}, u32[]{:S(2)}) %all-to-all-start.2) | async-done | bytes 2097184 | tf_op jit(solution)/shard_map/all_to_all | solution.py:964
  92.3 1.3 copy-done.1
  93.6 2.8 %payload_rows.1 = f32[8,520,128]{2,1,0:T(8,128)} custom-call(s32[8,8]{1,0:T(8,128)} %dynamic-slice_bitcast_fusion.asked_ref, f32[4,64,128]{2,1,0:T(8,128)} %copy-done.8, f32[28,64,128]{2,1,0:T(8,128)} %collective-permute-done.5.late_ref, f32[8,128]{1,0:T(8,128)} %reshape.156.child_ref), custom_call_target="tpu_custom_call" | custom-call | tf_op jit(solution)/shard_map/payload_rows/pallas_call | solution.py:865
  96.5 6.9 %all-to-all-start.3 = ((f32[8,520,128]{2,1,0:T(8,128)}), f32[8,520,128]{2,1,0:T(8,128)}, u32[]{:S(2)}, u32[]{:S(2)}) async-start(f32[8,520,128]{2,1,0:T(8,128)} %payload_rows.1), calls=%async_computation.3 | async-start | bytes 4259840 | tf_op jit(solution)/shard_map/all_to_all | solution.py:992
  103.4 3.9 %collective-permute-start.6 = (f32[72,128]{1,0:T(8,128)S(1)}, f32[72,128]{1,0:T(8,128)S(1)}, u32[]{:S(2)}, u32[]{:S(2)}) collective-permute-start(f32[72,128]{1,0:T(8,128)S(1)} %get-tuple-element.59), channel_id=1, source_target_pairs={{0,2},{2,4},{4,6},{6,8},{8,10},{10,12},{12,14},{14,16},{16,18},{18... | collective-permute-start | bytes 110600 | tf_op jit(solution)/shard_map/ppermute | solution.py:955
  107.4 1.5 collective-permute-start.7
  108.9 0.1 copy.55
  109.0 0.6 reshape.158.mask_ref
  109.6 0.4 copy.57
  110.0 18.2 %collective-permute-done.6 = f32[72,128]{1,0:T(8,128)S(1)} collective-permute-done((f32[72,128]{1,0:T(8,128)S(1)}, f32[72,128]{1,0:T(8,128)S(1)}, u32[]{:S(2)}, u32[]{:S(2)}) %collective-permute-start.6) | collective-permute-done | bytes 36896 | tf_op jit(solution)/shard_map/ppermute | solution.py:955
  128.2 0.6 collective-permute-done.7
  129.0 1.1 maximum_maximum_fusion.rows_ref
  130.2 0.8 slice.64
  130.9 0.8 pad_maximum_fusion.coords_ref
  131.7 6.1 %near_products.1 = f32[128,2048]{1,0:T(8,128)} custom-call(s32[96]{0:T(128)} %reshape.158.mask_ref, f32[35,64,128]{2,1,0:T(8,128)} %maximum_maximum_fusion.rows_ref, f32[35,8,128]{2,1,0:T(8,128)} %pad_maximum_fusion.coords_ref, f32[32,64,3]{2,1,0:T(8,128)} %bitcast.63), custom_call_target="tpu_custom_call" | custom-call | flops 1000000 | bytes 10000 | tf_op jit(solution)/shard_map/near_products/pallas_call | solution.py:315
  137.8 7.4 %bases.1 = (f32[32,2048]{1,0:T(8,128)}, f32[32,2048]{1,0:T(8,128)}) custom-call(f32[32,32,128]{2,1,0:T(8,128)} %get-tuple-element.57.inverse_ref, f32[6,32,32,128]{3,2,1,0:T(8,128)} %get-tuple-element.61.ratio_ref, f32[32,32]{1,0:T(8,128)} %get-tuple-element.62.top_ref, f32[32,32,64]{2,1,0:T(8,128)} %get-tuple-element.63.sketched_ref), custom_call_target="tpu_custom_call" | custom-call | flops 1000000 | bytes 10000 | tf_op jit(solution)/shard_map/bases/pallas_call | solution.py:623
  145.2 8.0 %far_products.1 = (f32[128,2048]{1,0:T(8,128)}, f32[32,128]{1,0:T(8,128)}, f32[16,32,128]{2,1,0:T(8,128)}) custom-call(s32[1]{0:T(128)} %slice.43.total_ref, s32[128]{0:T(128)} %copy-done.12, s32[512]{0:T(512)} %reshape.151.slot_ref, s32[1]{0:T(128)} %bitcast.5.side_ref, f32[64,64,128]{2,1,0:T(8,128)} %bitcast.65, ...), custom_call_target="tpu_custom_call" | custom-call | flops 1000000 | bytes 10000 | tf_op jit(solution)/shard_map/far_products/pallas_call | solution.py:238
  153.1 8.4 %all-to-all-start.4 = ((f32[16,32,128]{2,1,0:T(8,128)}), f32[16,32,128]{2,1,0:T(8,128)S(1)}, u32[]{:S(2)}, u32[]{:S(2)}) async-start(f32[16,32,128]{2,1,0:T(8,128)} %get-tuple-element.75), calls=%async_computation.4 | async-start | bytes 524288 | tf_op jit(solution)/shard_map/all_to_all | solution.py:1022
  161.5 0.8 broadcast_select_fusion.1
  162.3 0.8 reshape.159.children_ref
  163.1 13.1 %top_factors.1 = (f32[15,32,64]{2,1,0:T(8,128)}, f32[512,32]{1,0:T(8,128)}) custom-call(f32[16,32,32]{2,1,0:T(8,128)} %reshape.159.children_ref), custom_call_target="tpu_custom_call" | custom-call | flops 10000000000 | bytes 10000000 | tf_op jit(solution)/shard_map/top_factors/pallas_call | solution.py:696
  176.2 2.1 %fusion.5 = f32[32,128]{1,0:T(8,128)} fusion(f32[512,32]{1,0:T(8,128)} %get-tuple-element.74, f32[512,128]{1,0:T(8,128)S(1)} %bitcast.66), kind=kOutput, calls=%fused_computation.42 | convolution fusion | flops 25165824 | bytes 344064 | tf_op jit(solution)/shard_map/dot_general | solution.py:1026
  (56 shorter events, 0.5 us)
Async XLA Ops:
  0.6 17.1 %copy-start.11 = (s32[32,16]{0,1:T(8,128)S(1)}, s32[32,16]{0,1:T(8,128)}, u32[]{:S(2)}) copy-start(s32[32,16]{0,1:T(8,128)} %param.11) | copy-start | bytes 6148
  3.2 15.9 %collective-permute-start.2 = (f32[256,128]{1,0:T(8,128)}, f32[256,128]{1,0:T(8,128)S(1)}, u32[]{:S(2)}, u32[]{:S(2)}) collective-permute-start(f32[256,128]{1,0:T(8,128)} %get-tuple-element.42), channel_id=1, source_target_pairs={{0,17},{1,16},{2,19},{3,18},{4,21},{5,20},{6,23},{7,22},{8,25},{9,... | collective-permute-start | bytes 393224 | tf_op jit(solution)/shard_map/ppermute | solution.py:907
  6.7 12.4 %collective-permute-start = (f32[256,128]{1,0:T(8,128)}, f32[256,128]{1,0:T(8,128)S(1)}, u32[]{:S(2)}, u32[]{:S(2)}) collective-permute-start(f32[256,128]{1,0:T(8,128)} %get-tuple-element.42), channel_id=1, source_target_pairs={{0,1},{1,0},{2,3},{3,2},{4,5},{5,4},{6,7},{7,6},{8,9},{9,8},{10,11... | collective-permute-start | bytes 393224 | tf_op jit(solution)/shard_map/ppermute | solution.py:905
  8.9 10.2 %all-to-all-start = ((s32[8,1,16]{2,1,0:T(1,128)}), s32[8,1,16]{2,1,0:T(1,128)S(1)}, u32[]{:S(2)}, u32[]{:S(2)}) async-start(s32[8,1,16]{2,1,0:T(1,128)} %bitcast.3), calls=%async_computation | async-start | bytes 8192 | tf_op jit(solution)/shard_map/all_to_all | solution.py:898
  13.7 10.4 %collective-permute-start.1 = (f32[320,128]{1,0:T(8,128)}, f32[320,128]{1,0:T(8,128)S(1)}, u32[]{:S(2)}, u32[]{:S(2)}) collective-permute-start(f32[320,128]{1,0:T(8,128)} %get-tuple-element.41.mine_ref), channel_id=1, source_target_pairs={{0,16},{2,18},{4,20},{6,22},{8,24},{10,26},{12,28},{14,30},{16,0},... | collective-permute-start | bytes 491528 | tf_op jit(solution)/shard_map/ppermute | solution.py:906
  16.0 15.1 %copy-start.14 = (s32[32]{0:T(128)S(1)}, s32[32]{0:T(128)}, u32[]{:S(2)}) copy-start(s32[32]{0:T(128)} %param.12) | copy-start | bytes 388
  19.1 5.0 %copy-start.9 = (s32[8,1,16]{2,1,0:T(1,128)}, s32[8,1,16]{2,1,0:T(1,128)S(1)}, u32[]{:S(2)}) copy-start(s32[8,1,16]{2,1,0:T(1,128)S(1)} %all-to-all-done) | copy-start | bytes 1540
  19.1 5.0 %copy-start.6 = (f32[256,128]{1,0:T(8,128)}, f32[256,128]{1,0:T(8,128)S(1)}, u32[]{:S(2)}) copy-start(f32[256,128]{1,0:T(8,128)S(1)} %collective-permute-done.2.crossed_ref) | copy-start | bytes 393220
  19.2 5.0 %copy-start.7 = (f32[256,128]{1,0:T(8,128)}, f32[256,128]{1,0:T(8,128)S(1)}, u32[]{:S(2)}) copy-start(f32[256,128]{1,0:T(8,128)S(1)} %collective-permute-done.arrived_ref) | copy-start | bytes 393220
  24.1 0.7 copy-start.4
  27.2 16.0 %all-to-all-start.1 = ((f32[8,160,128]{2,1,0:T(8,128)}), f32[8,160,128]{2,1,0:T(8,128)S(1)}, u32[]{:S(2)}, u32[]{:S(2)}) async-start(f32[8,160,128]{2,1,0:T(8,128)} %packed_rows.1), calls=%async_computation.1 | async-start | bytes 1310720 | tf_op jit(solution)/shard_map/all_to_all | solution.py:929
  31.1 6.9 %copy-start.12 = (s32[128]{0:T(128)}, s32[128]{0:T(128)S(1)}, u32[]{:S(2)}) copy-start(s32[128]{0:T(128)S(1)} %broadcast_minimum_fusion.leaf_ref) | copy-start | bytes 1540
  34.6 6.4 %collective-permute-start.3 = (f32[4,64,128]{2,1,0:T(8,128)S(1)}, f32[4,64,128]{2,1,0:T(8,128)S(1)}, u32[]{:S(2)}, u32[]{:S(2)}) collective-permute-start(f32[4,64,128]{2,1,0:T(8,128)S(1)} %slice.42), channel_id=1, source_target_pairs={{0,16},{2,18},{4,20},{6,22},{8,24},{10,26},{12,28},{14,30},{16,0},... | collective-permute-start | bytes 393224 | tf_op jit(solution)/shard_map/ppermute | solution.py:936
  41.0 51.3 %copy-start.8 = (f32[4,64,128]{2,1,0:T(8,128)}, f32[4,64,128]{2,1,0:T(8,128)S(1)}, u32[]{:S(2)}) copy-start(f32[4,64,128]{2,1,0:T(8,128)S(1)} %collective-permute-done.3.early_ref) | copy-start | bytes 393220
  43.2 0.8 copy-start.2
  44.0 48.3 %all-to-all-start.2 = ((f32[8,8,64,128]{3,2,1,0:T(8,128)}), f32[8,8,64,128]{3,2,1,0:T(8,128)S(1)}, u32[]{:S(2)}, u32[]{:S(2)}) async-start(f32[8,8,64,128]{3,2,1,0:T(8,128)} %bitcast.8), calls=%async_computation.2 | async-start | bytes 4194304 | tf_op jit(solution)/shard_map/all_to_all | solution.py:964
  48.7 2.8 %copy-start.3 = (f32[8,160,128]{2,1,0:T(8,128)S(1)}, f32[8,160,128]{2,1,0:T(8,128)}, u32[]{:S(2)}) copy-start(f32[8,160,128]{2,1,0:T(8,128)} %copy-done.2) | copy-start | bytes 1966084
  48.7 3.7 %copy-start.5 = (f32[3,2048]{1,0:T(4,128)S(1)}, f32[3,2048]{1,0:T(4,128)}, u32[]{:S(2)}) copy-start(f32[3,2048]{1,0:T(4,128)} %points_ref.1) | copy-start | bytes 73732
  48.7 5.0 %copy-start.10 = (s32[8,1,16]{2,1,0:T(1,128)S(1)}, s32[8,1,16]{2,1,0:T(1,128)}, u32[]{:S(2)}) copy-start(s32[8,1,16]{2,1,0:T(1,128)} %copy-done.9) | copy-start | bytes 1540
  49.8 40.5 %collective-permute-start.5 = (f32[28,64,128]{2,1,0:T(8,128)}, f32[28,64,128]{2,1,0:T(8,128)}, u32[]{:S(2)}, u32[]{:S(2)}) collective-permute-start(f32[28,64,128]{2,1,0:T(8,128)} %slice.46), channel_id=1, source_target_pairs={{0,16},{2,18},{4,20},{6,22},{8,24},{10,26},{12,28},{14,30},{16,0},... | collective-permute-start | bytes 2752520 | tf_op jit(solution)/shard_map/ppermute | solution.py:937
  52.4 3.6 %collective-permute-start.4 = (f32[1024,128]{1,0:T(8,128)}, f32[1024,128]{1,0:T(8,128)}, u32[]{:S(2)}, u32[]{:S(2)}) collective-permute-start(f32[1024,128]{1,0:T(8,128)} %bitcast.13.own_ref), channel_id=1, source_target_pairs={{0,1},{1,0},{2,3},{3,2},{4,5},{5,4},{6,7},{7,6},{8,9},{9,8},{10,11... | collective-permute-start | bytes 1572872 | tf_op jit(solution)/shard_map/ppermute | solution.py:973
  92.3 1.3 copy-start.1
  96.5 12.4 %copy-start.13 = (s32[32,3]{0,1:T(4,128)S(1)}, s32[32,3]{0,1:T(4,128)}, u32[]{:S(2)}) copy-start(s32[32,3]{0,1:T(4,128)} %param.13) | copy-start | bytes 1156
  96.5 13.1 %copy-start = (f32[3,2048]{0,1:T(8,128)S(1)}, f32[3,2048]{0,1:T(8,128)}, u32[]{:S(2)}) copy-start(f32[3,2048]{0,1:T(8,128)} %copy.51) | copy-start | bytes 73732
  96.5 33.7 %all-to-all-start.3 = ((f32[8,520,128]{2,1,0:T(8,128)}), f32[8,520,128]{2,1,0:T(8,128)}, u32[]{:S(2)}, u32[]{:S(2)}) async-start(f32[8,520,128]{2,1,0:T(8,128)} %payload_rows.1), calls=%async_computation.3 | async-start | bytes 4259840 | tf_op jit(solution)/shard_map/all_to_all | solution.py:992
  103.4 24.8 %collective-permute-start.6 = (f32[72,128]{1,0:T(8,128)S(1)}, f32[72,128]{1,0:T(8,128)S(1)}, u32[]{:S(2)}, u32[]{:S(2)}) collective-permute-start(f32[72,128]{1,0:T(8,128)S(1)} %get-tuple-element.59), channel_id=1, source_target_pairs={{0,2},{2,4},{4,6},{6,8},{8,10},{10,12},{12,14},{14,16},{16,18},{18... | collective-permute-start | bytes 110600 | tf_op jit(solution)/shard_map/ppermute | solution.py:955
  107.4 21.5 %collective-permute-start.7 = (f32[72,128]{1,0:T(8,128)S(1)}, f32[72,128]{1,0:T(8,128)S(1)}, u32[]{:S(2)}, u32[]{:S(2)}) collective-permute-start(f32[72,128]{1,0:T(8,128)S(1)} %get-tuple-element.60), channel_id=1, source_target_pairs={{2,0},{4,2},{6,4},{8,6},{10,8},{12,10},{14,12},{16,14},{18,16},{20... | collective-permute-start | bytes 110600 | tf_op jit(solution)/shard_map/ppermute | solution.py:956
  130.9 30.6 %collective-permute-start.8 = (f32[8,8,128]{2,1,0:T(8,128)S(1)}, f32[8,8,128]{2,1,0:T(8,128)S(1)}, u32[]{:S(2)}, u32[]{:S(2)}) collective-permute-start(f32[8,8,128]{2,1,0:T(8,128)S(1)} %slice.64), channel_id=1, source_target_pairs={{0,16},{2,18},{4,20},{6,22},{8,24},{10,26},{12,28},{14,30},{16,0},... | collective-permute-start | bytes 98312 | tf_op jit(solution)/shard_map/ppermute | solution.py:1012
  153.1 23.1 %all-to-all-start.4 = ((f32[16,32,128]{2,1,0:T(8,128)}), f32[16,32,128]{2,1,0:T(8,128)S(1)}, u32[]{:S(2)}, u32[]{:S(2)}) async-start(f32[16,32,128]{2,1,0:T(8,128)} %get-tuple-element.75), calls=%async_computation.4 | async-start | bytes 524288 | tf_op jit(solution)/shard_map/all_to_all | solution.py:1022

commit v7 on v6

--- a/solution.py
+++ b/solution.py
@@ -61,7 +61,7 @@
 
 def blocks_body(
     total_ref, leaf_ref, count_ref, slot_ref, place_ref,
-    own_ref, other_ref, coords_ref, target_ref,
+    own_ref, other_ref, target_ref,
     high_ref, low_ref, sketched_ref, gram_ref,
     packed,
     *, rank, cap,
@@ -81,13 +81,14 @@
         def unpack(peer, carry):
             for entry in range(2 * cap):
                 slot = (entry // cap) * (slots // 2) + peer * cap + entry % cap
-                at = pl.multiple_of((peer * 2 * cap + entry) * quarter, quarter)
+                at = entry * quarter
                 for ref, base in ((own_ref, own_at), (other_ref, other_at)):
-                    value = ref[pl.ds(at, quarter), :]
+                    value = ref[peer, at : at + quarter, :]
                     turned = pltpu.roll(value, LEAF, 1)
                     packed[slot, pl.ds(base, quarter), :] = jnp.where(first, value, turned)
                     packed[slot, pl.ds(base + quarter, quarter), :] = jnp.where(first, turned, value)
-                value = coords_ref[pl.ds((peer * 2 * cap + entry) * 2, 2), :]
+                at = 2 * cap * quarter + 2 * entry
+                value = own_ref[peer, at : at + 2, :]
                 turned = pltpu.roll(value, LEAF, 1)
                 packed[slot, rank : rank + 1, :] = jnp.where(first, value, turned)[0:1]
                 packed[slot, rank + 1 : rank + 2, :] = jnp.where(first, turned, value)[0:1]
@@ -117,7 +118,8 @@
             z_high, z_low = halves(jnp.concatenate(z_parts, axis=1))
             k_high = high_ref[member]
             k_low = low_ref[member]
-            update = dot_nt(z_high, k_high) + (dot_nt(z_low, k_high) + dot_nt(z_high, k_low))
+            both = dot_nt(jnp.concatenate([z_high, z_low], axis=0), k_high)
+            update = both[:rank] + (both[rank:] + dot_nt(z_high, k_low))
             sketched_ref[leaf] += update
 
     @pl.when(step == pl.num_programs(0) - 1)
@@ -127,17 +129,16 @@
             gram_ref[leaf] = dot_exact_nt(block, block)
 
 
-def kernel_blocks(total, group_leaf, group_count, group_slots, place, own, other, coords, targets, rank, cap):
+def kernel_blocks(total, group_leaf, group_count, group_slots, place, own, other, targets, rank, cap):
     leaves = targets.shape[0]
     groups = group_leaf.shape[0]
-    slots = coords.shape[0] // 2
+    slots = own.shape[0] * 2 * cap
     steps = groups // BATCH
 
     def block_index(step, total_ref, *unused):
         last = (total_ref[0] - 1) // BATCH
         return (jnp.minimum(step, last), 0, 0)
 
-    flat = lambda *unused: (0, 0)
     whole = lambda *unused: (0, 0, 0)
     once = pl.Buffered(1)
     return pl.pallas_call(
@@ -146,9 +147,8 @@
             num_scalar_prefetch=5,
             grid=(steps,),
             in_specs=[
-                pl.BlockSpec(own.shape, flat, pipeline_mode=once),
-                pl.BlockSpec(other.shape, flat, pipeline_mode=once),
-                pl.BlockSpec(coords.shape, flat, pipeline_mode=once),
+                pl.BlockSpec(own.shape, whole, pipeline_mode=once),
+                pl.BlockSpec(other.shape, whole, pipeline_mode=once),
                 pl.BlockSpec(targets.shape, whole, pipeline_mode=once),
             ],
             out_specs=[
@@ -170,7 +170,7 @@
         cost_estimate=pl.CostEstimate(
             flops=10**6, bytes_accessed=10**4, transcendentals=0
         ),
-    )(total, group_leaf, group_count, group_slots, place, own, other, coords, targets)
+    )(total, group_leaf, group_count, group_slots, place, own, other, targets)
 
 
 def far_body(
@@ -400,7 +400,14 @@
 
 
 def pair_up(value, level):
-    return value + pltpu.roll(value, LANES - lax.shift_left(1, level), 1)
+    reach = LANES - (1 << level if isinstance(level, int) else lax.shift_left(1, level))
+    return value + pltpu.roll(value, reach, 1)
+
+
+def when(condition):
+    if isinstance(condition, bool):
+        return lambda body: body() if condition else None
+    return pl.when(condition)
 
 
 def level_fast(level, levels, current, left, inverse, squared, ratio, child, lowest, rank, child_at):
@@ -426,7 +433,7 @@
                 squared[at + SUB * t : at + SUB * (t + 1), :] = sums[q][t]
 
     if child is not None:
-        @pl.when(child_at(level))
+        @when(child_at(level))
         def _():
             for r in range(rank):
                 for t in range(tiles):
@@ -484,7 +491,7 @@
         lambda k, offset: inverse[pl.ds(pl.multiple_of(k * rank + offset, SUB), SUB), :],
     )
     if child is not None:
-        @pl.when(child_at(level))
+        @when(child_at(level))
         def _():
             for r in range(rank):
                 for t in range(tiles):
@@ -510,7 +517,7 @@
     )
 
 
-def run_levels(source, levels, nodes, current, left, inverse, squared, ratio, child, lowest, rank, child_at, finish):
+def run_levels(source, levels, nodes, current, left, inverse, squared, ratio, child, lowest, rank, child_at, finish, unrolled=False):
     lowest[...] = jnp.full((1, LANES), 1.0, jnp.float32)
 
     def sweep(level_step):
@@ -521,7 +528,11 @@
             finish(level)
             return carry
 
-        lax.fori_loop(0, levels, body, 0)
+        if unrolled and level_step is level_fast:
+            for level in range(levels):
+                body(level, 0)
+        else:
+            lax.fori_loop(0, levels, body, 0)
 
     sweep(level_fast)
     lane = lax.broadcasted_iota(jnp.int32, (1, LANES), 1)
@@ -544,7 +555,9 @@
         @pl.when(level == levels - 1)
         def _():
             for r in range(rank):
-                child_ref[r : r + 1, :] = child[r].T[0:1, :]
+                width = child_ref.shape[1]
+                at = r * rank
+                child_ref[at // width : at // width + 1, at % width : at % width + rank] = child[r].T[0:1, :]
                 top_ref[r : r + 1, :] = jnp.concatenate(
                     [inverse_row(inverse, r, t, rank) for t in range(rank // SUB)], axis=0
                 ).T[0:1, :]
@@ -569,7 +582,7 @@
     ]
 
 
-def branch_factors(gram, levels):
+def branch_factors(gram, levels, width):
     leaves, rank, unused = gram.shape
     return pl.pallas_call(
         functools.partial(branch_body, rank=rank, levels=levels),
@@ -579,7 +592,7 @@
             jax.ShapeDtypeStruct((rank, rank, LANES), jnp.float32),
             jax.ShapeDtypeStruct((levels, rank, rank, LANES), jnp.float32),
             jax.ShapeDtypeStruct((rank, rank), jnp.float32),
-            jax.ShapeDtypeStruct((rank, rank), jnp.float32),
+            jax.ShapeDtypeStruct((rank * rank // width, width), jnp.float32),
         ],
         scratch_shapes=tree_scratch(rank),
         compiler_params=pltpu.CompilerParams(vmem_limit_bytes=vmem_bytes),
@@ -632,10 +645,17 @@
     )(inverse, ratio, top, sketched)
 
 
-def top_body(children_ref, transfer_ref, paths_ref, source, current, left, inverse, squared, child, lowest, nat_inverse, nat_child, *, rank, levels):
-    nodes = children_ref.shape[0] // 2
+def top_body(packed_ref, transfer_ref, paths_ref, children_ref, source, current, left, inverse, squared, child, lowest, nat_inverse, nat_child, *, rank, levels):
+    branches, packed_rows_each, width = packed_ref.shape
+    nodes = branches // 2
+    every = width // rank
+    flat = packed_ref[...].reshape(branches * packed_rows_each, width)
+    for part in range(every):
+        children_ref[pl.ds(part, branches * packed_rows_each, stride=every), :] = flat[
+            :, part * rank : (part + 1) * rank
+        ]
     for node in range(nodes):
-        both = children_ref[2 * node : 2 * node + 2].reshape(2 * rank, rank)
+        both = children_ref[2 * node * rank : (2 * node + 2) * rank, :]
         source[node * rank : (node + 1) * rank, :] = lax.dot_general(
             both, both, tn_dims, precision=highest, preferred_element_type=jnp.float32
         )
@@ -647,13 +667,13 @@
 
     run_levels(
         source, levels, nodes, current, left, inverse, squared, None, child, lowest, rank,
-        lambda level: level >= 0, finish,
+        lambda level: True, finish, unrolled=True,
     )
     offset = 0
     for level in range(levels):
         for node in range(nodes >> level):
             if level == 0:
-                stacked = children_ref[2 * node : 2 * node + 2].reshape(2 * rank, rank)
+                stacked = children_ref[2 * node * rank : (2 * node + 2) * rank, :]
             else:
                 first = 2 * node << level - 1
                 second = 2 * node + 1 << level - 1
@@ -688,8 +708,8 @@
         paths_ref[branch * rank : (branch + 1) * rank, :] = above[branch]
 
 
-def top_factors(children):
-    branches, rank, unused = children.shape
+def top_factors(children, rank):
+    branches = children.shape[0]
     levels = branches.bit_length() - 1
     nodes = branches // 2
     natural = pltpu.VMEM((levels, nodes * rank, rank), jnp.float32)
@@ -701,7 +721,10 @@
             jax.ShapeDtypeStruct((branches - 1, rank, 2 * rank), jnp.float32),
             jax.ShapeDtypeStruct((branches * rank, rank), jnp.float32),
         ],
-        scratch_shapes=[pltpu.VMEM((nodes * rank, rank), jnp.float32)]
+        scratch_shapes=[
+            pltpu.VMEM((branches * rank, rank), jnp.float32),
+            pltpu.VMEM((nodes * rank, rank), jnp.float32),
+        ]
         + tree_scratch(rank)
         + [natural, natural],
         compiler_params=pltpu.CompilerParams(vmem_limit_bytes=vmem_bytes),
@@ -794,6 +817,7 @@
             at = leaves * quarter + (2 * pair + member) * 2
             mine_ref[at : at + 1, :] = xy[member]
             mine_ref[at + 1 : at + 2, :] = zs[member]
+    other_ref[leaves * quarter :, :] = jnp.zeros((2 * leaves, LANES), jnp.float32)
 
 
 def sketched_shares(place, sketch, samples, points):
@@ -805,7 +829,7 @@
         out_specs=[vmem_spec] * 2,
         out_shape=[
             jax.ShapeDtypeStruct((leaves * (rank // 4 + 2), LANES), jnp.float32),
-            jax.ShapeDtypeStruct((leaves * rank // 4, LANES), jnp.float32),
+            jax.ShapeDtypeStruct((leaves * (rank // 4 + 2), LANES), jnp.float32),
         ],
         compiler_params=pltpu.CompilerParams(vmem_limit_bytes=vmem_bytes),
         name="sketched_shares",
@@ -813,8 +837,8 @@
     )(place, sketch, samples, points)
 
 
-def pack_body(asked_ref, side_ref, mine_ref, arrived_ref, partner_ref, crossed_ref, out_ref, *, cap, leaves):
-    z_rows = arrived_ref.shape[0] // leaves
+def pack_body(asked_ref, side_ref, mine_ref, partner_ref, out_ref, *, cap, leaves):
+    z_rows = mine_ref.shape[0] // leaves - 2
     side = side_ref[0]
 
     def one(peer, carry):
@@ -823,7 +847,7 @@
             here = side == entry // cap
             at = pl.ds(leaf * z_rows, z_rows)
             out_ref[peer, z_rows * entry : z_rows * (entry + 1), :] = jnp.where(
-                here, mine_ref[at, :] + arrived_ref[at, :], partner_ref[at, :] + crossed_ref[at, :]
+                here, mine_ref[at, :], partner_ref[at, :]
             )
             base = z_rows * 2 * cap + 2 * entry
             at = pl.ds(leaves * z_rows + leaf * 2, 2)
@@ -833,43 +857,67 @@
     lax.fori_loop(0, out_ref.shape[0], one, 0)
 
 
-def packed_rows(asked, side, mine, arrived, partner, crossed, cap, leaves):
-    z_rows = arrived.shape[0] // leaves
+def packed_rows(asked, side, mine, partner, cap, leaves):
+    z_rows = mine.shape[0] // leaves - 2
     return pl.pallas_call(
         functools.partial(pack_body, cap=cap, leaves=leaves),
-        in_specs=[pl.BlockSpec(memory_space=pltpu.SMEM)] * 2 + [vmem_spec] * 4,
+        in_specs=[pl.BlockSpec(memory_space=pltpu.SMEM)] * 2 + [vmem_spec] * 2,
         out_specs=vmem_spec,
         out_shape=jax.ShapeDtypeStruct((asked.shape[0], 2 * cap * (z_rows + 2), LANES), jnp.float32),
         compiler_params=pltpu.CompilerParams(vmem_limit_bytes=vmem_bytes),
         name="packed_rows",
-    )(asked, side, mine, arrived, partner, crossed)
-
-
-def payload_body(asked_ref, early_ref, late_ref, child_ref, out_ref, *, cap):
+    )(asked, side, mine, partner)
+
+
+def payload_body(asked_ref, side_ref, early_ref, late_ref, child_ref, out_ref, sems, *, cap):
     early = early_ref.shape[0]
-
-    def one(peer, carry):
+    peers = out_ref.shape[0]
+    rows = child_ref.shape[0]
+    base = (1 - side_ref[0]) * cap
+
+    def place(peer, entry):
+        return out_ref.at[peer, pl.ds(LEAF * entry, LEAF)], sems.at[peer, entry]
+
+    def child_place(peer):
+        return out_ref.at[peer, pl.ds(LEAF * cap, rows)], sems.at[peer, cap]
+
+    for peer in range(peers):
         for entry in range(cap):
-            leaf = asked_ref[peer, entry]
-            first = early_ref[jnp.minimum(leaf, early - 1)]
-            second = late_ref[jnp.maximum(leaf - early, 0)]
-            out_ref[peer, LEAF * entry : LEAF * (entry + 1), :] = jnp.where(leaf < early, first, second)
-        out_ref[peer, LEAF * cap :, :] = child_ref[...]
-        return carry
-
-    lax.fori_loop(0, out_ref.shape[0], one, 0)
-
-
-def payload_rows(asked, early, late, child):
-    half, cap = asked.shape
+            leaf = asked_ref[peer, base + entry]
+            target, sem = place(peer, entry)
+
+            @pl.when(leaf < early)
+            def _():
+                pltpu.make_async_copy(early_ref.at[leaf], target, sem).start()
+
+            @pl.when(leaf >= early)
+            def _():
+                pltpu.make_async_copy(late_ref.at[leaf - early], target, sem).start()
+
+        target, sem = child_place(peer)
+        pltpu.make_async_copy(child_ref, target, sem).start()
+    for peer in range(peers):
+        for entry in range(cap):
+            target, sem = place(peer, entry)
+            pltpu.make_async_copy(late_ref.at[0], target, sem).wait()
+        target, sem = child_place(peer)
+        pltpu.make_async_copy(child_ref, target, sem).wait()
+
+
+def payload_rows(asked, side, early, late, child):
+    half = asked.shape[0]
+    cap = asked.shape[1] // 2
+    smem = pl.BlockSpec(memory_space=pltpu.SMEM)
+    anywhere = pl.BlockSpec(memory_space=pl.ANY)
     return pl.pallas_call(
         functools.partial(payload_body, cap=cap),
-        in_specs=[pl.BlockSpec(memory_space=pltpu.SMEM)] + [vmem_spec] * 3,
-        out_specs=vmem_spec,
+        in_specs=[smem, smem, anywhere, anywhere, anywhere],
+        out_specs=anywhere,
         out_shape=jax.ShapeDtypeStruct((half, cap * LEAF + child.shape[0], late.shape[2]), jnp.float32),
+        scratch_shapes=[pltpu.SemaphoreType.DMA((half, cap + 1))],
         compiler_params=pltpu.CompilerParams(vmem_limit_bytes=vmem_bytes),
         name="payload_rows",
-    )(asked, early, late, child)
+    )(asked, side, early, late, child)
 
 
 def two_rows(values, rows):
@@ -902,13 +950,7 @@
     if columns == 2:
         place = column.astype(jnp.int32).reshape(1)
         mine, other = sketched_shares(place, sketch, samples, points)
-        arrived = lax.ppermute(other, "cols", [(0, 1), (1, 0)])
-        partner = lax.ppermute(mine, "leaf", mirror)
-        crossed = lax.ppermute(
-            other,
-            ("leaf", "cols"),
-            [(2 * i + c, 2 * ((i + half) % branches) + 1 - c) for i in range(branches) for c in range(2)],
-        )
+        mine = mine + lax.ppermute(other, "cols", [(0, 1), (1, 0)])
     else:
         z_part = jnp.dot(sketch, samples, precision=highest)
         z_mine = exchange_sum(z_part.reshape(columns, share, leaves * LEAF), "cols")
@@ -918,14 +960,13 @@
             jnp.concatenate([planes[0:1], planes[2:3], planes[1:2], jnp.zeros_like(planes[0:1])], axis=0), 2
         )
         mine = jnp.concatenate([z_rows.reshape(-1, LANES), c_rows.reshape(-1, LANES)], axis=0)
-        partner = lax.ppermute(mine, "leaf", mirror)
-        arrived = jnp.zeros((leaves * share // 2, LANES), jnp.float32)
-        crossed = arrived
-
+
+    partner = lax.ppermute(mine, "leaf", mirror)
     coords = jnp.transpose(points.reshape(3, leaves, LEAF), (1, 0, 2))
+    targets = jnp.transpose(coords, (0, 2, 1))
     rows = jnp.transpose(samples.reshape(samp_dev, leaves, LEAF), (1, 2, 0))
 
-    small_sent = packed_rows(asked, side_ref, mine, arrived, partner, crossed, cap, leaves)
+    small_sent = packed_rows(asked, side_ref, mine, partner, cap, leaves)
     small_got = lax.all_to_all(
         small_sent, "leaf", split_axis=0, concat_axis=0, axis_index_groups=groups, tiled=True
     )
@@ -934,7 +975,7 @@
     early = leaves // 8
     rows_out, unused = lax.optimization_barrier((rows, small_sent))
     partner_early = lax.ppermute(rows_out[:early], "leaf", mirror)
-    partner_late = lax.ppermute(rows_out[early:], "leaf", mirror)
+    rows_late = rows_out[early:]
 
     forward = [(i, i + 1) for i in range(branches - 1)]
     backward = [(target, source) for source, target in forward]
@@ -956,39 +997,42 @@
     high_edge = lax.ppermute(first, "leaf", backward)
 
     own_asked = lax.dynamic_slice_in_dim(asked, side * cap, cap, axis=1)
-    partner_asked = lax.dynamic_slice_in_dim(asked, (1 - side) * cap, cap, axis=1)
     own_sent = rows_out[own_asked.reshape(-1)].reshape(half, cap, LEAF, samp_dev)
-    own_sent, partner_early, total, group_leaf, group_count, group_slots = lax.optimization_barrier(
-        (own_sent, partner_early, total, group_leaf, group_count, group_slots)
-    )
+    (
+        own_sent, rows_late, partner_early, low_edge, high_edge, targets, total, group_leaf, group_count, group_slots,
+    ) = lax.optimization_barrier(
+        (
+            own_sent, rows_late, partner_early, low_edge, high_edge, targets,
+            total, group_leaf, group_count, group_slots,
+        )
+    )
+    partner_late = lax.ppermute(rows_late, "leaf", mirror)
     own_got = lax.all_to_all(
         own_sent, "leaf", split_axis=0, concat_axis=0, axis_index_groups=groups, tiled=True
     )
     own_got = own_got.reshape(half * cap, LEAF, samp_dev)
 
-    z_count = 2 * cap * share // 2
-    z_own = small_got[:, :z_count].reshape(half * z_count, LANES)
-    c_got = small_got[:, z_count:].reshape(half * 4 * cap, LANES)
     if columns == 2:
-        z_other = lax.ppermute(z_own, "cols", [(0, 1), (1, 0)])
+        small_other = lax.ppermute(small_got, "cols", [(0, 1), (1, 0)])
     else:
-        slots = branches * cap
-        z_all = exchange_all(z_own, "cols").reshape(columns, slots, share // 2, 2, LEAF)
-        z_all = jnp.transpose(z_all, (1, 0, 3, 2, 4)).reshape(slots, 2, 2, rank // 4, LEAF)
-        z_all = jnp.transpose(z_all, (1, 0, 3, 2, 4)).reshape(2, slots * rank // 4, LANES)
-        z_own, z_other = z_all[0], z_all[1]
+        z_count = cap * share
+        z_all = exchange_all(small_got[:, :z_count], "cols")
+        z_all = z_all.reshape(columns, half, 2 * cap, share // 2, 2, LEAF)
+        z_all = jnp.transpose(z_all, (1, 2, 0, 4, 3, 5)).reshape(half, 2 * cap, 2, 2, rank // 4, LEAF)
+        z_all = jnp.transpose(z_all, (2, 0, 1, 4, 3, 5)).reshape(2, half, cap * rank // 2, LANES)
+        c_got = small_got[:, z_count:]
+        small_got = jnp.concatenate([z_all[0], c_got], axis=1)
+        small_other = jnp.concatenate([z_all[1], c_got], axis=1)
         place = jnp.zeros((1,), jnp.int32)
 
-    targets = jnp.transpose(coords, (0, 2, 1))
     high, low, sketched, gram = kernel_blocks(
-        total, group_leaf, group_count, group_slots, place, z_own, z_other, c_got, targets, rank, cap
+        total, group_leaf, group_count, group_slots, place, small_got, small_other, targets, rank, cap
     )
 
     levels = leaves.bit_length()
-    inverse, ratio, top_inverse, own_child = branch_factors(gram, levels)
-    own_child = own_child.reshape(-1, min(samp_dev, LANES))
+    inverse, ratio, top_inverse, own_child = branch_factors(gram, levels, min(samp_dev, LANES))
     own_child, own_got, partner_late = lax.optimization_barrier((own_child, own_got, partner_late))
-    payload = payload_rows(partner_asked, partner_early, partner_late, own_child)
+    payload = payload_rows(asked, side_ref, partner_early, partner_late, own_child)
     arrived = lax.all_to_all(
         payload, "leaf", split_axis=0, concat_axis=0, axis_index_groups=groups, tiled=True
     )
@@ -1013,7 +1057,6 @@
     children = jnp.concatenate(
         [jnp.where(side == 0, children, mirrored), jnp.where(side == 0, mirrored, children)], axis=0
     )
-    children = children.reshape(branches, rank, rank)
 
     weights, near_sample = lax.optimization_barrier((weights, near_sample))
     far_sample, branch_samples, copies = far_products(
@@ -1021,7 +1064,7 @@
     )
     everyone = lax.all_to_all(copies, "leaf", split_axis=0, concat_axis=0, tiled=True)
     children, unused = lax.optimization_barrier((children, branch_samples))
-    transfer_t, paths = top_factors(children)
+    transfer_t, paths = top_factors(children, rank)
     top_transfer = jnp.swapaxes(transfer_t, 1, 2)
     root_sample = lax.dot_general(
         paths, everyone.reshape(branches * rank, samp_dev), tn_dims, precision=highest

time: 180 us -> 252 us (1.40)
  Pallas kernels: 65.6 us -> 129 us
  waiting for transfers between devices: 41.8 us -> 50.9 us
  local copies, waits for them, and re-layouts: 20.8 us -> 14.3 us
  starting transfers between devices: 41.6 us -> 45.9 us
    pallas_call x1, Pallas kernels: 2.82 us -> 67 us  [payload_rows(): pl.pallas_call(functools.partial(payload_body, cap=cap), in_specs=[smem,...]
    all_to_all x1, waiting for transfers between devices: 0.01 us -> 23.3 us  [on_device(): lax.all_to_all(payload, 'leaf', split_axis=0, concat_axis=0, axis_index_g...]
    ppermute x1, waiting for transfers between devices: 18.2 us -> 0.01 us  [on_device(): low_edge = lax.ppermute(last, 'leaf', forward)]
    ppermute x4 -> x3, waiting for transfers between devices: 9.68 us -> 15.2 us  [the longest x1 12.9 us: on_device(): partner_late = lax.ppermute(rows_late, 'leaf', mirror)]
    ppermute x4 -> x3, starting transfers between devices: 5.89 us -> 0.74 us  [the longest x1 0.73 us: on_device(): partner_late = lax.ppermute(rows_late, 'leaf', mirror)]
    ppermute x1, waiting for transfers between devices: 4.94 us -> 8.41 us  [on_device(): partner = lax.ppermute(mine, 'leaf', mirror)]
    ppermute x1, waiting for transfers between devices: 2.91 us -> 0.01 us  [on_device(): partner_early = lax.ppermute(rows_out[:early], 'leaf', mirror)]
    unnamed x35 -> x31, local copies, waits for them, and re-layouts: 5.96 us -> 5.37 us
  transfers between devices with their start and end apart: 14 -> 13, of which waited for: 8 -> 6; matrix products, arithmetic and copies ran while one was open for 12% -> 6% of each run, Pallas kernels for 32% -> 24%
where the time goes in v7:
time: 252 us; the launch traced here: 251 us
  Pallas kernels  129 us (51%)
  waiting for transfers between devices  50.9 us (20%)
  starting transfers between devices  45.9 us (18%)
  local copies, waits for them, and re-layouts  14.3 us (6%)
  other arithmetic  7.77 us (3%)
    pallas_call x1, Pallas kernels, payload_rows(): pl.pallas_call(functools.partial(payload_body, cap=cap), in_specs=[smem,...  67 us
    all_to_all x1, waiting for transfers between devices, on_device(): lax.all_to_all(payload, 'leaf', split_axis=0, concat_axis=0, axis_index_g...  23.3 us
    pallas_call x1, Pallas kernels, branch_factors(): pl.pallas_call(functools.partial(branch_body, rank=rank, levels=levels),...  14.6 us
    ppermute x1, waiting for transfers between devices, on_device(): partner_late = lax.ppermute(rows_late, 'leaf', mirror)  12.9 us
    pallas_call x1, Pallas kernels, top_factors(): pl.pallas_call(functools.partial(top_body, rank=rank, levels=levels), in_...  12.1 us
    all_to_all x1, starting transfers between devices, on_device(): lax.all_to_all(copies, 'leaf', split_axis=0, concat_axis=0, tiled=True)  9.95 us
    pallas_call x1, Pallas kernels, kernel_blocks(): pl.pallas_call(functools.partial(blocks_body, rank=rank, cap=cap), grid_s...  9.04 us
    ppermute x1, waiting for transfers between devices, on_device(): partner = lax.ppermute(mine, 'leaf', mirror)  8.41 us
  transfers between devices with their start and end apart: 13, of which 6 were waited for; matrix products, arithmetic and copies ran while one was open for 6% of the time, Pallas kernels for 24%

profile of v7, /device:TPU:0, one launch (start us, length us, event | category | flops | bytes accessed | tf_op | source)
XLA Modules:
  0.0 250.8 jit_solution(2131639118425124270)
XLA Ops:
  0.6 0.0 copy-start.2
  0.6 0.9 reshape.132
  1.5 0.1 copy.47
  1.6 0.7 all_to_all.19
  2.3 6.2 %all-to-all-start = ((s32[8,1,16]{2,1,0:T(1,128)}), s32[8,1,16]{2,1,0:T(1,128)S(1)}, u32[]{:S(2)}, u32[]{:S(2)}) async-start(s32[8,1,16]{2,1,0:T(1,128)} %bitcast.3), calls=%async_computation | async-start | bytes 8192 | tf_op jit(solution)/shard_map/all_to_all | solution.py:946
  8.4 2.6 %sketched_shares.1 = (f32[320,128]{1,0:T(8,128)}, f32[320,128]{1,0:T(8,128)}) custom-call(s32[1]{0:T(128)} %bitcast.6.place_ref, f32[32,128]{1,0:T(8,128)} %sketch_ref.1, f32[128,2048]{1,0:T(8,128)} %samples_ref.1, f32[3,2048]{1,0:T(4,128)} %points_ref.1), custom_call_target="tpu_custom_call" | custom-call | flops 1000000 | bytes 10000 | tf_op jit(solution)/shard_map/sketched_shares/pallas_call | solution.py:826
  11.1 0.7 and_select_fusion
  11.7 0.1 select_reduce_fusion.2
  11.8 0.1 convert_reduce_fusion
  11.9 0.7 fusion.8
  12.6 0.7 select_reduce_fusion
  13.4 0.9 add.55.mine_ref
  14.3 2.7 %collective-permute-start.1 = (f32[320,128]{1,0:T(8,128)S(1)}, f32[320,128]{1,0:T(8,128)S(1)}, u32[]{:S(2)}, u32[]{:S(2)}) collective-permute-start(f32[320,128]{1,0:T(8,128)S(1)} %add.55.mine_ref), channel_id=1, source_target_pairs={{0,16},{2,18},{4,20},{6,22},{8,24},{10,26},{12,28},{14,30},{16,0},... | collective-permute-start | bytes 491528 | tf_op jit(solution)/shard_map/ppermute | solution.py:964
  17.0 0.0 copy-start.8
  17.0 8.4 %collective-permute-done.1.partner_ref = f32[320,128]{1,0:T(8,128)S(1)} collective-permute-done((f32[320,128]{1,0:T(8,128)S(1)}, f32[320,128]{1,0:T(8,128)S(1)}, u32[]{:S(2)}, u32[]{:S(2)}) %collective-permute-start.1) | collective-permute-done | bytes 163872 | tf_op jit(solution)/shard_map/ppermute | solution.py:964
  25.4 0.7 copy-done.5
  26.1 2.2 packed_rows.1
  28.3 4.5 %all-to-all-start.1 = ((f32[8,160,128]{2,1,0:T(8,128)}), f32[8,160,128]{2,1,0:T(8,128)}, u32[]{:S(2)}, u32[]{:S(2)}) async-start(f32[8,160,128]{2,1,0:T(8,128)} %packed_rows.1), calls=%async_computation.1 | async-start | bytes 1310720 | tf_op jit(solution)/shard_map/all_to_all | solution.py:970
  32.7 0.6 slice.42.total_ref
  33.4 0.3 copy.46
  33.7 1.3 copy.51
  35.1 0.1 copy.52
  35.2 0.1 reshape.138
  35.2 0.7 gather_fusion.1
  35.9 0.7 reshape.139.slot_ref
  36.6 0.1 fusion.4
  36.7 1.1 compare_select_fusion.2.count_ref
  37.8 0.1 dynamic-slice_reduce_fusion
  37.9 0.1 reshape.135
  38.0 3.4 %collective-permute-start.2 = (f32[4,64,128]{2,1,0:T(8,128)S(1)}, f32[4,64,128]{2,1,0:T(8,128)S(1)}, u32[]{:S(2)}, u32[]{:S(2)}) collective-permute-start(f32[4,64,128]{2,1,0:T(8,128)S(1)} %slice.37), channel_id=1, source_target_pairs={{0,16},{2,18},{4,20},{6,22},{8,24},{10,26},{12,28},{14,30},{16,0},... | collective-permute-start | bytes 393224 | tf_op jit(solution)/shard_map/ppermute | solution.py:977
  41.4 3.9 %collective-permute-start.3 = (f32[72,128]{1,0:T(8,128)S(1)}, f32[72,128]{1,0:T(8,128)S(1)}, u32[]{:S(2)}, u32[]{:S(2)}) collective-permute-start(f32[72,128]{1,0:T(8,128)S(1)} %get-tuple-element.48), channel_id=1, source_target_pairs={{0,2},{2,4},{4,6},{6,8},{8,10},{10,12},{12,14},{14,16},{16,18},{18... | collective-permute-start | bytes 110600 | tf_op jit(solution)/shard_map/ppermute | solution.py:996
  45.3 1.3 collective-permute-start.4
  46.7 1.0 slice.36
  47.7 2.1 gather_fusion
  49.8 1.4 collective-permute-done.4
  51.2 0.6 copy-done.7
  51.9 5.4 %all-to-all-start.2 = ((f32[8,8,64,128]{3,2,1,0:T(8,128)}), f32[8,8,64,128]{3,2,1,0:T(8,128)S(1)}, u32[]{:S(2)}, u32[]{:S(2)}) async-start(f32[8,8,64,128]{3,2,1,0:T(8,128)} %bitcast.8), calls=%async_computation.2 | async-start | bytes 4194304 | tf_op jit(solution)/shard_map/all_to_all | solution.py:1010
  57.3 0.7 collective-permute-start.6
  58.0 2.3 collective-permute-done.5.other_ref
  60.3 0.8 copy-done.3
  61.2 9.0 %kernel_blocks.1 = (bf16[128,64,256]{2,1,0:T(8,128)(2,1)}, bf16[128,64,256]{2,1,0:T(8,128)(2,1)}, f32[32,32,64]{2,1,0:T(8,128)}, f32[32,32,32]{2,1,0:T(8,128)}) custom-call(s32[1]{0:T(128)} %slice.42.total_ref, s32[128]{0:T(128)} %copy-done.11, s32[128]{0:T(128)} %compare_select_fusion.2.count_ref, s32[512]{0:T(512)} %reshape.139.slot_ref, ...), custom_call_target="tpu_custom_call" | custom-call | flops 1000000 | bytes 10000 | tf_op jit(solution)/shard_map/kernel_blocks/pallas_call | solution.py:144
  70.2 14.6 %branch_factors.1 = (f32[32,32,128]{2,1,0:T(8,128)}, f32[6,32,32,128]{3,2,1,0:T(8,128)}, f32[32,32]{1,0:T(8,128)}, f32[8,128]{1,0:T(8,128)}) custom-call(f32[1024,32]{1,0:T(8,128)} %bitcast.62), custom_call_target="tpu_custom_call" | custom-call | flops 1000000 | bytes 10000 | tf_op jit(solution)/shard_map/branch_factors/pallas_call | solution.py:587
  84.8 12.9 %collective-permute-done.6.late_ref = f32[28,64,128]{2,1,0:T(8,128)} collective-permute-done((f32[28,64,128]{2,1,0:T(8,128)}, f32[28,64,128]{2,1,0:T(8,128)}, u32[]{:S(2)}, u32[]{:S(2)}) %collective-permute-start.6) | collective-permute-done | bytes 917536 | tf_op jit(solution)/shard_map/ppermute | solution.py:1009
  97.7 2.6 %all-to-all-done.2 = f32[8,8,64,128]{3,2,1,0:T(8,128)S(1)} async-done(((f32[8,8,64,128]{3,2,1,0:T(8,128)}), f32[8,8,64,128]{3,2,1,0:T(8,128)S(1)}, u32[]{:S(2)}, u32[]{:S(2)}) %all-to-all-start.2) | async-done | bytes 2097184 | tf_op jit(solution)/shard_map/all_to_all | solution.py:1010
  100.3 1.3 copy-done.1
  101.6 67.0 %payload_rows.1 = f32[8,520,128]{2,1,0:T(8,128)} custom-call(s32[8,16]{1,0:T(8,128)} %bitcast.64, s32[1]{0:T(128)} %bitcast.5.side_ref, f32[4,64,128]{2,1,0:T(8,128)} %copy-done.7, f32[28,64,128]{2,1,0:T(8,128)} %collective-permute-done.6.late_ref, f32[8,128]{1,0:T(8,128)} %get-tuple-element.62.child_ref), custom_call_target="tpu_custom_call" | custom-call | tf_op jit(solution)/shard_map/payload_rows/pallas_call | solution.py:912
  168.6 7.9 %all-to-all-start.3 = ((f32[8,520,128]{2,1,0:T(8,128)}), f32[8,520,128]{2,1,0:T(8,128)}, u32[]{:S(2)}, u32[]{:S(2)}) async-start(f32[8,520,128]{2,1,0:T(8,128)} %payload_rows.1), calls=%async_computation.3 | async-start | bytes 4259840 | tf_op jit(solution)/shard_map/all_to_all | solution.py:1036
  176.5 0.1 copy.53
  176.6 0.6 reshape.142.mask_ref
  177.2 0.4 copy.55
  177.6 0.1 pad.25.clone
  177.7 0.1 maximum_maximum_fusion.1
  177.8 1.1 maximum_maximum_fusion.rows_ref
  179.0 23.3 %all-to-all-done.3.partner_ref = f32[8,520,128]{2,1,0:T(8,128)} async-done(((f32[8,520,128]{2,1,0:T(8,128)}), f32[8,520,128]{2,1,0:T(8,128)}, u32[]{:S(2)}, u32[]{:S(2)}) %all-to-all-start.3) | async-done | bytes 2129952 | tf_op jit(solution)/shard_map/all_to_all | solution.py:1036
  202.2 0.8 slice.54
  203.0 0.8 pad_maximum_fusion.coords_ref
  203.8 6.1 %near_products.1 = f32[128,2048]{1,0:T(8,128)} custom-call(s32[96]{0:T(128)} %reshape.142.mask_ref, f32[35,64,128]{2,1,0:T(8,128)} %maximum_maximum_fusion.rows_ref, f32[35,8,128]{2,1,0:T(8,128)} %pad_maximum_fusion.coords_ref, f32[32,64,3]{2,1,0:T(8,128)} %bitcast.58), custom_call_target="tpu_custom_call" | custom-call | flops 1000000 | bytes 10000 | tf_op jit(solution)/shard_map/near_products/pallas_call | solution.py:315
  209.9 7.4 %bases.1 = (f32[32,2048]{1,0:T(8,128)}, f32[32,2048]{1,0:T(8,128)}) custom-call(f32[32,32,128]{2,1,0:T(8,128)} %get-tuple-element.65.inverse_ref, f32[6,32,32,128]{3,2,1,0:T(8,128)} %get-tuple-element.69.ratio_ref, f32[32,32]{1,0:T(8,128)} %get-tuple-element.70.top_ref, f32[32,32,64]{2,1,0:T(8,128)} %get-tuple-element.71.sketched_ref), custom_call_target="tpu_custom_call" | custom-call | flops 1000000 | bytes 10000 | tf_op jit(solution)/shard_map/bases/pallas_call | solution.py:636
  217.2 8.0 %far_products.1 = (f32[128,2048]{1,0:T(8,128)}, f32[32,128]{1,0:T(8,128)}, f32[16,32,128]{2,1,0:T(8,128)}) custom-call(s32[1]{0:T(128)} %slice.42.total_ref, s32[128]{0:T(128)} %copy-done.11, s32[512]{0:T(512)} %reshape.139.slot_ref, s32[1]{0:T(128)} %bitcast.5.side_ref, f32[64,64,128]{2,1,0:T(8,128)} %bitcast.60, ...), custom_call_target="tpu_custom_call" | custom-call | flops 1000000 | bytes 10000 | tf_op jit(solution)/shard_map/far_products/pallas_call | solution.py:238
  225.2 10.0 %all-to-all-start.4 = ((f32[16,32,128]{2,1,0:T(8,128)}), f32[16,32,128]{2,1,0:T(8,128)S(1)}, u32[]{:S(2)}, u32[]{:S(2)}) async-start(f32[16,32,128]{2,1,0:T(8,128)} %get-tuple-element.83), calls=%async_computation.4 | async-start | bytes 524288 | tf_op jit(solution)/shard_map/all_to_all | solution.py:1065
  235.2 0.8 broadcast_select_fusion.1
  236.0 0.6 pad_maximum_fusion.1.packed_ref
  236.6 12.1 %top_factors.1 = (f32[15,32,64]{2,1,0:T(8,128)}, f32[512,32]{1,0:T(8,128)}) custom-call(f32[16,8,128]{2,1,0:T(8,128)} %pad_maximum_fusion.1.packed_ref), custom_call_target="tpu_custom_call" | custom-call | flops 10000000000 | bytes 10000000 | tf_op jit(solution)/shard_map/top_factors/pallas_call | solution.py:716
  248.7 2.1 fusion.5
  (46 shorter events, 0.2 us)
Async XLA Ops:
  0.6 32.8 %copy-start.2 = (f32[128,2048]{1,0:T(8,128)S(1)}, f32[128,2048]{1,0:T(8,128)}, u32[]{:S(2)}) copy-start(f32[128,2048]{1,0:T(8,128)} %samples_ref.1) | copy-start | bytes 3145732
  2.3 14.7 %all-to-all-start = ((s32[8,1,16]{2,1,0:T(1,128)}), s32[8,1,16]{2,1,0:T(1,128)S(1)}, u32[]{:S(2)}, u32[]{:S(2)}) async-start(s32[8,1,16]{2,1,0:T(1,128)} %bitcast.3), calls=%async_computation | async-start | bytes 8192 | tf_op jit(solution)/shard_map/all_to_all | solution.py:946
  11.0 2.3 collective-permute-start
  12.6 21.1 %copy-start.11 = (s32[128]{0:T(128)}, s32[128]{0:T(128)S(1)}, u32[]{:S(2)}) copy-start(s32[128]{0:T(128)S(1)} %broadcast_minimum_fusion.leaf_ref) | copy-start | bytes 1540
  14.3 11.1 %copy-start.4 = (f32[320,128]{1,0:T(8,128)}, f32[320,128]{1,0:T(8,128)S(1)}, u32[]{:S(2)}) copy-start(f32[320,128]{1,0:T(8,128)S(1)} %add.55.mine_ref) | copy-start | bytes 491524
  14.3 11.1 %collective-permute-start.1 = (f32[320,128]{1,0:T(8,128)S(1)}, f32[320,128]{1,0:T(8,128)S(1)}, u32[]{:S(2)}, u32[]{:S(2)}) collective-permute-start(f32[320,128]{1,0:T(8,128)S(1)} %add.55.mine_ref), channel_id=1, source_target_pairs={{0,16},{2,18},{4,20},{6,22},{8,24},{10,26},{12,28},{14,30},{16,0},... | collective-permute-start | bytes 491528 | tf_op jit(solution)/shard_map/ppermute | solution.py:964
  17.0 8.4 %copy-start.8 = (s32[8,1,16]{2,1,0:T(1,128)}, s32[8,1,16]{2,1,0:T(1,128)S(1)}, u32[]{:S(2)}) copy-start(s32[8,1,16]{2,1,0:T(1,128)S(1)} %all-to-all-done) | copy-start | bytes 1540
  25.4 0.7 copy-start.5
  26.1 7.7 %copy-start.6 = (f32[3,2048]{1,0:T(4,128)S(1)}, f32[3,2048]{1,0:T(4,128)}, u32[]{:S(2)}) copy-start(f32[3,2048]{1,0:T(4,128)} %points_ref.1) | copy-start | bytes 73732
  28.3 6.8 %copy-start.10 = (s32[32,16]{0,1:T(8,128)S(1)}, s32[32,16]{0,1:T(8,128)}, u32[]{:S(2)}) copy-start(s32[32,16]{0,1:T(8,128)} %param.11) | copy-start | bytes 6148
  28.3 22.9 %all-to-all-start.1 = ((f32[8,160,128]{2,1,0:T(8,128)}), f32[8,160,128]{2,1,0:T(8,128)}, u32[]{:S(2)}, u32[]{:S(2)}) async-start(f32[8,160,128]{2,1,0:T(8,128)} %packed_rows.1), calls=%async_computation.1 | async-start | bytes 1310720 | tf_op jit(solution)/shard_map/all_to_all | solution.py:970
  33.4 4.4 %copy-start.9 = (s32[8,1,16]{2,1,0:T(1,128)S(1)}, s32[8,1,16]{2,1,0:T(1,128)}, u32[]{:S(2)}) copy-start(s32[8,1,16]{2,1,0:T(1,128)} %copy-done.8) | copy-start | bytes 1540
  38.0 13.2 %collective-permute-start.2 = (f32[4,64,128]{2,1,0:T(8,128)S(1)}, f32[4,64,128]{2,1,0:T(8,128)S(1)}, u32[]{:S(2)}, u32[]{:S(2)}) collective-permute-start(f32[4,64,128]{2,1,0:T(8,128)S(1)} %slice.37), channel_id=1, source_target_pairs={{0,16},{2,18},{4,20},{6,22},{8,24},{10,26},{12,28},{14,30},{16,0},... | collective-permute-start | bytes 393224 | tf_op jit(solution)/shard_map/ppermute | solution.py:977
  41.4 8.4 %collective-permute-start.3 = (f32[72,128]{1,0:T(8,128)S(1)}, f32[72,128]{1,0:T(8,128)S(1)}, u32[]{:S(2)}, u32[]{:S(2)}) collective-permute-start(f32[72,128]{1,0:T(8,128)S(1)} %get-tuple-element.48), channel_id=1, source_target_pairs={{0,2},{2,4},{4,6},{6,8},{8,10},{10,12},{12,14},{14,16},{16,18},{18... | collective-permute-start | bytes 110600 | tf_op jit(solution)/shard_map/ppermute | solution.py:996
  45.3 5.9 %collective-permute-start.4 = (f32[72,128]{1,0:T(8,128)S(1)}, f32[72,128]{1,0:T(8,128)S(1)}, u32[]{:S(2)}, u32[]{:S(2)}) collective-permute-start(f32[72,128]{1,0:T(8,128)S(1)} %get-tuple-element.49), channel_id=1, source_target_pairs={{2,0},{4,2},{6,4},{8,6},{10,8},{12,10},{14,12},{16,14},{18,16},{20... | collective-permute-start | bytes 110600 | tf_op jit(solution)/shard_map/ppermute | solution.py:997
  51.2 0.7 copy-start.7
  51.9 48.4 %all-to-all-start.2 = ((f32[8,8,64,128]{3,2,1,0:T(8,128)}), f32[8,8,64,128]{3,2,1,0:T(8,128)S(1)}, u32[]{:S(2)}, u32[]{:S(2)}) async-start(f32[8,8,64,128]{3,2,1,0:T(8,128)} %bitcast.8), calls=%async_computation.2 | async-start | bytes 4194304 | tf_op jit(solution)/shard_map/all_to_all | solution.py:1010
  57.3 40.4 %collective-permute-start.6 = (f32[28,64,128]{2,1,0:T(8,128)}, f32[28,64,128]{2,1,0:T(8,128)}, u32[]{:S(2)}, u32[]{:S(2)}) collective-permute-start(f32[28,64,128]{2,1,0:T(8,128)} %slice.36), channel_id=1, source_target_pairs={{0,16},{2,18},{4,20},{6,22},{8,24},{10,26},{12,28},{14,30},{16,0},... | collective-permute-start | bytes 2752520 | tf_op jit(solution)/shard_map/ppermute | solution.py:1009
  58.0 2.3 collective-permute-start.5
  60.3 0.8 copy-start.3
  100.3 1.3 copy-start.1
  168.6 7.9 %copy-start.12 = (s32[32,3]{0,1:T(4,128)S(1)}, s32[32,3]{0,1:T(4,128)}, u32[]{:S(2)}) copy-start(s32[32,3]{0,1:T(4,128)} %param.13) | copy-start | bytes 1156
  168.6 8.6 %copy-start = (f32[3,2048]{0,1:T(8,128)S(1)}, f32[3,2048]{0,1:T(8,128)}, u32[]{:S(2)}) copy-start(f32[3,2048]{0,1:T(8,128)} %copy.51) | copy-start | bytes 73732
  168.6 33.6 %all-to-all-start.3 = ((f32[8,520,128]{2,1,0:T(8,128)}), f32[8,520,128]{2,1,0:T(8,128)}, u32[]{:S(2)}, u32[]{:S(2)}) async-start(f32[8,520,128]{2,1,0:T(8,128)} %payload_rows.1), calls=%async_computation.3 | async-start | bytes 4259840 | tf_op jit(solution)/shard_map/all_to_all | solution.py:1036
  203.0 32.2 %collective-permute-start.7 = (f32[8,8,128]{2,1,0:T(8,128)S(1)}, f32[8,8,128]{2,1,0:T(8,128)S(1)}, u32[]{:S(2)}, u32[]{:S(2)}) collective-permute-start(f32[8,8,128]{2,1,0:T(8,128)S(1)} %slice.54), channel_id=1, source_target_pairs={{0,16},{2,18},{4,20},{6,22},{8,24},{10,26},{12,28},{14,30},{16,0},... | collective-permute-start | bytes 98312 | tf_op jit(solution)/shard_map/ppermute | solution.py:1056
  225.2 23.5 %all-to-all-start.4 = ((f32[16,32,128]{2,1,0:T(8,128)}), f32[16,32,128]{2,1,0:T(8,128)S(1)}, u32[]{:S(2)}, u32[]{:S(2)}) async-start(f32[16,32,128]{2,1,0:T(8,128)} %get-tuple-element.83), calls=%async_computation.4 | async-start | bytes 524288 | tf_op jit(solution)/shard_map/all_to_all | solution.py:1065

commit v8 on v7

--- a/solution.py
+++ b/solution.py
@@ -328,7 +328,7 @@
         compiler_params=pltpu.CompilerParams(vmem_limit_bytes=vmem_bytes),
         name="near_products",
         cost_estimate=pl.CostEstimate(
-            flops=10**6, bytes_accessed=10**4, transcendentals=0
+            flops=10**10, bytes_accessed=10**7, transcendentals=0
         ),
     )(mask, rows, coords, targets)
 
@@ -641,19 +641,20 @@
         scratch_shapes=[pltpu.VMEM((leaves * rank, rank), jnp.float32)],
         compiler_params=pltpu.CompilerParams(vmem_limit_bytes=vmem_bytes),
         name="bases",
-        cost_estimate=pl.CostEstimate(flops=10**6, bytes_accessed=10**4, transcendentals=0),
+        cost_estimate=pl.CostEstimate(flops=10**10, bytes_accessed=10**7, transcendentals=0),
     )(inverse, ratio, top, sketched)
 
 
-def top_body(packed_ref, transfer_ref, paths_ref, children_ref, source, current, left, inverse, squared, child, lowest, nat_inverse, nat_child, *, rank, levels):
-    branches, packed_rows_each, width = packed_ref.shape
-    nodes = branches // 2
+def top_body(side_ref, mine_ref, mirrored_ref, transfer_ref, paths_ref, children_ref, source, current, left, inverse, squared, child, lowest, nat_inverse, nat_child, *, rank, levels):
+    half, packed_rows_each, width = mine_ref.shape
+    nodes = half
     every = width // rank
-    flat = packed_ref[...].reshape(branches * packed_rows_each, width)
-    for part in range(every):
-        children_ref[pl.ds(part, branches * packed_rows_each, stride=every), :] = flat[
-            :, part * rank : (part + 1) * rank
-        ]
+    count = half * packed_rows_each
+    for ref, side in ((mine_ref, side_ref[0]), (mirrored_ref, 1 - side_ref[0])):
+        flat = ref[...].reshape(count, width)
+        base = pl.multiple_of(side * (half * rank), half * rank)
+        for part in range(every):
+            children_ref[pl.ds(base + part, count, stride=every), :] = flat[:, part * rank : (part + 1) * rank]
     for node in range(nodes):
         both = children_ref[2 * node * rank : (2 * node + 2) * rank, :]
         source[node * rank : (node + 1) * rank, :] = lax.dot_general(
@@ -708,14 +709,14 @@
         paths_ref[branch * rank : (branch + 1) * rank, :] = above[branch]
 
 
-def top_factors(children, rank):
-    branches = children.shape[0]
+def top_factors(side, mine, mirrored, rank):
+    branches = 2 * mine.shape[0]
     levels = branches.bit_length() - 1
     nodes = branches // 2
     natural = pltpu.VMEM((levels, nodes * rank, rank), jnp.float32)
     return pl.pallas_call(
         functools.partial(top_body, rank=rank, levels=levels),
-        in_specs=[vmem_spec],
+        in_specs=[pl.BlockSpec(memory_space=pltpu.SMEM), vmem_spec, vmem_spec],
         out_specs=[vmem_spec] * 2,
         out_shape=[
             jax.ShapeDtypeStruct((branches - 1, rank, 2 * rank), jnp.float32),
@@ -730,7 +731,7 @@
         compiler_params=pltpu.CompilerParams(vmem_limit_bytes=vmem_bytes),
         name="top_factors",
         cost_estimate=pl.CostEstimate(flops=10**10, bytes_accessed=10**7, transcendentals=0),
-    )(children)
+    )(side, mine, mirrored)
 
 
 def exchange_sum(pieces, axis):
@@ -869,55 +870,46 @@
     )(asked, side, mine, partner)
 
 
-def payload_body(asked_ref, side_ref, early_ref, late_ref, child_ref, out_ref, sems, *, cap):
-    early = early_ref.shape[0]
-    peers = out_ref.shape[0]
-    rows = child_ref.shape[0]
+def payload_body(asked_ref, side_ref, rows_ref, child_ref, out_ref, *, cap):
     base = (1 - side_ref[0]) * cap
 
-    def place(peer, entry):
-        return out_ref.at[peer, pl.ds(LEAF * entry, LEAF)], sems.at[peer, entry]
-
-    def child_place(peer):
-        return out_ref.at[peer, pl.ds(LEAF * cap, rows)], sems.at[peer, cap]
-
-    for peer in range(peers):
+    def one(peer, carry):
         for entry in range(cap):
-            leaf = asked_ref[peer, base + entry]
-            target, sem = place(peer, entry)
-
-            @pl.when(leaf < early)
-            def _():
-                pltpu.make_async_copy(early_ref.at[leaf], target, sem).start()
-
-            @pl.when(leaf >= early)
-            def _():
-                pltpu.make_async_copy(late_ref.at[leaf - early], target, sem).start()
-
-        target, sem = child_place(peer)
-        pltpu.make_async_copy(child_ref, target, sem).start()
-    for peer in range(peers):
-        for entry in range(cap):
-            target, sem = place(peer, entry)
-            pltpu.make_async_copy(late_ref.at[0], target, sem).wait()
-        target, sem = child_place(peer)
-        pltpu.make_async_copy(child_ref, target, sem).wait()
-
-
-def payload_rows(asked, side, early, late, child):
+            out_ref[peer, LEAF * entry : LEAF * (entry + 1), :] = rows_ref[asked_ref[peer, base + entry]]
+        out_ref[peer, LEAF * cap :, :] = child_ref[...]
+        return carry
+
+    lax.fori_loop(0, out_ref.shape[0], one, 0)
+
+
+def payload_rows(asked, side, rows, child):
     half = asked.shape[0]
     cap = asked.shape[1] // 2
-    smem = pl.BlockSpec(memory_space=pltpu.SMEM)
-    anywhere = pl.BlockSpec(memory_space=pl.ANY)
     return pl.pallas_call(
         functools.partial(payload_body, cap=cap),
-        in_specs=[smem, smem, anywhere, anywhere, anywhere],
-        out_specs=anywhere,
-        out_shape=jax.ShapeDtypeStruct((half, cap * LEAF + child.shape[0], late.shape[2]), jnp.float32),
-        scratch_shapes=[pltpu.SemaphoreType.DMA((half, cap + 1))],
+        in_specs=[pl.BlockSpec(memory_space=pltpu.SMEM)] * 2 + [vmem_spec] * 2,
+        out_specs=vmem_spec,
+        out_shape=jax.ShapeDtypeStruct((half, cap * LEAF + child.shape[0], rows.shape[2]), jnp.float32),
         compiler_params=pltpu.CompilerParams(vmem_limit_bytes=vmem_bytes),
         name="payload_rows",
-    )(asked, side, early, late, child)
+    )(asked, side, rows, child)
+
+
+def root_body(paths_ref, parts_ref, root_ref):
+    root_ref[...] = lax.dot_general(
+        paths_ref[...], parts_ref[...], tn_dims, precision=highest, preferred_element_type=jnp.float32
+    )
+
+
+def root_product(paths, parts):
+    return pl.pallas_call(
+        root_body,
+        in_specs=[vmem_spec] * 2,
+        out_specs=vmem_spec,
+        out_shape=jax.ShapeDtypeStruct((paths.shape[1], parts.shape[1]), jnp.float32),
+        compiler_params=pltpu.CompilerParams(vmem_limit_bytes=vmem_bytes),
+        name="root_product",
+    )(paths, parts)
 
 
 def two_rows(values, rows):
@@ -966,17 +958,6 @@
     targets = jnp.transpose(coords, (0, 2, 1))
     rows = jnp.transpose(samples.reshape(samp_dev, leaves, LEAF), (1, 2, 0))
 
-    small_sent = packed_rows(asked, side_ref, mine, partner, cap, leaves)
-    small_got = lax.all_to_all(
-        small_sent, "leaf", split_axis=0, concat_axis=0, axis_index_groups=groups, tiled=True
-    )
-    total, group_leaf, group_count, group_slots = group_tables(far_slots, far_count)
-
-    early = leaves // 8
-    rows_out, unused = lax.optimization_barrier((rows, small_sent))
-    partner_early = lax.ppermute(rows_out[:early], "leaf", mirror)
-    rows_late = rows_out[early:]
-
     forward = [(i, i + 1) for i in range(branches - 1)]
     backward = [(target, source) for source, target in forward]
     width = max(samp_dev, LEAF)
@@ -992,21 +973,24 @@
             axis=0,
         )
 
-    last, first, unused = lax.optimization_barrier((edge((leaves - 1) * LEAF), edge(0), small_sent))
-    low_edge = lax.ppermute(last, "leaf", forward)
-    high_edge = lax.ppermute(first, "leaf", backward)
+    low_edge = lax.ppermute(edge((leaves - 1) * LEAF), "leaf", forward)
+    high_edge = lax.ppermute(edge(0), "leaf", backward)
+
+    tables = group_tables(far_slots, far_count)
+    asked, low_edge, high_edge, rows, targets, tables = lax.optimization_barrier(
+        (asked, low_edge, high_edge, rows, targets, tables)
+    )
+    total, group_leaf, group_count, group_slots = tables
+    small_sent = packed_rows(asked, side_ref, mine, partner, cap, leaves)
+    small_got = lax.all_to_all(
+        small_sent, "leaf", split_axis=0, concat_axis=0, axis_index_groups=groups, tiled=True
+    )
+
+    rows_out, unused = lax.optimization_barrier((rows, small_sent))
+    partner_rows = lax.ppermute(rows_out, "leaf", mirror)
 
     own_asked = lax.dynamic_slice_in_dim(asked, side * cap, cap, axis=1)
     own_sent = rows_out[own_asked.reshape(-1)].reshape(half, cap, LEAF, samp_dev)
-    (
-        own_sent, rows_late, partner_early, low_edge, high_edge, targets, total, group_leaf, group_count, group_slots,
-    ) = lax.optimization_barrier(
-        (
-            own_sent, rows_late, partner_early, low_edge, high_edge, targets,
-            total, group_leaf, group_count, group_slots,
-        )
-    )
-    partner_late = lax.ppermute(rows_late, "leaf", mirror)
     own_got = lax.all_to_all(
         own_sent, "leaf", split_axis=0, concat_axis=0, axis_index_groups=groups, tiled=True
     )
@@ -1031,8 +1015,8 @@
 
     levels = leaves.bit_length()
     inverse, ratio, top_inverse, own_child = branch_factors(gram, levels, min(samp_dev, LANES))
-    own_child, own_got, partner_late = lax.optimization_barrier((own_child, own_got, partner_late))
-    payload = payload_rows(asked, side_ref, partner_early, partner_late, own_child)
+    own_child, own_got, partner_rows = lax.optimization_barrier((own_child, own_got, partner_rows))
+    payload = payload_rows(asked, side_ref, partner_rows, own_child)
     arrived = lax.all_to_all(
         payload, "leaf", split_axis=0, concat_axis=0, axis_index_groups=groups, tiled=True
     )
@@ -1054,21 +1038,15 @@
 
     children = arrived[:, cap * LEAF :]
     mirrored = lax.ppermute(children, "leaf", mirror)
-    children = jnp.concatenate(
-        [jnp.where(side == 0, children, mirrored), jnp.where(side == 0, mirrored, children)], axis=0
-    )
-
     weights, near_sample = lax.optimization_barrier((weights, near_sample))
     far_sample, branch_samples, copies = far_products(
         total, group_leaf, group_slots, side_ref, own_got, arrived, high, low, weights, branches
     )
     everyone = lax.all_to_all(copies, "leaf", split_axis=0, concat_axis=0, tiled=True)
-    children, unused = lax.optimization_barrier((children, branch_samples))
-    transfer_t, paths = top_factors(children, rank)
+    children, mirrored, unused = lax.optimization_barrier((children, mirrored, branch_samples))
+    transfer_t, paths = top_factors(side_ref, children, mirrored, rank)
     top_transfer = jnp.swapaxes(transfer_t, 1, 2)
-    root_sample = lax.dot_general(
-        paths, everyone.reshape(branches * rank, samp_dev), tn_dims, precision=highest
-    )
+    root_sample = root_product(paths, everyone.reshape(branches * rank, samp_dev))
     return (far_sample, near_sample, leaf_basis, branch_samples, top_transfer, root_sample)
 
 

time: 252 us -> 178 us (0.71)
  Pallas kernels: 129 us -> 68.7 us
  waiting for transfers between devices: 50.9 us -> 44.6 us
  starting transfers between devices: 45.9 us -> 41.7 us
  other arithmetic: 7.77 us -> 3.6 us
  local copies, waits for them, and re-layouts: 14.3 us -> 17.3 us
    pallas_call x1 -> x2, Pallas kernels: 67 us -> 4.7 us  [the longest x1 2.78 us: payload_rows(): pl.pallas_call(functools.partial(payload_body, cap=cap), in_specs=[pl.Blo...]
    all_to_all x1, waiting for transfers between devices: 23.3 us -> 15.6 us  [on_device(): lax.all_to_all(payload, 'leaf', split_axis=0, concat_axis=0, axis_index_g...]
    all_to_all x1, waiting for transfers between devices: 0.01 us -> 7.19 us  [on_device(): lax.all_to_all(small_sent, 'leaf', split_axis=0, concat_axis=0, axis_inde...]
    ppermute x1, waiting for transfers between devices: 8.41 us -> 3.74 us  [on_device(): partner = lax.ppermute(mine, 'leaf', mirror)]
    unnamed x31 -> x37, local copies, waits for them, and re-layouts: 5.37 us -> 8.17 us
    all_to_all x1, starting transfers between devices: 9.95 us -> 7.18 us  [on_device(): lax.all_to_all(copies, 'leaf', split_axis=0, concat_axis=0, tiled=True)]
    ppermute x4 -> x3, starting transfers between devices: 9.36 us -> 7.95 us  [the longest x1 3.93 us: on_device(): low_edge = lax.ppermute(edge((leaves - 1) * LEAF), 'leaf', forward)]
    ppermute x4 -> x3, waiting for transfers between devices: 14.3 us -> 13.8 us  [the longest x1 13.8 us: on_device(): partner_rows = lax.ppermute(rows_out, 'leaf', mirror)]
  transfers between devices with their start and end apart: 13 -> 12, of which waited for: 6 -> 6; matrix products, arithmetic and copies ran while one was open for 6% -> 8% of each run, Pallas kernels for 24% -> 35%
where the time goes in v8:
time: 178 us; the launch traced here: 177 us
  Pallas kernels  68.7 us (39%)
  waiting for transfers between devices  44.6 us (25%)
  starting transfers between devices  41.7 us (23%)
  local copies, waits for them, and re-layouts  17.3 us (10%)
  other arithmetic  3.6 us (2%)
    all_to_all x1, waiting for transfers between devices, on_device(): lax.all_to_all(payload, 'leaf', split_axis=0, concat_axis=0, axis_index_g...  15.6 us
    pallas_call x1, Pallas kernels, branch_factors(): pl.pallas_call(functools.partial(branch_body, rank=rank, levels=levels),...  14.5 us
    ppermute x1, waiting for transfers between devices, on_device(): partner_rows = lax.ppermute(rows_out, 'leaf', mirror)  13.8 us
    pallas_call x1, Pallas kernels, top_factors(): pl.pallas_call(functools.partial(top_body, rank=rank, levels=levels), in_...  11.9 us
    pallas_call x1, Pallas kernels, kernel_blocks(): pl.pallas_call(functools.partial(blocks_body, rank=rank, cap=cap), grid_s...  10.2 us
    pallas_call x1, Pallas kernels, far_products(): pl.pallas_call(functools.partial(far_body, cap=part // partner.shape[0]),...  9.1 us
    unnamed x37, local copies, waits for them, and re-layouts  8.17 us
    all_to_all x1, starting transfers between devices, on_device(): lax.all_to_all(payload, 'leaf', split_axis=0, concat_axis=0, axis_index_g...  7.43 us
  transfers between devices with their start and end apart: 12, of which 6 were waited for; matrix products, arithmetic and copies ran while one was open for 8% of the time, Pallas kernels for 35%

profile of v8, /device:TPU:0, one launch (start us, length us, event | category | flops | bytes accessed | tf_op | source)
XLA Modules:
  0.0 176.9 jit_solution(9847908152399385273)
XLA Ops:
  0.6 0.0 copy-start.8
  0.7 0.8 reshape.129
  1.4 0.1 copy.46
  1.5 0.7 all_to_all.20
  2.2 6.2 %all-to-all-start = ((s32[8,1,16]{2,1,0:T(1,128)}), s32[8,1,16]{2,1,0:T(1,128)S(1)}, u32[]{:S(2)}, u32[]{:S(2)}) async-start(s32[8,1,16]{2,1,0:T(1,128)} %bitcast.1), calls=%async_computation | async-start | bytes 8192 | tf_op jit(solution)/shard_map/all_to_all | solution.py:938
  8.4 2.6 %sketched_shares.1 = (f32[320,128]{1,0:T(8,128)}, f32[320,128]{1,0:T(8,128)}) custom-call(s32[1]{0:T(128)} %bitcast.14.place_ref, f32[32,128]{1,0:T(8,128)} %sketch_ref.1, f32[128,2048]{1,0:T(8,128)} %samples_ref.1, f32[3,2048]{1,0:T(4,128)} %points_ref.1), custom_call_target="tpu_custom_call" | custom-call | flops 1000000 | bytes 10000 | tf_op jit(solution)/shard_map/sketched_shares/pallas_call | solution.py:827
  11.0 0.0 collective-permute-start.2
  11.0 0.8 fusion.4
  11.8 1.5 copy.48
  13.4 3.9 %collective-permute-start = (f32[72,128]{1,0:T(8,128)S(1)}, f32[72,128]{1,0:T(8,128)S(1)}, u32[]{:S(2)}, u32[]{:S(2)}) collective-permute-start(f32[72,128]{1,0:T(8,128)S(1)} %select_maximum_fusion.1), channel_id=1, source_target_pairs={{0,2},{2,4},{4,6},{6,8},{8,10},{10,12},{12,14},{14,16},{16,18},{18... | collective-permute-start | bytes 110600 | tf_op jit(solution)/shard_map/ppermute | solution.py:976
  17.3 1.3 collective-permute-start.1
  18.7 0.1 select_reduce_fusion.2
  18.8 0.6 slice.34.total_ref
  19.4 0.1 convert_reduce_fusion
  19.5 0.1 select_reduce_fusion
  19.6 0.0 collective-permute-done.2
  19.7 0.0 copy-start.5
  19.7 5.1 %collective-permute-start.3 = (f32[320,128]{1,0:T(8,128)S(1)}, f32[320,128]{1,0:T(8,128)S(1)}, u32[]{:S(2)}, u32[]{:S(2)}) collective-permute-start(f32[320,128]{1,0:T(8,128)S(1)} %add.58.mine_ref), channel_id=1, source_target_pairs={{0,16},{2,18},{4,20},{6,22},{8,24},{10,26},{12,28},{14,30},{16,0},... | collective-permute-start | bytes 491528 | tf_op jit(solution)/shard_map/ppermute | solution.py:956
  24.7 1.2 compare_select_fusion.2.count_ref
  26.0 1.3 copy.51
  27.3 0.1 copy.52
  27.4 0.1 reshape.132
  27.5 0.7 gather_fusion
  28.1 0.7 reshape.133.slot_ref
  28.8 0.0 collective-permute-done.1
  28.8 3.7 %collective-permute-done.3.partner_ref = f32[320,128]{1,0:T(8,128)S(1)} collective-permute-done((f32[320,128]{1,0:T(8,128)S(1)}, f32[320,128]{1,0:T(8,128)S(1)}, u32[]{:S(2)}, u32[]{:S(2)}) %collective-permute-start.3) | collective-permute-done | bytes 163872 | tf_op jit(solution)/shard_map/ppermute | solution.py:956
  32.6 0.7 copy-done.6
  33.3 2.2 %packed_rows.1 = f32[8,160,128]{2,1,0:T(8,128)} custom-call(s32[8,16]{1,0:T(8,128)} %bitcast.60, s32[1]{0:T(128)} %bitcast.13.side_ref, f32[320,128]{1,0:T(8,128)} %copy-done.5, f32[320,128]{1,0:T(8,128)} %copy-done.6), custom_call_target="tpu_custom_call" | custom-call | tf_op jit(solution)/shard_map/packed_rows/pallas_call | solution.py:863
  35.4 3.5 %all-to-all-start.1 = ((f32[8,160,128]{2,1,0:T(8,128)}), f32[8,160,128]{2,1,0:T(8,128)S(1)}, u32[]{:S(2)}, u32[]{:S(2)}) async-start(f32[8,160,128]{2,1,0:T(8,128)} %packed_rows.1), calls=%async_computation.1 | async-start | bytes 1310720 | tf_op jit(solution)/shard_map/all_to_all | solution.py:985
  39.0 0.8 constant_dynamic-slice_fusion
  39.8 0.1 reshape.137
  39.8 2.1 %gather_fusion.1 = f32[64,64,128]{2,1,0:T(8,128)} fusion(f32[32,64,128]{2,1,0:T(8,128)S(1)} %bitcast.51, s32[1024]{0:T(1024)S(1)} %pad_clamp_fusion), kind=kCustom, calls=%fused_computation.1 | custom fusion | bytes 4194560 | tf_op jit(solution)/shard_map/gather | solution.py:993
  41.9 7.2 %all-to-all-done.1.own_ref = f32[8,160,128]{2,1,0:T(8,128)S(1)} async-done(((f32[8,160,128]{2,1,0:T(8,128)}), f32[8,160,128]{2,1,0:T(8,128)S(1)}, u32[]{:S(2)}, u32[]{:S(2)}) %all-to-all-start.1) | async-done | bytes 655392 | tf_op jit(solution)/shard_map/all_to_all | solution.py:985
  49.1 0.8 copy-done.2
  50.0 3.6 %all-to-all-start.2 = ((f32[8,8,64,128]{3,2,1,0:T(8,128)}), f32[8,8,64,128]{3,2,1,0:T(8,128)S(1)}, u32[]{:S(2)}, u32[]{:S(2)}) async-start(f32[8,8,64,128]{3,2,1,0:T(8,128)} %bitcast.17), calls=%async_computation.2 | async-start | bytes 4194304 | tf_op jit(solution)/shard_map/all_to_all | solution.py:994
  53.6 2.7 %collective-permute-start.5 = (f32[32,64,128]{2,1,0:T(8,128)S(1)}, f32[32,64,128]{2,1,0:T(8,128)}, u32[]{:S(2)}, u32[]{:S(2)}) collective-permute-start(f32[32,64,128]{2,1,0:T(8,128)S(1)} %bitcast.52), channel_id=1, source_target_pairs={{0,16},{2,18},{4,20},{6,22},{8,24},{10,26},{12,28},{14,30},{16,0},... | collective-permute-start | bytes 3145736 | tf_op jit(solution)/shard_map/ppermute | solution.py:990
  56.3 0.0 collective-permute-start.4
  56.3 2.3 %collective-permute-done.4.other_ref = f32[8,160,128]{2,1,0:T(8,128)S(1)} collective-permute-done((f32[8,160,128]{2,1,0:T(8,128)}, f32[8,160,128]{2,1,0:T(8,128)S(1)}, u32[]{:S(2)}, u32[]{:S(2)}) %collective-permute-start.4) | collective-permute-done | bytes 655392 | tf_op jit(solution)/shard_map/ppermute | solution.py:1000
  58.6 0.9 copy-done.4
  59.5 10.2 %kernel_blocks.1 = (bf16[128,64,256]{2,1,0:T(8,128)(2,1)}, bf16[128,64,256]{2,1,0:T(8,128)(2,1)}, f32[32,32,64]{2,1,0:T(8,128)}, f32[32,32,32]{2,1,0:T(8,128)}) custom-call(s32[1]{0:T(128)} %slice.34.total_ref, s32[128]{0:T(128)} %copy-done.12, s32[128]{0:T(128)} %compare_select_fusion.2.count_ref, s32[512]{0:T(512)} %reshape.133.slot_ref, ...), custom_call_target="tpu_custom_call" | custom-call | flops 1000000 | bytes 10000 | tf_op jit(solution)/shard_map/kernel_blocks/pallas_call | solution.py:144
  69.7 14.5 %branch_factors.1 = (f32[32,32,128]{2,1,0:T(8,128)}, f32[6,32,32,128]{3,2,1,0:T(8,128)}, f32[32,32]{1,0:T(8,128)}, f32[8,128]{1,0:T(8,128)}) custom-call(f32[1024,32]{1,0:T(8,128)} %bitcast.59), custom_call_target="tpu_custom_call" | custom-call | flops 1000000 | bytes 10000 | tf_op jit(solution)/shard_map/branch_factors/pallas_call | solution.py:587
  84.3 13.8 %collective-permute-done.5.rows_ref = f32[32,64,128]{2,1,0:T(8,128)} collective-permute-done((f32[32,64,128]{2,1,0:T(8,128)S(1)}, f32[32,64,128]{2,1,0:T(8,128)}, u32[]{:S(2)}, u32[]{:S(2)}) %collective-permute-start.5) | collective-permute-done | bytes 1048608 | tf_op jit(solution)/shard_map/ppermute | solution.py:990
  98.1 2.0 %all-to-all-done.2 = f32[8,8,64,128]{3,2,1,0:T(8,128)S(1)} async-done(((f32[8,8,64,128]{3,2,1,0:T(8,128)}), f32[8,8,64,128]{3,2,1,0:T(8,128)S(1)}, u32[]{:S(2)}, u32[]{:S(2)}) %all-to-all-start.2) | async-done | bytes 2097184 | tf_op jit(solution)/shard_map/all_to_all | solution.py:994
  100.1 1.3 copy-done.1
  101.4 2.8 %payload_rows.1 = f32[8,520,128]{2,1,0:T(8,128)} custom-call(s32[8,16]{1,0:T(8,128)} %bitcast.62, s32[1]{0:T(128)} %bitcast.13.side_ref, f32[32,64,128]{2,1,0:T(8,128)} %collective-permute-done.5.rows_ref, f32[8,128]{1,0:T(8,128)} %get-tuple-element.57.child_ref), custom_call_target="tpu_custom_call" | custom-call | tf_op jit(solution)/shard_map/payload_rows/pallas_call | solution.py:888
  104.2 7.4 %all-to-all-start.3 = ((f32[8,520,128]{2,1,0:T(8,128)}), f32[8,520,128]{2,1,0:T(8,128)}, u32[]{:S(2)}, u32[]{:S(2)}) async-start(f32[8,520,128]{2,1,0:T(8,128)} %payload_rows.1), calls=%async_computation.3 | async-start | bytes 4259840 | tf_op jit(solution)/shard_map/all_to_all | solution.py:1020
  111.6 0.1 copy.53
  111.7 0.6 reshape.140.mask_ref
  112.3 0.4 copy.55
  112.7 0.1 pad.23.clone
  112.8 0.1 maximum_maximum_fusion.1
  112.9 0.8 pad_maximum_fusion.coords_ref
  113.7 1.1 maximum_maximum_fusion.rows_ref
  114.9 6.1 %near_products.1 = f32[128,2048]{1,0:T(8,128)} custom-call(s32[96]{0:T(128)} %reshape.140.mask_ref, f32[35,64,128]{2,1,0:T(8,128)} %maximum_maximum_fusion.rows_ref, f32[35,8,128]{2,1,0:T(8,128)} %pad_maximum_fusion.coords_ref, f32[32,64,3]{2,1,0:T(8,128)} %bitcast.55), custom_call_target="tpu_custom_call" | custom-call | flops 10000000000 | bytes 10000000 | tf_op jit(solution)/shard_map/near_products/pallas_call | solution.py:315
  120.9 15.6 %all-to-all-done.3.partner_ref = f32[8,520,128]{2,1,0:T(8,128)} async-done(((f32[8,520,128]{2,1,0:T(8,128)}), f32[8,520,128]{2,1,0:T(8,128)}, u32[]{:S(2)}, u32[]{:S(2)}) %all-to-all-start.3) | async-done | bytes 2129952 | tf_op jit(solution)/shard_map/all_to_all | solution.py:1020
  136.5 0.8 slice.46.mine_ref
  137.3 0.7 collective-permute-start.6
  138.0 7.4 %bases.1 = (f32[32,2048]{1,0:T(8,128)}, f32[32,2048]{1,0:T(8,128)}) custom-call(f32[32,32,128]{2,1,0:T(8,128)} %get-tuple-element.60.inverse_ref, f32[6,32,32,128]{3,2,1,0:T(8,128)} %get-tuple-element.64.ratio_ref, f32[32,32]{1,0:T(8,128)} %get-tuple-element.65.top_ref, f32[32,32,64]{2,1,0:T(8,128)} %get-tuple-element.66.sketched_ref), custom_call_target="tpu_custom_call" | custom-call | flops 10000000000 | bytes 10000000 | tf_op jit(solution)/shard_map/bases/pallas_call | solution.py:636
  145.4 9.1 %far_products.1 = (f32[128,2048]{1,0:T(8,128)}, f32[32,128]{1,0:T(8,128)}, f32[16,32,128]{2,1,0:T(8,128)}) custom-call(s32[1]{0:T(128)} %slice.34.total_ref, s32[128]{0:T(128)} %copy-done.12, s32[512]{0:T(512)} %reshape.133.slot_ref, s32[1]{0:T(128)} %bitcast.13.side_ref, f32[64,64,128]{2,1,0:T(8,128)} %bitcast.57, ...), custom_call_target="tpu_custom_call" | custom-call | flops 1000000 | bytes 10000 | tf_op jit(solution)/shard_map/far_products/pallas_call | solution.py:238
  154.5 7.2 %all-to-all-start.4 = ((f32[16,32,128]{2,1,0:T(8,128)}), f32[16,32,128]{2,1,0:T(8,128)S(1)}, u32[]{:S(2)}, u32[]{:S(2)}) async-start(f32[16,32,128]{2,1,0:T(8,128)} %get-tuple-element.79), calls=%async_computation.4 | async-start | bytes 524288 | tf_op jit(solution)/shard_map/all_to_all | solution.py:1045
  161.7 0.6 copy-done.15
  162.3 11.9 %top_factors.1 = (f32[15,32,64]{2,1,0:T(8,128)}, f32[512,32]{1,0:T(8,128)}) custom-call(s32[1]{0:T(128)} %bitcast.13.side_ref, f32[8,8,128]{2,1,0:T(8,128)} %copy-done.10, f32[8,8,128]{2,1,0:T(8,128)} %copy-done.15), custom_call_target="tpu_custom_call" | custom-call | flops 10000000000 | bytes 10000000 | tf_op jit(solution)/shard_map/top_factors/pallas_call | solution.py:717
  174.2 0.7 copy-done.3
  174.9 1.9 %root_product.1 = f32[32,128]{1,0:T(8,128)} custom-call(f32[512,32]{1,0:T(8,128)} %get-tuple-element.78.paths_ref, f32[512,128]{1,0:T(8,128)} %bitcast.58), custom_call_target="tpu_custom_call" | custom-call | tf_op jit(solution)/shard_map/root_product/pallas_call | solution.py:905
  (45 shorter events, 0.2 us)
Async XLA Ops:
  0.6 25.3 %copy-start.8 = (f32[3,2048]{1,0:T(4,128)S(1)}, f32[3,2048]{1,0:T(4,128)}, u32[]{:S(2)}) copy-start(f32[3,2048]{1,0:T(4,128)} %points_ref.1) | copy-start | bytes 73732
  0.6 18.0 %copy-start.14 = (s32[32]{0:T(128)S(1)}, s32[32]{0:T(128)}, u32[]{:S(2)}) copy-start(s32[32]{0:T(128)} %param.12) | copy-start | bytes 388
  2.2 26.6 %all-to-all-start = ((s32[8,1,16]{2,1,0:T(1,128)}), s32[8,1,16]{2,1,0:T(1,128)S(1)}, u32[]{:S(2)}, u32[]{:S(2)}) async-start(s32[8,1,16]{2,1,0:T(1,128)} %bitcast.1), calls=%async_computation | async-start | bytes 8192 | tf_op jit(solution)/shard_map/all_to_all | solution.py:938
  11.0 8.6 %copy-start.7 = (f32[320,128]{1,0:T(8,128)S(1)}, f32[320,128]{1,0:T(8,128)}, u32[]{:S(2)}) copy-start(f32[320,128]{1,0:T(8,128)} %get-tuple-element.48) | copy-start | bytes 491524
  11.0 16.3 %copy-start.11 = (s32[32,16]{0,1:T(8,128)S(1)}, s32[32,16]{0,1:T(8,128)}, u32[]{:S(2)}) copy-start(s32[32,16]{0,1:T(8,128)} %param.11) | copy-start | bytes 6148
  11.0 8.6 %collective-permute-start.2 = (f32[320,128]{1,0:T(8,128)}, f32[320,128]{1,0:T(8,128)S(1)}, u32[]{:S(2)}, u32[]{:S(2)}) collective-permute-start(f32[320,128]{1,0:T(8,128)} %get-tuple-element.49), channel_id=1, source_target_pairs={{0,1},{1,0},{2,3},{3,2},{4,5},{5,4},{6,7},{7,6},{8,9},{9,8},{10,11... | collective-permute-start | bytes 491528 | tf_op jit(solution)/shard_map/ppermute | solution.py:945
  13.4 15.4 %collective-permute-start = (f32[72,128]{1,0:T(8,128)S(1)}, f32[72,128]{1,0:T(8,128)S(1)}, u32[]{:S(2)}, u32[]{:S(2)}) collective-permute-start(f32[72,128]{1,0:T(8,128)S(1)} %select_maximum_fusion.1), channel_id=1, source_target_pairs={{0,2},{2,4},{4,6},{6,8},{8,10},{10,12},{12,14},{14,16},{16,18},{18... | collective-permute-start | bytes 110600 | tf_op jit(solution)/shard_map/ppermute | solution.py:976
  17.3 11.5 %collective-permute-start.1 = (f32[72,128]{1,0:T(8,128)S(1)}, f32[72,128]{1,0:T(8,128)S(1)}, u32[]{:S(2)}, u32[]{:S(2)}) collective-permute-start(f32[72,128]{1,0:T(8,128)S(1)} %select_maximum_fusion), channel_id=1, source_target_pairs={{2,0},{4,2},{6,4},{8,6},{10,8},{12,10},{14,12},{16,14},{18,16},{20... | collective-permute-start | bytes 110600 | tf_op jit(solution)/shard_map/ppermute | solution.py:977
  19.5 15.9 %copy-start.12 = (s32[128]{0:T(128)}, s32[128]{0:T(128)S(1)}, u32[]{:S(2)}) copy-start(s32[128]{0:T(128)S(1)} %broadcast_minimum_fusion.leaf_ref) | copy-start | bytes 1540
  19.7 12.9 %copy-start.5 = (f32[320,128]{1,0:T(8,128)}, f32[320,128]{1,0:T(8,128)S(1)}, u32[]{:S(2)}) copy-start(f32[320,128]{1,0:T(8,128)S(1)} %add.58.mine_ref) | copy-start | bytes 491524
  19.7 12.9 %collective-permute-start.3 = (f32[320,128]{1,0:T(8,128)S(1)}, f32[320,128]{1,0:T(8,128)S(1)}, u32[]{:S(2)}, u32[]{:S(2)}) collective-permute-start(f32[320,128]{1,0:T(8,128)S(1)} %add.58.mine_ref), channel_id=1, source_target_pairs={{0,16},{2,18},{4,20},{6,22},{8,24},{10,26},{12,28},{14,30},{16,0},... | collective-permute-start | bytes 491528 | tf_op jit(solution)/shard_map/ppermute | solution.py:956
  28.8 3.8 %copy-start.9 = (s32[8,1,16]{2,1,0:T(1,128)}, s32[8,1,16]{2,1,0:T(1,128)S(1)}, u32[]{:S(2)}) copy-start(s32[8,1,16]{2,1,0:T(1,128)S(1)} %all-to-all-done) | copy-start | bytes 1540
  32.6 0.7 copy-start.6
  35.4 13.7 %all-to-all-start.1 = ((f32[8,160,128]{2,1,0:T(8,128)}), f32[8,160,128]{2,1,0:T(8,128)S(1)}, u32[]{:S(2)}, u32[]{:S(2)}) async-start(f32[8,160,128]{2,1,0:T(8,128)} %packed_rows.1), calls=%async_computation.1 | async-start | bytes 1310720 | tf_op jit(solution)/shard_map/all_to_all | solution.py:985
  49.1 0.8 copy-start.2
  50.0 50.1 %all-to-all-start.2 = ((f32[8,8,64,128]{3,2,1,0:T(8,128)}), f32[8,8,64,128]{3,2,1,0:T(8,128)S(1)}, u32[]{:S(2)}, u32[]{:S(2)}) async-start(f32[8,8,64,128]{3,2,1,0:T(8,128)} %bitcast.17), calls=%async_computation.2 | async-start | bytes 4194304 | tf_op jit(solution)/shard_map/all_to_all | solution.py:994
  53.6 44.5 %collective-permute-start.5 = (f32[32,64,128]{2,1,0:T(8,128)S(1)}, f32[32,64,128]{2,1,0:T(8,128)}, u32[]{:S(2)}, u32[]{:S(2)}) collective-permute-start(f32[32,64,128]{2,1,0:T(8,128)S(1)} %bitcast.52), channel_id=1, source_target_pairs={{0,16},{2,18},{4,20},{6,22},{8,24},{10,26},{12,28},{14,30},{16,0},... | collective-permute-start | bytes 3145736 | tf_op jit(solution)/shard_map/ppermute | solution.py:990
  56.3 2.3 %collective-permute-start.4 = (f32[8,160,128]{2,1,0:T(8,128)}, f32[8,160,128]{2,1,0:T(8,128)S(1)}, u32[]{:S(2)}, u32[]{:S(2)}) collective-permute-start(f32[8,160,128]{2,1,0:T(8,128)} %copy-done.2), channel_id=1, source_target_pairs={{0,1},{1,0},{2,3},{3,2},{4,5},{5,4},{6,7},{7,6},{8,9},{9,8},{10,11... | collective-permute-start | bytes 1966088 | tf_op jit(solution)/shard_map/ppermute | solution.py:1000
  58.6 0.9 copy-start.4
  100.1 1.3 copy-start.1
  104.2 7.4 %copy-start.13 = (s32[32,3]{0,1:T(4,128)S(1)}, s32[32,3]{0,1:T(4,128)}, u32[]{:S(2)}) copy-start(s32[32,3]{0,1:T(4,128)} %param.13) | copy-start | bytes 1156
  104.2 8.2 %copy-start = (f32[3,2048]{0,1:T(8,128)S(1)}, f32[3,2048]{0,1:T(8,128)}, u32[]{:S(2)}) copy-start(f32[3,2048]{0,1:T(8,128)} %copy.51) | copy-start | bytes 73732
  104.2 32.3 %all-to-all-start.3 = ((f32[8,520,128]{2,1,0:T(8,128)}), f32[8,520,128]{2,1,0:T(8,128)}, u32[]{:S(2)}, u32[]{:S(2)}) async-start(f32[8,520,128]{2,1,0:T(8,128)} %payload_rows.1), calls=%async_computation.3 | async-start | bytes 4259840 | tf_op jit(solution)/shard_map/all_to_all | solution.py:1020
  137.3 8.1 %copy-start.10 = (f32[8,8,128]{2,1,0:T(8,128)}, f32[8,8,128]{2,1,0:T(8,128)S(1)}, u32[]{:S(2)}) copy-start(f32[8,8,128]{2,1,0:T(8,128)S(1)} %slice.46.mine_ref) | copy-start | bytes 98308
  137.3 24.4 %collective-permute-start.6 = (f32[8,8,128]{2,1,0:T(8,128)S(1)}, f32[8,8,128]{2,1,0:T(8,128)S(1)}, u32[]{:S(2)}, u32[]{:S(2)}) collective-permute-start(f32[8,8,128]{2,1,0:T(8,128)S(1)} %slice.46.mine_ref), channel_id=1, source_target_pairs={{0,16},{2,18},{4,20},{6,22},{8,24},{10,26},{12,28},{14,30},{16,0},... | collective-permute-start | bytes 98312 | tf_op jit(solution)/shard_map/ppermute | solution.py:1040
  154.5 19.7 %all-to-all-start.4 = ((f32[16,32,128]{2,1,0:T(8,128)}), f32[16,32,128]{2,1,0:T(8,128)S(1)}, u32[]{:S(2)}, u32[]{:S(2)}) async-start(f32[16,32,128]{2,1,0:T(8,128)} %get-tuple-element.79), calls=%async_computation.4 | async-start | bytes 524288 | tf_op jit(solution)/shard_map/all_to_all | solution.py:1045
  161.7 0.6 copy-start.15
  174.2 0.7 copy-start.3

commit v9 on v8

--- a/solution.py
+++ b/solution.py
@@ -328,7 +328,7 @@
         compiler_params=pltpu.CompilerParams(vmem_limit_bytes=vmem_bytes),
         name="near_products",
         cost_estimate=pl.CostEstimate(
-            flops=10**10, bytes_accessed=10**7, transcendentals=0
+            flops=10**9, bytes_accessed=10**6, transcendentals=0
         ),
     )(mask, rows, coords, targets)
 
@@ -641,7 +641,7 @@
         scratch_shapes=[pltpu.VMEM((leaves * rank, rank), jnp.float32)],
         compiler_params=pltpu.CompilerParams(vmem_limit_bytes=vmem_bytes),
         name="bases",
-        cost_estimate=pl.CostEstimate(flops=10**10, bytes_accessed=10**7, transcendentals=0),
+        cost_estimate=pl.CostEstimate(flops=10**9, bytes_accessed=10**6, transcendentals=0),
     )(inverse, ratio, top, sketched)
 
 
@@ -870,46 +870,33 @@
     )(asked, side, mine, partner)
 
 
-def payload_body(asked_ref, side_ref, rows_ref, child_ref, out_ref, *, cap):
+def payload_body(asked_ref, side_ref, early_ref, late_ref, child_ref, out_ref, *, cap):
+    early = early_ref.shape[0]
     base = (1 - side_ref[0]) * cap
 
     def one(peer, carry):
         for entry in range(cap):
-            out_ref[peer, LEAF * entry : LEAF * (entry + 1), :] = rows_ref[asked_ref[peer, base + entry]]
+            leaf = asked_ref[peer, base + entry]
+            first = early_ref[jnp.minimum(leaf, early - 1)]
+            second = late_ref[jnp.maximum(leaf - early, 0)]
+            out_ref[peer, LEAF * entry : LEAF * (entry + 1), :] = jnp.where(leaf < early, first, second)
         out_ref[peer, LEAF * cap :, :] = child_ref[...]
         return carry
 
     lax.fori_loop(0, out_ref.shape[0], one, 0)
 
 
-def payload_rows(asked, side, rows, child):
+def payload_rows(asked, side, early, late, child):
     half = asked.shape[0]
     cap = asked.shape[1] // 2
     return pl.pallas_call(
         functools.partial(payload_body, cap=cap),
-        in_specs=[pl.BlockSpec(memory_space=pltpu.SMEM)] * 2 + [vmem_spec] * 2,
+        in_specs=[pl.BlockSpec(memory_space=pltpu.SMEM)] * 2 + [vmem_spec] * 3,
         out_specs=vmem_spec,
-        out_shape=jax.ShapeDtypeStruct((half, cap * LEAF + child.shape[0], rows.shape[2]), jnp.float32),
+        out_shape=jax.ShapeDtypeStruct((half, cap * LEAF + child.shape[0], late.shape[2]), jnp.float32),
         compiler_params=pltpu.CompilerParams(vmem_limit_bytes=vmem_bytes),
         name="payload_rows",
-    )(asked, side, rows, child)
-
-
-def root_body(paths_ref, parts_ref, root_ref):
-    root_ref[...] = lax.dot_general(
-        paths_ref[...], parts_ref[...], tn_dims, precision=highest, preferred_element_type=jnp.float32
-    )
-
-
-def root_product(paths, parts):
-    return pl.pallas_call(
-        root_body,
-        in_specs=[vmem_spec] * 2,
-        out_specs=vmem_spec,
-        out_shape=jax.ShapeDtypeStruct((paths.shape[1], parts.shape[1]), jnp.float32),
-        compiler_params=pltpu.CompilerParams(vmem_limit_bytes=vmem_bytes),
-        name="root_product",
-    )(paths, parts)
+    )(asked, side, early, late, child)
 
 
 def two_rows(values, rows):
@@ -935,13 +922,10 @@
     mirror = [(i, (i + half) % branches) for i in range(branches)]
     side_ref = side.astype(jnp.int32).reshape(1)
     wanted = jnp.transpose(far_requests.reshape(2, half, cap), (1, 0, 2)).reshape(half, 2 * cap)
-    asked = lax.all_to_all(
-        wanted, "leaf", split_axis=0, concat_axis=0, axis_index_groups=groups, tiled=True
-    )
-
     if columns == 2:
         place = column.astype(jnp.int32).reshape(1)
         mine, other = sketched_shares(place, sketch, samples, points)
+        wanted, other = lax.optimization_barrier((wanted, other))
         mine = mine + lax.ppermute(other, "cols", [(0, 1), (1, 0)])
     else:
         z_part = jnp.dot(sketch, samples, precision=highest)
@@ -954,9 +938,25 @@
         mine = jnp.concatenate([z_rows.reshape(-1, LANES), c_rows.reshape(-1, LANES)], axis=0)
 
     partner = lax.ppermute(mine, "leaf", mirror)
+    asked = lax.all_to_all(
+        wanted, "leaf", split_axis=0, concat_axis=0, axis_index_groups=groups, tiled=True
+    )
     coords = jnp.transpose(points.reshape(3, leaves, LEAF), (1, 0, 2))
     targets = jnp.transpose(coords, (0, 2, 1))
     rows = jnp.transpose(samples.reshape(samp_dev, leaves, LEAF), (1, 2, 0))
+
+    tables = group_tables(far_slots, far_count)
+    asked, rows, targets, tables = lax.optimization_barrier((asked, rows, targets, tables))
+    total, group_leaf, group_count, group_slots = tables
+    small_sent = packed_rows(asked, side_ref, mine, partner, cap, leaves)
+    small_got = lax.all_to_all(
+        small_sent, "leaf", split_axis=0, concat_axis=0, axis_index_groups=groups, tiled=True
+    )
+
+    early = leaves // 8
+    rows_out, unused = lax.optimization_barrier((rows, small_sent))
+    partner_early = lax.ppermute(rows_out[:early], "leaf", mirror)
+    rows_late = rows_out[early:]
 
     forward = [(i, i + 1) for i in range(branches - 1)]
     backward = [(target, source) for source, target in forward]
@@ -973,24 +973,16 @@
             axis=0,
         )
 
-    low_edge = lax.ppermute(edge((leaves - 1) * LEAF), "leaf", forward)
-    high_edge = lax.ppermute(edge(0), "leaf", backward)
-
-    tables = group_tables(far_slots, far_count)
-    asked, low_edge, high_edge, rows, targets, tables = lax.optimization_barrier(
-        (asked, low_edge, high_edge, rows, targets, tables)
-    )
-    total, group_leaf, group_count, group_slots = tables
-    small_sent = packed_rows(asked, side_ref, mine, partner, cap, leaves)
-    small_got = lax.all_to_all(
-        small_sent, "leaf", split_axis=0, concat_axis=0, axis_index_groups=groups, tiled=True
-    )
-
-    rows_out, unused = lax.optimization_barrier((rows, small_sent))
-    partner_rows = lax.ppermute(rows_out, "leaf", mirror)
+    last, first, unused = lax.optimization_barrier((edge((leaves - 1) * LEAF), edge(0), small_sent))
+    low_edge = lax.ppermute(last, "leaf", forward)
+    high_edge = lax.ppermute(first, "leaf", backward)
 
     own_asked = lax.dynamic_slice_in_dim(asked, side * cap, cap, axis=1)
     own_sent = rows_out[own_asked.reshape(-1)].reshape(half, cap, LEAF, samp_dev)
+    own_sent, rows_late, partner_early, low_edge, high_edge = lax.optimization_barrier(
+        (own_sent, rows_late, partner_early, low_edge, high_edge)
+    )
+    partner_late = lax.ppermute(rows_late, "leaf", mirror)
     own_got = lax.all_to_all(
         own_sent, "leaf", split_axis=0, concat_axis=0, axis_index_groups=groups, tiled=True
     )
@@ -1015,8 +1007,8 @@
 
     levels = leaves.bit_length()
     inverse, ratio, top_inverse, own_child = branch_factors(gram, levels, min(samp_dev, LANES))
-    own_child, own_got, partner_rows = lax.optimization_barrier((own_child, own_got, partner_rows))
-    payload = payload_rows(asked, side_ref, partner_rows, own_child)
+    own_child, own_got, partner_late = lax.optimization_barrier((own_child, own_got, partner_late))
+    payload = payload_rows(asked, side_ref, partner_early, partner_late, own_child)
     arrived = lax.all_to_all(
         payload, "leaf", split_axis=0, concat_axis=0, axis_index_groups=groups, tiled=True
     )
@@ -1046,7 +1038,9 @@
     children, mirrored, unused = lax.optimization_barrier((children, mirrored, branch_samples))
     transfer_t, paths = top_factors(side_ref, children, mirrored, rank)
     top_transfer = jnp.swapaxes(transfer_t, 1, 2)
-    root_sample = root_product(paths, everyone.reshape(branches * rank, samp_dev))
+    root_sample = lax.dot_general(
+        paths, everyone.reshape(branches * rank, samp_dev), tn_dims, precision=highest
+    )
     return (far_sample, near_sample, leaf_basis, branch_samples, top_transfer, root_sample)
 
 

time: 178 us -> 173 us (0.972)
  waiting for transfers between devices: 44.6 us -> 37.9 us
  other arithmetic: 3.6 us -> 6.34 us
  matrix products: 0 us -> 2.13 us
  Pallas kernels: 68.7 us -> 66.8 us
    all_to_all x1, waiting for transfers between devices: 7.19 us -> 0.01 us  [on_device(): lax.all_to_all(small_sent, 'leaf', split_axis=0, concat_axis=0, axis_inde...]
    ppermute x1, starting transfers between devices: 5.08 us -> 2.66 us  [on_device(): partner = lax.ppermute(mine, 'leaf', mirror)]
    dot_general x0 -> x1, matrix products: none -> 2.13 us  [on_device(): lax.dot_general(paths, everyone.reshape(branches * rank, samp_dev), tn_di...]
    unnamed x37 -> x35, local copies, waits for them, and re-layouts: 8.17 us -> 6.24 us
    pallas_call x1 -> x0, Pallas kernels: 1.92 us -> none  [root_product(): pl.pallas_call(root_body, in_specs=[vmem_spec] * 2, out_specs=vmem_spec,...]
    all_to_all x1, starting transfers between devices: 3.6 us -> 5.49 us  [on_device(): lax.all_to_all(own_sent, 'leaf', split_axis=0, concat_axis=0, axis_index_...]
    ppermute x3 -> x4, starting transfers between devices: 7.95 us -> 9.29 us  [the longest x1 3.92 us: on_device(): low_edge = lax.ppermute(last, 'leaf', forward)]
    ppermute x3 -> x4, waiting for transfers between devices: 13.8 us -> 13.9 us  [the longest x1 12.4 us: on_device(): partner_late = lax.ppermute(rows_late, 'leaf', mirror)]
  transfers between devices with their start and end apart: 12 -> 13, of which waited for: 6 -> 6; matrix products, arithmetic and copies ran while one was open for 8% -> 9% of each run, Pallas kernels for 35% -> 34%
where the time goes in v9:
time: 173 us; the launch traced here: 171 us
  Pallas kernels  66.8 us (39%)
  starting transfers between devices  41.8 us (24%)
  waiting for transfers between devices  37.9 us (22%)
  local copies, waits for them, and re-layouts  15.8 us (9%)
  other arithmetic  6.34 us (4%)
  matrix products  2.13 us (1%)
    all_to_all x1, waiting for transfers between devices, on_device(): lax.all_to_all(payload, 'leaf', split_axis=0, concat_axis=0, axis_index_g...  15.6 us
    pallas_call x1, Pallas kernels, branch_factors(): pl.pallas_call(functools.partial(branch_body, rank=rank, levels=levels),...  14.5 us
    ppermute x1, waiting for transfers between devices, on_device(): partner_late = lax.ppermute(rows_late, 'leaf', mirror)  12.4 us
    pallas_call x1, Pallas kernels, top_factors(): pl.pallas_call(functools.partial(top_body, rank=rank, levels=levels), in_...  11.9 us
    pallas_call x1, Pallas kernels, kernel_blocks(): pl.pallas_call(functools.partial(blocks_body, rank=rank, cap=cap), grid_s...  10.1 us
    pallas_call x1, Pallas kernels, far_products(): pl.pallas_call(functools.partial(far_body, cap=part // partner.shape[0]),...  9.04 us
    all_to_all x1, starting transfers between devices, on_device(): lax.all_to_all(copies, 'leaf', split_axis=0, concat_axis=0, tiled=True)  7.51 us
    pallas_call x1, Pallas kernels, bases(): pl.pallas_call(functools.partial(basis_body, rank=rank, levels=levels), i...  7.39 us
  transfers between devices with their start and end apart: 13, of which 6 were waited for; matrix products, arithmetic and copies ran while one was open for 9% of the time, Pallas kernels for 34%

profile of v9, /device:TPU:0, one launch (start us, length us, event | category | flops | bytes accessed | tf_op | source)
XLA Modules:
  0.0 171.5 jit_solution(18257987232004493474)
XLA Ops:
  0.6 0.0 copy-start.7
  0.6 0.0 copy-start.2
  0.7 0.9 reshape.130
  1.5 0.1 copy.46
  1.6 0.7 reshape.131
  2.3 2.6 %sketched_shares.1 = (f32[320,128]{1,0:T(8,128)}, f32[320,128]{1,0:T(8,128)}) custom-call(s32[1]{0:T(128)} %bitcast.1.place_ref, f32[32,128]{1,0:T(8,128)} %sketch_ref.1, f32[128,2048]{1,0:T(8,128)} %samples_ref.1, f32[3,2048]{1,0:T(4,128)} %points_ref.1), custom_call_target="tpu_custom_call" | custom-call | flops 1000000 | bytes 10000 | tf_op jit(solution)/shard_map/sketched_shares/pallas_call | solution.py:827
  4.9 6.3 %all-to-all-start = ((s32[8,1,16]{2,1,0:T(1,128)}), s32[8,1,16]{2,1,0:T(1,128)S(1)}, u32[]{:S(2)}, u32[]{:S(2)}) async-start(s32[8,1,16]{2,1,0:T(1,128)} %bitcast.3), calls=%async_computation | async-start | bytes 8192 | tf_op jit(solution)/shard_map/all_to_all | solution.py:941
  11.2 0.7 and_select_fusion
  11.9 0.1 select_reduce_fusion.2
  12.0 0.6 slice.36.total_ref
  12.6 0.1 convert_reduce_fusion
  12.7 0.7 fusion.8
  13.3 0.7 select_reduce_fusion
  14.1 0.9 add.58.mine_ref
  15.0 0.0 copy-start.5
  15.1 2.7 %collective-permute-start.1 = (f32[320,128]{1,0:T(8,128)S(1)}, f32[320,128]{1,0:T(8,128)S(1)}, u32[]{:S(2)}, u32[]{:S(2)}) collective-permute-start(f32[320,128]{1,0:T(8,128)S(1)} %add.58.mine_ref), channel_id=1, source_target_pairs={{0,16},{2,18},{4,20},{6,22},{8,24},{10,26},{12,28},{14,30},{16,0},... | collective-permute-start | bytes 491528 | tf_op jit(solution)/shard_map/ppermute | solution.py:940
  17.7 1.1 compare_select_fusion.2.count_ref
  18.8 0.3 copy.48
  19.2 1.3 copy.49
  20.5 0.1 copy.50
  20.6 0.1 reshape.135
  20.7 0.7 gather_fusion
  21.3 0.7 reshape.136.slot_ref
  22.0 4.1 %collective-permute-done.1.partner_ref = f32[320,128]{1,0:T(8,128)S(1)} collective-permute-done((f32[320,128]{1,0:T(8,128)S(1)}, f32[320,128]{1,0:T(8,128)S(1)}, u32[]{:S(2)}, u32[]{:S(2)}) %collective-permute-start.1) | collective-permute-done | bytes 163872 | tf_op jit(solution)/shard_map/ppermute | solution.py:940
  26.1 0.7 copy-done.6
  26.8 2.2 %packed_rows.1 = f32[8,160,128]{2,1,0:T(8,128)} custom-call(s32[8,16]{1,0:T(8,128)} %bitcast.65, s32[1]{0:T(128)} %bitcast.13.side_ref, f32[320,128]{1,0:T(8,128)} %copy-done.5, f32[320,128]{1,0:T(8,128)} %copy-done.6), custom_call_target="tpu_custom_call" | custom-call | tf_op jit(solution)/shard_map/packed_rows/pallas_call | solution.py:863
  29.0 4.3 %all-to-all-start.1 = ((f32[8,160,128]{2,1,0:T(8,128)}), f32[8,160,128]{2,1,0:T(8,128)S(1)}, u32[]{:S(2)}, u32[]{:S(2)}) async-start(f32[8,160,128]{2,1,0:T(8,128)} %packed_rows.1), calls=%async_computation.1 | async-start | bytes 1310720 | tf_op jit(solution)/shard_map/all_to_all | solution.py:952
  33.3 0.1 fusion.4
  33.4 0.8 constant_dynamic-slice_fusion
  34.2 0.1 reshape.139
  34.3 3.4 %collective-permute-start.3 = (f32[4,64,128]{2,1,0:T(8,128)S(1)}, f32[4,64,128]{2,1,0:T(8,128)S(1)}, u32[]{:S(2)}, u32[]{:S(2)}) collective-permute-start(f32[4,64,128]{2,1,0:T(8,128)S(1)} %slice.38), channel_id=1, source_target_pairs={{0,16},{2,18},{4,20},{6,22},{8,24},{10,26},{12,28},{14,30},{16,0},... | collective-permute-start | bytes 393224 | tf_op jit(solution)/shard_map/ppermute | solution.py:958
  37.7 3.9 %collective-permute-start.4 = (f32[72,128]{1,0:T(8,128)S(1)}, f32[72,128]{1,0:T(8,128)S(1)}, u32[]{:S(2)}, u32[]{:S(2)}) collective-permute-start(f32[72,128]{1,0:T(8,128)S(1)} %get-tuple-element.64), channel_id=1, source_target_pairs={{0,2},{2,4},{4,6},{6,8},{8,10},{10,12},{12,14},{14,16},{16,18},{18... | collective-permute-start | bytes 110600 | tf_op jit(solution)/shard_map/ppermute | solution.py:977
  41.6 1.3 collective-permute-start.5
  42.9 1.0 slice.37
  43.9 2.1 %gather_fusion.1 = f32[64,64,128]{2,1,0:T(8,128)} fusion(f32[32,64,128]{2,1,0:T(8,128)S(1)} %bitcast.57, s32[1024]{0:T(1024)S(1)} %pad_clamp_fusion), kind=kCustom, calls=%fused_computation.1 | custom fusion | bytes 4194560 | tf_op jit(solution)/shard_map/gather | solution.py:981
  46.0 1.4 collective-permute-done.5
  47.5 0.9 copy-done.3
  48.4 5.5 %all-to-all-start.2 = ((f32[8,8,64,128]{3,2,1,0:T(8,128)}), f32[8,8,64,128]{3,2,1,0:T(8,128)S(1)}, u32[]{:S(2)}, u32[]{:S(2)}) async-start(f32[8,8,64,128]{3,2,1,0:T(8,128)} %bitcast.16), calls=%async_computation.2 | async-start | bytes 4194304 | tf_op jit(solution)/shard_map/all_to_all | solution.py:986
  53.9 0.7 collective-permute-start.6
  54.6 2.3 %collective-permute-done.2.other_ref = f32[8,160,128]{2,1,0:T(8,128)S(1)} collective-permute-done((f32[8,160,128]{2,1,0:T(8,128)}, f32[8,160,128]{2,1,0:T(8,128)S(1)}, u32[]{:S(2)}, u32[]{:S(2)}) %collective-permute-start.2) | collective-permute-done | bytes 655392 | tf_op jit(solution)/shard_map/ppermute | solution.py:992
  56.9 0.8 copy-done.4
  57.7 10.1 %kernel_blocks.1 = (bf16[128,64,256]{2,1,0:T(8,128)(2,1)}, bf16[128,64,256]{2,1,0:T(8,128)(2,1)}, f32[32,32,64]{2,1,0:T(8,128)}, f32[32,32,32]{2,1,0:T(8,128)}) custom-call(s32[1]{0:T(128)} %slice.36.total_ref, s32[128]{0:T(128)} %copy-done.12, s32[128]{0:T(128)} %compare_select_fusion.2.count_ref, s32[512]{0:T(512)} %reshape.136.slot_ref, ...), custom_call_target="tpu_custom_call" | custom-call | flops 1000000 | bytes 10000 | tf_op jit(solution)/shard_map/kernel_blocks/pallas_call | solution.py:144
  67.8 14.5 %branch_factors.1 = (f32[32,32,128]{2,1,0:T(8,128)}, f32[6,32,32,128]{3,2,1,0:T(8,128)}, f32[32,32]{1,0:T(8,128)}, f32[8,128]{1,0:T(8,128)}) custom-call(f32[1024,32]{1,0:T(8,128)} %bitcast.64), custom_call_target="tpu_custom_call" | custom-call | flops 1000000 | bytes 10000 | tf_op jit(solution)/shard_map/branch_factors/pallas_call | solution.py:587
  82.4 12.4 %collective-permute-done.6.late_ref = f32[28,64,128]{2,1,0:T(8,128)} collective-permute-done((f32[28,64,128]{2,1,0:T(8,128)}, f32[28,64,128]{2,1,0:T(8,128)}, u32[]{:S(2)}, u32[]{:S(2)}) %collective-permute-start.6) | collective-permute-done | bytes 917536 | tf_op jit(solution)/shard_map/ppermute | solution.py:985
  94.8 2.0 %all-to-all-done.2 = f32[8,8,64,128]{3,2,1,0:T(8,128)S(1)} async-done(((f32[8,8,64,128]{3,2,1,0:T(8,128)}), f32[8,8,64,128]{3,2,1,0:T(8,128)S(1)}, u32[]{:S(2)}, u32[]{:S(2)}) %all-to-all-start.2) | async-done | bytes 2097184 | tf_op jit(solution)/shard_map/all_to_all | solution.py:986
  96.8 1.3 copy-done.1
  98.2 2.9 %payload_rows.1 = f32[8,520,128]{2,1,0:T(8,128)} custom-call(s32[8,16]{1,0:T(8,128)} %bitcast.67, s32[1]{0:T(128)} %bitcast.13.side_ref, f32[4,64,128]{2,1,0:T(8,128)} %copy-done.8, f32[28,64,128]{2,1,0:T(8,128)} %collective-permute-done.6.late_ref, f32[8,128]{1,0:T(8,128)} %get-tuple-element.71.child_ref), custom_call_target="tpu_custom_call" | custom-call | tf_op jit(solution)/shard_map/payload_rows/pallas_call | solution.py:892
  101.1 6.2 %all-to-all-start.3 = ((f32[8,520,128]{2,1,0:T(8,128)}), f32[8,520,128]{2,1,0:T(8,128)}, u32[]{:S(2)}, u32[]{:S(2)}) async-start(f32[8,520,128]{2,1,0:T(8,128)} %payload_rows.1), calls=%async_computation.3 | async-start | bytes 4259840 | tf_op jit(solution)/shard_map/all_to_all | solution.py:1012
  107.2 0.1 copy.53
  107.3 0.6 reshape.142.mask_ref
  107.9 0.4 copy.55
  108.3 0.1 pad.23.clone
  108.4 0.1 maximum_maximum_fusion.1
  108.5 0.8 pad_maximum_fusion.coords_ref
  109.3 1.1 maximum_maximum_fusion.rows_ref
  110.5 6.1 %near_products.1 = f32[128,2048]{1,0:T(8,128)} custom-call(s32[96]{0:T(128)} %reshape.142.mask_ref, f32[35,64,128]{2,1,0:T(8,128)} %maximum_maximum_fusion.rows_ref, f32[35,8,128]{2,1,0:T(8,128)} %pad_maximum_fusion.coords_ref, f32[32,64,3]{2,1,0:T(8,128)} %bitcast.60), custom_call_target="tpu_custom_call" | custom-call | flops 1000000000 | bytes 1000000 | tf_op jit(solution)/shard_map/near_products/pallas_call | solution.py:315
  116.5 15.6 %all-to-all-done.3.partner_ref = f32[8,520,128]{2,1,0:T(8,128)} async-done(((f32[8,520,128]{2,1,0:T(8,128)}), f32[8,520,128]{2,1,0:T(8,128)}, u32[]{:S(2)}, u32[]{:S(2)}) %all-to-all-start.3) | async-done | bytes 2129952 | tf_op jit(solution)/shard_map/all_to_all | solution.py:1012
  132.1 0.8 slice.54.mine_ref
  132.9 7.4 %bases.1 = (f32[32,2048]{1,0:T(8,128)}, f32[32,2048]{1,0:T(8,128)}) custom-call(f32[32,32,128]{2,1,0:T(8,128)} %get-tuple-element.74.inverse_ref, f32[6,32,32,128]{3,2,1,0:T(8,128)} %get-tuple-element.78.ratio_ref, f32[32,32]{1,0:T(8,128)} %get-tuple-element.79.top_ref, f32[32,32,64]{2,1,0:T(8,128)} %get-tuple-element.80.sketched_ref), custom_call_target="tpu_custom_call" | custom-call | flops 1000000000 | bytes 1000000 | tf_op jit(solution)/shard_map/bases/pallas_call | solution.py:636
  140.3 9.0 %far_products.1 = (f32[128,2048]{1,0:T(8,128)}, f32[32,128]{1,0:T(8,128)}, f32[16,32,128]{2,1,0:T(8,128)}) custom-call(s32[1]{0:T(128)} %slice.36.total_ref, s32[128]{0:T(128)} %copy-done.12, s32[512]{0:T(512)} %reshape.136.slot_ref, s32[1]{0:T(128)} %bitcast.13.side_ref, f32[64,64,128]{2,1,0:T(8,128)} %bitcast.62, ...), custom_call_target="tpu_custom_call" | custom-call | flops 1000000 | bytes 10000 | tf_op jit(solution)/shard_map/far_products/pallas_call | solution.py:238
  149.3 7.5 %all-to-all-start.4 = ((f32[16,32,128]{2,1,0:T(8,128)}), f32[16,32,128]{2,1,0:T(8,128)S(1)}, u32[]{:S(2)}, u32[]{:S(2)}) async-start(f32[16,32,128]{2,1,0:T(8,128)} %get-tuple-element.93), calls=%async_computation.4 | async-start | bytes 524288 | tf_op jit(solution)/shard_map/all_to_all | solution.py:1037
  156.9 0.6 copy-done.14
  157.5 11.9 %top_factors.1 = (f32[15,32,64]{2,1,0:T(8,128)}, f32[512,32]{1,0:T(8,128)}) custom-call(s32[1]{0:T(128)} %bitcast.13.side_ref, f32[8,8,128]{2,1,0:T(8,128)} %copy-done.10, f32[8,8,128]{2,1,0:T(8,128)} %copy-done.14), custom_call_target="tpu_custom_call" | custom-call | flops 10000000000 | bytes 10000000 | tf_op jit(solution)/shard_map/top_factors/pallas_call | solution.py:717
  169.4 2.1 %fusion.5 = f32[32,128]{1,0:T(8,128)} fusion(f32[512,32]{1,0:T(8,128)} %get-tuple-element.92, f32[512,128]{1,0:T(8,128)S(1)} %bitcast.63), kind=kOutput, calls=%fused_computation.38 | convolution fusion | flops 25165824 | bytes 344064 | tf_op jit(solution)/shard_map/dot_general | solution.py:1041
  (48 shorter events, 0.2 us)
Async XLA Ops:
  0.6 18.5 %copy-start.7 = (f32[3,2048]{1,0:T(4,128)S(1)}, f32[3,2048]{1,0:T(4,128)}, u32[]{:S(2)}) copy-start(f32[3,2048]{1,0:T(4,128)} %points_ref.1) | copy-start | bytes 73732
  0.6 18.2 %copy-start.2 = (f32[128,2048]{1,0:T(8,128)S(1)}, f32[128,2048]{1,0:T(8,128)}, u32[]{:S(2)}) copy-start(f32[128,2048]{1,0:T(8,128)} %samples_ref.1) | copy-start | bytes 3145732
  4.9 15.6 %copy-start.11 = (s32[32,16]{0,1:T(8,128)S(1)}, s32[32,16]{0,1:T(8,128)}, u32[]{:S(2)}) copy-start(s32[32,16]{0,1:T(8,128)} %param.11) | copy-start | bytes 6148
  4.9 17.1 %all-to-all-start = ((s32[8,1,16]{2,1,0:T(1,128)}), s32[8,1,16]{2,1,0:T(1,128)S(1)}, u32[]{:S(2)}, u32[]{:S(2)}) async-start(s32[8,1,16]{2,1,0:T(1,128)} %bitcast.3), calls=%async_computation | async-start | bytes 8192 | tf_op jit(solution)/shard_map/all_to_all | solution.py:941
  11.2 2.9 %collective-permute-start = (f32[320,128]{1,0:T(8,128)}, f32[320,128]{1,0:T(8,128)S(1)}, u32[]{:S(2)}, u32[]{:S(2)}) collective-permute-start(f32[320,128]{1,0:T(8,128)} %get-tuple-element.58), channel_id=1, source_target_pairs={{0,1},{1,0},{2,3},{3,2},{4,5},{5,4},{6,7},{7,6},{8,9},{9,8},{10,11... | collective-permute-start | bytes 491528 | tf_op jit(solution)/shard_map/ppermute | solution.py:929
  13.3 8.0 %copy-start.12 = (s32[128]{0:T(128)}, s32[128]{0:T(128)S(1)}, u32[]{:S(2)}) copy-start(s32[128]{0:T(128)S(1)} %broadcast_minimum_fusion.leaf_ref) | copy-start | bytes 1540
  15.0 11.1 %copy-start.5 = (f32[320,128]{1,0:T(8,128)}, f32[320,128]{1,0:T(8,128)S(1)}, u32[]{:S(2)}) copy-start(f32[320,128]{1,0:T(8,128)S(1)} %add.58.mine_ref) | copy-start | bytes 491524
  15.1 11.1 %collective-permute-start.1 = (f32[320,128]{1,0:T(8,128)S(1)}, f32[320,128]{1,0:T(8,128)S(1)}, u32[]{:S(2)}, u32[]{:S(2)}) collective-permute-start(f32[320,128]{1,0:T(8,128)S(1)} %add.58.mine_ref), channel_id=1, source_target_pairs={{0,16},{2,18},{4,20},{6,22},{8,24},{10,26},{12,28},{14,30},{16,0},... | collective-permute-start | bytes 491528 | tf_op jit(solution)/shard_map/ppermute | solution.py:940
  22.0 4.1 %copy-start.9 = (s32[8,1,16]{2,1,0:T(1,128)}, s32[8,1,16]{2,1,0:T(1,128)S(1)}, u32[]{:S(2)}) copy-start(s32[8,1,16]{2,1,0:T(1,128)S(1)} %all-to-all-done) | copy-start | bytes 1540
  26.1 0.7 copy-start.6
  29.0 18.5 %all-to-all-start.1 = ((f32[8,160,128]{2,1,0:T(8,128)}), f32[8,160,128]{2,1,0:T(8,128)S(1)}, u32[]{:S(2)}, u32[]{:S(2)}) async-start(f32[8,160,128]{2,1,0:T(8,128)} %packed_rows.1), calls=%async_computation.1 | async-start | bytes 1310720 | tf_op jit(solution)/shard_map/all_to_all | solution.py:952
  34.3 13.2 %collective-permute-start.3 = (f32[4,64,128]{2,1,0:T(8,128)S(1)}, f32[4,64,128]{2,1,0:T(8,128)S(1)}, u32[]{:S(2)}, u32[]{:S(2)}) collective-permute-start(f32[4,64,128]{2,1,0:T(8,128)S(1)} %slice.38), channel_id=1, source_target_pairs={{0,16},{2,18},{4,20},{6,22},{8,24},{10,26},{12,28},{14,30},{16,0},... | collective-permute-start | bytes 393224 | tf_op jit(solution)/shard_map/ppermute | solution.py:958
  37.7 8.3 %collective-permute-start.4 = (f32[72,128]{1,0:T(8,128)S(1)}, f32[72,128]{1,0:T(8,128)S(1)}, u32[]{:S(2)}, u32[]{:S(2)}) collective-permute-start(f32[72,128]{1,0:T(8,128)S(1)} %get-tuple-element.64), channel_id=1, source_target_pairs={{0,2},{2,4},{4,6},{6,8},{8,10},{10,12},{12,14},{14,16},{16,18},{18... | collective-permute-start | bytes 110600 | tf_op jit(solution)/shard_map/ppermute | solution.py:977
  41.6 5.9 %collective-permute-start.5 = (f32[72,128]{1,0:T(8,128)S(1)}, f32[72,128]{1,0:T(8,128)S(1)}, u32[]{:S(2)}, u32[]{:S(2)}) collective-permute-start(f32[72,128]{1,0:T(8,128)S(1)} %get-tuple-element.65), channel_id=1, source_target_pairs={{2,0},{4,2},{6,4},{8,6},{10,8},{12,10},{14,12},{16,14},{18,16},{20... | collective-permute-start | bytes 110600 | tf_op jit(solution)/shard_map/ppermute | solution.py:978
  47.5 49.4 %copy-start.8 = (f32[4,64,128]{2,1,0:T(8,128)}, f32[4,64,128]{2,1,0:T(8,128)S(1)}, u32[]{:S(2)}) copy-start(f32[4,64,128]{2,1,0:T(8,128)S(1)} %collective-permute-done.3.early_ref) | copy-start | bytes 393220
  47.5 0.9 copy-start.3
  48.4 48.4 %all-to-all-start.2 = ((f32[8,8,64,128]{3,2,1,0:T(8,128)}), f32[8,8,64,128]{3,2,1,0:T(8,128)S(1)}, u32[]{:S(2)}, u32[]{:S(2)}) async-start(f32[8,8,64,128]{3,2,1,0:T(8,128)} %bitcast.16), calls=%async_computation.2 | async-start | bytes 4194304 | tf_op jit(solution)/shard_map/all_to_all | solution.py:986
  53.9 40.9 %collective-permute-start.6 = (f32[28,64,128]{2,1,0:T(8,128)}, f32[28,64,128]{2,1,0:T(8,128)}, u32[]{:S(2)}, u32[]{:S(2)}) collective-permute-start(f32[28,64,128]{2,1,0:T(8,128)} %slice.37), channel_id=1, source_target_pairs={{0,16},{2,18},{4,20},{6,22},{8,24},{10,26},{12,28},{14,30},{16,0},... | collective-permute-start | bytes 2752520 | tf_op jit(solution)/shard_map/ppermute | solution.py:985
  54.5 2.3 %collective-permute-start.2 = (f32[8,160,128]{2,1,0:T(8,128)}, f32[8,160,128]{2,1,0:T(8,128)S(1)}, u32[]{:S(2)}, u32[]{:S(2)}) collective-permute-start(f32[8,160,128]{2,1,0:T(8,128)} %copy-done.3), channel_id=1, source_target_pairs={{0,1},{1,0},{2,3},{3,2},{4,5},{5,4},{6,7},{7,6},{8,9},{9,8},{10,11... | collective-permute-start | bytes 1966088 | tf_op jit(solution)/shard_map/ppermute | solution.py:992
  56.9 0.8 copy-start.4
  96.8 1.3 copy-start.1
  101.1 6.2 %copy-start.13 = (s32[32,3]{0,1:T(4,128)S(1)}, s32[32,3]{0,1:T(4,128)}, u32[]{:S(2)}) copy-start(s32[32,3]{0,1:T(4,128)} %param.13) | copy-start | bytes 1156
  101.1 6.9 %copy-start = (f32[3,2048]{0,1:T(8,128)S(1)}, f32[3,2048]{0,1:T(8,128)}, u32[]{:S(2)}) copy-start(f32[3,2048]{0,1:T(8,128)} %copy.49) | copy-start | bytes 73732
  101.1 31.1 %all-to-all-start.3 = ((f32[8,520,128]{2,1,0:T(8,128)}), f32[8,520,128]{2,1,0:T(8,128)}, u32[]{:S(2)}, u32[]{:S(2)}) async-start(f32[8,520,128]{2,1,0:T(8,128)} %payload_rows.1), calls=%async_computation.3 | async-start | bytes 4259840 | tf_op jit(solution)/shard_map/all_to_all | solution.py:1012
  132.9 7.4 %copy-start.10 = (f32[8,8,128]{2,1,0:T(8,128)}, f32[8,8,128]{2,1,0:T(8,128)S(1)}, u32[]{:S(2)}) copy-start(f32[8,8,128]{2,1,0:T(8,128)S(1)} %slice.54.mine_ref) | copy-start | bytes 98308
  132.9 24.0 %collective-permute-start.7 = (f32[8,8,128]{2,1,0:T(8,128)S(1)}, f32[8,8,128]{2,1,0:T(8,128)S(1)}, u32[]{:S(2)}, u32[]{:S(2)}) collective-permute-start(f32[8,8,128]{2,1,0:T(8,128)S(1)} %slice.54.mine_ref), channel_id=1, source_target_pairs={{0,16},{2,18},{4,20},{6,22},{8,24},{10,26},{12,28},{14,30},{16,0},... | collective-permute-start | bytes 98312 | tf_op jit(solution)/shard_map/ppermute | solution.py:1032
  149.3 20.0 %all-to-all-start.4 = ((f32[16,32,128]{2,1,0:T(8,128)}), f32[16,32,128]{2,1,0:T(8,128)S(1)}, u32[]{:S(2)}, u32[]{:S(2)}) async-start(f32[16,32,128]{2,1,0:T(8,128)} %get-tuple-element.93), calls=%async_computation.4 | async-start | bytes 524288 | tf_op jit(solution)/shard_map/all_to_all | solution.py:1037
  156.8 0.6 copy-start.14

commit v10 on v9

--- a/solution.py
+++ b/solution.py
@@ -42,6 +42,16 @@
 
 def dot_exact_nt(a, b):
     return lax.dot_general(a, b, nt_dims, precision=highest, preferred_element_type=jnp.float32)
+
+
+def stacked_halves(value, axis):
+    return jnp.concatenate(halves(value), axis=axis)
+
+
+def quadrants(product):
+    rows, columns = product.shape[0] // 2, product.shape[1] // 2
+    top = product[:rows, :columns] + product[:rows, columns:]
+    return top + (product[rows:, :columns] + product[rows:, columns:])
 
 
 def dot_nt(a, b):
@@ -62,7 +72,7 @@
 def blocks_body(
     total_ref, leaf_ref, count_ref, slot_ref, place_ref,
     own_ref, other_ref, target_ref,
-    high_ref, low_ref, sketched_ref, gram_ref,
+    both_ref, sketched_ref, gram_ref,
     packed,
     *, rank, cap,
 ):
@@ -111,16 +121,10 @@
                 right = packed[slots[2 * half + 1]]
                 both = jnp.where(first, left, right)
                 values = kernel_half(both[rank : rank + 3], target, lane, (count - 2 * half) * LEAF)
-                high, low = halves(values)
-                high_ref[member, :, half * LANES : (half + 1) * LANES] = high
-                low_ref[member, :, half * LANES : (half + 1) * LANES] = low
+                both_ref[member, :, half * LANES : (half + 1) * LANES] = stacked_halves(values, 0)
                 z_parts.append(both[:rank])
-            z_high, z_low = halves(jnp.concatenate(z_parts, axis=1))
-            k_high = high_ref[member]
-            k_low = low_ref[member]
-            both = dot_nt(jnp.concatenate([z_high, z_low], axis=0), k_high)
-            update = both[:rank] + (both[rank:] + dot_nt(z_high, k_low))
-            sketched_ref[leaf] += update
+            z_both = stacked_halves(jnp.concatenate(z_parts, axis=1), 0)
+            sketched_ref[leaf] += quadrants(dot_nt(z_both, both_ref[member]))
 
     @pl.when(step == pl.num_programs(0) - 1)
     def _():
@@ -152,16 +156,14 @@
                 pl.BlockSpec(targets.shape, whole, pipeline_mode=once),
             ],
             out_specs=[
-                pl.BlockSpec((BATCH, LEAF, GROUP * LEAF), block_index),
-                pl.BlockSpec((BATCH, LEAF, GROUP * LEAF), block_index),
+                pl.BlockSpec((BATCH, 2 * LEAF, GROUP * LEAF), block_index),
                 pl.BlockSpec((leaves, rank, LEAF), whole),
                 pl.BlockSpec((leaves, rank, rank), whole),
             ],
             scratch_shapes=[pltpu.VMEM((slots, rank + SUB, LANES), jnp.float32)],
         ),
         out_shape=[
-            jax.ShapeDtypeStruct((groups, LEAF, GROUP * LEAF), jnp.bfloat16),
-            jax.ShapeDtypeStruct((groups, LEAF, GROUP * LEAF), jnp.bfloat16),
+            jax.ShapeDtypeStruct((groups, 2 * LEAF, GROUP * LEAF), jnp.bfloat16),
             jax.ShapeDtypeStruct((leaves, rank, LEAF), jnp.float32),
             jax.ShapeDtypeStruct((leaves, rank, rank), jnp.float32),
         ],
@@ -175,9 +177,9 @@
 
 def far_body(
     total_ref, leaf_ref, slot_ref, side_ref,
-    own_ref, partner_ref, high_ref, low_ref, weights_ref,
+    own_ref, partner_ref, blocks_ref, weights_ref,
     out_ref, projected_ref, copies_ref,
-    s_high, s_low, acc,
+    s_both, acc,
     *, cap,
 ):
     step = pl.program_id(0)
@@ -191,9 +193,9 @@
         def split(slot, carry):
             here = side_ref[0] * part + slot
             there = (1 - side_ref[0]) * part + slot
-            s_high[here], s_low[here] = halves(own_ref[slot])
+            s_both[here] = stacked_halves(own_ref[slot], 1)
             at = pl.multiple_of((slot % cap) * LEAF, LEAF)
-            s_high[there], s_low[there] = halves(partner_ref[slot // cap, pl.ds(at, LEAF), :])
+            s_both[there] = stacked_halves(partner_ref[slot // cap, pl.ds(at, LEAF), :], 1)
             return carry
 
         lax.fori_loop(0, part, split, 0, unroll=4)
@@ -204,11 +206,8 @@
             group = step * BATCH + member
             leaf = leaf_ref[group]
             slots = [slot_ref[group * GROUP + e] for e in range(GROUP)]
-            rows_high = jnp.concatenate([s_high[slot] for slot in slots], axis=0)
-            rows_low = jnp.concatenate([s_low[slot] for slot in slots], axis=0)
-            k_high = high_ref[member]
-            k_low = low_ref[member]
-            acc[leaf] += dot(k_high, rows_high) + (dot(k_high, rows_low) + dot(k_low, rows_high))
+            rows = jnp.concatenate([s_both[slot] for slot in slots], axis=0)
+            acc[leaf] += quadrants(dot(blocks_ref[member], rows))
 
     @pl.when(step == pl.num_programs(0) - 1)
     def _():
@@ -223,7 +222,7 @@
             out_ref[:, 2 * pair * LEAF : 2 * (pair + 1) * LEAF] = block.T
 
 
-def far_products(total, group_leaf, group_slots, side, own, partner, high, low, weights, branches):
+def far_products(total, group_leaf, group_slots, side, own, partner, blocks, weights, branches):
     part, unused, samp_dev = own.shape
     slots = 2 * part
     groups = group_leaf.shape[0]
@@ -243,8 +242,7 @@
             in_specs=[
                 pl.BlockSpec(own.shape, lambda *unused: (0, 0, 0), pipeline_mode=pl.Buffered(1)),
                 pl.BlockSpec(partner.shape, lambda *unused: (0, 0, 0), pipeline_mode=pl.Buffered(1)),
-                pl.BlockSpec((BATCH, LEAF, GROUP * LEAF), block_index),
-                pl.BlockSpec((BATCH, LEAF, GROUP * LEAF), block_index),
+                pl.BlockSpec((BATCH, 2 * LEAF, GROUP * LEAF), block_index),
                 pl.BlockSpec(weights.shape, lambda *unused: (0, 0), pipeline_mode=pl.Buffered(1)),
             ],
             out_specs=[
@@ -253,8 +251,7 @@
                 pl.BlockSpec((branches, weights.shape[0], samp_dev), lambda *unused: (0, 0, 0)),
             ],
             scratch_shapes=[
-                pltpu.VMEM((slots, LEAF, samp_dev), jnp.bfloat16),
-                pltpu.VMEM((slots, LEAF, samp_dev), jnp.bfloat16),
+                pltpu.VMEM((slots, LEAF, 2 * samp_dev), jnp.bfloat16),
                 pltpu.VMEM((leaves, LEAF, samp_dev), jnp.float32),
             ],
         ),
@@ -266,9 +263,9 @@
         compiler_params=pltpu.CompilerParams(vmem_limit_bytes=vmem_bytes),
         name="far_products",
         cost_estimate=pl.CostEstimate(
-            flops=10**6, bytes_accessed=10**4, transcendentals=0
+            flops=10**10, bytes_accessed=10**7, transcendentals=0
         ),
-    )(total, group_leaf, group_slots, side, own, partner, high, low, weights)
+    )(total, group_leaf, group_slots, side, own, partner, blocks, weights)
 
 
 NEAR_LEAVES = 8
@@ -284,8 +281,7 @@
         for member in range(2):
             leaf = step * NEAR_LEAVES + 2 * pair + member
             target = target_ref[leaf]
-            k_high = []
-            k_low = []
+            k_parts = []
             for half in range(2):
                 both = jnp.where(first, coords_ref[leaf + 2 * half], coords_ref[leaf + 2 * half + 1])
                 values = kernel_half(both, target, lane, LANES)
@@ -294,16 +290,10 @@
                     right = mask_ref[leaf * 3 + 1].astype(jnp.float32)
                 else:
                     right = jnp.float32(0.0)
-                high, low = halves(values * jnp.where(first, left, right))
-                k_high.append(high)
-                k_low.append(low)
-            k_high = jnp.concatenate(k_high, axis=1)
-            k_low = jnp.concatenate(k_low, axis=1)
+                k_parts.append(stacked_halves(values * jnp.where(first, left, right), 0))
             rows = rows_ref[pl.ds(leaf, 4)].reshape(4 * LEAF, samp_dev)
-            rows_high, rows_low = halves(rows)
-            results.append(
-                dot(k_high, rows_high) + (dot(k_high, rows_low) + dot(k_low, rows_high))
-            )
+            product = dot(jnp.concatenate(k_parts, axis=1), stacked_halves(rows, 1))
+            results.append(quadrants(product))
         block = jnp.concatenate(results, axis=0)
         out_ref[:, 2 * pair * LEAF : 2 * (pair + 1) * LEAF] = block.T
 
@@ -870,33 +860,29 @@
     )(asked, side, mine, partner)
 
 
-def payload_body(asked_ref, side_ref, early_ref, late_ref, child_ref, out_ref, *, cap):
-    early = early_ref.shape[0]
+def payload_body(asked_ref, side_ref, rows_ref, child_ref, out_ref, *, cap):
     base = (1 - side_ref[0]) * cap
 
     def one(peer, carry):
         for entry in range(cap):
-            leaf = asked_ref[peer, base + entry]
-            first = early_ref[jnp.minimum(leaf, early - 1)]
-            second = late_ref[jnp.maximum(leaf - early, 0)]
-            out_ref[peer, LEAF * entry : LEAF * (entry + 1), :] = jnp.where(leaf < early, first, second)
+            out_ref[peer, LEAF * entry : LEAF * (entry + 1), :] = rows_ref[asked_ref[peer, base + entry]]
         out_ref[peer, LEAF * cap :, :] = child_ref[...]
         return carry
 
     lax.fori_loop(0, out_ref.shape[0], one, 0)
 
 
-def payload_rows(asked, side, early, late, child):
+def payload_rows(asked, side, rows, child):
     half = asked.shape[0]
     cap = asked.shape[1] // 2
     return pl.pallas_call(
         functools.partial(payload_body, cap=cap),
-        in_specs=[pl.BlockSpec(memory_space=pltpu.SMEM)] * 2 + [vmem_spec] * 3,
+        in_specs=[pl.BlockSpec(memory_space=pltpu.SMEM)] * 2 + [vmem_spec] * 2,
         out_specs=vmem_spec,
-        out_shape=jax.ShapeDtypeStruct((half, cap * LEAF + child.shape[0], late.shape[2]), jnp.float32),
+        out_shape=jax.ShapeDtypeStruct((half, cap * LEAF + child.shape[0], rows.shape[2]), jnp.float32),
         compiler_params=pltpu.CompilerParams(vmem_limit_bytes=vmem_bytes),
         name="payload_rows",
-    )(asked, side, early, late, child)
+    )(asked, side, rows, child)
 
 
 def two_rows(values, rows):
@@ -925,8 +911,8 @@
     if columns == 2:
         place = column.astype(jnp.int32).reshape(1)
         mine, other = sketched_shares(place, sketch, samples, points)
-        wanted, other = lax.optimization_barrier((wanted, other))
         mine = mine + lax.ppermute(other, "cols", [(0, 1), (1, 0)])
+        wanted, mine = lax.optimization_barrier((wanted, mine))
     else:
         z_part = jnp.dot(sketch, samples, precision=highest)
         z_mine = exchange_sum(z_part.reshape(columns, share, leaves * LEAF), "cols")
@@ -953,10 +939,8 @@
         small_sent, "leaf", split_axis=0, concat_axis=0, axis_index_groups=groups, tiled=True
     )
 
-    early = leaves // 8
     rows_out, unused = lax.optimization_barrier((rows, small_sent))
-    partner_early = lax.ppermute(rows_out[:early], "leaf", mirror)
-    rows_late = rows_out[early:]
+    partner_rows = lax.ppermute(rows_out, "leaf", mirror)
 
     forward = [(i, i + 1) for i in range(branches - 1)]
     backward = [(target, source) for source, target in forward]
@@ -979,10 +963,7 @@
 
     own_asked = lax.dynamic_slice_in_dim(asked, side * cap, cap, axis=1)
     own_sent = rows_out[own_asked.reshape(-1)].reshape(half, cap, LEAF, samp_dev)
-    own_sent, rows_late, partner_early, low_edge, high_edge = lax.optimization_barrier(
-        (own_sent, rows_late, partner_early, low_edge, high_edge)
-    )
-    partner_late = lax.ppermute(rows_late, "leaf", mirror)
+    own_sent, low_edge, high_edge = lax.optimization_barrier((own_sent, low_edge, high_edge))
     own_got = lax.all_to_all(
         own_sent, "leaf", split_axis=0, concat_axis=0, axis_index_groups=groups, tiled=True
     )
@@ -1001,14 +982,14 @@
         small_other = jnp.concatenate([z_all[1], c_got], axis=1)
         place = jnp.zeros((1,), jnp.int32)
 
-    high, low, sketched, gram = kernel_blocks(
+    blocks, sketched, gram = kernel_blocks(
         total, group_leaf, group_count, group_slots, place, small_got, small_other, targets, rank, cap
     )
 
     levels = leaves.bit_length()
     inverse, ratio, top_inverse, own_child = branch_factors(gram, levels, min(samp_dev, LANES))
-    own_child, own_got, partner_late = lax.optimization_barrier((own_child, own_got, partner_late))
-    payload = payload_rows(asked, side_ref, partner_early, partner_late, own_child)
+    own_child, own_got, partner_rows = lax.optimization_barrier((own_child, own_got, partner_rows))
+    payload = payload_rows(asked, side_ref, partner_rows, own_child)
     arrived = lax.all_to_all(
         payload, "leaf", split_axis=0, concat_axis=0, axis_index_groups=groups, tiled=True
     )
@@ -1032,7 +1013,7 @@
     mirrored = lax.ppermute(children, "leaf", mirror)
     weights, near_sample = lax.optimization_barrier((weights, near_sample))
     far_sample, branch_samples, copies = far_products(
-        total, group_leaf, group_slots, side_ref, own_got, arrived, high, low, weights, branches
+        total, group_leaf, group_slots, side_ref, own_got, arrived, blocks, weights, branches
     )
     everyone = lax.all_to_all(copies, "leaf", split_axis=0, concat_axis=0, tiled=True)
     children, mirrored, unused = lax.optimization_barrier((children, mirrored, branch_samples))

time: 173 us -> 160 us (0.925)
  starting transfers between devices: 41.8 us -> 36.4 us
  waiting for transfers between devices: 37.9 us -> 34.3 us
  local copies, waits for them, and re-layouts: 15.8 us -> 13.4 us
    all_to_all x1, waiting for transfers between devices: 15.6 us -> 7.76 us  [on_device(): lax.all_to_all(payload, 'leaf', split_axis=0, concat_axis=0, axis_index_g...]
    ppermute x2 -> x1, waiting for transfers between devices: 12.4 us -> 18 us  [on_device(): partner_rows = lax.ppermute(rows_out, 'leaf', mirror)]
    ppermute x1, waiting for transfers between devices: 4.11 us -> 0.01 us  [on_device(): partner = lax.ppermute(mine, 'leaf', mirror)]
    all_to_all x1, waiting for transfers between devices: 0.01 us -> 3.97 us  [on_device(): lax.all_to_all(wanted, 'leaf', split_axis=0, concat_axis=0, axis_index_gr...]
    ppermute x2 -> x1, starting transfers between devices: 4.08 us -> 0.49 us  [on_device(): partner_rows = lax.ppermute(rows_out, 'leaf', mirror)]
    all_to_all x1, waiting for transfers between devices: 2.02 us -> 0.01 us  [on_device(): lax.all_to_all(own_sent, 'leaf', split_axis=0, concat_axis=0, axis_index_...]
    unnamed x35 -> x33, local copies, waits for them, and re-layouts: 6.24 us -> 4.94 us
  transfers between devices with their start and end apart: 13 -> 12, of which waited for: 6 -> 5; matrix products, arithmetic and copies ran while one was open for 9% -> 9% of each run, Pallas kernels for 34% -> 36%
where the time goes in v10:
time: 160 us; the launch traced here: 159 us
  Pallas kernels  65.1 us (41%)
  starting transfers between devices  36.4 us (23%)
  waiting for transfers between devices  34.3 us (21%)
  local copies, waits for them, and re-layouts  13.4 us (8%)
  other arithmetic  6.32 us (4%)
  matrix products  2.13 us (1%)
    ppermute x1, waiting for transfers between devices, on_device(): partner_rows = lax.ppermute(rows_out, 'leaf', mirror)  18 us
    pallas_call x1, Pallas kernels, branch_factors(): pl.pallas_call(functools.partial(branch_body, rank=rank, levels=levels),...  14.5 us
    pallas_call x1, Pallas kernels, top_factors(): pl.pallas_call(functools.partial(top_body, rank=rank, levels=levels), in_...  11.9 us
    pallas_call x1, Pallas kernels, kernel_blocks(): pl.pallas_call(functools.partial(blocks_body, rank=rank, cap=cap), grid_s...  10.2 us
    all_to_all x1, starting transfers between devices, on_device(): lax.all_to_all(copies, 'leaf', split_axis=0, concat_axis=0, tiled=True)  8.05 us
    pallas_call x1, Pallas kernels, far_products(): pl.pallas_call(functools.partial(far_body, cap=part // partner.shape[0]),...  7.79 us
    all_to_all x1, waiting for transfers between devices, on_device(): lax.all_to_all(payload, 'leaf', split_axis=0, concat_axis=0, axis_index_g...  7.76 us
    pallas_call x1, Pallas kernels, bases(): pl.pallas_call(functools.partial(basis_body, rank=rank, levels=levels), i...  7.38 us
  transfers between devices with their start and end apart: 12, of which 5 were waited for; matrix products, arithmetic and copies ran while one was open for 9% of the time, Pallas kernels for 36%

profile of v10, /device:TPU:0, one launch (start us, length us, event | category | flops | bytes accessed | tf_op | source)
XLA Modules:
  0.0 158.6 jit_solution(13902696498427859994)
XLA Ops:
  0.7 2.7 %sketched_shares.1 = (f32[320,128]{1,0:T(8,128)}, f32[320,128]{1,0:T(8,128)}) custom-call(s32[1]{0:T(128)} %bitcast.1.place_ref, f32[32,128]{1,0:T(8,128)} %sketch_ref.1, f32[128,2048]{1,0:T(8,128)} %samples_ref.1, f32[3,2048]{1,0:T(4,128)} %points_ref.1), custom_call_target="tpu_custom_call" | custom-call | flops 1000000 | bytes 10000 | tf_op jit(solution)/shard_map/sketched_shares/pallas_call | solution.py:817
  3.4 0.5 collective-permute-start
  3.8 0.7 and_select_fusion
  4.5 0.1 select_reduce_fusion.2
  4.6 0.6 slice.30.total_ref
  5.2 0.1 convert_reduce_fusion
  5.3 0.7 fusion.8
  6.0 0.8 reshape.130
  6.7 0.1 copy.46
  6.8 0.7 reshape.131
  7.5 0.7 select_reduce_fusion
  8.2 0.0 collective-permute-done
  8.2 0.9 add.55.mine_ref
  9.2 0.0 copy-start.5
  9.2 3.7 %collective-permute-start.1 = (f32[320,128]{1,0:T(8,128)S(1)}, f32[320,128]{1,0:T(8,128)S(1)}, u32[]{:S(2)}, u32[]{:S(2)}) collective-permute-start(f32[320,128]{1,0:T(8,128)S(1)} %add.55.mine_ref), channel_id=1, source_target_pairs={{0,16},{2,18},{4,20},{6,22},{8,24},{10,26},{12,28},{14,30},{16,0},... | collective-permute-start | bytes 491528 | tf_op jit(solution)/shard_map/ppermute | solution.py:926
  12.9 1.1 compare_select_fusion.2.count_ref
  13.9 0.3 copy.48
  14.3 1.3 copy.49
  15.6 4.7 %all-to-all-start = ((s32[8,1,16]{2,1,0:T(1,128)}), s32[8,1,16]{2,1,0:T(1,128)S(1)}, u32[]{:S(2)}, u32[]{:S(2)}) async-start(s32[8,1,16]{2,1,0:T(1,128)} %bitcast.3), calls=%async_computation | async-start | bytes 8192 | tf_op jit(solution)/shard_map/all_to_all | solution.py:927
  20.4 0.1 copy.50
  20.5 0.1 reshape.135
  20.5 0.7 gather_fusion
  21.2 0.7 reshape.136.slot_ref
  21.9 4.0 %all-to-all-done = s32[8,1,16]{2,1,0:T(1,128)S(1)} async-done(((s32[8,1,16]{2,1,0:T(1,128)}), s32[8,1,16]{2,1,0:T(1,128)S(1)}, u32[]{:S(2)}, u32[]{:S(2)}) %all-to-all-start) | async-done | bytes 544 | tf_op jit(solution)/shard_map/all_to_all | solution.py:927
  25.9 0.0 collective-permute-done.1.partner_ref
  25.9 0.6 copy-done.8
  26.4 0.1 copy-done.6
  26.5 2.2 %packed_rows.1 = f32[8,160,128]{2,1,0:T(8,128)} custom-call(s32[8,16]{1,0:T(8,128)} %bitcast.63, s32[1]{0:T(128)} %bitcast.13.side_ref, f32[320,128]{1,0:T(8,128)} %copy-done.5, f32[320,128]{1,0:T(8,128)} %copy-done.6), custom_call_target="tpu_custom_call" | custom-call | tf_op jit(solution)/shard_map/packed_rows/pallas_call | solution.py:853
  28.7 3.5 %all-to-all-start.1 = ((f32[8,160,128]{2,1,0:T(8,128)}), f32[8,160,128]{2,1,0:T(8,128)S(1)}, u32[]{:S(2)}, u32[]{:S(2)}) async-start(f32[8,160,128]{2,1,0:T(8,128)} %packed_rows.1), calls=%async_computation.1 | async-start | bytes 1310720 | tf_op jit(solution)/shard_map/all_to_all | solution.py:938
  32.3 0.1 fusion.4
  32.3 0.8 constant_dynamic-slice_fusion
  33.1 0.1 reshape.139
  33.2 3.8 %collective-permute-start.3 = (f32[72,128]{1,0:T(8,128)S(1)}, f32[72,128]{1,0:T(8,128)S(1)}, u32[]{:S(2)}, u32[]{:S(2)}) collective-permute-start(f32[72,128]{1,0:T(8,128)S(1)} %get-tuple-element.61), channel_id=1, source_target_pairs={{0,2},{2,4},{4,6},{6,8},{8,10},{10,12},{12,14},{14,16},{16,18},{18... | collective-permute-start | bytes 110600 | tf_op jit(solution)/shard_map/ppermute | solution.py:961
  37.0 1.3 collective-permute-start.4
  38.3 2.1 %gather_fusion.1 = f32[64,64,128]{2,1,0:T(8,128)} fusion(f32[32,64,128]{2,1,0:T(8,128)S(1)} %bitcast.55, s32[1024]{0:T(1024)S(1)} %pad_clamp_fusion), kind=kCustom, calls=%fused_computation.1 | custom fusion | bytes 4194560 | tf_op jit(solution)/shard_map/gather | solution.py:965
  40.4 0.0 collective-permute-done.3
  40.4 2.4 %collective-permute-done.4 = f32[72,128]{1,0:T(8,128)S(1)} collective-permute-done((f32[72,128]{1,0:T(8,128)S(1)}, f32[72,128]{1,0:T(8,128)S(1)}, u32[]{:S(2)}, u32[]{:S(2)}) %collective-permute-start.4) | collective-permute-done | bytes 36896 | tf_op jit(solution)/shard_map/ppermute | solution.py:962
  42.9 5.5 %all-to-all-start.2 = ((f32[8,8,64,128]{3,2,1,0:T(8,128)}), f32[8,8,64,128]{3,2,1,0:T(8,128)}, u32[]{:S(2)}, u32[]{:S(2)}) async-start(f32[8,8,64,128]{3,2,1,0:T(8,128)} %bitcast.16), calls=%async_computation.2 | async-start | bytes 4194304 | tf_op jit(solution)/shard_map/all_to_all | solution.py:967
  48.3 0.5 collective-permute-start.5
  48.8 2.1 %collective-permute-done.2.other_ref = f32[8,160,128]{2,1,0:T(8,128)S(1)} collective-permute-done((f32[8,160,128]{2,1,0:T(8,128)S(1)}, f32[8,160,128]{2,1,0:T(8,128)S(1)}, u32[]{:S(2)}, u32[]{:S(2)}) %collective-permute-start.2) | collective-permute-done | bytes 655392 | tf_op jit(solution)/shard_map/ppermute | solution.py:973
  50.9 0.8 copy-done.4
  51.8 10.2 %kernel_blocks.1 = (bf16[128,128,256]{2,1,0:T(8,128)(2,1)}, f32[32,32,64]{2,1,0:T(8,128)}, f32[32,32,32]{2,1,0:T(8,128)}) custom-call(s32[1]{0:T(128)} %slice.30.total_ref, s32[128]{0:T(128)} %copy-done.11, s32[128]{0:T(128)} %compare_select_fusion.2.count_ref, s32[512]{0:T(512)} %reshape.136.slot_ref, s32[1]{0:T(128)} %bitcast.1.place_ref, ...), custom_call_target="tpu_custom_call" | custom-call | flops 1000000 | bytes 10000 | tf_op jit(solution)/shard_map/kernel_blocks/pallas_call | solution.py:148
  61.9 14.5 %branch_factors.1 = (f32[32,32,128]{2,1,0:T(8,128)}, f32[6,32,32,128]{3,2,1,0:T(8,128)}, f32[32,32]{1,0:T(8,128)}, f32[8,128]{1,0:T(8,128)}) custom-call(f32[1024,32]{1,0:T(8,128)} %bitcast.62), custom_call_target="tpu_custom_call" | custom-call | flops 1000000 | bytes 10000 | tf_op jit(solution)/shard_map/branch_factors/pallas_call | solution.py:577
  76.5 18.0 %collective-permute-done.5.rows_ref = f32[32,64,128]{2,1,0:T(8,128)S(1)} collective-permute-done((f32[32,64,128]{2,1,0:T(8,128)S(1)}, f32[32,64,128]{2,1,0:T(8,128)S(1)}, u32[]{:S(2)}, u32[]{:S(2)}) %collective-permute-start.5) | collective-permute-done | bytes 1048608 | tf_op jit(solution)/shard_map/ppermute | solution.py:943
  94.5 1.0 copy-done.3
  95.5 2.8 %payload_rows.1 = f32[8,520,128]{2,1,0:T(8,128)} custom-call(s32[8,16]{1,0:T(8,128)} %bitcast.65, s32[1]{0:T(128)} %bitcast.13.side_ref, f32[32,64,128]{2,1,0:T(8,128)} %copy-done.3, f32[8,128]{1,0:T(8,128)} %get-tuple-element.66.child_ref), custom_call_target="tpu_custom_call" | custom-call | tf_op jit(solution)/shard_map/payload_rows/pallas_call | solution.py:878
  98.2 4.7 %all-to-all-start.3 = ((f32[8,520,128]{2,1,0:T(8,128)}), f32[8,520,128]{2,1,0:T(8,128)}, u32[]{:S(2)}, u32[]{:S(2)}) async-start(f32[8,520,128]{2,1,0:T(8,128)} %payload_rows.1), calls=%async_computation.3 | async-start | bytes 4259840 | tf_op jit(solution)/shard_map/all_to_all | solution.py:993
  102.9 0.1 copy.53
  103.0 0.6 reshape.142.mask_ref
  103.6 0.4 copy.55
  104.0 0.1 pad.23.clone
  104.1 0.1 maximum_maximum_fusion.1
  104.2 0.8 pad_maximum_fusion.coords_ref
  105.0 1.1 maximum_maximum_fusion.rows_ref
  106.2 5.7 %near_products.1 = f32[128,2048]{1,0:T(8,128)} custom-call(s32[96]{0:T(128)} %reshape.142.mask_ref, f32[35,64,128]{2,1,0:T(8,128)} %maximum_maximum_fusion.rows_ref, f32[35,8,128]{2,1,0:T(8,128)} %pad_maximum_fusion.coords_ref, f32[32,64,3]{2,1,0:T(8,128)} %bitcast.59), custom_call_target="tpu_custom_call" | custom-call | flops 1000000000 | bytes 1000000 | tf_op jit(solution)/shard_map/near_products/pallas_call | solution.py:305
  111.9 7.4 %bases.1 = (f32[32,2048]{1,0:T(8,128)}, f32[32,2048]{1,0:T(8,128)}) custom-call(f32[32,32,128]{2,1,0:T(8,128)} %get-tuple-element.68.inverse_ref, f32[6,32,32,128]{3,2,1,0:T(8,128)} %get-tuple-element.72.ratio_ref, f32[32,32]{1,0:T(8,128)} %get-tuple-element.73.top_ref, f32[32,32,64]{2,1,0:T(8,128)} %get-tuple-element.74.sketched_ref), custom_call_target="tpu_custom_call" | custom-call | flops 1000000000 | bytes 1000000 | tf_op jit(solution)/shard_map/bases/pallas_call | solution.py:626
  119.3 7.8 %all-to-all-done.3.partner_ref = f32[8,520,128]{2,1,0:T(8,128)} async-done(((f32[8,520,128]{2,1,0:T(8,128)}), f32[8,520,128]{2,1,0:T(8,128)}, u32[]{:S(2)}, u32[]{:S(2)}) %all-to-all-start.3) | async-done | bytes 2129952 | tf_op jit(solution)/shard_map/all_to_all | solution.py:993
  127.0 0.8 slice.46.mine_ref
  127.8 0.3 collective-permute-start.6
  128.1 7.8 %far_products.1 = (f32[128,2048]{1,0:T(8,128)}, f32[32,128]{1,0:T(8,128)}, f32[16,32,128]{2,1,0:T(8,128)}) custom-call(s32[1]{0:T(128)} %slice.30.total_ref, s32[128]{0:T(128)} %copy-done.11, s32[512]{0:T(512)} %reshape.136.slot_ref, s32[1]{0:T(128)} %bitcast.13.side_ref, f32[64,64,128]{2,1,0:T(8,128)} %bitcast.19.own_ref, ...), custom_call_target="tpu_custom_call" | custom-call | flops 10000000000 | bytes 10000000 | tf_op jit(solution)/shard_map/far_products/pallas_call | solution.py:237
  135.9 8.0 %all-to-all-start.4 = ((f32[16,32,128]{2,1,0:T(8,128)}), f32[16,32,128]{2,1,0:T(8,128)S(1)}, u32[]{:S(2)}, u32[]{:S(2)}) async-start(f32[16,32,128]{2,1,0:T(8,128)} %get-tuple-element.87), calls=%async_computation.4 | async-start | bytes 524288 | tf_op jit(solution)/shard_map/all_to_all | solution.py:1018
  143.9 0.6 copy-done.13
  144.5 11.9 %top_factors.1 = (f32[15,32,64]{2,1,0:T(8,128)}, f32[512,32]{1,0:T(8,128)}) custom-call(s32[1]{0:T(128)} %bitcast.13.side_ref, f32[8,8,128]{2,1,0:T(8,128)} %copy-done.9, f32[8,8,128]{2,1,0:T(8,128)} %copy-done.13), custom_call_target="tpu_custom_call" | custom-call | flops 10000000000 | bytes 10000000 | tf_op jit(solution)/shard_map/top_factors/pallas_call | solution.py:707
  156.4 2.1 %fusion.5 = f32[32,128]{1,0:T(8,128)} fusion(f32[512,32]{1,0:T(8,128)} %get-tuple-element.86, f32[512,128]{1,0:T(8,128)S(1)} %bitcast.61), kind=kOutput, calls=%fused_computation.38 | convolution fusion | flops 25165824 | bytes 344064 | tf_op jit(solution)/shard_map/dot_general | solution.py:1022
  (42 shorter events, 0.2 us)
Async XLA Ops:
  0.6 13.6 %copy-start.7 = (f32[3,2048]{1,0:T(4,128)S(1)}, f32[3,2048]{1,0:T(4,128)}, u32[]{:S(2)}) copy-start(f32[3,2048]{1,0:T(4,128)} %points_ref.1) | copy-start | bytes 73732
  0.6 13.3 %copy-start.1 = (f32[128,2048]{1,0:T(8,128)S(1)}, f32[128,2048]{1,0:T(8,128)}, u32[]{:S(2)}) copy-start(f32[128,2048]{1,0:T(8,128)} %samples_ref.1) | copy-start | bytes 3145732
  3.4 17.0 %copy-start.10 = (s32[32,16]{0,1:T(8,128)S(1)}, s32[32,16]{0,1:T(8,128)}, u32[]{:S(2)}) copy-start(s32[32,16]{0,1:T(8,128)} %param.11) | copy-start | bytes 6148
  3.4 4.9 %collective-permute-start = (f32[320,128]{1,0:T(8,128)}, f32[320,128]{1,0:T(8,128)S(1)}, u32[]{:S(2)}, u32[]{:S(2)}) collective-permute-start(f32[320,128]{1,0:T(8,128)} %get-tuple-element.48), channel_id=1, source_target_pairs={{0,1},{1,0},{2,3},{3,2},{4,5},{5,4},{6,7},{7,6},{8,9},{9,8},{10,11... | collective-permute-start | bytes 491528 | tf_op jit(solution)/shard_map/ppermute | solution.py:914
  5.9 15.2 %copy-start.11 = (s32[128]{0:T(128)}, s32[128]{0:T(128)S(1)}, u32[]{:S(2)}) copy-start(s32[128]{0:T(128)S(1)} %broadcast_minimum_fusion.leaf_ref) | copy-start | bytes 1540
  9.2 16.7 %copy-start.5 = (f32[320,128]{1,0:T(8,128)}, f32[320,128]{1,0:T(8,128)S(1)}, u32[]{:S(2)}) copy-start(f32[320,128]{1,0:T(8,128)S(1)} %add.55.mine_ref) | copy-start | bytes 491524
  9.2 16.7 %collective-permute-start.1 = (f32[320,128]{1,0:T(8,128)S(1)}, f32[320,128]{1,0:T(8,128)S(1)}, u32[]{:S(2)}, u32[]{:S(2)}) collective-permute-start(f32[320,128]{1,0:T(8,128)S(1)} %add.55.mine_ref), channel_id=1, source_target_pairs={{0,16},{2,18},{4,20},{6,22},{8,24},{10,26},{12,28},{14,30},{16,0},... | collective-permute-start | bytes 491528 | tf_op jit(solution)/shard_map/ppermute | solution.py:926
  15.6 10.2 %all-to-all-start = ((s32[8,1,16]{2,1,0:T(1,128)}), s32[8,1,16]{2,1,0:T(1,128)S(1)}, u32[]{:S(2)}, u32[]{:S(2)}) async-start(s32[8,1,16]{2,1,0:T(1,128)} %bitcast.3), calls=%async_computation | async-start | bytes 8192 | tf_op jit(solution)/shard_map/all_to_all | solution.py:927
  25.8 0.6 copy-start.8
  25.9 0.7 copy-start.6
  28.7 14.2 %all-to-all-start.1 = ((f32[8,160,128]{2,1,0:T(8,128)}), f32[8,160,128]{2,1,0:T(8,128)S(1)}, u32[]{:S(2)}, u32[]{:S(2)}) async-start(f32[8,160,128]{2,1,0:T(8,128)} %packed_rows.1), calls=%async_computation.1 | async-start | bytes 1310720 | tf_op jit(solution)/shard_map/all_to_all | solution.py:938
  33.2 7.2 %collective-permute-start.3 = (f32[72,128]{1,0:T(8,128)S(1)}, f32[72,128]{1,0:T(8,128)S(1)}, u32[]{:S(2)}, u32[]{:S(2)}) collective-permute-start(f32[72,128]{1,0:T(8,128)S(1)} %get-tuple-element.61), channel_id=1, source_target_pairs={{0,2},{2,4},{4,6},{6,8},{8,10},{10,12},{12,14},{14,16},{16,18},{18... | collective-permute-start | bytes 110600 | tf_op jit(solution)/shard_map/ppermute | solution.py:961
  37.0 5.9 %collective-permute-start.4 = (f32[72,128]{1,0:T(8,128)S(1)}, f32[72,128]{1,0:T(8,128)S(1)}, u32[]{:S(2)}, u32[]{:S(2)}) collective-permute-start(f32[72,128]{1,0:T(8,128)S(1)} %get-tuple-element.62), channel_id=1, source_target_pairs={{2,0},{4,2},{6,4},{8,6},{10,8},{12,10},{14,12},{16,14},{18,16},{20... | collective-permute-start | bytes 110600 | tf_op jit(solution)/shard_map/ppermute | solution.py:962
  42.9 6.0 %copy-start.2 = (f32[8,160,128]{2,1,0:T(8,128)}, f32[8,160,128]{2,1,0:T(8,128)S(1)}, u32[]{:S(2)}) copy-start(f32[8,160,128]{2,1,0:T(8,128)S(1)} %all-to-all-done.1.own_ref) | copy-start | bytes 1966084
  42.9 51.6 %all-to-all-start.2 = ((f32[8,8,64,128]{3,2,1,0:T(8,128)}), f32[8,8,64,128]{3,2,1,0:T(8,128)}, u32[]{:S(2)}, u32[]{:S(2)}) async-start(f32[8,8,64,128]{3,2,1,0:T(8,128)} %bitcast.16), calls=%async_computation.2 | async-start | bytes 4194304 | tf_op jit(solution)/shard_map/all_to_all | solution.py:967
  48.3 46.2 %collective-permute-start.5 = (f32[32,64,128]{2,1,0:T(8,128)S(1)}, f32[32,64,128]{2,1,0:T(8,128)S(1)}, u32[]{:S(2)}, u32[]{:S(2)}) collective-permute-start(f32[32,64,128]{2,1,0:T(8,128)S(1)} %bitcast.56), channel_id=1, source_target_pairs={{0,16},{2,18},{4,20},{6,22},{8,24},{10,26},{12,28},{14,30},{16,0},... | collective-permute-start | bytes 3145736 | tf_op jit(solution)/shard_map/ppermute | solution.py:943
  48.8 2.1 %collective-permute-start.2 = (f32[8,160,128]{2,1,0:T(8,128)S(1)}, f32[8,160,128]{2,1,0:T(8,128)S(1)}, u32[]{:S(2)}, u32[]{:S(2)}) collective-permute-start(f32[8,160,128]{2,1,0:T(8,128)S(1)} %all-to-all-done.1.own_ref), channel_id=1, source_target_pairs={{0,1},{1,0},{2,3},{3,2},{4,5},{5,4},{6,7},{7,6},{8,9},{9,8},{10,11... | collective-permute-start | bytes 1966088 | tf_op jit(solution)/shard_map/ppermute | solution.py:973
  50.9 0.8 copy-start.4
  94.5 1.0 copy-start.3
  98.2 4.7 %copy-start.12 = (s32[32,3]{0,1:T(4,128)S(1)}, s32[32,3]{0,1:T(4,128)}, u32[]{:S(2)}) copy-start(s32[32,3]{0,1:T(4,128)} %param.13) | copy-start | bytes 1156
  98.2 5.4 %copy-start = (f32[3,2048]{0,1:T(8,128)S(1)}, f32[3,2048]{0,1:T(8,128)}, u32[]{:S(2)}) copy-start(f32[3,2048]{0,1:T(8,128)} %copy.49) | copy-start | bytes 73732
  98.2 28.8 %all-to-all-start.3 = ((f32[8,520,128]{2,1,0:T(8,128)}), f32[8,520,128]{2,1,0:T(8,128)}, u32[]{:S(2)}, u32[]{:S(2)}) async-start(f32[8,520,128]{2,1,0:T(8,128)} %payload_rows.1), calls=%async_computation.3 | async-start | bytes 4259840 | tf_op jit(solution)/shard_map/all_to_all | solution.py:993
  127.8 8.1 %copy-start.9 = (f32[8,8,128]{2,1,0:T(8,128)}, f32[8,8,128]{2,1,0:T(8,128)S(1)}, u32[]{:S(2)}) copy-start(f32[8,8,128]{2,1,0:T(8,128)S(1)} %slice.46.mine_ref) | copy-start | bytes 98308
  127.8 16.1 %collective-permute-start.6 = (f32[8,8,128]{2,1,0:T(8,128)S(1)}, f32[8,8,128]{2,1,0:T(8,128)S(1)}, u32[]{:S(2)}, u32[]{:S(2)}) collective-permute-start(f32[8,8,128]{2,1,0:T(8,128)S(1)} %slice.46.mine_ref), channel_id=1, source_target_pairs={{0,16},{2,18},{4,20},{6,22},{8,24},{10,26},{12,28},{14,30},{16,0},... | collective-permute-start | bytes 98312 | tf_op jit(solution)/shard_map/ppermute | solution.py:1013
  135.9 20.6 %all-to-all-start.4 = ((f32[16,32,128]{2,1,0:T(8,128)}), f32[16,32,128]{2,1,0:T(8,128)S(1)}, u32[]{:S(2)}, u32[]{:S(2)}) async-start(f32[16,32,128]{2,1,0:T(8,128)} %get-tuple-element.87), calls=%async_computation.4 | async-start | bytes 524288 | tf_op jit(solution)/shard_map/all_to_all | solution.py:1018
  143.9 0.6 copy-start.13

commit v11 on v10

--- a/solution.py
+++ b/solution.py
@@ -175,39 +175,59 @@
     )(total, group_leaf, group_count, group_slots, place, own, other, targets)
 
 
-def far_body(
-    total_ref, leaf_ref, slot_ref, side_ref,
-    own_ref, partner_ref, blocks_ref, weights_ref,
+def far_groups(sizes_ref, leaf_ref, slot_ref, first_batch, live, blocks_ref, s_both, acc):
+    step = pl.program_id(0)
+
+    @pl.when(step * BATCH < live)
+    def _():
+        for member in range(BATCH):
+            group = first_batch * BATCH + step * BATCH + member
+            leaf = leaf_ref[group]
+            slots = [slot_ref[group * GROUP + e] for e in range(GROUP)]
+            rows = jnp.concatenate([s_both[slot] for slot in slots], axis=0)
+            acc[leaf] += quadrants(dot(blocks_ref[member], rows))
+
+
+def far_own_body(sizes_ref, leaf_ref, slot_ref, own_ref, blocks_ref, acc_ref, s_both):
+    @pl.when(pl.program_id(0) == 0)
+    def _():
+        acc_ref[...] = jnp.zeros_like(acc_ref)
+
+        def split(slot, carry):
+            s_both[slot] = stacked_halves(own_ref[slot], 1)
+            return carry
+
+        lax.fori_loop(0, own_ref.shape[0], split, 0, unroll=8)
+
+    far_groups(sizes_ref, leaf_ref, slot_ref, 0, sizes_ref[1], blocks_ref, s_both, acc_ref)
+
+
+def far_partner_body(
+    sizes_ref, leaf_ref, slot_ref,
+    partner_ref, blocks_ref, start_ref, weights_ref,
     out_ref, projected_ref, copies_ref,
     s_both, acc,
     *, cap,
 ):
     step = pl.program_id(0)
-    samp_dev = own_ref.shape[2]
-    part = own_ref.shape[0]
+    samp_dev = partner_ref.shape[2]
 
     @pl.when(step == 0)
     def _():
-        acc[...] = jnp.zeros_like(acc)
-
-        def split(slot, carry):
-            here = side_ref[0] * part + slot
-            there = (1 - side_ref[0]) * part + slot
-            s_both[here] = stacked_halves(own_ref[slot], 1)
-            at = pl.multiple_of((slot % cap) * LEAF, LEAF)
-            s_both[there] = stacked_halves(partner_ref[slot // cap, pl.ds(at, LEAF), :], 1)
+        acc[...] = start_ref[...]
+
+        def split(peer, carry):
+            for entry in range(cap):
+                s_both[peer * cap + entry] = stacked_halves(
+                    partner_ref[peer, LEAF * entry : LEAF * (entry + 1), :], 1
+                )
             return carry
 
-        lax.fori_loop(0, part, split, 0, unroll=4)
-
-    @pl.when(step * BATCH < total_ref[0])
-    def _():
-        for member in range(BATCH):
-            group = step * BATCH + member
-            leaf = leaf_ref[group]
-            slots = [slot_ref[group * GROUP + e] for e in range(GROUP)]
-            rows = jnp.concatenate([s_both[slot] for slot in slots], axis=0)
-            acc[leaf] += quadrants(dot(blocks_ref[member], rows))
+        lax.fori_loop(0, partner_ref.shape[0], split, 0)
+
+    far_groups(
+        sizes_ref, leaf_ref, slot_ref, sizes_ref[2] // BATCH, sizes_ref[3], blocks_ref, s_both, acc
+    )
 
     @pl.when(step == pl.num_programs(0) - 1)
     def _():
@@ -222,50 +242,79 @@
             out_ref[:, 2 * pair * LEAF : 2 * (pair + 1) * LEAF] = block.T
 
 
-def far_products(total, group_leaf, group_slots, side, own, partner, blocks, weights, branches):
+def far_own(sizes, group_leaf, group_slots, own, blocks, leaves):
     part, unused, samp_dev = own.shape
-    slots = 2 * part
-    groups = group_leaf.shape[0]
-    points_dev = weights.shape[1]
-    leaves = points_dev // LEAF
-    steps = groups // BATCH
-
-    def block_index(step, total_ref, *unused):
-        last = (total_ref[0] - 1) // BATCH
+    steps = leaves * FAR // GROUP // BATCH
+
+    def block_index(step, sizes_ref, *unused):
+        last = jnp.maximum(sizes_ref[1] - 1, 0) // BATCH
         return (jnp.minimum(step, last), 0, 0)
 
+    whole = lambda *unused: (0, 0, 0)
     return pl.pallas_call(
-        functools.partial(far_body, cap=part // partner.shape[0]),
+        far_own_body,
         grid_spec=pltpu.PrefetchScalarGridSpec(
-            num_scalar_prefetch=4,
+            num_scalar_prefetch=3,
             grid=(steps,),
             in_specs=[
-                pl.BlockSpec(own.shape, lambda *unused: (0, 0, 0), pipeline_mode=pl.Buffered(1)),
-                pl.BlockSpec(partner.shape, lambda *unused: (0, 0, 0), pipeline_mode=pl.Buffered(1)),
+                pl.BlockSpec(own.shape, whole, pipeline_mode=pl.Buffered(1)),
                 pl.BlockSpec((BATCH, 2 * LEAF, GROUP * LEAF), block_index),
-                pl.BlockSpec(weights.shape, lambda *unused: (0, 0), pipeline_mode=pl.Buffered(1)),
+            ],
+            out_specs=pl.BlockSpec((leaves, LEAF, samp_dev), whole),
+            scratch_shapes=[pltpu.VMEM((part, LEAF, 2 * samp_dev), jnp.bfloat16)],
+        ),
+        out_shape=jax.ShapeDtypeStruct((leaves, LEAF, samp_dev), jnp.float32),
+        compiler_params=pltpu.CompilerParams(vmem_limit_bytes=vmem_bytes),
+        name="far_own",
+        cost_estimate=pl.CostEstimate(flops=10**9, bytes_accessed=10**6, transcendentals=0),
+    )(sizes, group_leaf, group_slots, own, blocks)
+
+
+def far_partner(sizes, group_leaf, group_slots, partner, blocks, start, weights, cap, branches):
+    leaves, unused, samp_dev = start.shape
+    part = partner.shape[0] * cap
+    points_dev = leaves * LEAF
+    rank = weights.shape[0]
+    steps = leaves * FAR // GROUP // BATCH
+
+    def block_index(step, sizes_ref, *unused):
+        last = jnp.maximum(sizes_ref[3] - 1, 0) // BATCH
+        most = blocks.shape[0] // BATCH - 1
+        return (jnp.minimum(sizes_ref[2] // BATCH + jnp.minimum(step, last), most), 0, 0)
+
+    flat = lambda *unused: (0, 0)
+    whole = lambda *unused: (0, 0, 0)
+    once = pl.Buffered(1)
+    return pl.pallas_call(
+        functools.partial(far_partner_body, cap=cap),
+        grid_spec=pltpu.PrefetchScalarGridSpec(
+            num_scalar_prefetch=3,
+            grid=(steps,),
+            in_specs=[
+                pl.BlockSpec(partner.shape, whole, pipeline_mode=once),
+                pl.BlockSpec((BATCH, 2 * LEAF, GROUP * LEAF), block_index),
+                pl.BlockSpec(start.shape, whole, pipeline_mode=once),
+                pl.BlockSpec(weights.shape, flat, pipeline_mode=once),
             ],
             out_specs=[
-                pl.BlockSpec((samp_dev, points_dev), lambda *unused: (0, 0)),
-                pl.BlockSpec((weights.shape[0], samp_dev), lambda *unused: (0, 0)),
-                pl.BlockSpec((branches, weights.shape[0], samp_dev), lambda *unused: (0, 0, 0)),
+                pl.BlockSpec((samp_dev, points_dev), flat),
+                pl.BlockSpec((rank, samp_dev), flat),
+                pl.BlockSpec((branches, rank, samp_dev), whole),
             ],
             scratch_shapes=[
-                pltpu.VMEM((slots, LEAF, 2 * samp_dev), jnp.bfloat16),
+                pltpu.VMEM((part, LEAF, 2 * samp_dev), jnp.bfloat16),
                 pltpu.VMEM((leaves, LEAF, samp_dev), jnp.float32),
             ],
         ),
         out_shape=[
             jax.ShapeDtypeStruct((samp_dev, points_dev), jnp.float32),
-            jax.ShapeDtypeStruct((weights.shape[0], samp_dev), jnp.float32),
-            jax.ShapeDtypeStruct((branches, weights.shape[0], samp_dev), jnp.float32),
+            jax.ShapeDtypeStruct((rank, samp_dev), jnp.float32),
+            jax.ShapeDtypeStruct((branches, rank, samp_dev), jnp.float32),
         ],
         compiler_params=pltpu.CompilerParams(vmem_limit_bytes=vmem_bytes),
-        name="far_products",
-        cost_estimate=pl.CostEstimate(
-            flops=10**10, bytes_accessed=10**7, transcendentals=0
-        ),
-    )(total, group_leaf, group_slots, side, own, partner, blocks, weights)
+        name="far_partner",
+        cost_estimate=pl.CostEstimate(flops=10**10, bytes_accessed=10**7, transcendentals=0),
+    )(sizes, group_leaf, group_slots, partner, blocks, start, weights)
 
 
 NEAR_LEAVES = 8
@@ -750,27 +799,46 @@
     return result
 
 
-def group_tables(far_slots, far_count):
+def group_tables(far_slots, far_count, side, part):
     leaves = far_slots.shape[0]
-    groups = leaves * FAR // GROUP
-    per_leaf = (far_count + GROUP - 1) // GROUP
-    before = jnp.arange(leaves)[:, None] >= jnp.arange(leaves)[None, :]
-    ends = jnp.sum(jnp.where(before, per_leaf[None, :], 0), axis=1)
-    total = ends[leaves - 1 :]
+    groups = -(-(leaves * (FAR // GROUP + 1) + BATCH - 1) // BATCH) * BATCH
+    places = jnp.arange(FAR, dtype=jnp.int32)
+    valid = places[None, :] < far_count[:, None]
+    here = far_slots // part == side
+    local = far_slots % part
+    held = jnp.concatenate([valid & here, valid & ~here], axis=0)
+    local = jnp.concatenate([local, local], axis=0)
+    earlier = places[None, :] < places[:, None]
+    rank = jnp.sum((held[:, None, :] & earlier[None]).astype(jnp.int32), axis=2)
+    chosen = held[:, None, :] & (rank[:, None, :] == places[None, :, None])
+    ordered = jnp.sum(jnp.where(chosen, local[:, None, :], 0), axis=2)
+    lengths = jnp.sum(held.astype(jnp.int32), axis=1)
+    lists = 2 * leaves
+    per_list = (lengths + GROUP - 1) // GROUP
+    before = jnp.arange(lists)[:, None] >= jnp.arange(lists)[None, :]
+    ends = jnp.sum(jnp.where(before, per_list[None, :], 0), axis=1)
+    own_total = ends[leaves - 1]
+    total = ends[lists - 1]
+    base = (own_total + BATCH - 1) // BATCH * BATCH
     ids = jnp.arange(groups, dtype=jnp.int32)
-    leaf = jnp.minimum(jnp.sum((ends[None, :] <= ids[:, None]).astype(jnp.int32), axis=1), leaves - 1)
-    hit = leaf[:, None] == jnp.arange(leaves)[None, :]
-    start = jnp.sum(jnp.where(hit, (ends - per_leaf)[None, :], 0), axis=1)
-    length = jnp.sum(jnp.where(hit, far_count[None, :], 0), axis=1)
-    sub = ids - start
-    count = jnp.where(ids < total, jnp.clip(length - GROUP * sub, 0, GROUP), 0)
-    first = jnp.minimum(sub, FAR // GROUP - 1)
-    slots = far_slots.reshape(leaves * FAR // GROUP, GROUP)[leaf * (FAR // GROUP) + first]
+    at = jnp.where(ids < base, ids, ids - base + own_total)
+    dead = ((ids < base) & (ids >= own_total)) | (at >= total)
+    index = jnp.minimum(jnp.sum((ends[None, :] <= at[:, None]).astype(jnp.int32), axis=1), lists - 1)
+    hit = index[:, None] == jnp.arange(lists)[None, :]
+    start = jnp.sum(jnp.where(hit, (ends - per_list)[None, :], 0), axis=1)
+    length = jnp.sum(jnp.where(hit, lengths[None, :], 0), axis=1)
+    sub = at - start
+    count = jnp.where(dead, 0, jnp.clip(length - GROUP * sub, 0, GROUP))
+    first = jnp.clip(sub, 0, FAR // GROUP - 1)
+    slots = ordered.reshape(lists * FAR // GROUP, GROUP)[index * (FAR // GROUP) + first]
+    lift = jnp.where(ids < base, side, 1 - side) * part
+    sizes = jnp.stack([base + total - own_total, own_total, base, total - own_total])
     return (
-        total.astype(jnp.int32),
-        leaf.astype(jnp.int32),
+        sizes.astype(jnp.int32),
+        (index % leaves).astype(jnp.int32),
         count.astype(jnp.int32),
         slots.reshape(-1).astype(jnp.int32),
+        (slots + lift[:, None]).reshape(-1).astype(jnp.int32),
     )
 
 
@@ -931,9 +999,7 @@
     targets = jnp.transpose(coords, (0, 2, 1))
     rows = jnp.transpose(samples.reshape(samp_dev, leaves, LEAF), (1, 2, 0))
 
-    tables = group_tables(far_slots, far_count)
-    asked, rows, targets, tables = lax.optimization_barrier((asked, rows, targets, tables))
-    total, group_leaf, group_count, group_slots = tables
+    asked, rows, targets = lax.optimization_barrier((asked, rows, targets))
     small_sent = packed_rows(asked, side_ref, mine, partner, cap, leaves)
     small_got = lax.all_to_all(
         small_sent, "leaf", split_axis=0, concat_axis=0, axis_index_groups=groups, tiled=True
@@ -963,7 +1029,12 @@
 
     own_asked = lax.dynamic_slice_in_dim(asked, side * cap, cap, axis=1)
     own_sent = rows_out[own_asked.reshape(-1)].reshape(half, cap, LEAF, samp_dev)
-    own_sent, low_edge, high_edge = lax.optimization_barrier((own_sent, low_edge, high_edge))
+    own_sent, low_edge, high_edge, far_slots, far_count = lax.optimization_barrier(
+        (own_sent, low_edge, high_edge, far_slots, far_count)
+    )
+    sizes, group_leaf, group_count, group_slots, group_places = group_tables(
+        far_slots, far_count, side, half * cap
+    )
     own_got = lax.all_to_all(
         own_sent, "leaf", split_axis=0, concat_axis=0, axis_index_groups=groups, tiled=True
     )
@@ -983,7 +1054,7 @@
         place = jnp.zeros((1,), jnp.int32)
 
     blocks, sketched, gram = kernel_blocks(
-        total, group_leaf, group_count, group_slots, place, small_got, small_other, targets, rank, cap
+        sizes, group_leaf, group_count, group_places, place, small_got, small_other, targets, rank, cap
     )
 
     levels = leaves.bit_length()
@@ -1011,9 +1082,11 @@
 
     children = arrived[:, cap * LEAF :]
     mirrored = lax.ppermute(children, "leaf", mirror)
+    own_got, unused = lax.optimization_barrier((own_got, payload))
+    far_start = far_own(sizes, group_leaf, group_slots, own_got, blocks, leaves)
     weights, near_sample = lax.optimization_barrier((weights, near_sample))
-    far_sample, branch_samples, copies = far_products(
-        total, group_leaf, group_slots, side_ref, own_got, arrived, blocks, weights, branches
+    far_sample, branch_samples, copies = far_partner(
+        sizes, group_leaf, group_slots, arrived, blocks, far_start, weights, cap, branches
     )
     everyone = lax.all_to_all(copies, "leaf", split_axis=0, concat_axis=0, tiled=True)
     children, mirrored, unused = lax.optimization_barrier((children, mirrored, branch_samples))

time: 160 us -> 159 us (level)
  waiting for transfers between devices: 34.3 us -> 12 us
  Pallas kernels: 65.1 us -> 80.1 us
  between operations: 0.85 us -> 4.14 us
  other arithmetic: 6.32 us -> 9.26 us
    ppermute x1, waiting for transfers between devices: 18 us -> 0.01 us  [on_device(): partner_rows = lax.ppermute(rows_out, 'leaf', mirror)]
    pallas_call x1, Pallas kernels: 10.2 us -> 18.4 us  [kernel_blocks(): pl.pallas_call(functools.partial(blocks_body, rank=rank, cap=cap), grid_s...]
    pallas_call x1 -> x2, Pallas kernels: 7.79 us -> 14.5 us  [the longest x1 7.58 us: far_partner(): pl.pallas_call(functools.partial(far_partner_body, cap=cap), grid_spec=pl...]
    all_to_all x1, waiting for transfers between devices: 7.76 us -> 3.98 us  [on_device(): lax.all_to_all(payload, 'leaf', split_axis=0, concat_axis=0, axis_index_g...]
    ppermute x1, waiting for transfers between devices: 2.09 us -> 0.01 us  [on_device(): small_other = lax.ppermute(small_got, 'cols', [(0, 1), (1, 0)])]
    unnamed x33 -> x32, local copies, waits for them, and re-layouts: 4.94 us -> 5.2 us
  transfers between devices with their start and end apart: 12 -> 12, of which waited for: 5 -> 3; matrix products, arithmetic and copies ran while one was open for 9% -> 11% of each run, Pallas kernels for 36% -> 46%
where the time goes in v11:
time: 159 us; the launch traced here: 157 us
  Pallas kernels  80.1 us (50%)
  starting transfers between devices  36 us (23%)
  local copies, waits for them, and re-layouts  13.3 us (8%)
  waiting for transfers between devices  12 us (8%)
  other arithmetic  9.26 us (6%)
  between operations  4.14 us (3%)
  matrix products  2.13 us (1%)
    pallas_call x1, Pallas kernels, kernel_blocks(): pl.pallas_call(functools.partial(blocks_body, rank=rank, cap=cap), grid_s...  18.4 us
    pallas_call x1, Pallas kernels, branch_factors(): pl.pallas_call(functools.partial(branch_body, rank=rank, levels=levels),...  14.6 us
    pallas_call x1, Pallas kernels, top_factors(): pl.pallas_call(functools.partial(top_body, rank=rank, levels=levels), in_...  11.9 us
    pallas_call x1, Pallas kernels, far_partner(): pl.pallas_call(functools.partial(far_partner_body, cap=cap), grid_spec=pl...  7.58 us
    pallas_call x1, Pallas kernels, bases(): pl.pallas_call(functools.partial(basis_body, rank=rank, levels=levels), i...  7.38 us
    pallas_call x1, Pallas kernels, far_own(): pl.pallas_call(far_own_body, grid_spec=pltpu.PrefetchScalarGridSpec(num_s...  6.88 us
    all_to_all x1, starting transfers between devices, on_device(): lax.all_to_all(copies, 'leaf', split_axis=0, concat_axis=0, tiled=True)  6.61 us
    pallas_call x1, Pallas kernels, near_products(): pl.pallas_call(near_body, grid_spec=pltpu.PrefetchScalarGridSpec(num_scal...  5.72 us
  transfers between devices with their start and end apart: 12, of which 3 were waited for; matrix products, arithmetic and copies ran while one was open for 11% of the time, Pallas kernels for 46%

profile of v11, /device:TPU:0, one launch (start us, length us, event | category | flops | bytes accessed | tf_op | source)
XLA Modules:
  0.0 157.0 jit_solution(1930015392519950728)
XLA Ops:
  0.7 2.7 %sketched_shares.1 = (f32[320,128]{1,0:T(8,128)}, f32[320,128]{1,0:T(8,128)}) custom-call(s32[1]{0:T(128)} %bitcast.1.place_ref, f32[32,128]{1,0:T(8,128)} %sketch_ref.1, f32[128,2048]{1,0:T(8,128)} %samples_ref.1, f32[3,2048]{1,0:T(4,128)} %points_ref.1), custom_call_target="tpu_custom_call" | custom-call | flops 1000000 | bytes 10000 | tf_op jit(solution)/shard_map/sketched_shares/pallas_call | solution.py:885
  3.4 0.5 collective-permute-start
  3.8 0.8 reshape.194
  4.6 0.1 copy.49
  4.7 0.7 reshape.195
  5.3 0.9 add.123.mine_ref
  6.3 3.7 %collective-permute-start.1 = (f32[320,128]{1,0:T(8,128)S(1)}, f32[320,128]{1,0:T(8,128)S(1)}, u32[]{:S(2)}, u32[]{:S(2)}) collective-permute-start(f32[320,128]{1,0:T(8,128)S(1)} %add.123.mine_ref), channel_id=1, source_target_pairs={{0,16},{2,18},{4,20},{6,22},{8,24},{10,26},{12,28},{14,30},{16,0},... | collective-permute-start | bytes 491528 | tf_op jit(solution)/shard_map/ppermute | solution.py:994
  10.0 0.3 copy.51
  10.4 1.3 copy.52
  11.7 4.7 %all-to-all-start = ((s32[8,1,16]{2,1,0:T(1,128)}), s32[8,1,16]{2,1,0:T(1,128)S(1)}, u32[]{:S(2)}, u32[]{:S(2)}) async-start(s32[8,1,16]{2,1,0:T(1,128)} %bitcast.3), calls=%async_computation | async-start | bytes 8192 | tf_op jit(solution)/shard_map/all_to_all | solution.py:995
  16.4 5.5 %all-to-all-done = s32[8,1,16]{2,1,0:T(1,128)S(1)} async-done(((s32[8,1,16]{2,1,0:T(1,128)}), s32[8,1,16]{2,1,0:T(1,128)S(1)}, u32[]{:S(2)}, u32[]{:S(2)}) %all-to-all-start) | async-done | bytes 544 | tf_op jit(solution)/shard_map/all_to_all | solution.py:995
  21.9 0.6 copy-done.7
  22.5 0.1 copy-done.5
  22.6 2.2 %packed_rows.1 = f32[8,160,128]{2,1,0:T(8,128)} custom-call(s32[8,16]{1,0:T(8,128)} %bitcast.58, s32[1]{0:T(128)} %bitcast.9.side_ref, f32[320,128]{1,0:T(8,128)} %copy-done.4, f32[320,128]{1,0:T(8,128)} %copy-done.5), custom_call_target="tpu_custom_call" | custom-call | tf_op jit(solution)/shard_map/packed_rows/pallas_call | solution.py:921
  24.8 3.5 %all-to-all-start.1 = ((f32[8,160,128]{2,1,0:T(8,128)}), f32[8,160,128]{2,1,0:T(8,128)S(1)}, u32[]{:S(2)}, u32[]{:S(2)}) async-start(f32[8,160,128]{2,1,0:T(8,128)} %packed_rows.1), calls=%async_computation.1 | async-start | bytes 1310720 | tf_op jit(solution)/shard_map/all_to_all | solution.py:1004
  28.4 0.8 constant_dynamic-slice_fusion
  29.2 0.1 reshape.200
  29.3 3.8 %collective-permute-start.2 = (f32[72,128]{1,0:T(8,128)S(1)}, f32[72,128]{1,0:T(8,128)S(1)}, u32[]{:S(2)}, u32[]{:S(2)}) collective-permute-start(f32[72,128]{1,0:T(8,128)S(1)} %get-tuple-element.53), channel_id=1, source_target_pairs={{0,2},{2,4},{4,6},{6,8},{8,10},{10,12},{12,14},{14,16},{16,18},{18... | collective-permute-start | bytes 110600 | tf_op jit(solution)/shard_map/ppermute | solution.py:1027
  33.1 1.3 collective-permute-start.3
  34.4 2.0 %gather_fusion = f32[64,64,128]{2,1,0:T(8,128)} fusion(f32[32,64,128]{2,1,0:T(8,128)S(1)} %bitcast.48, s32[1024]{0:T(1024)S(1)} %pad_clamp_fusion.1), kind=kCustom, calls=%fused_computation | custom fusion | bytes 4194560 | tf_op jit(solution)/shard_map/gather | solution.py:1031
  36.4 2.5 %collective-permute-done.3 = f32[72,128]{1,0:T(8,128)S(1)} collective-permute-done((f32[72,128]{1,0:T(8,128)S(1)}, f32[72,128]{1,0:T(8,128)S(1)}, u32[]{:S(2)}, u32[]{:S(2)}) %collective-permute-start.3) | collective-permute-done | bytes 36896 | tf_op jit(solution)/shard_map/ppermute | solution.py:1028
  39.0 0.8 copy-done.3
  39.8 5.5 %all-to-all-start.2 = ((f32[8,8,64,128]{3,2,1,0:T(8,128)}), f32[8,8,64,128]{3,2,1,0:T(8,128)S(1)}, u32[]{:S(2)}, u32[]{:S(2)}) async-start(f32[8,8,64,128]{3,2,1,0:T(8,128)} %bitcast.55), calls=%async_computation.2 | async-start | bytes 4194304 | tf_op jit(solution)/shard_map/all_to_all | solution.py:1038
  45.3 0.4 collective-permute-start.5
  45.7 0.1 convert_reduce_fusion.2
  45.8 0.1 select_reduce_fusion.3
  45.9 0.6 fusion.11
  47.2 0.6 add_select_fusion.2
  48.0 0.1 convert_reduce_fusion.1
  48.1 0.1 convert_reduce_fusion
  50.8 0.1 copy.55
  50.9 0.1 add.137
  50.9 0.1 add.138
  51.1 0.1 reshape.202
  51.1 0.5 broadcast_minimum_fusion
  51.7 0.1 select_reduce_fusion.1
  51.9 0.7 compare_select_fusion
  52.6 0.7 gather_fusion.1
  53.2 0.1 reshape.203.slot_ref
  53.4 0.6 add.139.slot_ref
  53.9 1.3 pad_add_fusion.2.total_ref.sizes_ref
  55.2 1.8 %or_select_fusion.count_ref = s32[176]{0:T(256)} fusion(s32[176]{0:T(256)S(1)} %get-tuple-element.86, s32[176]{0:T(256)S(1)} %get-tuple-element.87, s32[]{:T(128)} %bitcast.15, s32[]{:T(128)} %bitcast.14, s32[]{:T(128)} %mul.33), kind=kLoop, calls=%fused_computation.47 | loop fusion | flops 2288 | bytes 2124 | tf_op jit(solution)/shard_map/jit(_where)/select_n | solution.py:831
  57.0 18.4 %kernel_blocks.1 = (bf16[176,128,256]{2,1,0:T(8,128)(2,1)}, f32[32,32,64]{2,1,0:T(8,128)}, f32[32,32,32]{2,1,0:T(8,128)}) custom-call(s32[4]{0:T(128)} %pad_add_fusion.2.total_ref.sizes_ref, s32[176]{0:T(256)} %get-tuple-element.97.leaf_ref, s32[176]{0:T(256)} %or_select_fusion.count_ref, s32[704]{0:T(1024)} %add.139.slot_ref, s32[1]{0:T(128)} %bitcast.1.place_ref, ...), custom_call_target="tpu_custom_call" | custom-call | flops 1000000 | bytes 10000 | tf_op jit(solution)/shard_map/kernel_blocks/pallas_call | solution.py:148
  75.4 14.6 %branch_factors.1 = (f32[32,32,128]{2,1,0:T(8,128)}, f32[6,32,32,128]{3,2,1,0:T(8,128)}, f32[32,32]{1,0:T(8,128)}, f32[8,128]{1,0:T(8,128)}) custom-call(f32[1024,32]{1,0:T(8,128)} %bitcast.57), custom_call_target="tpu_custom_call" | custom-call | flops 1000000 | bytes 10000 | tf_op jit(solution)/shard_map/branch_factors/pallas_call | solution.py:626
  90.0 1.3 copy-done.1
  91.3 2.8 %payload_rows.1 = f32[8,520,128]{2,1,0:T(8,128)} custom-call(s32[8,16]{1,0:T(8,128)} %bitcast.60, s32[1]{0:T(128)} %bitcast.9.side_ref, f32[32,64,128]{2,1,0:T(8,128)} %collective-permute-done.5.rows_ref, f32[8,128]{1,0:T(8,128)} %get-tuple-element.62.child_ref), custom_call_target="tpu_custom_call" | custom-call | tf_op jit(solution)/shard_map/payload_rows/pallas_call | solution.py:946
  94.2 4.7 %all-to-all-start.3 = ((f32[8,520,128]{2,1,0:T(8,128)}), f32[8,520,128]{2,1,0:T(8,128)}, u32[]{:S(2)}, u32[]{:S(2)}) async-start(f32[8,520,128]{2,1,0:T(8,128)} %payload_rows.1), calls=%async_computation.3 | async-start | bytes 4259840 | tf_op jit(solution)/shard_map/all_to_all | solution.py:1064
  98.8 0.1 copy.56
  98.9 0.6 reshape.206.mask_ref
  99.6 0.4 copy.58
  100.0 0.1 maximum_maximum_fusion.1
  100.2 0.8 pad_maximum_fusion.coords_ref
  100.9 1.2 maximum_maximum_fusion.rows_ref
  102.1 5.7 %near_products.1 = f32[128,2048]{1,0:T(8,128)} custom-call(s32[96]{0:T(128)} %reshape.206.mask_ref, f32[35,64,128]{2,1,0:T(8,128)} %maximum_maximum_fusion.rows_ref, f32[35,8,128]{2,1,0:T(8,128)} %pad_maximum_fusion.coords_ref, f32[32,64,3]{2,1,0:T(8,128)} %bitcast.52), custom_call_target="tpu_custom_call" | custom-call | flops 1000000000 | bytes 1000000 | tf_op jit(solution)/shard_map/near_products/pallas_call | solution.py:354
  107.9 7.4 %bases.1 = (f32[32,2048]{1,0:T(8,128)}, f32[32,2048]{1,0:T(8,128)}) custom-call(f32[32,32,128]{2,1,0:T(8,128)} %get-tuple-element.66.inverse_ref, f32[6,32,32,128]{3,2,1,0:T(8,128)} %get-tuple-element.70.ratio_ref, f32[32,32]{1,0:T(8,128)} %get-tuple-element.71.top_ref, f32[32,32,64]{2,1,0:T(8,128)} %get-tuple-element.72.sketched_ref), custom_call_target="tpu_custom_call" | custom-call | flops 1000000000 | bytes 1000000 | tf_op jit(solution)/shard_map/bases/pallas_call | solution.py:675
  115.2 6.9 %far_own.1.start_ref = f32[32,64,128]{2,1,0:T(8,128)} custom-call(s32[4]{0:T(128)} %pad_add_fusion.2.total_ref.sizes_ref, s32[176]{0:T(256)} %get-tuple-element.97.leaf_ref, s32[704]{0:T(1024)} %copy-done.8, f32[64,64,128]{2,1,0:T(8,128)} %bitcast.54, bf16[176,128,256]{2,1,0:T(8,128)(2,1)} %get-tuple-element.63.blocks_ref), custom_call_target="tpu_custom_call" | custom-call | flops 1000000000 | bytes 1000000 | tf_op jit(solution)/shard_map/far_own/pallas_call | solution.py:254
  122.1 4.0 %all-to-all-done.3.partner_ref = f32[8,520,128]{2,1,0:T(8,128)} async-done(((f32[8,520,128]{2,1,0:T(8,128)}), f32[8,520,128]{2,1,0:T(8,128)}, u32[]{:S(2)}, u32[]{:S(2)}) %all-to-all-start.3) | async-done | bytes 2129952 | tf_op jit(solution)/shard_map/all_to_all | solution.py:1064
  126.1 0.8 slice.50.mine_ref
  126.9 1.2 collective-permute-start.6
  128.1 7.6 %far_partner.1 = (f32[128,2048]{1,0:T(8,128)}, f32[32,128]{1,0:T(8,128)}, f32[16,32,128]{2,1,0:T(8,128)}) custom-call(s32[4]{0:T(128)} %pad_add_fusion.2.total_ref.sizes_ref, s32[176]{0:T(256)} %get-tuple-element.97.leaf_ref, s32[704]{0:T(1024)} %copy-done.8, f32[8,520,128]{2,1,0:T(8,128)} %all-to-all-done.3.partner_ref, ...), custom_call_target="tpu_custom_call" | custom-call | flops 10000000000 | bytes 10000000 | tf_op jit(solution)/shard_map/far_partner/pallas_call | solution.py:288
  135.7 6.6 %all-to-all-start.4 = ((f32[16,32,128]{2,1,0:T(8,128)}), f32[16,32,128]{2,1,0:T(8,128)S(1)}, u32[]{:S(2)}, u32[]{:S(2)}) async-start(f32[16,32,128]{2,1,0:T(8,128)} %get-tuple-element.85), calls=%async_computation.4 | async-start | bytes 524288 | tf_op jit(solution)/shard_map/all_to_all | solution.py:1091
  142.3 0.6 copy-done.13
  142.9 11.9 %top_factors.1 = (f32[15,32,64]{2,1,0:T(8,128)}, f32[512,32]{1,0:T(8,128)}) custom-call(s32[1]{0:T(128)} %bitcast.9.side_ref, f32[8,8,128]{2,1,0:T(8,128)} %copy-done.9, f32[8,8,128]{2,1,0:T(8,128)} %copy-done.13), custom_call_target="tpu_custom_call" | custom-call | flops 10000000000 | bytes 10000000 | tf_op jit(solution)/shard_map/top_factors/pallas_call | solution.py:756
  154.8 2.1 %fusion.12 = f32[32,128]{1,0:T(8,128)} fusion(f32[512,32]{1,0:T(8,128)} %get-tuple-element.84, f32[512,128]{1,0:T(8,128)S(1)} %bitcast.56), kind=kOutput, calls=%fused_computation.65 | convolution fusion | flops 25165824 | bytes 344064 | tf_op jit(solution)/shard_map/dot_general | solution.py:1095
  (57 shorter events, 0.6 us)
Async XLA Ops:
  0.6 9.7 %copy-start.6 = (f32[3,2048]{1,0:T(4,128)S(1)}, f32[3,2048]{1,0:T(4,128)}, u32[]{:S(2)}) copy-start(f32[3,2048]{1,0:T(4,128)} %points_ref.1) | copy-start | bytes 73732
  0.6 9.4 %copy-start.2 = (f32[128,2048]{1,0:T(8,128)S(1)}, f32[128,2048]{1,0:T(8,128)}, u32[]{:S(2)}) copy-start(f32[128,2048]{1,0:T(8,128)} %samples_ref.1) | copy-start | bytes 3145732
  3.4 2.0 %collective-permute-start = (f32[320,128]{1,0:T(8,128)}, f32[320,128]{1,0:T(8,128)S(1)}, u32[]{:S(2)}, u32[]{:S(2)}) collective-permute-start(f32[320,128]{1,0:T(8,128)} %get-tuple-element.47), channel_id=1, source_target_pairs={{0,1},{1,0},{2,3},{3,2},{4,5},{5,4},{6,7},{7,6},{8,9},{9,8},{10,11... | collective-permute-start | bytes 491528 | tf_op jit(solution)/shard_map/ppermute | solution.py:982
  6.3 15.7 %copy-start.4 = (f32[320,128]{1,0:T(8,128)}, f32[320,128]{1,0:T(8,128)S(1)}, u32[]{:S(2)}) copy-start(f32[320,128]{1,0:T(8,128)S(1)} %add.123.mine_ref) | copy-start | bytes 491524
  6.3 15.6 %collective-permute-start.1 = (f32[320,128]{1,0:T(8,128)S(1)}, f32[320,128]{1,0:T(8,128)S(1)}, u32[]{:S(2)}, u32[]{:S(2)}) collective-permute-start(f32[320,128]{1,0:T(8,128)S(1)} %add.123.mine_ref), channel_id=1, source_target_pairs={{0,16},{2,18},{4,20},{6,22},{8,24},{10,26},{12,28},{14,30},{16,0},... | collective-permute-start | bytes 491528 | tf_op jit(solution)/shard_map/ppermute | solution.py:994
  11.7 10.2 %all-to-all-start = ((s32[8,1,16]{2,1,0:T(1,128)}), s32[8,1,16]{2,1,0:T(1,128)S(1)}, u32[]{:S(2)}, u32[]{:S(2)}) async-start(s32[8,1,16]{2,1,0:T(1,128)} %bitcast.3), calls=%async_computation | async-start | bytes 8192 | tf_op jit(solution)/shard_map/all_to_all | solution.py:995
  21.9 0.6 copy-start.7
  21.9 0.7 copy-start.5
  24.8 14.2 %all-to-all-start.1 = ((f32[8,160,128]{2,1,0:T(8,128)}), f32[8,160,128]{2,1,0:T(8,128)S(1)}, u32[]{:S(2)}, u32[]{:S(2)}) async-start(f32[8,160,128]{2,1,0:T(8,128)} %packed_rows.1), calls=%async_computation.1 | async-start | bytes 1310720 | tf_op jit(solution)/shard_map/all_to_all | solution.py:1004
  29.3 7.1 %collective-permute-start.2 = (f32[72,128]{1,0:T(8,128)S(1)}, f32[72,128]{1,0:T(8,128)S(1)}, u32[]{:S(2)}, u32[]{:S(2)}) collective-permute-start(f32[72,128]{1,0:T(8,128)S(1)} %get-tuple-element.53), channel_id=1, source_target_pairs={{0,2},{2,4},{4,6},{6,8},{8,10},{10,12},{12,14},{14,16},{16,18},{18... | collective-permute-start | bytes 110600 | tf_op jit(solution)/shard_map/ppermute | solution.py:1027
  33.1 5.9 %collective-permute-start.3 = (f32[72,128]{1,0:T(8,128)S(1)}, f32[72,128]{1,0:T(8,128)S(1)}, u32[]{:S(2)}, u32[]{:S(2)}) collective-permute-start(f32[72,128]{1,0:T(8,128)S(1)} %get-tuple-element.54), channel_id=1, source_target_pairs={{2,0},{4,2},{6,4},{8,6},{10,8},{12,10},{14,12},{16,14},{18,16},{20... | collective-permute-start | bytes 110600 | tf_op jit(solution)/shard_map/ppermute | solution.py:1028
  38.9 6.7 %copy-start.10 = (s32[32,16]{0,1:T(8,128)S(1)}, s32[32,16]{0,1:T(8,128)}, u32[]{:S(2)}) copy-start(s32[32,16]{0,1:T(8,128)} %param.11) | copy-start | bytes 6148
  38.9 6.7 %copy-start.12 = (s32[32]{0:T(128)S(1)}, s32[32]{0:T(128)}, u32[]{:S(2)}) copy-start(s32[32]{0:T(128)} %param.12) | copy-start | bytes 388
  38.9 0.8 copy-start.3
  39.8 50.3 %all-to-all-start.2 = ((f32[8,8,64,128]{3,2,1,0:T(8,128)}), f32[8,8,64,128]{3,2,1,0:T(8,128)S(1)}, u32[]{:S(2)}, u32[]{:S(2)}) async-start(f32[8,8,64,128]{3,2,1,0:T(8,128)} %bitcast.55), calls=%async_computation.2 | async-start | bytes 4194304 | tf_op jit(solution)/shard_map/all_to_all | solution.py:1038
  45.3 44.8 %collective-permute-start.5 = (f32[32,64,128]{2,1,0:T(8,128)S(1)}, f32[32,64,128]{2,1,0:T(8,128)}, u32[]{:S(2)}, u32[]{:S(2)}) collective-permute-start(f32[32,64,128]{2,1,0:T(8,128)S(1)} %bitcast.49), channel_id=1, source_target_pairs={{0,16},{2,18},{4,20},{6,22},{8,24},{10,26},{12,28},{14,30},{16,0},... | collective-permute-start | bytes 3145736 | tf_op jit(solution)/shard_map/ppermute | solution.py:1009
  51.8 5.2 %collective-permute-start.4 = (f32[8,160,128]{2,1,0:T(8,128)}, f32[8,160,128]{2,1,0:T(8,128)}, u32[]{:S(2)}, u32[]{:S(2)}) collective-permute-start(f32[8,160,128]{2,1,0:T(8,128)} %copy-done.3), channel_id=1, source_target_pairs={{0,1},{1,0},{2,3},{3,2},{4,5},{5,4},{6,7},{7,6},{8,9},{9,8},{10,11... | collective-permute-start | bytes 1966088 | tf_op jit(solution)/shard_map/ppermute | solution.py:1044
  53.3 40.8 %copy-start.8 = (s32[704]{0:T(1024)}, s32[704]{0:T(1024)S(1)}, u32[]{:S(2)}) copy-start(s32[704]{0:T(1024)S(1)} %reshape.203.slot_ref) | copy-start | bytes 8452
  90.0 1.3 copy-start.1
  94.1 4.7 %copy-start.11 = (s32[32,3]{0,1:T(4,128)S(1)}, s32[32,3]{0,1:T(4,128)}, u32[]{:S(2)}) copy-start(s32[32,3]{0,1:T(4,128)} %param.13) | copy-start | bytes 1156
  94.1 5.4 %copy-start = (f32[3,2048]{0,1:T(8,128)S(1)}, f32[3,2048]{0,1:T(8,128)}, u32[]{:S(2)}) copy-start(f32[3,2048]{0,1:T(8,128)} %copy.52) | copy-start | bytes 73732
  94.2 32.0 %all-to-all-start.3 = ((f32[8,520,128]{2,1,0:T(8,128)}), f32[8,520,128]{2,1,0:T(8,128)}, u32[]{:S(2)}, u32[]{:S(2)}) async-start(f32[8,520,128]{2,1,0:T(8,128)} %payload_rows.1), calls=%async_computation.3 | async-start | bytes 4259840 | tf_op jit(solution)/shard_map/all_to_all | solution.py:1064
  126.9 8.8 %copy-start.9 = (f32[8,8,128]{2,1,0:T(8,128)}, f32[8,8,128]{2,1,0:T(8,128)S(1)}, u32[]{:S(2)}) copy-start(f32[8,8,128]{2,1,0:T(8,128)S(1)} %slice.50.mine_ref) | copy-start | bytes 98308
  126.9 15.4 %collective-permute-start.6 = (f32[8,8,128]{2,1,0:T(8,128)S(1)}, f32[8,8,128]{2,1,0:T(8,128)S(1)}, u32[]{:S(2)}, u32[]{:S(2)}) collective-permute-start(f32[8,8,128]{2,1,0:T(8,128)S(1)} %slice.50.mine_ref), channel_id=1, source_target_pairs={{0,16},{2,18},{4,20},{6,22},{8,24},{10,26},{12,28},{14,30},{16,0},... | collective-permute-start | bytes 98312 | tf_op jit(solution)/shard_map/ppermute | solution.py:1084
  135.7 19.1 %all-to-all-start.4 = ((f32[16,32,128]{2,1,0:T(8,128)}), f32[16,32,128]{2,1,0:T(8,128)S(1)}, u32[]{:S(2)}, u32[]{:S(2)}) async-start(f32[16,32,128]{2,1,0:T(8,128)} %get-tuple-element.85), calls=%async_computation.4 | async-start | bytes 524288 | tf_op jit(solution)/shard_map/all_to_all | solution.py:1091
  142.3 0.6 copy-start.13

commit v12 on v11

--- a/solution.py
+++ b/solution.py
@@ -124,7 +124,9 @@
                 both_ref[member, :, half * LANES : (half + 1) * LANES] = stacked_halves(values, 0)
                 z_parts.append(both[:rank])
             z_both = stacked_halves(jnp.concatenate(z_parts, axis=1), 0)
-            sketched_ref[leaf] += quadrants(dot_nt(z_both, both_ref[member]))
+            by_high = dot_nt(z_both, both_ref[member, :LEAF])
+            by_low = dot_nt(z_both[:rank], both_ref[member, LEAF:])
+            sketched_ref[leaf] += by_high[:rank] + (by_high[rank:] + by_low)
 
     @pl.when(step == pl.num_programs(0) - 1)
     def _():
@@ -455,22 +457,6 @@
     shift, share = eliminate(current, left, inverse, level, rank)
     lowest[...] = jnp.minimum(lowest[...], share)
 
-    for block in range(tiles):
-        sums = [[None] * tiles for _ in range(SUB)]
-        for r in range(SUB * block, rank):
-            parts = [inverse_row(inverse, r, t, rank) for t in range(block, r // SUB + 1)]
-            for q in range(SUB):
-                if SUB * block + q > r:
-                    continue
-                factor = parts[0][q : q + 1, :]
-                for t in range(block, r // SUB + 1):
-                    term = parts[t - block] * factor
-                    sums[q][t] = term if sums[q][t] is None else sums[q][t] + term
-        for q in range(SUB):
-            at = (SUB * block + q) * rank
-            for t in range(block, tiles):
-                squared[at + SUB * t : at + SUB * (t + 1), :] = sums[q][t]
-
     if child is not None:
         @when(child_at(level))
         def _():
@@ -481,19 +467,37 @@
                         value = value - shift * inverse_row(inverse, r, t, rank)
                     child[r, SUB * t : SUB * (t + 1), :] = value
 
-    for q in range(rank):
-        for t in range(tiles):
-            if t >= q // SUB:
-                value = squared[q * rank + SUB * t : q * rank + SUB * (t + 1), :]
-            else:
-                value = squared[pl.ds(SUB * t * rank + q, SUB, stride=rank), :]
-            value = -shift * value
-            if t == q // SUB:
-                value = value + jnp.where(row == q % SUB, 1.0, 0.0)
-            if ratio is not None:
-                ratio[level, q, SUB * t : SUB * (t + 1), :] = value
-            here = current[q, SUB * t : SUB * (t + 1), :] - shift * value
-            current[q, SUB * t : SUB * (t + 1), :] = pair_up(here, level)
+    @when(level < levels - 1)
+    def _():
+        for block in range(tiles):
+            sums = [[None] * tiles for _ in range(SUB)]
+            for r in range(SUB * block, rank):
+                parts = [inverse_row(inverse, r, t, rank) for t in range(block, r // SUB + 1)]
+                for q in range(SUB):
+                    if SUB * block + q > r:
+                        continue
+                    factor = parts[0][q : q + 1, :]
+                    for t in range(block, r // SUB + 1):
+                        term = parts[t - block] * factor
+                        sums[q][t] = term if sums[q][t] is None else sums[q][t] + term
+            for q in range(SUB):
+                at = (SUB * block + q) * rank
+                for t in range(block, tiles):
+                    squared[at + SUB * t : at + SUB * (t + 1), :] = sums[q][t]
+
+        for q in range(rank):
+            for t in range(tiles):
+                if t >= q // SUB:
+                    value = squared[q * rank + SUB * t : q * rank + SUB * (t + 1), :]
+                else:
+                    value = squared[pl.ds(SUB * t * rank + q, SUB, stride=rank), :]
+                value = -shift * value
+                if t == q // SUB:
+                    value = value + jnp.where(row == q % SUB, 1.0, 0.0)
+                if ratio is not None:
+                    ratio[level, q, SUB * t : SUB * (t + 1), :] = value
+                here = current[q, SUB * t : SUB * (t + 1), :] - shift * value
+                current[q, SUB * t : SUB * (t + 1), :] = pair_up(here, level)
 
 
 def level_plain(level, levels, current, left, inverse, squared, ratio, child, lowest, rank, child_at):
@@ -701,8 +705,12 @@
         )
 
     def finish(level):
+        @when(level < levels - 1)
+        def _():
+            for r in range(rank):
+                from_lanes(child[r], nat_child.at[level], r, nodes, rank)
+
         for r in range(rank):
-            from_lanes(child[r], nat_child.at[level], r, nodes, rank)
             from_lanes(inverse[r * rank : (r + 1) * rank, :], nat_inverse.at[level], r, nodes, rank)
 
     run_levels(

time: 159 us -> 155 us (0.975)
  Pallas kernels: 80.1 us -> 74.1 us
  waiting for transfers between devices: 12 us -> 16 us
  starting transfers between devices: 36 us -> 34.4 us
    pallas_call x1, Pallas kernels: 18.4 us -> 14.2 us  [kernel_blocks(): pl.pallas_call(functools.partial(blocks_body, rank=rank, cap=cap), grid_s...]
    ppermute x1, waiting for transfers between devices: 0.01 us -> 2.94 us  [on_device(): partner_rows = lax.ppermute(rows_out, 'leaf', mirror)]
    all_to_all x1, waiting for transfers between devices: 0.01 us -> 1.94 us  [on_device(): lax.all_to_all(own_sent, 'leaf', split_axis=0, concat_axis=0, axis_index_...]
  transfers between devices with their start and end apart: 12 -> 12, of which waited for: 3 -> 5; matrix products, arithmetic and copies ran while one was open for 11% -> 11% of each run, Pallas kernels for 46% -> 43%
where the time goes in v12:
time: 155 us; the launch traced here: 153 us
  Pallas kernels  74.1 us (48%)
  starting transfers between devices  34.4 us (22%)
  waiting for transfers between devices  16 us (10%)
  local copies, waits for them, and re-layouts  13.3 us (9%)
  other arithmetic  9.26 us (6%)
  between operations  4.11 us (3%)
  matrix products  2.13 us (1%)
    pallas_call x1, Pallas kernels, kernel_blocks(): pl.pallas_call(functools.partial(blocks_body, rank=rank, cap=cap), grid_s...  14.2 us
    pallas_call x1, Pallas kernels, branch_factors(): pl.pallas_call(functools.partial(branch_body, rank=rank, levels=levels),...  13.6 us
    pallas_call x1, Pallas kernels, top_factors(): pl.pallas_call(functools.partial(top_body, rank=rank, levels=levels), in_...  11.1 us
    pallas_call x1, Pallas kernels, far_partner(): pl.pallas_call(functools.partial(far_partner_body, cap=cap), grid_spec=pl...  8.11 us
    pallas_call x1, Pallas kernels, bases(): pl.pallas_call(functools.partial(basis_body, rank=rank, levels=levels), i...  7.38 us
    pallas_call x1, Pallas kernels, far_own(): pl.pallas_call(far_own_body, grid_spec=pltpu.PrefetchScalarGridSpec(num_s...  6.37 us
    all_to_all x1, starting transfers between devices, on_device(): lax.all_to_all(copies, 'leaf', split_axis=0, concat_axis=0, tiled=True)  5.91 us
    pallas_call x1, Pallas kernels, near_products(): pl.pallas_call(near_body, grid_spec=pltpu.PrefetchScalarGridSpec(num_scal...  5.72 us
  transfers between devices with their start and end apart: 12, of which 5 were waited for; matrix products, arithmetic and copies ran while one was open for 11% of the time, Pallas kernels for 43%

profile of v12, /device:TPU:0, one launch (start us, length us, event | category | flops | bytes accessed | tf_op | source)
XLA Modules:
  0.0 153.3 jit_solution(202206330499877486)
XLA Ops:
  0.7 2.7 %sketched_shares.1 = (f32[320,128]{1,0:T(8,128)}, f32[320,128]{1,0:T(8,128)}) custom-call(s32[1]{0:T(128)} %bitcast.1.place_ref, f32[32,128]{1,0:T(8,128)} %sketch_ref.1, f32[128,2048]{1,0:T(8,128)} %samples_ref.1, f32[3,2048]{1,0:T(4,128)} %points_ref.1), custom_call_target="tpu_custom_call" | custom-call | flops 1000000 | bytes 10000 | tf_op jit(solution)/shard_map/sketched_shares/pallas_call | solution.py:893
  3.4 0.5 collective-permute-start
  3.8 0.8 reshape.194
  4.6 0.1 copy.49
  4.7 0.7 reshape.195
  5.3 0.9 add.123.mine_ref
  6.3 3.7 %collective-permute-start.1 = (f32[320,128]{1,0:T(8,128)S(1)}, f32[320,128]{1,0:T(8,128)S(1)}, u32[]{:S(2)}, u32[]{:S(2)}) collective-permute-start(f32[320,128]{1,0:T(8,128)S(1)} %add.123.mine_ref), channel_id=1, source_target_pairs={{0,16},{2,18},{4,20},{6,22},{8,24},{10,26},{12,28},{14,30},{16,0},... | collective-permute-start | bytes 491528 | tf_op jit(solution)/shard_map/ppermute | solution.py:1002
  10.0 0.3 copy.51
  10.4 1.3 copy.52
  11.7 4.7 %all-to-all-start = ((s32[8,1,16]{2,1,0:T(1,128)}), s32[8,1,16]{2,1,0:T(1,128)S(1)}, u32[]{:S(2)}, u32[]{:S(2)}) async-start(s32[8,1,16]{2,1,0:T(1,128)} %bitcast.3), calls=%async_computation | async-start | bytes 8192 | tf_op jit(solution)/shard_map/all_to_all | solution.py:1003
  16.4 5.5 %all-to-all-done = s32[8,1,16]{2,1,0:T(1,128)S(1)} async-done(((s32[8,1,16]{2,1,0:T(1,128)}), s32[8,1,16]{2,1,0:T(1,128)S(1)}, u32[]{:S(2)}, u32[]{:S(2)}) %all-to-all-start) | async-done | bytes 544 | tf_op jit(solution)/shard_map/all_to_all | solution.py:1003
  21.9 0.6 copy-done.7
  22.5 0.1 copy-done.5
  22.6 2.2 %packed_rows.1 = f32[8,160,128]{2,1,0:T(8,128)} custom-call(s32[8,16]{1,0:T(8,128)} %bitcast.58, s32[1]{0:T(128)} %bitcast.9.side_ref, f32[320,128]{1,0:T(8,128)} %copy-done.4, f32[320,128]{1,0:T(8,128)} %copy-done.5), custom_call_target="tpu_custom_call" | custom-call | tf_op jit(solution)/shard_map/packed_rows/pallas_call | solution.py:929
  24.8 3.5 %all-to-all-start.1 = ((f32[8,160,128]{2,1,0:T(8,128)}), f32[8,160,128]{2,1,0:T(8,128)S(1)}, u32[]{:S(2)}, u32[]{:S(2)}) async-start(f32[8,160,128]{2,1,0:T(8,128)} %packed_rows.1), calls=%async_computation.1 | async-start | bytes 1310720 | tf_op jit(solution)/shard_map/all_to_all | solution.py:1012
  28.4 0.8 constant_dynamic-slice_fusion
  29.2 0.1 reshape.200
  29.3 3.8 %collective-permute-start.2 = (f32[72,128]{1,0:T(8,128)S(1)}, f32[72,128]{1,0:T(8,128)S(1)}, u32[]{:S(2)}, u32[]{:S(2)}) collective-permute-start(f32[72,128]{1,0:T(8,128)S(1)} %get-tuple-element.53), channel_id=1, source_target_pairs={{0,2},{2,4},{4,6},{6,8},{8,10},{10,12},{12,14},{14,16},{16,18},{18... | collective-permute-start | bytes 110600 | tf_op jit(solution)/shard_map/ppermute | solution.py:1035
  33.1 1.3 collective-permute-start.3
  34.4 2.0 %gather_fusion = f32[64,64,128]{2,1,0:T(8,128)} fusion(f32[32,64,128]{2,1,0:T(8,128)S(1)} %bitcast.48, s32[1024]{0:T(1024)S(1)} %pad_clamp_fusion.1), kind=kCustom, calls=%fused_computation | custom fusion | bytes 4194560 | tf_op jit(solution)/shard_map/gather | solution.py:1039
  36.4 2.5 %collective-permute-done.3 = f32[72,128]{1,0:T(8,128)S(1)} collective-permute-done((f32[72,128]{1,0:T(8,128)S(1)}, f32[72,128]{1,0:T(8,128)S(1)}, u32[]{:S(2)}, u32[]{:S(2)}) %collective-permute-start.3) | collective-permute-done | bytes 36896 | tf_op jit(solution)/shard_map/ppermute | solution.py:1036
  39.0 0.8 copy-done.3
  39.8 5.5 %all-to-all-start.2 = ((f32[8,8,64,128]{3,2,1,0:T(8,128)}), f32[8,8,64,128]{3,2,1,0:T(8,128)S(1)}, u32[]{:S(2)}, u32[]{:S(2)}) async-start(f32[8,8,64,128]{3,2,1,0:T(8,128)} %bitcast.55), calls=%async_computation.2 | async-start | bytes 4194304 | tf_op jit(solution)/shard_map/all_to_all | solution.py:1046
  45.3 0.4 collective-permute-start.5
  45.7 0.1 convert_reduce_fusion.2
  45.8 0.1 select_reduce_fusion.3
  45.9 0.6 fusion.11
  47.2 0.6 add_select_fusion.2
  48.0 0.1 convert_reduce_fusion.1
  48.1 0.1 convert_reduce_fusion
  50.8 0.1 copy.55
  50.9 0.1 add.137
  50.9 0.1 add.138
  51.1 0.1 reshape.202
  51.1 0.5 broadcast_minimum_fusion
  51.7 0.1 select_reduce_fusion.1
  51.9 0.7 compare_select_fusion
  52.6 0.7 gather_fusion.1
  53.2 0.1 reshape.203.slot_ref
  53.4 0.6 add.139.slot_ref
  53.9 1.3 pad_add_fusion.2.total_ref.sizes_ref
  55.2 1.8 %or_select_fusion.count_ref = s32[176]{0:T(256)} fusion(s32[176]{0:T(256)S(1)} %get-tuple-element.86, s32[176]{0:T(256)S(1)} %get-tuple-element.87, s32[]{:T(128)} %bitcast.15, s32[]{:T(128)} %bitcast.14, s32[]{:T(128)} %mul.33), kind=kLoop, calls=%fused_computation.47 | loop fusion | flops 2288 | bytes 2124 | tf_op jit(solution)/shard_map/jit(_where)/select_n | solution.py:839
  57.0 14.2 %kernel_blocks.1 = (bf16[176,128,256]{2,1,0:T(8,128)(2,1)}, f32[32,32,64]{2,1,0:T(8,128)}, f32[32,32,32]{2,1,0:T(8,128)}) custom-call(s32[4]{0:T(128)} %pad_add_fusion.2.total_ref.sizes_ref, s32[176]{0:T(256)} %get-tuple-element.97.leaf_ref, s32[176]{0:T(256)} %or_select_fusion.count_ref, s32[704]{0:T(1024)} %add.139.slot_ref, s32[1]{0:T(128)} %bitcast.1.place_ref, ...), custom_call_target="tpu_custom_call" | custom-call | flops 1000000 | bytes 10000 | tf_op jit(solution)/shard_map/kernel_blocks/pallas_call | solution.py:150
  71.2 13.6 %branch_factors.1 = (f32[32,32,128]{2,1,0:T(8,128)}, f32[6,32,32,128]{3,2,1,0:T(8,128)}, f32[32,32]{1,0:T(8,128)}, f32[8,128]{1,0:T(8,128)}) custom-call(f32[1024,32]{1,0:T(8,128)} %bitcast.57), custom_call_target="tpu_custom_call" | custom-call | flops 1000000 | bytes 10000 | tf_op jit(solution)/shard_map/branch_factors/pallas_call | solution.py:630
  84.8 2.9 %collective-permute-done.5.rows_ref = f32[32,64,128]{2,1,0:T(8,128)} collective-permute-done((f32[32,64,128]{2,1,0:T(8,128)S(1)}, f32[32,64,128]{2,1,0:T(8,128)}, u32[]{:S(2)}, u32[]{:S(2)}) %collective-permute-start.5) | collective-permute-done | bytes 1048608 | tf_op jit(solution)/shard_map/ppermute | solution.py:1017
  87.8 1.9 %all-to-all-done.2 = f32[8,8,64,128]{3,2,1,0:T(8,128)S(1)} async-done(((f32[8,8,64,128]{3,2,1,0:T(8,128)}), f32[8,8,64,128]{3,2,1,0:T(8,128)S(1)}, u32[]{:S(2)}, u32[]{:S(2)}) %all-to-all-start.2) | async-done | bytes 2097184 | tf_op jit(solution)/shard_map/all_to_all | solution.py:1046
  89.7 1.3 copy-done.1
  91.0 2.8 %payload_rows.1 = f32[8,520,128]{2,1,0:T(8,128)} custom-call(s32[8,16]{1,0:T(8,128)} %bitcast.60, s32[1]{0:T(128)} %bitcast.9.side_ref, f32[32,64,128]{2,1,0:T(8,128)} %collective-permute-done.5.rows_ref, f32[8,128]{1,0:T(8,128)} %get-tuple-element.62.child_ref), custom_call_target="tpu_custom_call" | custom-call | tf_op jit(solution)/shard_map/payload_rows/pallas_call | solution.py:954
  93.8 5.0 %all-to-all-start.3 = ((f32[8,520,128]{2,1,0:T(8,128)}), f32[8,520,128]{2,1,0:T(8,128)}, u32[]{:S(2)}, u32[]{:S(2)}) async-start(f32[8,520,128]{2,1,0:T(8,128)} %payload_rows.1), calls=%async_computation.3 | async-start | bytes 4259840 | tf_op jit(solution)/shard_map/all_to_all | solution.py:1072
  98.8 0.1 copy.56
  98.9 0.6 reshape.206.mask_ref
  99.5 0.4 copy.58
  100.1 0.8 pad_maximum_fusion.coords_ref
  100.9 1.2 maximum_maximum_fusion.rows_ref
  102.1 5.7 %near_products.1 = f32[128,2048]{1,0:T(8,128)} custom-call(s32[96]{0:T(128)} %reshape.206.mask_ref, f32[35,64,128]{2,1,0:T(8,128)} %maximum_maximum_fusion.rows_ref, f32[35,8,128]{2,1,0:T(8,128)} %pad_maximum_fusion.coords_ref, f32[32,64,3]{2,1,0:T(8,128)} %bitcast.52), custom_call_target="tpu_custom_call" | custom-call | flops 1000000000 | bytes 1000000 | tf_op jit(solution)/shard_map/near_products/pallas_call | solution.py:356
  107.9 7.4 %bases.1 = (f32[32,2048]{1,0:T(8,128)}, f32[32,2048]{1,0:T(8,128)}) custom-call(f32[32,32,128]{2,1,0:T(8,128)} %get-tuple-element.66.inverse_ref, f32[6,32,32,128]{3,2,1,0:T(8,128)} %get-tuple-element.70.ratio_ref, f32[32,32]{1,0:T(8,128)} %get-tuple-element.71.top_ref, f32[32,32,64]{2,1,0:T(8,128)} %get-tuple-element.72.sketched_ref), custom_call_target="tpu_custom_call" | custom-call | flops 1000000000 | bytes 1000000 | tf_op jit(solution)/shard_map/bases/pallas_call | solution.py:679
  115.2 6.4 %far_own.1.start_ref = f32[32,64,128]{2,1,0:T(8,128)} custom-call(s32[4]{0:T(128)} %pad_add_fusion.2.total_ref.sizes_ref, s32[176]{0:T(256)} %get-tuple-element.97.leaf_ref, s32[704]{0:T(1024)} %copy-done.8, f32[64,64,128]{2,1,0:T(8,128)} %bitcast.54, bf16[176,128,256]{2,1,0:T(8,128)(2,1)} %get-tuple-element.63.blocks_ref), custom_call_target="tpu_custom_call" | custom-call | flops 1000000000 | bytes 1000000 | tf_op jit(solution)/shard_map/far_own/pallas_call | solution.py:256
  121.6 3.1 %all-to-all-done.3.partner_ref = f32[8,520,128]{2,1,0:T(8,128)} async-done(((f32[8,520,128]{2,1,0:T(8,128)}), f32[8,520,128]{2,1,0:T(8,128)}, u32[]{:S(2)}, u32[]{:S(2)}) %all-to-all-start.3) | async-done | bytes 2129952 | tf_op jit(solution)/shard_map/all_to_all | solution.py:1072
  124.7 0.8 slice.50.mine_ref
  125.4 8.1 %far_partner.1 = (f32[128,2048]{1,0:T(8,128)}, f32[32,128]{1,0:T(8,128)}, f32[16,32,128]{2,1,0:T(8,128)}) custom-call(s32[4]{0:T(128)} %pad_add_fusion.2.total_ref.sizes_ref, s32[176]{0:T(256)} %get-tuple-element.97.leaf_ref, s32[704]{0:T(1024)} %copy-done.8, f32[8,520,128]{2,1,0:T(8,128)} %all-to-all-done.3.partner_ref, ...), custom_call_target="tpu_custom_call" | custom-call | flops 10000000000 | bytes 10000000 | tf_op jit(solution)/shard_map/far_partner/pallas_call | solution.py:290
  133.6 5.9 %all-to-all-start.4 = ((f32[16,32,128]{2,1,0:T(8,128)}), f32[16,32,128]{2,1,0:T(8,128)S(1)}, u32[]{:S(2)}, u32[]{:S(2)}) async-start(f32[16,32,128]{2,1,0:T(8,128)} %get-tuple-element.85), calls=%async_computation.4 | async-start | bytes 524288 | tf_op jit(solution)/shard_map/all_to_all | solution.py:1099
  139.5 0.6 copy-done.13
  140.1 11.1 %top_factors.1 = (f32[15,32,64]{2,1,0:T(8,128)}, f32[512,32]{1,0:T(8,128)}) custom-call(s32[1]{0:T(128)} %bitcast.9.side_ref, f32[8,8,128]{2,1,0:T(8,128)} %copy-done.9, f32[8,8,128]{2,1,0:T(8,128)} %copy-done.13), custom_call_target="tpu_custom_call" | custom-call | flops 10000000000 | bytes 10000000 | tf_op jit(solution)/shard_map/top_factors/pallas_call | solution.py:764
  151.2 2.1 %fusion.12 = f32[32,128]{1,0:T(8,128)} fusion(f32[512,32]{1,0:T(8,128)} %get-tuple-element.84, f32[512,128]{1,0:T(8,128)S(1)} %bitcast.56), kind=kOutput, calls=%fused_computation.65 | convolution fusion | flops 25165824 | bytes 344064 | tf_op jit(solution)/shard_map/dot_general | solution.py:1103
  (57 shorter events, 0.6 us)
Async XLA Ops:
  0.6 9.7 %copy-start.6 = (f32[3,2048]{1,0:T(4,128)S(1)}, f32[3,2048]{1,0:T(4,128)}, u32[]{:S(2)}) copy-start(f32[3,2048]{1,0:T(4,128)} %points_ref.1) | copy-start | bytes 73732
  0.6 9.4 %copy-start.2 = (f32[128,2048]{1,0:T(8,128)S(1)}, f32[128,2048]{1,0:T(8,128)}, u32[]{:S(2)}) copy-start(f32[128,2048]{1,0:T(8,128)} %samples_ref.1) | copy-start | bytes 3145732
  3.4 2.0 %collective-permute-start = (f32[320,128]{1,0:T(8,128)}, f32[320,128]{1,0:T(8,128)S(1)}, u32[]{:S(2)}, u32[]{:S(2)}) collective-permute-start(f32[320,128]{1,0:T(8,128)} %get-tuple-element.47), channel_id=1, source_target_pairs={{0,1},{1,0},{2,3},{3,2},{4,5},{5,4},{6,7},{7,6},{8,9},{9,8},{10,11... | collective-permute-start | bytes 491528 | tf_op jit(solution)/shard_map/ppermute | solution.py:990
  6.3 15.7 %copy-start.4 = (f32[320,128]{1,0:T(8,128)}, f32[320,128]{1,0:T(8,128)S(1)}, u32[]{:S(2)}) copy-start(f32[320,128]{1,0:T(8,128)S(1)} %add.123.mine_ref) | copy-start | bytes 491524
  6.3 15.6 %collective-permute-start.1 = (f32[320,128]{1,0:T(8,128)S(1)}, f32[320,128]{1,0:T(8,128)S(1)}, u32[]{:S(2)}, u32[]{:S(2)}) collective-permute-start(f32[320,128]{1,0:T(8,128)S(1)} %add.123.mine_ref), channel_id=1, source_target_pairs={{0,16},{2,18},{4,20},{6,22},{8,24},{10,26},{12,28},{14,30},{16,0},... | collective-permute-start | bytes 491528 | tf_op jit(solution)/shard_map/ppermute | solution.py:1002
  11.7 10.2 %all-to-all-start = ((s32[8,1,16]{2,1,0:T(1,128)}), s32[8,1,16]{2,1,0:T(1,128)S(1)}, u32[]{:S(2)}, u32[]{:S(2)}) async-start(s32[8,1,16]{2,1,0:T(1,128)} %bitcast.3), calls=%async_computation | async-start | bytes 8192 | tf_op jit(solution)/shard_map/all_to_all | solution.py:1003
  21.9 0.6 copy-start.7
  21.9 0.7 copy-start.5
  24.8 14.2 %all-to-all-start.1 = ((f32[8,160,128]{2,1,0:T(8,128)}), f32[8,160,128]{2,1,0:T(8,128)S(1)}, u32[]{:S(2)}, u32[]{:S(2)}) async-start(f32[8,160,128]{2,1,0:T(8,128)} %packed_rows.1), calls=%async_computation.1 | async-start | bytes 1310720 | tf_op jit(solution)/shard_map/all_to_all | solution.py:1012
  29.3 7.1 %collective-permute-start.2 = (f32[72,128]{1,0:T(8,128)S(1)}, f32[72,128]{1,0:T(8,128)S(1)}, u32[]{:S(2)}, u32[]{:S(2)}) collective-permute-start(f32[72,128]{1,0:T(8,128)S(1)} %get-tuple-element.53), channel_id=1, source_target_pairs={{0,2},{2,4},{4,6},{6,8},{8,10},{10,12},{12,14},{14,16},{16,18},{18... | collective-permute-start | bytes 110600 | tf_op jit(solution)/shard_map/ppermute | solution.py:1035
  33.1 5.9 %collective-permute-start.3 = (f32[72,128]{1,0:T(8,128)S(1)}, f32[72,128]{1,0:T(8,128)S(1)}, u32[]{:S(2)}, u32[]{:S(2)}) collective-permute-start(f32[72,128]{1,0:T(8,128)S(1)} %get-tuple-element.54), channel_id=1, source_target_pairs={{2,0},{4,2},{6,4},{8,6},{10,8},{12,10},{14,12},{16,14},{18,16},{20... | collective-permute-start | bytes 110600 | tf_op jit(solution)/shard_map/ppermute | solution.py:1036
  38.9 6.7 %copy-start.10 = (s32[32,16]{0,1:T(8,128)S(1)}, s32[32,16]{0,1:T(8,128)}, u32[]{:S(2)}) copy-start(s32[32,16]{0,1:T(8,128)} %param.11) | copy-start | bytes 6148
  38.9 6.7 %copy-start.12 = (s32[32]{0:T(128)S(1)}, s32[32]{0:T(128)}, u32[]{:S(2)}) copy-start(s32[32]{0:T(128)} %param.12) | copy-start | bytes 388
  38.9 0.8 copy-start.3
  39.8 49.9 %all-to-all-start.2 = ((f32[8,8,64,128]{3,2,1,0:T(8,128)}), f32[8,8,64,128]{3,2,1,0:T(8,128)S(1)}, u32[]{:S(2)}, u32[]{:S(2)}) async-start(f32[8,8,64,128]{3,2,1,0:T(8,128)} %bitcast.55), calls=%async_computation.2 | async-start | bytes 4194304 | tf_op jit(solution)/shard_map/all_to_all | solution.py:1046
  45.3 42.5 %collective-permute-start.5 = (f32[32,64,128]{2,1,0:T(8,128)S(1)}, f32[32,64,128]{2,1,0:T(8,128)}, u32[]{:S(2)}, u32[]{:S(2)}) collective-permute-start(f32[32,64,128]{2,1,0:T(8,128)S(1)} %bitcast.49), channel_id=1, source_target_pairs={{0,16},{2,18},{4,20},{6,22},{8,24},{10,26},{12,28},{14,30},{16,0},... | collective-permute-start | bytes 3145736 | tf_op jit(solution)/shard_map/ppermute | solution.py:1017
  51.8 5.2 %collective-permute-start.4 = (f32[8,160,128]{2,1,0:T(8,128)}, f32[8,160,128]{2,1,0:T(8,128)}, u32[]{:S(2)}, u32[]{:S(2)}) collective-permute-start(f32[8,160,128]{2,1,0:T(8,128)} %copy-done.3), channel_id=1, source_target_pairs={{0,1},{1,0},{2,3},{3,2},{4,5},{5,4},{6,7},{7,6},{8,9},{9,8},{10,11... | collective-permute-start | bytes 1966088 | tf_op jit(solution)/shard_map/ppermute | solution.py:1052
  53.3 40.5 %copy-start.8 = (s32[704]{0:T(1024)}, s32[704]{0:T(1024)S(1)}, u32[]{:S(2)}) copy-start(s32[704]{0:T(1024)S(1)} %reshape.203.slot_ref) | copy-start | bytes 8452
  89.7 1.3 copy-start.1
  93.8 5.0 %copy-start.11 = (s32[32,3]{0,1:T(4,128)S(1)}, s32[32,3]{0,1:T(4,128)}, u32[]{:S(2)}) copy-start(s32[32,3]{0,1:T(4,128)} %param.13) | copy-start | bytes 1156
  93.8 5.7 %copy-start = (f32[3,2048]{0,1:T(8,128)S(1)}, f32[3,2048]{0,1:T(8,128)}, u32[]{:S(2)}) copy-start(f32[3,2048]{0,1:T(8,128)} %copy.52) | copy-start | bytes 73732
  93.8 30.8 %all-to-all-start.3 = ((f32[8,520,128]{2,1,0:T(8,128)}), f32[8,520,128]{2,1,0:T(8,128)}, u32[]{:S(2)}, u32[]{:S(2)}) async-start(f32[8,520,128]{2,1,0:T(8,128)} %payload_rows.1), calls=%async_computation.3 | async-start | bytes 4259840 | tf_op jit(solution)/shard_map/all_to_all | solution.py:1072
  125.4 8.1 %copy-start.9 = (f32[8,8,128]{2,1,0:T(8,128)}, f32[8,8,128]{2,1,0:T(8,128)S(1)}, u32[]{:S(2)}) copy-start(f32[8,8,128]{2,1,0:T(8,128)S(1)} %slice.50.mine_ref) | copy-start | bytes 98308
  125.4 14.0 %collective-permute-start.6 = (f32[8,8,128]{2,1,0:T(8,128)S(1)}, f32[8,8,128]{2,1,0:T(8,128)S(1)}, u32[]{:S(2)}, u32[]{:S(2)}) collective-permute-start(f32[8,8,128]{2,1,0:T(8,128)S(1)} %slice.50.mine_ref), channel_id=1, source_target_pairs={{0,16},{2,18},{4,20},{6,22},{8,24},{10,26},{12,28},{14,30},{16,0},... | collective-permute-start | bytes 98312 | tf_op jit(solution)/shard_map/ppermute | solution.py:1092
  133.6 17.6 %all-to-all-start.4 = ((f32[16,32,128]{2,1,0:T(8,128)}), f32[16,32,128]{2,1,0:T(8,128)S(1)}, u32[]{:S(2)}, u32[]{:S(2)}) async-start(f32[16,32,128]{2,1,0:T(8,128)} %get-tuple-element.85), calls=%async_computation.4 | async-start | bytes 524288 | tf_op jit(solution)/shard_map/all_to_all | solution.py:1099
  139.5 0.6 copy-start.13
